TPU v7x, 32 devices: a whole 2x2x4 slice. The times are simulated.
32 devices in a mesh: dp: 8 (over z, y), cls: 4 (over x, core).
Axes of the slice: x: 2, y: 2, z: 4, core: 2. Of those that a mesh axis runs over, the one named last changes fastest.
Arguments:
- patches: bfloat16 [16384, 768], P(('dp', 'cls')), may hold values from -6 to 6
- image_ids: int32 [32, 512], P('dp'), may hold values from 0 to 16, as said below
- patch_place: int32 [32, 2, 512], P(('dp', 'cls')), may hold values from 0 to 33, as said below
- labels: int32 [32, 16], P('dp'), may hold values from 0 to 21842
- attn_w: float32 [3072, 768], P(('dp', 'cls')), may hold values from -0.21875 to 0.21875
- mlp_w: float32 [3072, 1536], P(('dp', 'cls')), may hold values from -0.21875 to 0.21875
- embed_w: float32 [1024, 768], P(('dp', 'cls'))
- vec_w: float32 [15, 768], replicated
- head_w: float32 [768, 21848], P('dp', 'cls')
- attn_mom: float32 [3072, 768], P(('dp', 'cls')), may hold values from -0.00015258789 to 0.00015258789
- mlp_mom: float32 [3072, 1536], P(('dp', 'cls')), may hold values from -0.00015258789 to 0.00015258789
- embed_m: float32 [1024, 768], P(('dp', 'cls')), may hold values from -0.00015258789 to 0.00015258789
- embed_v: float32 [1024, 768], P(('dp', 'cls')), may hold values from 5.069944e-14 to 8.1119107e-13
- vec_m: float32 [15, 768], replicated, may hold values from -0.00061035156 to 0.00061035156
- vec_v: float32 [15, 768], replicated, may hold values from 8.1119107e-13 to 1.2979057e-11
- head_m: float32 [768, 21848], P('dp', 'cls'), may hold values from -0.00015258789 to 0.00015258789
- head_v: float32 [768, 21848], P('dp', 'cls'), may hold values from 5.069944e-14 to 8.1119107e-13
Outputs:
- loss_sum: float32 [], replicated
- image_total: float32 [], replicated
- grad_norm: float32 [], replicated
- attn_out: float32 [3072, 768], P(('dp', 'cls'))
- attn_mom_out: float32 [3072, 768], P(('dp', 'cls'))
- attn_copy: bfloat16 [3072, 768], P(('dp', 'cls'))
- mlp_out: float32 [3072, 1536], P(('dp', 'cls'))
- mlp_mom_out: float32 [3072, 1536], P(('dp', 'cls'))
- mlp_copy: bfloat16 [3072, 1536], P(('dp', 'cls'))
- embed_out: float32 [1024, 768], P(('dp', 'cls'))
- embed_m_out: float32 [1024, 768], P(('dp', 'cls'))
- embed_v_out: float32 [1024, 768], P(('dp', 'cls'))
- embed_copy: bfloat16 [1024, 768], P(('dp', 'cls'))
- vec_out: float32 [15, 768], replicated
- vec_m_out: float32 [15, 768], replicated
- vec_v_out: float32 [15, 768], replicated
- vec_copy: bfloat16 [15, 768], replicated
- head_out: float32 [768, 21848], P('dp', 'cls')
- head_m_out: float32 [768, 21848], P('dp', 'cls')
- head_v_out: float32 [768, 21848], P('dp', 'cls')
- head_copy: bfloat16 [768, 21848], P('dp', 'cls')
Inputs may be any that keep to these rules, and one draw needn't show every extreme that they name: `image_ids`: in each pack the patches of an image stand together, images in slot order from slot 0, padding patches (slot 16) at the end; the last pack fills all 16 slots. `patch_place`: row and column of a patch within its image grid, 0 for padding patches.
All inputs are finite; a program needn't handle non-finite values.
Results may differ from a plain program's by a relative error of at most 0.015.
Values may be sent and summed in bfloat16 or wider, within the bound.
No kernel may reach another device: no remote copies, remote signals or barrier semaphores. Data moves between devices by JAX's collectives and lax.ppermute only.
A program may use at most 192 MiB of HBM per device.

v0:
```python
import math

import jax
import jax.numpy as jnp
from jax import lax
from jax.sharding import PartitionSpec as P

H = 12
CLASSES = 21843
STEP = 10


highest = lax.Precision.HIGHEST
newton_one = 3.4445
newton_two = -4.775
newton_three = 2.0315
clip_limit = 0.05
muon_rate = 0.3
decay_rate = 0.05
adam_rate = 0.01
vector_rate = 0.05
momentum_keep = 0.5
adam_first = 0.5
adam_second = 0.999


def from_root(value, axis, root):
    mine = lax.axis_index(axis) == root
    return lax.psum(jnp.where(mine, value, jnp.zeros_like(value)), axis)


def product(left_side, right_side):
    return jnp.dot(left_side, right_side, precision=highest)


def low_dot(left_side, right_side):
    return jnp.dot(left_side, right_side, preferred_element_type=jnp.float32)


def contract_rows(left_side, right_side):
    return lax.dot_general(
        left_side, right_side, (((0,), (0,)), ((), ())), preferred_element_type=jnp.float32
    )


def contract_cols(left_side, right_side):
    return lax.dot_general(
        left_side, right_side, (((1,), (1,)), ((), ())), preferred_element_type=jnp.float32
    )


def layer_norm(inputs, gain_row, shift_row):
    mean_row = jnp.mean(inputs, axis=-1, keepdims=True)
    centred = inputs - mean_row
    variance = jnp.mean(centred * centred, axis=-1, keepdims=True)
    return centred * lax.rsqrt(variance + 1e-06) * gain_row + shift_row


def exact_gelu(value):
    return jax.nn.gelu(value, approximate=False)


def attend(queries, key_rows, same_image):
    token_count, model_width = queries.shape
    head_shape = (token_count, H, model_width // H)
    scores = jnp.einsum(
        "qhd,khd->hqk",
        queries.reshape(head_shape),
        key_rows.reshape(head_shape),
        preferred_element_type=jnp.float32,
    ) * (model_width // H) ** (-0.5)
    return jnp.where(same_image[None], scores, -1e30)


def layer_forward(weights, vec_w, patches, image_index, position):
    attn_b, mlp_b, embed_b = weights
    token_count = patches.shape[0]
    model_width = attn_b.shape[1]
    patch_dim = patches.shape[1]
    grid_size = (embed_b.shape[0] - patch_dim) // 2
    head_shape = (token_count, H, model_width // H)
    embedded = (
        low_dot(patches, embed_b[:patch_dim])
        + vec_w[10]
        + jnp.take(embed_b[patch_dim : patch_dim + grid_size], position[0], axis=0).astype(
            jnp.float32
        )
        + jnp.take(embed_b[patch_dim + grid_size :], position[1], axis=0).astype(jnp.float32)
    )
    normed = layer_norm(embedded, vec_w[4], vec_w[5]).astype(jnp.bfloat16)
    queries = (low_dot(normed, attn_b[:model_width]) + vec_w[0]).astype(jnp.bfloat16)
    key_rows = low_dot(normed, attn_b[model_width : 2 * model_width]).astype(jnp.bfloat16)
    values = (low_dot(normed, attn_b[2 * model_width : 3 * model_width]) + vec_w[1]).astype(
        jnp.bfloat16
    )
    same_image = image_index[:, None] == image_index[None, :]
    scores = attend(queries, key_rows, same_image)
    row_max = jnp.max(scores, axis=-1, keepdims=True)
    exponents = jnp.exp(scores - row_max)
    row_total = jnp.sum(exponents, axis=-1, keepdims=True)
    probs_low = (exponents / row_total).astype(jnp.bfloat16)
    summary = row_max + jnp.log(row_total)
    mixed_out = (
        jnp.einsum(
            "hqk,khd->qhd",
            probs_low,
            values.reshape(head_shape),
            preferred_element_type=jnp.float32,
        )
        .reshape(token_count, model_width)
        .astype(jnp.bfloat16)
    )
    middle = embedded + low_dot(mixed_out, attn_b[3 * model_width :]) + vec_w[2]
    normed_two = layer_norm(middle, vec_w[6], vec_w[7]).astype(jnp.bfloat16)
    hidden = contract_cols(normed_two, mlp_b[:, :model_width]) + vec_w[11:].reshape(-1)
    active = exact_gelu(hidden).astype(jnp.bfloat16)
    final_rows = middle + low_dot(active, mlp_b[:, model_width:]) + vec_w[3]
    kept_rows = (
        embedded,
        normed,
        queries,
        key_rows,
        values,
        summary,
        mixed_out,
        middle,
        normed_two,
        hidden,
        active,
    )
    return (final_rows, kept_rows)


def layer_backward(weights, vec_w, patches, image_index, position, kept_rows, d_final):
    attn_b, mlp_b, embed_b = weights
    (
        embedded,
        normed,
        queries,
        key_rows,
        values,
        summary,
        mixed_out,
        middle,
        normed_two,
        hidden,
        active,
    ) = kept_rows
    token_count, model_width = embedded.shape
    patch_dim = patches.shape[1]
    grid_size = (embed_b.shape[0] - patch_dim) // 2
    head_shape = (token_count, H, model_width // H)
    d_out = d_final.astype(jnp.bfloat16)
    g_second_bias = jnp.sum(d_out.astype(jnp.float32), axis=0)
    g_second = contract_rows(active, d_out)
    d_active = contract_cols(d_out, mlp_b[:, model_width:])
    d_hidden = jax.vjp(exact_gelu, hidden)[1](d_active)[0].astype(jnp.bfloat16)
    g_first_bias = jnp.sum(d_hidden.astype(jnp.float32), axis=0)
    g_first = contract_rows(d_hidden, normed_two)
    d_normed_two = low_dot(d_hidden, mlp_b[:, :model_width])
    d_mid_norm, g_gain_two, g_shift_two = jax.vjp(layer_norm, middle, vec_w[6], vec_w[7])[1](
        d_normed_two
    )
    d_middle = d_final + d_mid_norm
    d_proj = d_middle.astype(jnp.bfloat16)
    g_out_bias = jnp.sum(d_proj.astype(jnp.float32), axis=0)
    g_out = contract_rows(mixed_out, d_proj)
    d_mixed = (
        contract_cols(d_proj, attn_b[3 * model_width :]).astype(jnp.bfloat16).reshape(head_shape)
    )
    same_image = image_index[:, None] == image_index[None, :]
    scores = attend(queries, key_rows, same_image)
    probs_full = jnp.exp(scores - summary)
    probs_low = probs_full.astype(jnp.bfloat16)
    d_values = jnp.einsum("hqk,qhd->khd", probs_low, d_mixed, preferred_element_type=jnp.float32)
    d_values = d_values.reshape(token_count, model_width).astype(jnp.bfloat16)
    d_probs = jnp.einsum(
        "qhd,khd->hqk", d_mixed, values.reshape(head_shape), preferred_element_type=jnp.float32
    )
    d_scores = probs_full * (d_probs - jnp.sum(probs_full * d_probs, axis=-1, keepdims=True))
    d_scores = d_scores.astype(jnp.bfloat16)
    scale = (model_width // H) ** (-0.5)
    d_queries = jnp.einsum(
        "hqk,khd->qhd", d_scores, key_rows.reshape(head_shape), preferred_element_type=jnp.float32
    )
    d_queries = (d_queries * scale).reshape(token_count, model_width).astype(jnp.bfloat16)
    d_keys = jnp.einsum(
        "hqk,qhd->khd", d_scores, queries.reshape(head_shape), preferred_element_type=jnp.float32
    )
    d_keys = (d_keys * scale).reshape(token_count, model_width).astype(jnp.bfloat16)
    g_query = contract_rows(normed, d_queries)
    g_key = contract_rows(normed, d_keys)
    g_value = contract_rows(normed, d_values)
    g_query_bias = jnp.sum(d_queries.astype(jnp.float32), axis=0)
    g_value_bias = jnp.sum(d_values.astype(jnp.float32), axis=0)
    d_normed = (
        contract_cols(d_queries, attn_b[:model_width])
        + contract_cols(d_keys, attn_b[model_width : 2 * model_width])
        + contract_cols(d_values, attn_b[2 * model_width : 3 * model_width])
    )
    d_emb_norm, g_gain_one, g_shift_one = jax.vjp(layer_norm, embedded, vec_w[4], vec_w[5])[1](
        d_normed
    )
    d_embed_low = (d_middle + d_emb_norm).astype(jnp.bfloat16)
    g_patch_bias = jnp.sum(d_embed_low.astype(jnp.float32), axis=0)
    grid_index = jnp.arange(grid_size)
    row_hot = (position[0][:, None] == grid_index[None]).astype(jnp.bfloat16)
    col_hot = (position[1][:, None] == grid_index[None]).astype(jnp.bfloat16)
    embed_grad = jnp.concatenate(
        [
            contract_rows(patches, d_embed_low),
            contract_rows(row_hot, d_embed_low),
            contract_rows(col_hot, d_embed_low),
        ],
        axis=0,
    )
    attn_grad = jnp.concatenate([g_query, g_key, g_value, g_out], axis=0)
    mlp_grad = jnp.concatenate([g_first, g_second], axis=1)
    small_rows = [
        g_query_bias,
        g_value_bias,
        g_out_bias,
        g_second_bias,
        g_gain_one,
        g_shift_one,
        g_gain_two,
        g_shift_two,
    ]
    return (attn_grad, mlp_grad, embed_grad, small_rows, g_patch_bias, g_first_bias)


def orthogonal(matrix):
    scaled = matrix / (jnp.sqrt(jnp.sum(matrix * matrix)) + 1e-07)
    for sweep_index in range(5):
        gram_matrix = jnp.dot(scaled.T, scaled, precision=highest)
        polynomial = newton_two * gram_matrix + newton_three * jnp.dot(
            gram_matrix, gram_matrix, precision=highest
        )
        scaled = newton_one * scaled + jnp.dot(scaled, polynomial, precision=highest)
    return scaled


def adam_step(weight, first_moment, second_moment, gradient, step_rate):
    first_moment = adam_first * first_moment + (1.0 - adam_first) * gradient
    second_moment = adam_second * second_moment + (1.0 - adam_second) * gradient * gradient
    first_hat = first_moment / (1.0 - adam_first**STEP)
    second_hat = second_moment / (1.0 - adam_second**STEP)
    weight = weight * (1.0 - step_rate * decay_rate) - step_rate * first_hat / (
        jnp.sqrt(second_hat) + 1e-08
    )
    return (weight, first_moment, second_moment)


def on_device(
    patches,
    image_ids,
    patch_place,
    labels,
    attn_w,
    mlp_w,
    embed_w,
    vec_w,
    head_w,
    attn_mom,
    mlp_mom,
    embed_m,
    embed_v,
    vec_m,
    vec_v,
    head_m,
    head_v,
):
    groups = lax.axis_size("cls")
    member_index = lax.axis_index("cls")
    owner_index = lax.axis_index("dp")
    flat_index = owner_index * groups + member_index
    model_width = vec_w.shape[1]
    slot_count = labels.shape[1]
    weights = (
        lax.all_gather(attn_w.astype(jnp.bfloat16), ("dp", "cls"), axis=0, tiled=True),
        lax.all_gather(mlp_w.astype(jnp.bfloat16), ("dp", "cls"), axis=0, tiled=True),
        lax.all_gather(embed_w.astype(jnp.bfloat16), ("dp", "cls"), axis=0, tiled=True),
    )
    head_b = lax.all_gather(head_w.astype(jnp.bfloat16), "dp", axis=0, tiled=True)
    image_index = lax.dynamic_index_in_dim(image_ids, member_index, 0, keepdims=False)
    position = patch_place[0]
    final_rows, kept_rows = layer_forward(weights, vec_w, patches, image_index, position)
    closing, close_pull = jax.vjp(layer_norm, final_rows, vec_w[8], vec_w[9])
    member = (image_index[None, :] == jnp.arange(slot_count)[:, None]).astype(jnp.float32)
    divisor = jnp.maximum(jnp.sum(member, axis=1), 1.0)[:, None]
    pooled = product(member, closing) / divisor
    group_pooled = lax.all_gather(pooled.astype(jnp.bfloat16), "cls", axis=0, tiled=True)
    logits = low_dot(group_pooled, head_b)
    shard_width = head_b.shape[1]
    columns = member_index * shard_width + jnp.arange(shard_width)
    logits = jnp.where((columns < CLASSES)[None], logits, -1e30)
    onehot = (columns[None, :] == labels.reshape(-1)[:, None]).astype(jnp.float32)
    target_part = jnp.sum(onehot * logits, axis=1)
    row_max = lax.pmax(jnp.max(logits, axis=1), "cls")
    exp_sums, target = lax.psum(
        (jnp.sum(jnp.exp(logits - row_max[:, None]), axis=1), target_part), "cls"
    )
    normaliser = row_max + jnp.log(exp_sums)
    group_counts = jnp.sum(
        (image_ids[:, None, :] == jnp.arange(slot_count)[None, :, None]).astype(jnp.float32), axis=2
    )
    valid = group_counts.reshape(-1) > 0.5
    loss_part = jnp.sum(jnp.where(valid, normaliser - target, 0.0))
    loss_sum, image_total = lax.psum((loss_part, jnp.sum(valid.astype(jnp.float32))), "dp")
    probs_class = jnp.exp(logits - normaliser[:, None])
    d_logits = (jnp.where(valid[:, None], probs_class - onehot, 0.0) / image_total).astype(
        jnp.bfloat16
    )
    d_pooled = lax.psum_scatter(
        contract_cols(d_logits, head_b).astype(jnp.bfloat16), "cls", scatter_dimension=0, tiled=True
    ).astype(jnp.float32)
    head_grad = lax.psum_scatter(
        contract_rows(group_pooled, d_logits).astype(jnp.bfloat16),
        "dp",
        scatter_dimension=0,
        tiled=True,
    ).astype(jnp.float32)
    d_closing = product(member.T, d_pooled / divisor)
    d_final, g_gain_final, g_shift_final = close_pull(d_closing)
    attn_grad, mlp_grad, embed_grad, small_rows, g_patch_bias, g_first_bias = layer_backward(
        weights, vec_w, patches, image_index, position, kept_rows, d_final
    )
    vec_grad = jnp.concatenate(
        [
            jnp.stack(small_rows + [g_gain_final, g_shift_final, g_patch_bias]),
            g_first_bias.reshape(-1, model_width),
        ],
        axis=0,
    )
    attn_sum, mlp_sum, embed_sum = (
        lax.psum_scatter(attn_grad, ("dp", "cls"), scatter_dimension=0, tiled=True),
        lax.psum_scatter(mlp_grad, ("dp", "cls"), scatter_dimension=0, tiled=True),
        lax.psum_scatter(embed_grad, ("dp", "cls"), scatter_dimension=0, tiled=True),
    )
    local_squares = (
        jnp.sum(attn_sum * attn_sum)
        + jnp.sum(mlp_sum * mlp_sum)
        + jnp.sum(embed_sum * embed_sum)
        + jnp.sum(head_grad * head_grad)
    )
    vec_sum, all_squares = lax.psum((vec_grad, local_squares), ("dp", "cls"))
    grad_norm = jnp.sqrt(all_squares + jnp.sum(vec_sum * vec_sum))
    factor = jnp.minimum(1.0, clip_limit / (grad_norm + 1e-06))
    attn_mom_out = momentum_keep * attn_mom + factor * attn_sum
    mlp_mom_out = momentum_keep * mlp_mom + factor * mlp_sum
    attn_full, mlp_full = (
        lax.all_gather(attn_mom_out, ("dp", "cls"), axis=0, tiled=True),
        lax.all_gather(mlp_mom_out, ("dp", "cls"), axis=0, tiled=True),
    )
    attn_pick = lax.dynamic_slice_in_dim(
        attn_full, jnp.minimum(owner_index, 3) * model_width, model_width, 0
    )
    attn_result = lax.cond(owner_index < 4, orthogonal, jnp.zeros_like, attn_pick)
    mlp_pick = lax.dynamic_slice_in_dim(
        mlp_full, jnp.clip(owner_index - 4, 0, 1) * model_width, model_width, 1
    )
    mlp_result = lax.cond(
        (owner_index >= 4) & (owner_index < 6), orthogonal, jnp.zeros_like, mlp_pick
    )
    attn_rows = attn_w.shape[0]
    mlp_rows = mlp_w.shape[0]
    attn_all = jnp.concatenate(
        [
            from_root(attn_result.astype(jnp.bfloat16), "dp", slot_index).astype(attn_result.dtype)
            for slot_index in range(4)
        ],
        axis=0,
    )
    mlp_all = jnp.concatenate(
        [
            from_root(mlp_result.astype(jnp.bfloat16), "dp", 4 + slot_index).astype(
                mlp_result.dtype
            )
            for slot_index in range(2)
        ],
        axis=1,
    )
    attn_dir = lax.dynamic_slice_in_dim(attn_all, flat_index * attn_rows, attn_rows, 0)
    mlp_dir = lax.dynamic_slice_in_dim(mlp_all, flat_index * mlp_rows, mlp_rows, 0)
    mlp_scale = math.sqrt(mlp_full.shape[0] / model_width)
    attn_out = attn_w * (1.0 - muon_rate * decay_rate) - muon_rate * attn_dir
    mlp_out = mlp_w * (1.0 - muon_rate * decay_rate) - muon_rate * mlp_scale * mlp_dir
    embed_out, embed_m_out, embed_v_out = adam_step(
        embed_w, embed_m, embed_v, factor * embed_sum, adam_rate
    )
    vec_out, vec_m_out, vec_v_out = adam_step(vec_w, vec_m, vec_v, factor * vec_sum, vector_rate)
    head_out, head_m_out, head_v_out = adam_step(
        head_w, head_m, head_v, factor * head_grad, adam_rate
    )
    return (
        loss_sum,
        image_total,
        grad_norm,
        attn_out,
        attn_mom_out,
        attn_out.astype(jnp.bfloat16),
        mlp_out,
        mlp_mom_out,
        mlp_out.astype(jnp.bfloat16),
        embed_out,
        embed_m_out,
        embed_v_out,
        embed_out.astype(jnp.bfloat16),
        vec_out,
        vec_m_out,
        vec_v_out,
        vec_out.astype(jnp.bfloat16),
        head_out,
        head_m_out,
        head_v_out,
        head_out.astype(jnp.bfloat16),
    )


def solution(mesh):
    return jax.shard_map(
        on_device,
        mesh=mesh,
        in_specs=(
            P(("dp", "cls"), None),
            P("dp", None),
            P(("dp", "cls"), None, None),
            P("dp", None),
            P(("dp", "cls"), None),
            P(("dp", "cls"), None),
            P(("dp", "cls"), None),
            P(),
            P("dp", "cls"),
            P(("dp", "cls"), None),
            P(("dp", "cls"), None),
            P(("dp", "cls"), None),
            P(("dp", "cls"), None),
            P(),
            P(),
            P("dp", "cls"),
            P("dp", "cls"),
        ),
        out_specs=(
            P(),
            P(),
            P(),
            P(("dp", "cls"), None),
            P(("dp", "cls"), None),
            P(("dp", "cls"), None),
            P(("dp", "cls"), None),
            P(("dp", "cls"), None),
            P(("dp", "cls"), None),
            P(("dp", "cls"), None),
            P(("dp", "cls"), None),
            P(("dp", "cls"), None),
            P(("dp", "cls"), None),
            P(),
            P(),
            P(),
            P(),
            P("dp", "cls"),
            P("dp", "cls"),
            P("dp", "cls"),
            P("dp", "cls"),
        ),
        check_vma=False,
    )
```

profile of v0, /device:TPU:0, one launch (start us, length us, event | category | flops | bytes accessed | tf_op | source)
XLA Modules:
  0.0 2104.5 jit_solution(2252775477748295780)
XLA Ops:
  19.2 50.0 %all-gather.7.cloned.1.call-done = bf16[1024,768]{1,0:T(8,128)(2,1)} async-done(((bf16[32,768]{1,0:T(8,128)(2,1)}), bf16[1024,768]{1,0:T(8,128)(2,1)}) %all-gather.7.cloned.1.call-update) | async-done | bytes 1572880 | tf_op jit(solution)/shard_map/all_gather | solution.py:282
  78.1 57.0 %all-gather.9.cloned.1.call-done = bf16[3072,768]{1,0:T(8,128)(2,1)} async-done(((bf16[96,768]{1,0:T(8,128)(2,1)}), bf16[3072,768]{1,0:T(8,128)(2,1)}) %all-gather.9.cloned.1.call-update) | async-done | bytes 4718608 | tf_op jit(solution)/shard_map/all_gather | solution.py:280
  157.8 4.9 fusion.131
  166.7 52.9 %all-gather.11.cloned.1.call-done = bf16[3072,1536]{1,0:T(8,128)(2,1)} async-done(((bf16[96,1536]{1,0:T(8,128)(2,1)}), bf16[3072,1536]{1,0:T(8,128)(2,1)}) %all-gather.11.cloned.1.call-update) | async-done | bytes 9437200 | tf_op jit(solution)/shard_map/all_gather | solution.py:281
  219.6 20.8 multiply_convert_fusion.1
  245.3 5.3 all_gather.24
  250.6 96.0 %all-gather.13.cloned.1.call-done = bf16[768,5462]{1,0:T(8,128)(2,1)} async-done(((bf16[96,5462]{1,0:T(8,128)(2,1)}), bf16[768,5462]{1,0:T(8,128)(2,1)}) %all-gather.13.cloned.1.call-update) | async-done | bytes 8389648 | tf_op jit(solution)/shard_map/all_gather | solution.py:284
  346.6 6.7 fusion.201
  353.3 6.8 pmax.7
  362.4 6.7 all-reduce.2
  371.0 19.6 all-reduce.1
  390.6 7.6 convolution_convert_fusion.3
  399.7 14.5 reduce-scatter.8.cloned.1.call-done
  420.5 10.0 convert_reduce_fusion
  442.0 8.8 convert_reduce_fusion.4
  450.8 9.8 multiply_reduce_fusion.2
  460.6 7.2 multiply_convert_fusion
  490.8 6.4 convolution_convert_fusion
  498.3 5.0 fusion.223
  506.3 7.1 pad_maximum_fusion
  513.4 18.7 copy.90
  533.2 47.7 %reduce-scatter.12.cloned.1.call-done = f32[32,768]{1,0:T(8,128)} async-done(((f32[1024,768]{1,0:T(8,128)}), f32[32,768]{1,0:T(8,128)}) %reduce-scatter.12.cloned.1.call-update) | async-done | bytes 98320 | tf_op jit(solution)/shard_map/reduce_scatter | solution.py:338
  582.4 139.1 %reduce-scatter.10.cloned.1.call-done = f32[96,768]{1,0:T(8,128)} async-done(((f32[3072,768]{1,0:T(8,128)}), f32[96,768]{1,0:T(8,128)}) %reduce-scatter.10.cloned.1.call-update) | async-done | bytes 294928 | tf_op jit(solution)/shard_map/reduce_scatter | solution.py:336
  723.2 152.1 %reduce-scatter.14.cloned.1.call-done = bf16[96,5462]{1,0:T(8,128)(2,1)} async-done(((bf16[768,5462]{1,0:T(8,128)(2,1)}), bf16[96,5462]{1,0:T(8,128)(2,1)}) %reduce-scatter.14.cloned.1.call-update) | async-done | bytes 1048720 | tf_op jit(solution)/shard_map/reduce_scatter | solution.py:317
  877.7 209.7 %reduce-scatter.16.cloned.1.call-done = f32[96,1536]{1,0:T(8,128)} async-done(((f32[3072,1536]{1,0:T(8,128)}), f32[96,1536]{1,0:T(8,128)}) %reduce-scatter.16.cloned.1.call-update) | async-done | bytes 589840
  1092.1 39.7 %all-reduce = (f32[]{:T(128)}, f32[15,768]{1,0:T(8,128)S(1)}) all-reduce(f32[]{:T(128)S(6)} %add.451, f32[15,768]{1,0:T(8,128)S(1)} %concatenate.27), channel_id=1, replica_groups=mesh['dp'=8,'cls'=4] {'dp','cls'}, use_global_device_ids=true, to_apply=%region_36.38 | all-reduce | flops 11521 | bytes 92168 | tf_op jit(solution)/shard_map/psum | solution.py:346
  1136.2 80.2 %all-gather.15.cloned.1.call-done = f32[3072,768]{1,0:T(8,128)} async-done(((f32[96,768]{1,0:T(8,128)}), f32[3072,768]{1,0:T(8,128)}) %all-gather.15.cloned.1.call-update) | async-done | bytes 9437200 | tf_op jit(solution)/shard_map/all_gather | solution.py:352
  1216.4 102.1 %conditional.2 = (bf16[768,768]{1,0:T(8,128)(2,1)S(1)}) conditional(s32[]{:T(128)} %convert_element_type.250, () %tuple.39, (s32[]{:T(128)}, f32[3072,768]{1,0:T(8,128)}) %tuple.40), branch_computations={%region_51.53_spmd, %region_52.55_spmd} | conditional | flops 81555554304 | bytes 126224560 | solution.py:358
  1220.5 8.9 fusion.40
  1229.4 6.0 fusion.202
  1235.4 6.4 multiply_add_fusion.3
  1241.8 6.6 fusion.203
  1248.4 6.2 fusion.204
  1254.6 6.2 multiply_add_fusion.2
  1260.8 7.0 fusion.205
  1267.8 6.0 fusion.206
  1273.8 6.4 multiply_add_fusion.1
  1280.2 6.6 fusion.207
  1286.7 6.4 fusion.208
  1293.1 6.2 multiply_add_fusion
  1299.3 6.8 fusion.209
  1306.1 6.0 fusion.210
  1312.1 6.1 add_convert_fusion
  1320.7 22.4 %all-gather.17.cloned.1.call-done = f32[3072,1536]{1,0:T(8,128)} async-done(((f32[96,1536]{1,0:T(8,128)}), f32[3072,1536]{1,0:T(8,128)}) %all-gather.17.cloned.1.call-update) | async-done | bytes 18874384 | tf_op jit(solution)/shard_map/all_gather | solution.py:353
  1343.2 5.8 conditional.3
  1349.0 6.6 broadcast_select_fusion
  1358.0 7.4 fusion.184
  1365.4 727.0 %all-reduce.6.cloned.1.call-done = (bf16[768,768]{1,0:T(8,128)(2,1)}, bf16[768,768]{1,0:T(8,128)(2,1)}, bf16[768,768]{1,0:T(8,128)(2,1)}, bf16[768,768]{1,0:T(8,...) async-done(((bf16[768,768]{1,0:T(8,128)(2,1)}, bf16[768,768]{1,0:T(8,128)(2,1)}, bf16[768,768]{1,0:T(8,128)(2,1)}, bf16[768,768]{1,0:T(8,128)(2,1)}, ...) | async-done | bytes 14155792 | tf_op jit(solution)/shard_map/psum | solution.py:29
  (349 shorter events, 127.6 us)
Async XLA Ops:
  7.2 67.8 %copy-start = (bf16[512,768]{1,0:T(8,128)(2,1)S(1)}, bf16[512,768]{1,0:T(8,128)(2,1)}, u32[]{:S(2)}) copy-start(bf16[512,768]{1,0:T(8,128)(2,1)} %param.23) | copy-start | bytes 2359300
  7.2 61.9 %all-gather.7.cloned.1.call-start = ((), (), s32[]{:S(2)}) async-start(), calls=%async_computation.5 | async-start | bytes 1622016 | tf_op jit(solution)/shard_map/all_gather | solution.py:282
  8.9 126.3 %all-gather.9.cloned.1.call-start = ((), (), s32[]{:S(2)}) async-start(), calls=%async_computation.6 | async-start | bytes 4866048 | tf_op jit(solution)/shard_map/all_gather | solution.py:280
  10.6 209.0 %all-gather.11.cloned.1.call-start = ((), (), s32[]{:S(2)}) async-start(), calls=%async_computation.7 | async-start | bytes 9732096 | tf_op jit(solution)/shard_map/all_gather | solution.py:281
  12.5 334.1 %all-gather.13.cloned.1.call-start = ((), (), s32[]{:S(2)}) async-start(), calls=%async_computation.8 | async-start | bytes 9510912 | tf_op jit(solution)/shard_map/all_gather | solution.py:284
  15.2 398.9 %reduce-scatter.8.cloned.1.call-start = ((), (), s32[]{:S(2)}) async-start(), calls=%async_computation.9 | async-start | bytes 122880 | tf_op jit(solution)/shard_map/reduce_scatter | solution.py:314
  16.7 202.9 %copy-start.70 = (f32[3072]{0:T(1024)}, f32[3072]{0:T(1024)S(1)}, u32[]{:S(2)}) copy-start(f32[3072]{0:T(1024)S(1)} %add.432) | copy-start | bytes 36868
  17.4 54.9 %copy-start.51 = (s32[1,1,512]{2,1,0:T(1,128)}, s32[1,1,512]{2,1,0:T(1,128)S(1)}, u32[]{:S(2)}) copy-start(s32[1,1,512]{2,1,0:T(1,128)S(1)} %get-tuple-element.284) | copy-start | bytes 6148
  17.4 54.9 %copy-start.53 = (s32[1,1,512]{2,1,0:T(1,128)}, s32[1,1,512]{2,1,0:T(1,128)S(1)}, u32[]{:S(2)}) copy-start(s32[1,1,512]{2,1,0:T(1,128)S(1)} %get-tuple-element.285) | copy-start | bytes 6148
  18.9 200.7 %copy-start.65 = (f32[768]{0:T(1024)}, f32[768]{0:T(1024)S(1)}, u32[]{:S(2)}) copy-start(f32[768]{0:T(1024)S(1)} %get-tuple-element.222) | copy-start | bytes 9220
  18.9 200.7 %copy-start.79 = (f32[768]{0:T(1024)}, f32[768]{0:T(1024)S(1)}, u32[]{:S(2)}) copy-start(f32[768]{0:T(1024)S(1)} %get-tuple-element.221) | copy-start | bytes 9220
  18.9 224.7 %copy-start.68 = (f32[768]{0:T(1024)}, f32[768]{0:T(1024)S(1)}, u32[]{:S(2)}) copy-start(f32[768]{0:T(1024)S(1)} %get-tuple-element.219) | copy-start | bytes 9220
  18.9 224.6 %copy-start.90 = (f32[16]{0:T(128)}, f32[16]{0:T(128)S(1)}, u32[]{:S(2)}) copy-start(f32[16]{0:T(128)S(1)} %broadcast_maximum_fusion) | copy-start | bytes 196
  77.8 60.3 %copy-start.58 = (f32[512]{0:T(512)}, f32[512]{0:T(512)S(1)}, u32[]{:S(2)}) copy-start(f32[512]{0:T(512)S(1)} %multiply_reduce_fusion.11) | copy-start | bytes 6148
  78.1 67.5 %copy-start.7 = (bf16[512,768]{1,0:T(8,128)(2,1)}, bf16[512,768]{1,0:T(8,128)(2,1)S(1)}, u32[]{:S(2)}) copy-start(bf16[512,768]{1,0:T(8,128)(2,1)S(1)} %add_convert_fusion.7) | copy-start | bytes 2359300
  165.2 75.2 %copy-start.55 = (f32[512]{0:T(512)}, f32[512]{0:T(512)S(1)}, u32[]{:S(2)}) copy-start(f32[512]{0:T(512)S(1)} %broadcast_multiply_fusion.3) | copy-start | bytes 6148
  166.6 73.8 %copy-start.60 = (f32[512]{0:T(512)}, f32[512]{0:T(512)S(1)}, u32[]{:S(2)}) copy-start(f32[512]{0:T(512)S(1)} %multiply_reduce_fusion.10) | copy-start | bytes 6148
  166.7 73.7 %copy-start.73 = (f32[512]{0:T(512)}, f32[512]{0:T(512)S(1)}, u32[]{:S(2)}) copy-start(f32[512]{0:T(512)S(1)} %fusion.172) | copy-start | bytes 6148
  219.6 20.9 copy-start.14
  219.6 20.9 copy-start.89
  398.2 182.6 %reduce-scatter.12.cloned.1.call-start = ((), (), s32[]{:S(2)}) async-start(), calls=%async_computation.11 | async-start | bytes 3244032 | tf_op jit(solution)/shard_map/reduce_scatter | solution.py:338
  414.1 16.4 slice-start.13
  420.5 10.1 copy-start.34
  420.5 10.1 copy-start.15
  420.5 10.1 copy-start.56
  420.5 10.1 copy-start.66
  420.5 10.1 copy-start.74
  420.5 10.1 slice-start.14
  420.5 10.1 slice-start.15
  442.0 8.8 copy-start.19
  442.0 8.8 copy-start.20
  442.0 18.6 slice-start
  442.0 18.6 slice-start.1
  450.8 22.1 %copy-start.21 = (bf16[12,64,512]{2,1,0:T(8,128)(2,1)}, bf16[12,64,512]{2,1,0:T(8,128)(2,1)S(1)}, u32[]{:S(2)}) copy-start(bf16[12,64,512]{2,1,0:T(8,128)(2,1)S(1)} %get-tuple-element.305) | copy-start | bytes 2359300
  450.8 9.8 slice-start.2
  479.6 241.8 %reduce-scatter.10.cloned.1.call-start = ((), (), s32[]{:S(2)}) async-start(), calls=%async_computation.10 | async-start | bytes 9732096 | tf_op jit(solution)/shard_map/reduce_scatter | solution.py:336
  489.4 385.9 %reduce-scatter.14.cloned.1.call-start = ((), (), s32[]{:S(2)}) async-start(), calls=%async_computation.12 | async-start | bytes 9510912 | tf_op jit(solution)/shard_map/reduce_scatter | solution.py:317
  497.3 590.1 %reduce-scatter.16.cloned.1.call-start = ((), (), s32[]{:S(2)}) async-start(), calls=%async_computation.15 | async-start | bytes 19464192
  532.2 601.6 %copy-start.39 = (f32[96,768]{1,0:T(8,128)S(1)}, f32[96,768]{1,0:T(8,128)}, u32[]{:S(2)}) copy-start(f32[96,768]{1,0:T(8,128)} %param.32) | copy-start | bytes 884740
  532.2 684.2 %all-gather.15.cloned.1.call-start = ((), (), s32[]{:S(2)}) async-start(), calls=%async_computation.13 | async-start | bytes 9732096 | tf_op jit(solution)/shard_map/all_gather | solution.py:352
  582.4 552.3 %copy-start.36 = (f32[96,1536]{1,0:T(8,128)S(1)}, f32[96,1536]{1,0:T(8,128)}, u32[]{:S(2)}) copy-start(f32[96,1536]{1,0:T(8,128)} %param.33) | copy-start | bytes 1769476
  721.4 412.4 %copy-start.27 = (f32[96,768]{1,0:T(8,128)S(1)}, f32[96,768]{1,0:T(8,128)}, u32[]{:S(2)}) copy-start(f32[96,768]{1,0:T(8,128)} %reduce-scatter.10.cloned.1.call-done) | copy-start | bytes 884740
  1134.6 208.6 %all-gather.17.cloned.1.call-start = ((), (), s32[]{:S(2)}) async-start(), calls=%async_computation.14 | async-start | bytes 19464192 | tf_op jit(solution)/shard_map/all_gather | solution.py:353
  1136.1 956.2 %all-reduce.6.cloned.1.call-start = ((), (), s32[]{:S(2)}) async-start(), calls=%async_computation.16 | async-start | bytes 28311552 | tf_op jit(solution)/shard_map/psum | solution.py:29
  1216.8 18.6 slice-start.8
  1220.5 15.0 slice-start.9
  1220.5 15.0 slice-start.10
  1358.0 734.4 %copy-start.25 = (f32[96,1536]{1,0:T(8,128)S(1)}, f32[96,1536]{1,0:T(8,128)}, u32[]{:S(2)}) copy-start(f32[96,1536]{1,0:T(8,128)} %param.28) | copy-start | bytes 1769476
  (69 other events, 157.4 us)
Sparse Core Ops, SparseCore 0:
  11.5 57.6 all-gather.6
  72.6 62.5 all-gather.8
  138.7 80.8 all-gather.10
  222.2 124.3 all-gather.12
  398.3 15.7 reduce-scatter.7
  479.7 101.0 reduce-scatter.11
  586.8 134.6 reduce-scatter.9
  725.5 149.7 reduce-scatter.13
  881.7 205.6 reduce-scatter.15
  1134.7 81.6 all-gather.14
  1219.9 123.2 all-gather.16
  1355.8 736.5 all-reduce.5
where the time goes:
time: 2120 us; the launch traced here: 2100 us
  waiting for transfers between devices  1650 us (78%)
  matrix products  222 us (10%)
  blocking collectives  78 us (4%)
  other arithmetic  76.8 us (4%)
  local copies, waits for them, and re-layouts  52.4 us (2%)
    psum x1, waiting for transfers between devices, from_root(): return lax.psum(jnp.where(mine, value, jnp.zeros_like(value)), axis)  727 us
    unnamed x13, waiting for transfers between devices  210 us
    reduce_scatter x1, waiting for transfers between devices, on_device(): lax.psum_scatter(contract_rows(group_pooled, d_logits).astype(jnp.bfloat1...  152 us
    reduce_scatter x1, waiting for transfers between devices, on_device(): lax.psum_scatter(attn_grad, ('dp', 'cls'), scatter_dimension=0, tiled=True)  139 us
    all_gather x1, waiting for transfers between devices, on_device(): lax.all_gather(head_w.astype(jnp.bfloat16), 'dp', axis=0, tiled=True)  96 us
    all_gather x1, waiting for transfers between devices, on_device(): lax.all_gather(attn_mom_out, ('dp', 'cls'), axis=0, tiled=True)  80.2 us
    all_gather x1, waiting for transfers between devices, on_device(): lax.all_gather(attn_w.astype(jnp.bfloat16), ('dp', 'cls'), axis=0, tiled=...  57 us
    all_gather x1, waiting for transfers between devices, on_device(): lax.all_gather(mlp_w.astype(jnp.bfloat16), ('dp', 'cls'), axis=0, tiled=T...  52.9 us
  transfers between devices with their start and end apart: 12, of which 12 were waited for; matrix products, arithmetic and copies ran while one was open for 11% of the time, Pallas kernels for 0%

commit v1 on v0

--- a/solution.py
+++ b/solution.py
@@ -24,9 +24,28 @@
 adam_second = 0.999
 
 
-def from_root(value, axis, root):
-    mine = lax.axis_index(axis) == root
-    return lax.psum(jnp.where(mine, value, jnp.zeros_like(value)), axis)
+AXES = ("dp", "cls")
+
+
+def swap(value, count, masks):
+    return lax.ppermute(value, AXES, [(i, i ^ masks[i & 1]) for i in range(count)])
+
+
+def pick(value, index, axis):
+    return lax.dynamic_index_in_dim(value, index, axis, keepdims=False)
+
+
+def codes(masks):
+    found = [0]
+    for mask in masks:
+        found = found + [code ^ mask for code in found]
+    return found
+
+
+def ordered_pair(bit, mine, other, axis):
+    return jnp.where(
+        bit == 0, jnp.stack([mine, other], axis=axis), jnp.stack([other, mine], axis=axis)
+    )
 
 
 def product(left_side, right_side):
@@ -72,8 +91,8 @@
     return jnp.where(same_image[None], scores, -1e30)
 
 
-def layer_forward(weights, vec_w, patches, image_index, position):
-    attn_b, mlp_b, embed_b = weights
+def layer_forward(weights, vec_w, first_bias, patches, image_index, position):
+    attn_b, embed_b, mlp_parts = weights
     token_count = patches.shape[0]
     model_width = attn_b.shape[1]
     patch_dim = patches.shape[1]
@@ -112,9 +131,12 @@
     )
     middle = embedded + low_dot(mixed_out, attn_b[3 * model_width :]) + vec_w[2]
     normed_two = layer_norm(middle, vec_w[6], vec_w[7]).astype(jnp.bfloat16)
-    hidden = contract_cols(normed_two, mlp_b[:, :model_width]) + vec_w[11:].reshape(-1)
-    active = exact_gelu(hidden).astype(jnp.bfloat16)
-    final_rows = middle + low_dot(active, mlp_b[:, model_width:]) + vec_w[3]
+    final_rows = middle + vec_w[3]
+    hidden, active = [], []
+    for part, bias in zip(mlp_parts, first_bias):
+        hidden.append(contract_cols(normed_two, part[:, :model_width]) + bias)
+        active.append(exact_gelu(hidden[-1]).astype(jnp.bfloat16))
+        final_rows = final_rows + low_dot(active[-1], part[:, model_width:])
     kept_rows = (
         embedded,
         normed,
@@ -131,37 +153,28 @@
     return (final_rows, kept_rows)
 
 
-def layer_backward(weights, vec_w, patches, image_index, position, kept_rows, d_final):
-    attn_b, mlp_b, embed_b = weights
-    (
-        embedded,
-        normed,
-        queries,
-        key_rows,
-        values,
-        summary,
-        mixed_out,
-        middle,
-        normed_two,
-        hidden,
-        active,
-    ) = kept_rows
+def mlp_backward(mlp_parts, normed_two, hidden, active, d_out, send):
+    model_width = d_out.shape[1]
+    d_normed_two = 0.0
+    bias_grads, grads = [None] * 4, [None] * 4
+    for index in (2, 3, 1, 0):
+        part = mlp_parts[index]
+        d_active = contract_cols(d_out, part[:, model_width:])
+        d_hidden = jax.vjp(exact_gelu, hidden[index])[1](d_active)[0].astype(jnp.bfloat16)
+        bias_grads[index] = jnp.sum(d_hidden.astype(jnp.float32), axis=0)
+        both = (contract_rows(d_hidden, normed_two), contract_rows(active[index], d_out))
+        grads[index] = send(index, both, grads)
+        d_normed_two = d_normed_two + low_dot(d_hidden, part[:, :model_width])
+    return d_normed_two, jnp.stack(bias_grads), grads[0]
+
+
+def attention_backward(weights, vec_w, patches, image_index, position, kept_rows, d_middle):
+    attn_b, embed_b = weights
+    embedded, normed, queries, key_rows, values, summary, mixed_out = kept_rows
     token_count, model_width = embedded.shape
     patch_dim = patches.shape[1]
     grid_size = (embed_b.shape[0] - patch_dim) // 2
     head_shape = (token_count, H, model_width // H)
-    d_out = d_final.astype(jnp.bfloat16)
-    g_second_bias = jnp.sum(d_out.astype(jnp.float32), axis=0)
-    g_second = contract_rows(active, d_out)
-    d_active = contract_cols(d_out, mlp_b[:, model_width:])
-    d_hidden = jax.vjp(exact_gelu, hidden)[1](d_active)[0].astype(jnp.bfloat16)
-    g_first_bias = jnp.sum(d_hidden.astype(jnp.float32), axis=0)
-    g_first = contract_rows(d_hidden, normed_two)
-    d_normed_two = low_dot(d_hidden, mlp_b[:, :model_width])
-    d_mid_norm, g_gain_two, g_shift_two = jax.vjp(layer_norm, middle, vec_w[6], vec_w[7])[1](
-        d_normed_two
-    )
-    d_middle = d_final + d_mid_norm
     d_proj = d_middle.astype(jnp.bfloat16)
     g_out_bias = jnp.sum(d_proj.astype(jnp.float32), axis=0)
     g_out = contract_rows(mixed_out, d_proj)
@@ -215,29 +228,49 @@
         axis=0,
     )
     attn_grad = jnp.concatenate([g_query, g_key, g_value, g_out], axis=0)
-    mlp_grad = jnp.concatenate([g_first, g_second], axis=1)
-    small_rows = [
-        g_query_bias,
-        g_value_bias,
-        g_out_bias,
-        g_second_bias,
-        g_gain_one,
-        g_shift_one,
-        g_gain_two,
-        g_shift_two,
-    ]
-    return (attn_grad, mlp_grad, embed_grad, small_rows, g_patch_bias, g_first_bias)
-
-
-def orthogonal(matrix):
-    scaled = matrix / (jnp.sqrt(jnp.sum(matrix * matrix)) + 1e-07)
-    for sweep_index in range(5):
-        gram_matrix = jnp.dot(scaled.T, scaled, precision=highest)
-        polynomial = newton_two * gram_matrix + newton_three * jnp.dot(
-            gram_matrix, gram_matrix, precision=highest
-        )
-        scaled = newton_one * scaled + jnp.dot(scaled, polynomial, precision=highest)
-    return scaled
+    small = (g_query_bias, g_value_bias, g_out_bias, g_gain_one, g_shift_one, g_patch_bias)
+    return (attn_grad, embed_grad, small)
+
+
+def gram_of(parts):
+    total = contract_rows(parts[0], parts[0])
+    for part in parts[1:]:
+        total = total + contract_rows(part, part)
+    return total
+
+
+def update_of(gram_matrix):
+    low_gram = gram_matrix.astype(jnp.bfloat16)
+    return (newton_two * gram_matrix + newton_three * low_dot(low_gram, low_gram)).astype(
+        jnp.bfloat16
+    )
+
+
+def orthogonal_rows(parts, row_count, full_steps):
+    gram_matrix = gram_of(parts)
+    width = gram_matrix.shape[0]
+    trace = jnp.sum(jnp.where(jnp.eye(width, dtype=bool), gram_matrix, 0.0))
+    inverse = 1.0 / (jnp.sqrt(trace) + 1e-07)
+    gram_matrix = gram_matrix * (inverse * inverse)
+    rows = parts[0][:row_count].astype(jnp.float32)
+    for step in range(5):
+        change = update_of(gram_matrix)
+        if step < full_steps:
+            scale = inverse if step == 0 else 1.0
+            wide = [
+                scale * (newton_one * part.astype(jnp.float32) + low_dot(part, change))
+                for part in parts
+            ]
+            rows = wide[0][:row_count]
+            parts = [part.astype(jnp.bfloat16) for part in wide]
+            if step < 4:
+                gram_matrix = gram_of(parts)
+        else:
+            rows = newton_one * rows + low_dot(rows.astype(jnp.bfloat16), change)
+            if step < 4:
+                once = newton_one * gram_matrix + low_dot(gram_matrix.astype(jnp.bfloat16), change)
+                gram_matrix = newton_one * once + low_dot(once.astype(jnp.bfloat16), change)
+    return rows
 
 
 def adam_step(weight, first_moment, second_moment, gradient, step_rate):
@@ -271,118 +304,296 @@
     head_v,
 ):
     groups = lax.axis_size("cls")
+    owners = lax.axis_size("dp")
+    count = groups * owners
+    top = count.bit_length() - 1
+    low_bits = groups.bit_length() - 1
     member_index = lax.axis_index("cls")
     owner_index = lax.axis_index("dp")
-    flat_index = owner_index * groups + member_index
+    me = owner_index * groups + member_index
+    core = me & 1
     model_width = vec_w.shape[1]
     slot_count = labels.shape[1]
-    weights = (
-        lax.all_gather(attn_w.astype(jnp.bfloat16), ("dp", "cls"), axis=0, tiled=True),
-        lax.all_gather(mlp_w.astype(jnp.bfloat16), ("dp", "cls"), axis=0, tiled=True),
-        lax.all_gather(embed_w.astype(jnp.bfloat16), ("dp", "cls"), axis=0, tiled=True),
-    )
-    head_b = lax.all_gather(head_w.astype(jnp.bfloat16), "dp", axis=0, tiled=True)
+    high_bits = list(range(top - 1, 2, -1))
+    third, fourth, pair = (2, 4), (4, 2), (1, 1)
+    third_mine = jnp.where(core == 0, third[0], third[1])
+    fourth_mine = jnp.where(core == 0, fourth[0], fourth[1])
+
+    def exchange(value, masks):
+        return swap(value, count, masks)
+
+    def bit_of(bit):
+        return (me >> bit) & 1
+
+    attn_rows, embed_rows, mlp_rows = attn_w.shape[0], embed_w.shape[0], mlp_w.shape[0]
+    block = jnp.concatenate([attn_w, embed_w], axis=0).astype(jnp.bfloat16)
+    for axis, bit in enumerate(high_bits):
+        block = ordered_pair(bit_of(bit), block, exchange(block, (1 << bit,) * 2), axis)
+    block = block.reshape(-1, attn_rows + embed_rows, model_width)
+    pieces = [block, exchange(block, third)]
+    pieces = jnp.stack(pieces)
+    pieces = jnp.concatenate([pieces, exchange(pieces, fourth)], axis=0)
+    others = exchange(pieces, pair)
+    sibling = me ^ 1
+    places = [
+        me,
+        me ^ third_mine,
+        me ^ fourth_mine,
+        me ^ 6,
+        sibling,
+        sibling ^ fourth_mine,
+        sibling ^ third_mine,
+        sibling ^ 6,
+    ]
+    attn_b = jnp.zeros((count // 8, 8, attn_rows, model_width), jnp.bfloat16)
+    embed_b = jnp.zeros((count // 8, 8, embed_rows, model_width), jnp.bfloat16)
+    for index, place in enumerate(places):
+        piece = (pieces if index < 4 else others)[index % 4]
+        attn_b = lax.dynamic_update_slice_in_dim(attn_b, piece[:, None, :attn_rows], place & 7, 1)
+        embed_b = lax.dynamic_update_slice_in_dim(embed_b, piece[:, None, attn_rows:], place & 7, 1)
+    attn_b = attn_b.reshape(count * attn_rows, model_width)
+    embed_b = embed_b.reshape(count * embed_rows, model_width)
+
+    block = mlp_w.astype(jnp.bfloat16)[None]
+    for bit in high_bits:
+        block = jnp.concatenate([block, exchange(block, (1 << bit,) * 2)], axis=0)
+    part_a = jnp.concatenate([block, exchange(block, third)], axis=0)
+    part_b = exchange(part_a, fourth)
+    part_c = exchange(part_a, pair)
+    part_d = exchange(part_b, pair)
+    mlp_parts = [
+        part.reshape(-1, 2 * model_width) for part in (part_a, part_b, part_c, part_d)
+    ]
+    masks = [1 << bit for bit in high_bits]
+    own_codes = [jnp.array(codes(masks + [third[c], fourth[c]]), jnp.int32) for c in (0, 1)]
+    arrival = me ^ jnp.where(
+        core == 0,
+        jnp.concatenate([own_codes[0], own_codes[1] ^ 1]),
+        jnp.concatenate([own_codes[1], own_codes[0] ^ 1]),
+    )
+    first_bias = jnp.take(vec_w[11:].reshape(count, mlp_rows), arrival, axis=0)
+    first_bias = first_bias.reshape(4, -1)
+
+    shard_rows, shard_width = head_w.shape
+    chunk = -(-shard_width // (owners * 128)) * 128
+    padding = owners * chunk - shard_width
+    owner_bits = list(range(low_bits, top))
+
+    def transposed(value):
+        value = value.reshape((2,) * len(owner_bits) + value.shape[1:])
+        for bit in owner_bits:
+            axis = top - 1 - bit
+            mine = bit_of(bit)
+            stay, leave = pick(value, mine, axis), pick(value, 1 - mine, axis)
+            value = ordered_pair(mine, stay, exchange(leave, (1 << bit,) * 2), axis)
+        return value.reshape((owners,) + value.shape[len(owner_bits) :])
+
+    head_low = jnp.pad(head_w.astype(jnp.bfloat16), ((0, 0), (0, padding)))
+    head_low = head_low.reshape(shard_rows, owners, chunk).transpose(1, 0, 2)
+    head_b = transposed(head_low).reshape(owners * shard_rows, chunk)
+
     image_index = lax.dynamic_index_in_dim(image_ids, member_index, 0, keepdims=False)
+    my_labels = lax.dynamic_index_in_dim(labels, member_index, 0, keepdims=False)
     position = patch_place[0]
-    final_rows, kept_rows = layer_forward(weights, vec_w, patches, image_index, position)
+    final_rows, kept_rows = layer_forward(
+        (attn_b, embed_b, mlp_parts), vec_w, first_bias, patches, image_index, position
+    )
     closing, close_pull = jax.vjp(layer_norm, final_rows, vec_w[8], vec_w[9])
     member = (image_index[None, :] == jnp.arange(slot_count)[:, None]).astype(jnp.float32)
-    divisor = jnp.maximum(jnp.sum(member, axis=1), 1.0)[:, None]
+    slot_sizes = jnp.sum(member, axis=1)
+    divisor = jnp.maximum(slot_sizes, 1.0)[:, None]
     pooled = product(member, closing) / divisor
-    group_pooled = lax.all_gather(pooled.astype(jnp.bfloat16), "cls", axis=0, tiled=True)
-    logits = low_dot(group_pooled, head_b)
-    shard_width = head_b.shape[1]
-    columns = member_index * shard_width + jnp.arange(shard_width)
-    logits = jnp.where((columns < CLASSES)[None], logits, -1e30)
-    onehot = (columns[None, :] == labels.reshape(-1)[:, None]).astype(jnp.float32)
-    target_part = jnp.sum(onehot * logits, axis=1)
-    row_max = lax.pmax(jnp.max(logits, axis=1), "cls")
-    exp_sums, target = lax.psum(
-        (jnp.sum(jnp.exp(logits - row_max[:, None]), axis=1), target_part), "cls"
-    )
-    normaliser = row_max + jnp.log(exp_sums)
-    group_counts = jnp.sum(
-        (image_ids[:, None, :] == jnp.arange(slot_count)[None, :, None]).astype(jnp.float32), axis=2
-    )
-    valid = group_counts.reshape(-1) > 0.5
-    loss_part = jnp.sum(jnp.where(valid, normaliser - target, 0.0))
-    loss_sum, image_total = lax.psum((loss_part, jnp.sum(valid.astype(jnp.float32))), "dp")
+    facts = jnp.stack(
+        [(slot_sizes > 0.5).astype(jnp.int32), my_labels // 256, my_labels % 256], axis=1
+    )
+    facts = jnp.pad(facts, ((0, 0), (0, 125))).astype(jnp.bfloat16)
+    block = jnp.concatenate([pooled.astype(jnp.bfloat16), facts], axis=1)
+    for axis, bit in enumerate(range(top - 1, -1, -1)):
+        block = ordered_pair(bit_of(bit), block, exchange(block, (1 << bit,) * 2), axis)
+    block = block.reshape(count * slot_count, -1)
+    all_pooled = block[:, :model_width]
+    facts = block[:, model_width : model_width + 3].astype(jnp.int32)
+    valid = facts[:, 0] > 0
+    all_labels = facts[:, 1] * 256 + facts[:, 2]
+    image_total = jnp.sum(valid.astype(jnp.float32))
+
+    logits = low_dot(all_pooled, head_b)
+    within = owner_index * chunk + jnp.arange(chunk)
+    columns = member_index * shard_width + within
+    usable = (within < shard_width) & (columns < CLASSES)
+    logits = jnp.where(usable[None], logits, -1e30)
+    onehot = (usable[None] & (columns[None, :] == all_labels[:, None])).astype(jnp.float32)
+    row_max = jnp.max(logits, axis=1)
+    exp_sums = jnp.sum(jnp.exp(logits - row_max[:, None]), axis=1)
+    stats = jnp.stack([row_max, exp_sums, jnp.sum(onehot * logits, axis=1)])
+    for bit in range(top):
+        other = exchange(stats, (1 << bit,) * 2)
+        lower = jnp.where(bit_of(bit) == 0, stats, other)
+        upper = jnp.where(bit_of(bit) == 0, other, stats)
+        row_max = jnp.maximum(lower[0], upper[0])
+        exp_sums = lower[1] * jnp.exp(lower[0] - row_max) + upper[1] * jnp.exp(upper[0] - row_max)
+        stats = jnp.stack([row_max, exp_sums, lower[2] + upper[2]])
+    normaliser = stats[0] + jnp.log(stats[1])
+    loss_sum = jnp.sum(jnp.where(valid, normaliser - stats[2], 0.0))
     probs_class = jnp.exp(logits - normaliser[:, None])
     d_logits = (jnp.where(valid[:, None], probs_class - onehot, 0.0) / image_total).astype(
         jnp.bfloat16
     )
-    d_pooled = lax.psum_scatter(
-        contract_cols(d_logits, head_b).astype(jnp.bfloat16), "cls", scatter_dimension=0, tiled=True
-    ).astype(jnp.float32)
-    head_grad = lax.psum_scatter(
-        contract_rows(group_pooled, d_logits).astype(jnp.bfloat16),
-        "dp",
-        scatter_dimension=0,
-        tiled=True,
-    ).astype(jnp.float32)
+    d_pooled = contract_cols(d_logits, head_b)
+    d_pooled = d_pooled.reshape((2,) * top + (slot_count, model_width))
+    for bit in range(top):
+        axis = top - 1 - bit
+        mine = bit_of(bit)
+        leave = pick(d_pooled, 1 - mine, axis).astype(jnp.bfloat16)
+        d_pooled = pick(d_pooled, mine, axis) + exchange(leave, (1 << bit,) * 2).astype(
+            jnp.float32
+        )
+    head_grad = contract_rows(all_pooled, d_logits).astype(jnp.bfloat16)
+    head_grad = transposed(head_grad.reshape(owners, shard_rows, chunk)).transpose(1, 0, 2)
+    head_grad = head_grad.reshape(shard_rows, owners * chunk)[:, :shard_width].astype(jnp.float32)
+
     d_closing = product(member.T, d_pooled / divisor)
     d_final, g_gain_final, g_shift_final = close_pull(d_closing)
-    attn_grad, mlp_grad, embed_grad, small_rows, g_patch_bias, g_first_bias = layer_backward(
-        weights, vec_w, patches, image_index, position, kept_rows, d_final
-    )
+    d_out = d_final.astype(jnp.bfloat16)
+    g_second_bias = jnp.sum(d_out.astype(jnp.float32), axis=0)
+
+    def send(index, both, grads):
+        if index in (2, 3):
+            low = jnp.concatenate([grad.astype(jnp.bfloat16) for grad in both], axis=1)
+            return exchange(low, pair)
+        arrived = grads[3 if index == 1 else 2].astype(jnp.float32)
+        summed = jnp.concatenate(both, axis=1) + arrived
+        if index == 1:
+            return exchange(summed.astype(jnp.bfloat16), fourth)
+        return summed + grads[1].astype(jnp.float32)
+
+    (embedded, normed, queries, key_rows, values, summary, mixed_out, middle, normed_two, hidden, active) = (
+        kept_rows
+    )
+    d_normed_two, bias_grads, mlp_grad = mlp_backward(
+        mlp_parts, normed_two, hidden, active, d_out, send
+    )
+    mlp_grad = mlp_grad.reshape(-1, mlp_rows, 2 * model_width)
+    for stage in [third] + [(1 << bit,) * 2 for bit in reversed(high_bits)]:
+        half = mlp_grad.shape[0] // 2
+        mlp_grad = mlp_grad[:half] + exchange(
+            mlp_grad[half:].astype(jnp.bfloat16), stage
+        ).astype(jnp.float32)
+    mlp_sum = mlp_grad[0]
+
+    def by_core(value):
+        low = value.astype(jnp.bfloat16)
+        left, right = low[:, :model_width], low[:, model_width:]
+        mine = jnp.where(core == 0, left, right)
+        rows = jnp.stack([mine, exchange(jnp.where(core == 0, right, left), pair)])
+        for stage in [(1 << bit,) * 2 for bit in high_bits] + [third]:
+            rows = jnp.concatenate([rows, exchange(rows, stage)], axis=0)
+        return [part.reshape(-1, model_width) for part in (rows, exchange(rows, fourth))]
+
+    def by_block(value):
+        rows = value.astype(jnp.bfloat16)[None]
+        for stage in [(1 << bit,) * 2 for bit in high_bits[2:]] + [third, fourth, pair]:
+            rows = jnp.concatenate([rows, exchange(rows, stage)], axis=0)
+        return rows.reshape(-1, model_width)
+
+    mlp_mom_late, attn_mom_late, _ = lax.optimization_barrier((mlp_mom, attn_mom, part_d))
+    mlp_moms = by_core(mlp_mom_late)
+    attn_moms = by_block(attn_mom_late)
+    mlp_grads = by_core(mlp_sum)
+
+    d_mid_norm, g_gain_two, g_shift_two = jax.vjp(layer_norm, middle, vec_w[6], vec_w[7])[1](
+        d_normed_two
+    )
+    d_middle = d_final + d_mid_norm
+    attn_grad, embed_grad, small = attention_backward(
+        (attn_b, embed_b),
+        vec_w,
+        patches,
+        image_index,
+        position,
+        (embedded, normed, queries, key_rows, values, summary, mixed_out),
+        d_middle,
+    )
+    g_query_bias, g_value_bias, g_out_bias, g_gain_one, g_shift_one, g_patch_bias = small
+    g_first_bias = jnp.take(
+        bias_grads.reshape(count, mlp_rows), jnp.argsort(arrival), axis=0
+    )
+
+    def scattered(grad, rows):
+        grad = grad.reshape(count // 8, 4, 2, rows, model_width)
+        leave = pick(grad, 1 - core, 2).astype(jnp.bfloat16)
+        grad = pick(grad, core, 2) + exchange(leave, pair).astype(jnp.float32)
+        quarter = (me >> 1) & 3
+        to_third, to_fourth = third_mine >> 1, fourth_mine >> 1
+        leave = [pick(grad, quarter ^ to_fourth, 1), pick(grad, quarter ^ 3, 1)]
+        leave = exchange(jnp.stack(leave).astype(jnp.bfloat16), fourth).astype(jnp.float32)
+        leaving = (pick(grad, quarter ^ to_third, 1) + leave[1]).astype(jnp.bfloat16)
+        grad = pick(grad, quarter, 1) + leave[0]
+        grad = grad + exchange(leaving, third).astype(jnp.float32)
+        grad = grad.reshape((2,) * len(high_bits) + (rows, model_width))
+        for bit in reversed(high_bits):
+            axis = top - 1 - bit
+            mine = bit_of(bit)
+            leave = pick(grad, 1 - mine, axis).astype(jnp.bfloat16)
+            grad = pick(grad, mine, axis) + exchange(leave, (1 << bit,) * 2).astype(jnp.float32)
+        return grad
+
+    attn_sum = scattered(attn_grad, attn_rows)
+    embed_sum = scattered(embed_grad, embed_rows)
+    attn_grads = by_block(attn_sum)
     vec_grad = jnp.concatenate(
         [
-            jnp.stack(small_rows + [g_gain_final, g_shift_final, g_patch_bias]),
+            jnp.stack(
+                [
+                    g_query_bias,
+                    g_value_bias,
+                    g_out_bias,
+                    g_second_bias,
+                    g_gain_one,
+                    g_shift_one,
+                    g_gain_two,
+                    g_shift_two,
+                    g_gain_final,
+                    g_shift_final,
+                    g_patch_bias,
+                ]
+            ),
             g_first_bias.reshape(-1, model_width),
         ],
         axis=0,
     )
-    attn_sum, mlp_sum, embed_sum = (
-        lax.psum_scatter(attn_grad, ("dp", "cls"), scatter_dimension=0, tiled=True),
-        lax.psum_scatter(mlp_grad, ("dp", "cls"), scatter_dimension=0, tiled=True),
-        lax.psum_scatter(embed_grad, ("dp", "cls"), scatter_dimension=0, tiled=True),
-    )
-    local_squares = (
-        jnp.sum(attn_sum * attn_sum)
-        + jnp.sum(mlp_sum * mlp_sum)
-        + jnp.sum(embed_sum * embed_sum)
-        + jnp.sum(head_grad * head_grad)
-    )
-    vec_sum, all_squares = lax.psum((vec_grad, local_squares), ("dp", "cls"))
-    grad_norm = jnp.sqrt(all_squares + jnp.sum(vec_sum * vec_sum))
+    local_squares = sum(
+        jnp.sum(grad * grad, axis=0) for grad in (attn_sum, embed_sum, mlp_sum[:, :model_width], mlp_sum[:, model_width:])
+    )
+    head_squares = jnp.sum(head_grad * head_grad) / model_width
+    small_sums = jnp.concatenate([vec_grad, (local_squares + head_squares)[None]], axis=0)
+    for bit in range(top):
+        small_sums = small_sums + exchange(small_sums, (1 << bit,) * 2)
+    vec_sum = small_sums[:-1]
+    grad_norm = jnp.sqrt(jnp.sum(small_sums[-1]) + jnp.sum(vec_sum * vec_sum))
     factor = jnp.minimum(1.0, clip_limit / (grad_norm + 1e-06))
     attn_mom_out = momentum_keep * attn_mom + factor * attn_sum
     mlp_mom_out = momentum_keep * mlp_mom + factor * mlp_sum
-    attn_full, mlp_full = (
-        lax.all_gather(attn_mom_out, ("dp", "cls"), axis=0, tiled=True),
-        lax.all_gather(mlp_mom_out, ("dp", "cls"), axis=0, tiled=True),
-    )
-    attn_pick = lax.dynamic_slice_in_dim(
-        attn_full, jnp.minimum(owner_index, 3) * model_width, model_width, 0
-    )
-    attn_result = lax.cond(owner_index < 4, orthogonal, jnp.zeros_like, attn_pick)
-    mlp_pick = lax.dynamic_slice_in_dim(
-        mlp_full, jnp.clip(owner_index - 4, 0, 1) * model_width, model_width, 1
-    )
-    mlp_result = lax.cond(
-        (owner_index >= 4) & (owner_index < 6), orthogonal, jnp.zeros_like, mlp_pick
-    )
-    attn_rows = attn_w.shape[0]
-    mlp_rows = mlp_w.shape[0]
-    attn_all = jnp.concatenate(
+
+    def momentum_of(moment, grad):
+        return (
+            momentum_keep * moment.astype(jnp.float32) + factor * grad.astype(jnp.float32)
+        ).astype(jnp.bfloat16)
+
+    mlp_result = orthogonal_rows(
+        [momentum_of(moment, grad) for moment, grad in zip(mlp_moms, mlp_grads)], 2 * mlp_rows, 2
+    )
+    mlp_other = exchange(mlp_result[mlp_rows:], pair)
+    mlp_result = mlp_result[:mlp_rows]
+    mlp_dir = jnp.concatenate(
         [
-            from_root(attn_result.astype(jnp.bfloat16), "dp", slot_index).astype(attn_result.dtype)
-            for slot_index in range(4)
-        ],
-        axis=0,
-    )
-    mlp_all = jnp.concatenate(
-        [
-            from_root(mlp_result.astype(jnp.bfloat16), "dp", 4 + slot_index).astype(
-                mlp_result.dtype
-            )
-            for slot_index in range(2)
+            jnp.where(core == 0, mlp_result, mlp_other),
+            jnp.where(core == 0, mlp_other, mlp_result),
         ],
         axis=1,
     )
-    attn_dir = lax.dynamic_slice_in_dim(attn_all, flat_index * attn_rows, attn_rows, 0)
-    mlp_dir = lax.dynamic_slice_in_dim(mlp_all, flat_index * mlp_rows, mlp_rows, 0)
-    mlp_scale = math.sqrt(mlp_full.shape[0] / model_width)
+    attn_dir = orthogonal_rows([momentum_of(attn_moms, attn_grads)], attn_rows, 4)
+    mlp_scale = math.sqrt(mlp_rows * count / model_width)
     attn_out = attn_w * (1.0 - muon_rate * decay_rate) - muon_rate * attn_dir
     mlp_out = mlp_w * (1.0 - muon_rate * decay_rate) - muon_rate * mlp_scale * mlp_dir
     embed_out, embed_m_out, embed_v_out = adam_step(

time: 2120 us -> 748 us (0.35)
  waiting for transfers between devices: 1650 us -> 240 us
  blocking collectives: 78 us -> 0 us
  starting transfers between devices: 0.71 us -> 70.9 us
  other arithmetic: 76.8 us -> 109 us
  local copies, waits for them, and re-layouts: 52.4 us -> 82.7 us
    psum x1 -> x0, waiting for transfers between devices: 727 us -> none  [from_root(): return lax.psum(jnp.where(mine, value, jnp.zeros_like(value)), axis)]
    all_gather x6 -> x0, waiting for transfers between devices: 358 us -> none  [the longest x1 96 us: on_device(): lax.all_gather(head_w.astype(jnp.bfloat16), 'dp', axis=0, tiled=True)]
    reduce_scatter x4 -> x0, waiting for transfers between devices: 353 us -> none  [the longest x1 152 us: on_device(): lax.psum_scatter(contract_rows(group_pooled, d_logits).astype(jnp.bfloat1...]
    ppermute x0 -> x70, waiting for transfers between devices: none -> 240 us  [swap(): lax.ppermute(value, AXES, [(i, i ^ masks[i & 1]) for i in range(count)])]
    unnamed x13 -> x0, waiting for transfers between devices: 210 us -> none
    dot_general x19 -> x4, matrix products: 119 us -> 21.8 us  [the longest x1 14.1 us: attention_backward(): jnp.einsum('qhd,khd->hqk', d_mixed, values.reshape(head_shape), preferred...]
    ppermute x0 -> x70, starting transfers between devices: none -> 70.9 us  [swap(): lax.ppermute(value, AXES, [(i, i ^ masks[i & 1]) for i in range(count)])]
    psum x3 -> x0, blocking collectives: 65.9 us -> none  [the longest x1 39.7 us: on_device(): vec_sum, all_squares = lax.psum((vec_grad, local_squares), ('dp', 'cls'))]
  transfers between devices with their start and end apart: 12 -> 70, of which waited for: 12 -> 33; matrix products, arithmetic and copies ran while one was open for 11% -> 44% of each run, Pallas kernels for 0% -> 0%
where the time goes in v1:
time: 748 us; the launch traced here: 736 us
  waiting for transfers between devices  240 us (32%)
  matrix products  225 us (30%)
  other arithmetic  109 us (15%)
  local copies, waits for them, and re-layouts  82.7 us (11%)
  starting transfers between devices  70.9 us (9%)
  between operations  8.76 us (1%)
    ppermute x70, waiting for transfers between devices, swap(): lax.ppermute(value, AXES, [(i, i ^ masks[i & 1]) for i in range(count)])  240 us
    dot_general x33, matrix products, low_dot(): return jnp.dot(left_side, right_side, preferred_element_type=jnp.float32)  91.7 us
    ppermute x70, starting transfers between devices, swap(): lax.ppermute(value, AXES, [(i, i ^ masks[i & 1]) for i in range(count)])  70.9 us
    dot_general x27, matrix products, contract_rows(): lax.dot_general(left_side, right_side, (((0,), (0,)), ((), ())), preferre...  57.6 us
    dot_general x13, matrix products, contract_cols(): lax.dot_general(left_side, right_side, (((1,), (1,)), ((), ())), preferre...  42 us
    unnamed x362, local copies, waits for them, and re-layouts  25.8 us
  transfers between devices with their start and end apart: 70, of which 33 were waited for; matrix products, arithmetic and copies ran while one was open for 44% of the time, Pallas kernels for 0%

profile of v1, /device:TPU:0, one launch (start us, length us, event | category | flops | bytes accessed | tf_op | source)
XLA Modules:
  0.0 735.6 jit_solution(11269331997158302482)
XLA Ops:
  2.6 4.1 collective-permute-start
  19.6 3.4 collective-permute-done
  23.3 13.7 %collective-permute-done.1 = bf16[2,128,768]{2,1,0:T(8,128)(2,1)S(1)} collective-permute-done((bf16[2,128,768]{2,1,0:T(8,128)(2,1)S(1)}, bf16[2,128,768]{2,1,0:T(8,128)(2,1)S(1)}, u32[]{:S(2)}, u32[]{:S(2)}) %collective-permute-start.1) | collective-permute-done | bytes 393248 | tf_op jit(solution)/shard_map/ppermute | solution.py:31
  41.6 7.5 %collective-permute-done.2 = bf16[4,128,768]{2,1,0:T(8,128)(2,1)S(1)} collective-permute-done((bf16[4,128,768]{2,1,0:T(8,128)(2,1)S(1)}, bf16[4,128,768]{2,1,0:T(8,128)(2,1)S(1)}, u32[]{:S(2)}, u32[]{:S(2)}) %collective-permute-start.2) | collective-permute-done | bytes 786464 | tf_op jit(solution)/shard_map/ppermute | solution.py:31
  60.0 7.1 collective-permute-done.6
  72.0 3.4 pad_maximum_fusion.1
  77.7 7.1 collective-permute-done.7
  97.0 25.7 %collective-permute-done.18 = bf16[2,2,96,768]{3,2,1,0:T(8,128)(2,1)S(1)} collective-permute-done((bf16[2,2,96,768]{3,2,1,0:T(8,128)(2,1)S(1)}, bf16[2,2,96,768]{3,2,1,0:T(8,128)(2,1)S(1)}, u32[]{:S(2)}, u32[]{:S(2)}) %collective-permute-start.18) | collective-permute-done | bytes 589856 | tf_op jit(solution)/shard_map/ppermute | solution.py:31
  164.6 5.1 fusion.52
  171.6 6.7 multiply_convert_fusion.9
  178.3 6.7 multiply_convert_fusion.10
  189.5 6.4 multiply_convert_fusion.8
  198.3 6.6 multiply_convert_fusion.7
  209.8 4.8 collective-permute-done.11
  220.3 3.5 collective-permute-done.13
  223.8 3.5 collective-permute-start.14
  227.4 3.9 collective-permute-done.14
  245.3 4.0 collective-permute-done.60
  252.6 11.6 %collective-permute-done.22 = f32[3,512]{1,0:T(4,128)S(1)} collective-permute-done((f32[3,512]{1,0:T(4,128)S(1)}, f32[3,512]{1,0:T(4,128)S(1)}, u32[]{:S(2)}, u32[]{:S(2)}) %collective-permute-start.22) | collective-permute-done | bytes 6176 | tf_op jit(solution)/shard_map/ppermute | solution.py:31
  282.5 10.5 %collective-permute-done.26 = bf16[2,2,16,768]{3,2,0,1:T(8,128)(2,1)S(1)} collective-permute-done((bf16[2,2,16,768]{3,2,0,1:T(8,128)(2,1)S(1)}, bf16[2,2,16,768]{3,2,0,1:T(8,128)(2,1)S(1)}, u32[]{:S(2)}, u32[]{:S(2)}) %collective-permute-start.26) | collective-permute-done | bytes 98336 | tf_op jit(solution)/shard_map/ppermute | solution.py:31
  332.0 3.7 multiply_reduce_fusion.3
  342.3 14.1 %multiply_reduce_fusion = (f32[12,512]{1,0:T(8,128)S(1)}, f32[12,512,512]{1,2,0:T(8,128)}) fusion(f32[12,512]{1,0:T(8,128)S(1)} %log_add_fusion, f32[12,512,512]{1,2,0:T(8,128)} %copy-done.2, pred[512,512]{0,1:T(8,128)(4,1)S(1)} %broadcast_compare_fusion, bf16[512,12,64]{0,2,1:T(8,128)(2,1)} %bitcast.510, bf16[512,12,64]{0,2,1:T(8,128)(2,1)} %bitcast.509), kind=kOutput, calls=%fused_computation.5 | convolution fusion | flops 418375680 | bytes 27049984 | tf_op jit(solution)/shard_map/qhd,khd->hqk/dot_general | solution.py:190
  356.4 7.1 multiply_convert_fusion
  367.3 3.9 convert_reduce_fusion.7
  412.7 31.0 %collective-permute-done.35 = bf16[2,4,32,768]{3,2,1,0:T(8,128)(2,1)} collective-permute-done((bf16[2,4,32,768]{3,2,1,0:T(8,128)(2,1)S(1)}, bf16[2,4,32,768]{3,2,1,0:T(8,128)(2,1)}, u32[]{:S(2)}, u32[]{:S(2)}) %collective-permute-start.35) | collective-permute-done | bytes 393248 | tf_op jit(solution)/shard_map/ppermute | solution.py:31
  478.0 5.1 collective-permute-done.31
  498.3 12.1 %collective-permute-done.43 = bf16[2,96,1536]{2,1,0:T(8,128)(2,1)S(1)} collective-permute-done((bf16[2,96,1536]{2,1,0:T(8,128)(2,1)S(1)}, bf16[2,96,1536]{2,1,0:T(8,128)(2,1)S(1)}, u32[]{:S(2)}, u32[]{:S(2)}) %collective-permute-start.43) | collective-permute-done | bytes 589856 | tf_op jit(solution)/shard_map/ppermute | solution.py:31
  513.9 10.5 %collective-permute-done.44 = bf16[1,96,1536]{2,1,0:T(8,128)(2,1)} collective-permute-done((bf16[1,96,1536]{2,1,0:T(8,128)(2,1)}, bf16[1,96,1536]{2,1,0:T(8,128)(2,1)}, u32[]{:S(2)}, u32[]{:S(2)}) %collective-permute-start.44) | collective-permute-done | bytes 294944 | tf_op jit(solution)/shard_map/ppermute | solution.py:31
  530.3 3.7 collective-permute-done.49
  535.7 22.1 %collective-permute-done.50 = f32[16,768]{1,0:T(8,128)S(1)} collective-permute-done((f32[16,768]{1,0:T(8,128)S(1)}, f32[16,768]{1,0:T(8,128)S(1)}, u32[]{:S(2)}, u32[]{:S(2)}) %collective-permute-start.50) | collective-permute-done | bytes 49184 | tf_op jit(solution)/shard_map/ppermute | solution.py:31
  563.5 11.9 %collective-permute-done.52 = f32[16,768]{1,0:T(8,128)S(1)} collective-permute-done((f32[16,768]{1,0:T(8,128)S(1)}, f32[16,768]{1,0:T(8,128)S(1)}, u32[]{:S(2)}, u32[]{:S(2)}) %collective-permute-start.52) | collective-permute-done | bytes 49184 | tf_op jit(solution)/shard_map/ppermute | solution.py:31
  580.7 7.7 %fusion.249 = (bf16[96,5462]{1,0:T(8,128)(2,1)}, f32[96,5462]{1,0:T(8,128)}, f32[96,5462]{1,0:T(8,128)}, f32[96,5462]{1,0:T(8,128)}) fusion(f32[96,5462]{1,0:T(8,128)} %param.38, bf16[96,6144]{1,0:T(8,128)(2,1)S(1)} %bitcast.492, f32[]{:T(128)S(6)} %min.3, f32[96,5462]{1,0:T(8,128)} %param.31, f32[96,5462]{1,0:T(8,128)} %param.39), kind=kLoop, calls=%fused_computation.611 | loop fusion | flops 7865280 | bytes 14681860 | tf_op jit(solution)/shard_map/convert_element_type | solution.py:627
  591.5 4.7 collective-permute-done.57
  598.3 8.3 %collective-permute-done.65 = bf16[4,96,768]{2,1,0:T(8,128)(2,1)S(1)} collective-permute-done((bf16[4,96,768]{2,1,0:T(8,128)(2,1)S(1)}, bf16[4,96,768]{2,1,0:T(8,128)(2,1)S(1)}, u32[]{:S(2)}, u32[]{:S(2)}) %collective-permute-start.65) | collective-permute-done | bytes 589856 | tf_op jit(solution)/shard_map/ppermute | solution.py:31
  614.4 6.9 multiply_convert_fusion.3
  621.3 4.2 fusion.285
  625.5 7.1 add_convert_fusion.12
  632.6 4.2 fusion.286
  639.1 5.1 add_convert_fusion.10
  647.8 5.8 multiply_add_fusion.5
  662.2 5.0 collective-permute-done.68
  670.4 4.3 select_reduce_fusion
  675.4 4.4 add_convert_fusion.7
  690.5 4.3 multiply_add_fusion
  694.8 10.2 %fusion.85 = f32[768,768]{1,0:T(8,128)} fusion(bf16[1536,768]{1,0:T(8,128)(2,1)S(1)} %multiply_convert_fusion.1, bf16[768,768]{1,0:T(8,128)(2,1)} %copy-done.173), kind=kOutput, calls=%fused_computation.248 | convolution fusion | flops 3628597248 | bytes 5898240 | tf_op jit(solution)/shard_map/dot_general | solution.py:60
  705.0 6.6 fusion.45
  722.0 4.6 convolution_add_fusion.5
  726.8 5.4 fusion.277
  (801 shorter events, 357.7 us)
Async XLA Ops:
  2.6 20.4 %collective-permute-start = (bf16[128,768]{1,0:T(8,128)(2,1)S(1)}, bf16[128,768]{1,0:T(8,128)(2,1)S(1)}, u32[]{:S(2)}, u32[]{:S(2)}) collective-permute-start(bf16[128,768]{1,0:T(8,128)(2,1)S(1)} %pad_maximum_fusion.21), channel_id=1, source_target_pairs={{0,16},{1,17},{2,18},{3,19},{4,20},{5,21},{6,22},{7,23},{8,24},{9,... | collective-permute-start | bytes 589832 | tf_op jit(solution)/shard_map/ppermute | solution.py:31
  7.8 44.1 %collective-permute-start.5 = (bf16[1,96,1536]{2,1,0:T(8,128)(2,1)S(1)}, bf16[1,96,1536]{2,1,0:T(8,128)(2,1)S(1)}, u32[]{:S(2)}, u32[]{:S(2)}) collective-permute-start(bf16[1,96,1536]{2,1,0:T(8,128)(2,1)S(1)} %convert_bitcast_fusion), channel_id=1, source_target_pairs={{0,16},{1,17},{2,18},{3,19},{4,20},{5,21},{6,22},{7,23},{8,24},{9,... | collective-permute-start | bytes 884744 | tf_op jit(solution)/shard_map/ppermute | solution.py:31
  11.4 58.2 %collective-permute-start.16 = (bf16[2,2,96,768]{3,2,1,0:T(8,128)(2,1)}, bf16[2,2,96,768]{3,2,1,0:T(8,128)(2,1)}, u32[]{:S(2)}, u32[]{:S(2)}) collective-permute-start(bf16[2,2,96,768]{3,2,1,0:T(8,128)(2,1)} %get-tuple-element.130), channel_id=1, source_target_pairs={{0,4},{1,5},{2,6},{3,7},{4,0},{5,1},{6,2},{7,3},{8,12},{9,13},{10,... | collective-permute-start | bytes 1769480 | tf_op jit(solution)/shard_map/ppermute | solution.py:31
  23.1 13.8 %collective-permute-start.1 = (bf16[2,128,768]{2,1,0:T(8,128)(2,1)S(1)}, bf16[2,128,768]{2,1,0:T(8,128)(2,1)S(1)}, u32[]{:S(2)}, u32[]{:S(2)}) collective-permute-start(bf16[2,128,768]{2,1,0:T(8,128)(2,1)S(1)} %maximum_select_fusion.11), channel_id=1, source_target_pairs={{0,8},{1,9},{2,10},{3,11},{4,12},{5,13},{6,14},{7,15},{8,0},{9,1},... | collective-permute-start | bytes 1179656 | tf_op jit(solution)/shard_map/ppermute | solution.py:31
  37.0 12.1 %collective-permute-start.2 = (bf16[4,128,768]{2,1,0:T(8,128)(2,1)S(1)}, bf16[4,128,768]{2,1,0:T(8,128)(2,1)S(1)}, u32[]{:S(2)}, u32[]{:S(2)}) collective-permute-start(bf16[4,128,768]{2,1,0:T(8,128)(2,1)S(1)} %bitcast.481), channel_id=1, source_target_pairs={{0,2},{1,5},{2,0},{3,7},{4,6},{5,1},{6,4},{7,3},{8,10},{9,13},{10,... | collective-permute-start | bytes 2359304 | tf_op jit(solution)/shard_map/ppermute | solution.py:31
  50.4 21.6 %collective-permute-start.3 = (bf16[2,4,128,768]{3,2,1,0:T(8,128)(2,1)}, bf16[2,4,128,768]{3,2,1,0:T(8,128)(2,1)}, u32[]{:S(2)}, u32[]{:S(2)}) collective-permute-start(bf16[2,4,128,768]{3,2,1,0:T(8,128)(2,1)} %pad_maximum_fusion.6), channel_id=1, source_target_pairs={{0,4},{1,3},{2,6},{3,1},{4,0},{5,7},{6,2},{7,5},{8,12},{9,11},{10,... | collective-permute-start | bytes 4718600 | tf_op jit(solution)/shard_map/ppermute | solution.py:31
  52.8 14.3 %collective-permute-start.6 = (bf16[2,96,1536]{2,1,0:T(8,128)(2,1)}, bf16[2,96,1536]{2,1,0:T(8,128)(2,1)S(1)}, u32[]{:S(2)}, u32[]{:S(2)}) collective-permute-start(bf16[2,96,1536]{2,1,0:T(8,128)(2,1)} %pad_maximum_fusion.11), channel_id=1, source_target_pairs={{0,8},{1,9},{2,10},{3,11},{4,12},{5,13},{6,14},{7,15},{8,0},{9,1},... | collective-permute-start | bytes 1769480 | tf_op jit(solution)/shard_map/ppermute | solution.py:31
  68.3 16.5 %collective-permute-start.7 = (bf16[4,96,1536]{2,1,0:T(8,128)(2,1)}, bf16[4,96,1536]{2,1,0:T(8,128)(2,1)}, u32[]{:S(2)}, u32[]{:S(2)}) collective-permute-start(bf16[4,96,1536]{2,1,0:T(8,128)(2,1)} %pad_maximum_fusion.7), channel_id=1, source_target_pairs={{0,2},{1,5},{2,0},{3,7},{4,6},{5,1},{6,4},{7,3},{8,10},{9,13},{10,... | collective-permute-start | bytes 3538952 | tf_op jit(solution)/shard_map/ppermute | solution.py:31
  75.4 50.7 %collective-permute-start.4 = (bf16[4,4,128,768]{3,2,1,0:T(8,128)(2,1)}, bf16[4,4,128,768]{3,2,1,0:T(8,128)(2,1)}, u32[]{:S(2)}, u32[]{:S(2)}) collective-permute-start(bf16[4,4,128,768]{3,2,1,0:T(8,128)(2,1)} %pad_maximum_fusion.1), channel_id=1, source_target_pairs={{0,1},{1,0},{2,3},{3,2},{4,5},{5,4},{6,7},{7,6},{8,9},{9,8},{10,11... | collective-permute-start | bytes 9437192 | tf_op jit(solution)/shard_map/ppermute | solution.py:31
  76.6 16.0 %collective-permute-start.17 = (bf16[2,2,96,768]{3,2,1,0:T(8,128)(2,1)}, bf16[2,2,96,768]{3,2,1,0:T(8,128)(2,1)}, u32[]{:S(2)}, u32[]{:S(2)}) collective-permute-start(bf16[2,2,96,768]{3,2,1,0:T(8,128)(2,1)} %get-tuple-element.128), channel_id=1, source_target_pairs={{0,8},{1,9},{2,10},{3,11},{4,12},{5,13},{6,14},{7,15},{8,0},{9,1},... | collective-permute-start | bytes 1769480 | tf_op jit(solution)/shard_map/ppermute | solution.py:31
  87.7 37.8 %collective-permute-start.8 = (bf16[8,96,1536]{2,1,0:T(8,128)(2,1)}, bf16[8,96,1536]{2,1,0:T(8,128)(2,1)}, u32[]{:S(2)}, u32[]{:S(2)}) collective-permute-start(bf16[8,96,1536]{2,1,0:T(8,128)(2,1)} %pad_maximum_fusion.3), channel_id=1, source_target_pairs={{0,4},{1,3},{2,6},{3,1},{4,0},{5,7},{6,2},{7,5},{8,12},{9,11},{10,... | collective-permute-start | bytes 7077896 | tf_op jit(solution)/shard_map/ppermute | solution.py:31
  94.2 28.6 %collective-permute-start.18 = (bf16[2,2,96,768]{3,2,1,0:T(8,128)(2,1)S(1)}, bf16[2,2,96,768]{3,2,1,0:T(8,128)(2,1)S(1)}, u32[]{:S(2)}, u32[]{:S(2)}) collective-permute-start(bf16[2,2,96,768]{3,2,1,0:T(8,128)(2,1)S(1)} %get-tuple-element.126), channel_id=1, source_target_pairs={{0,16},{1,17},{2,18},{3,19},{4,20},{5,21},{6,22},{7,23},{8,24},{9,... | collective-permute-start | bytes 1769480 | tf_op jit(solution)/shard_map/ppermute | solution.py:31
  123.9 65.6 %collective-permute-start.9 = (bf16[8,96,1536]{2,1,0:T(8,128)(2,1)}, bf16[8,96,1536]{2,1,0:T(8,128)(2,1)}, u32[]{:S(2)}, u32[]{:S(2)}) collective-permute-start(bf16[8,96,1536]{2,1,0:T(8,128)(2,1)} %pad_maximum_fusion.3), channel_id=1, source_target_pairs={{0,1},{1,0},{2,3},{3,2},{4,5},{5,4},{6,7},{7,6},{8,9},{9,8},{10,11... | collective-permute-start | bytes 7077896 | tf_op jit(solution)/shard_map/ppermute | solution.py:31
  125.6 72.7 %collective-permute-start.10 = (bf16[8,96,1536]{2,1,0:T(8,128)(2,1)}, bf16[8,96,1536]{2,1,0:T(8,128)(2,1)}, u32[]{:S(2)}, u32[]{:S(2)}) collective-permute-start(bf16[8,96,1536]{2,1,0:T(8,128)(2,1)} %collective-permute-done.8), channel_id=1, source_target_pairs={{0,1},{1,0},{2,3},{3,2},{4,5},{5,4},{6,7},{7,6},{8,9},{9,8},{10,11... | collective-permute-start | bytes 7077896 | tf_op jit(solution)/shard_map/ppermute | solution.py:31
  209.7 23.9 %collective-permute-start.59 = (bf16[96,768]{1,0:T(8,128)(2,1)S(1)}, bf16[96,768]{1,0:T(8,128)(2,1)S(1)}, u32[]{:S(2)}, u32[]{:S(2)}) collective-permute-start(bf16[96,768]{1,0:T(8,128)(2,1)S(1)} %broadcast_select_fusion.1), channel_id=1, source_target_pairs={{0,1},{1,0},{2,3},{3,2},{4,5},{5,4},{6,7},{7,6},{8,9},{9,8},{10,11... | collective-permute-start | bytes 442376 | tf_op jit(solution)/shard_map/ppermute | solution.py:31
  233.7 15.7 %collective-permute-start.60 = (bf16[2,96,768]{2,1,0:T(8,128)(2,1)S(1)}, bf16[2,96,768]{2,1,0:T(8,128)(2,1)S(1)}, u32[]{:S(2)}, u32[]{:S(2)}) collective-permute-start(bf16[2,96,768]{2,1,0:T(8,128)(2,1)S(1)} %pad_maximum_fusion.19), channel_id=1, source_target_pairs={{0,16},{1,17},{2,18},{3,19},{4,20},{5,21},{6,22},{7,23},{8,24},{9,... | collective-permute-start | bytes 884744 | tf_op jit(solution)/shard_map/ppermute | solution.py:31
  238.9 12.8 %collective-permute-start.54 = (bf16[2,96,768]{2,1,0:T(8,128)(2,1)S(1)}, bf16[2,96,768]{2,1,0:T(8,128)(2,1)S(1)}, u32[]{:S(2)}, u32[]{:S(2)}) collective-permute-start(bf16[2,96,768]{2,1,0:T(8,128)(2,1)S(1)} %pad_maximum_fusion.17), channel_id=1, source_target_pairs={{0,4},{1,3},{2,6},{3,1},{4,0},{5,7},{6,2},{7,5},{8,12},{9,11},{10,... | collective-permute-start | bytes 884744 | tf_op jit(solution)/shard_map/ppermute | solution.py:31
  249.4 27.9 %collective-permute-start.61 = (bf16[4,96,768]{2,1,0:T(8,128)(2,1)S(1)}, bf16[4,96,768]{2,1,0:T(8,128)(2,1)S(1)}, u32[]{:S(2)}, u32[]{:S(2)}) collective-permute-start(bf16[4,96,768]{2,1,0:T(8,128)(2,1)S(1)} %pad_maximum_fusion.14), channel_id=1, source_target_pairs={{0,8},{1,9},{2,10},{3,11},{4,12},{5,13},{6,14},{7,15},{8,0},{9,1},... | collective-permute-start | bytes 1769480 | tf_op jit(solution)/shard_map/ppermute | solution.py:31
  249.6 14.6 %collective-permute-start.22 = (f32[3,512]{1,0:T(4,128)S(1)}, f32[3,512]{1,0:T(4,128)S(1)}, u32[]{:S(2)}, u32[]{:S(2)}) collective-permute-start(f32[3,512]{1,0:T(4,128)S(1)} %pad_maximum_fusion.26), channel_id=1, source_target_pairs={{0,8},{1,9},{2,10},{3,11},{4,12},{5,13},{6,14},{7,15},{8,0},{9,1},... | collective-permute-start | bytes 18440 | tf_op jit(solution)/shard_map/ppermute | solution.py:31
  275.8 18.0 %collective-permute-start.45 = (bf16[2,2,96,768]{3,2,1,0:T(8,128)(2,1)S(1)}, bf16[2,2,96,768]{3,2,1,0:T(8,128)(2,1)S(1)}, u32[]{:S(2)}, u32[]{:S(2)}) collective-permute-start(bf16[2,2,96,768]{3,2,1,0:T(8,128)(2,1)S(1)} %get-tuple-element.124), channel_id=1, source_target_pairs={{0,4},{1,5},{2,6},{3,7},{4,0},{5,1},{6,2},{7,3},{8,12},{9,13},{10,... | collective-permute-start | bytes 1769480 | tf_op jit(solution)/shard_map/ppermute | solution.py:31
  281.0 12.1 %collective-permute-start.26 = (bf16[2,2,16,768]{3,2,0,1:T(8,128)(2,1)S(1)}, bf16[2,2,16,768]{3,2,0,1:T(8,128)(2,1)S(1)}, u32[]{:S(2)}, u32[]{:S(2)}) collective-permute-start(bf16[2,2,16,768]{3,2,0,1:T(8,128)(2,1)S(1)} %fusion.193), channel_id=1, source_target_pairs={{0,4},{1,5},{2,6},{3,7},{4,0},{5,1},{6,2},{7,3},{8,12},{9,13},{10,... | collective-permute-start | bytes 294920 | tf_op jit(solution)/shard_map/ppermute | solution.py:31
  300.2 109.5 %collective-permute-start.46 = (bf16[2,2,96,768]{3,2,1,0:T(8,128)(2,1)}, bf16[2,2,96,768]{3,2,1,0:T(8,128)(2,1)}, u32[]{:S(2)}, u32[]{:S(2)}) collective-permute-start(bf16[2,2,96,768]{3,2,1,0:T(8,128)(2,1)} %get-tuple-element.122), channel_id=1, source_target_pairs={{0,8},{1,9},{2,10},{3,11},{4,12},{5,13},{6,14},{7,15},{8,0},{9,1},... | collective-permute-start | bytes 1769480 | tf_op jit(solution)/shard_map/ppermute | solution.py:31
  388.1 11.9 %collective-permute-start.34 = (bf16[4,4,32,768]{3,2,0,1:T(8,128)(2,1)}, bf16[4,4,32,768]{3,2,0,1:T(8,128)(2,1)}, u32[]{:S(2)}, u32[]{:S(2)}) collective-permute-start(bf16[4,4,32,768]{3,2,0,1:T(8,128)(2,1)} %fusion.128), channel_id=1, source_target_pairs={{0,1},{1,0},{2,3},{3,2},{4,5},{5,4},{6,7},{7,6},{8,9},{9,8},{10,11... | collective-permute-start | bytes 2359304 | tf_op jit(solution)/shard_map/ppermute | solution.py:31
  389.8 11.6 %collective-permute-start.29 = (bf16[4,4,96,768]{3,2,0,1:T(8,128)(2,1)S(1)}, bf16[4,4,96,768]{3,2,0,1:T(8,128)(2,1)S(1)}, u32[]{:S(2)}, u32[]{:S(2)}) collective-permute-start(bf16[4,4,96,768]{3,2,0,1:T(8,128)(2,1)S(1)} %fusion.10), channel_id=1, source_target_pairs={{0,1},{1,0},{2,3},{3,2},{4,5},{5,4},{6,7},{7,6},{8,9},{9,8},{10,11... | collective-permute-start | bytes 7077896 | tf_op jit(solution)/shard_map/ppermute | solution.py:31
  393.7 57.4 %collective-permute-start.39 = (bf16[768,1536]{0,1:T(8,128)(2,1)}, bf16[768,1536]{0,1:T(8,128)(2,1)}, u32[]{:S(2)}, u32[]{:S(2)}) collective-permute-start(bf16[768,1536]{0,1:T(8,128)(2,1)} %pad_maximum_fusion.4), channel_id=1, source_target_pairs={{0,1},{1,0},{2,3},{3,2},{4,5},{5,4},{6,7},{7,6},{8,9},{9,8},{10,11... | collective-permute-start | bytes 7077896 | tf_op jit(solution)/shard_map/ppermute | solution.py:31
  397.7 53.4 %collective-permute-start.41 = (bf16[768,1536]{0,1:T(8,128)(2,1)}, bf16[768,1536]{0,1:T(8,128)(2,1)}, u32[]{:S(2)}, u32[]{:S(2)}) collective-permute-start(bf16[768,1536]{0,1:T(8,128)(2,1)} %fusion.7), channel_id=1, source_target_pairs={{0,4},{1,3},{2,6},{3,1},{4,0},{5,7},{6,2},{7,5},{8,12},{9,11},{10,... | collective-permute-start | bytes 7077896 | tf_op jit(solution)/shard_map/ppermute | solution.py:31
  404.4 43.1 %collective-permute-start.30 = (bf16[2,4,96,768]{3,2,1,0:T(8,128)(2,1)}, bf16[2,4,96,768]{3,2,1,0:T(8,128)(2,1)}, u32[]{:S(2)}, u32[]{:S(2)}) collective-permute-start(bf16[2,4,96,768]{3,2,1,0:T(8,128)(2,1)} %pad_maximum_fusion.8), channel_id=1, source_target_pairs={{0,4},{1,3},{2,6},{3,1},{4,0},{5,7},{6,2},{7,5},{8,12},{9,11},{10,... | collective-permute-start | bytes 3538952 | tf_op jit(solution)/shard_map/ppermute | solution.py:31
  405.1 38.6 %collective-permute-start.35 = (bf16[2,4,32,768]{3,2,1,0:T(8,128)(2,1)S(1)}, bf16[2,4,32,768]{3,2,1,0:T(8,128)(2,1)}, u32[]{:S(2)}, u32[]{:S(2)}) collective-permute-start(bf16[2,4,32,768]{3,2,1,0:T(8,128)(2,1)S(1)} %pad_maximum_fusion.16), channel_id=1, source_target_pairs={{0,4},{1,3},{2,6},{3,1},{4,0},{5,7},{6,2},{7,5},{8,12},{9,11},{10,... | collective-permute-start | bytes 1179656 | tf_op jit(solution)/shard_map/ppermute | solution.py:31
  409.7 199.2 %collective-permute-start.55 = (bf16[4,96,768]{2,1,0:T(8,128)(2,1)}, bf16[4,96,768]{2,1,0:T(8,128)(2,1)}, u32[]{:S(2)}, u32[]{:S(2)}) collective-permute-start(bf16[4,96,768]{2,1,0:T(8,128)(2,1)} %pad_maximum_fusion.12), channel_id=1, source_target_pairs={{0,1},{1,0},{2,3},{3,2},{4,5},{5,4},{6,7},{7,6},{8,9},{9,8},{10,11... | collective-permute-start | bytes 1769480 | tf_op jit(solution)/shard_map/ppermute | solution.py:31
  443.7 28.4 %collective-permute-start.47 = (bf16[2,2,96,768]{3,2,1,0:T(8,128)(2,1)}, bf16[2,2,96,768]{3,2,1,0:T(8,128)(2,1)}, u32[]{:S(2)}, u32[]{:S(2)}) collective-permute-start(bf16[2,2,96,768]{3,2,1,0:T(8,128)(2,1)} %get-tuple-element.120), channel_id=1, source_target_pairs={{0,16},{1,17},{2,18},{3,19},{4,20},{5,21},{6,22},{7,23},{8,24},{9,... | collective-permute-start | bytes 1769480 | tf_op jit(solution)/shard_map/ppermute | solution.py:31
  447.5 27.8 %collective-permute-start.36 = (bf16[4,32,768]{2,1,0:T(8,128)(2,1)S(1)}, bf16[4,32,768]{2,1,0:T(8,128)(2,1)}, u32[]{:S(2)}, u32[]{:S(2)}) collective-permute-start(bf16[4,32,768]{2,1,0:T(8,128)(2,1)S(1)} %fusion.162), channel_id=1, source_target_pairs={{0,2},{1,5},{2,0},{3,7},{4,6},{5,1},{6,4},{7,3},{8,10},{9,13},{10,... | collective-permute-start | bytes 589832 | tf_op jit(solution)/shard_map/ppermute | solution.py:31
  460.2 29.8 %collective-permute-start.42 = (bf16[4,96,1536]{2,1,0:T(8,128)(2,1)}, bf16[4,96,1536]{2,1,0:T(8,128)(2,1)}, u32[]{:S(2)}, u32[]{:S(2)}) collective-permute-start(bf16[4,96,1536]{2,1,0:T(8,128)(2,1)} %bitcast.535), channel_id=1, source_target_pairs={{0,2},{1,5},{2,0},{3,7},{4,6},{5,1},{6,4},{7,3},{8,10},{9,13},{10,... | collective-permute-start | bytes 3538952 | tf_op jit(solution)/shard_map/ppermute | solution.py:31
  463.9 19.2 %collective-permute-start.31 = (bf16[4,96,768]{2,1,0:T(8,128)(2,1)}, bf16[4,96,768]{2,1,0:T(8,128)(2,1)}, u32[]{:S(2)}, u32[]{:S(2)}) collective-permute-start(bf16[4,96,768]{2,1,0:T(8,128)(2,1)} %fusion.58), channel_id=1, source_target_pairs={{0,2},{1,5},{2,0},{3,7},{4,6},{5,1},{6,4},{7,3},{8,10},{9,13},{10,... | collective-permute-start | bytes 1769480 | tf_op jit(solution)/shard_map/ppermute | solution.py:31
  472.1 53.6 %collective-permute-start.62 = (bf16[8,96,768]{2,1,0:T(8,128)(2,1)}, bf16[8,96,768]{2,1,0:T(8,128)(2,1)}, u32[]{:S(2)}, u32[]{:S(2)}) collective-permute-start(bf16[8,96,768]{2,1,0:T(8,128)(2,1)} %pad_maximum_fusion.9), channel_id=1, source_target_pairs={{0,2},{1,5},{2,0},{3,7},{4,6},{5,1},{6,4},{7,3},{8,10},{9,13},{10,... | collective-permute-start | bytes 3538952 | tf_op jit(solution)/shard_map/ppermute | solution.py:31
  476.5 17.6 %collective-permute-start.37 = (bf16[2,32,768]{2,1,0:T(8,128)(2,1)S(1)}, bf16[2,32,768]{2,1,0:T(8,128)(2,1)S(1)}, u32[]{:S(2)}, u32[]{:S(2)}) collective-permute-start(bf16[2,32,768]{2,1,0:T(8,128)(2,1)S(1)} %fusion.194), channel_id=1, source_target_pairs={{0,8},{1,9},{2,10},{3,11},{4,12},{5,13},{6,14},{7,15},{8,0},{9,1},... | collective-permute-start | bytes 294920 | tf_op jit(solution)/shard_map/ppermute | solution.py:31
  492.4 17.9 %collective-permute-start.43 = (bf16[2,96,1536]{2,1,0:T(8,128)(2,1)S(1)}, bf16[2,96,1536]{2,1,0:T(8,128)(2,1)S(1)}, u32[]{:S(2)}, u32[]{:S(2)}) collective-permute-start(bf16[2,96,1536]{2,1,0:T(8,128)(2,1)S(1)} %slice.833), channel_id=1, source_target_pairs={{0,8},{1,9},{2,10},{3,11},{4,12},{5,13},{6,14},{7,15},{8,0},{9,1},... | collective-permute-start | bytes 1769480 | tf_op jit(solution)/shard_map/ppermute | solution.py:31
  494.1 18.9 %collective-permute-start.38 = (bf16[32,768]{1,0:T(8,128)(2,1)S(1)}, bf16[32,768]{1,0:T(8,128)(2,1)S(1)}, u32[]{:S(2)}, u32[]{:S(2)}) collective-permute-start(bf16[32,768]{1,0:T(8,128)(2,1)S(1)} %fusion.198), channel_id=1, source_target_pairs={{0,16},{1,17},{2,18},{3,19},{4,20},{5,21},{6,22},{7,23},{8,24},{9,... | collective-permute-start | bytes 147464 | tf_op jit(solution)/shard_map/ppermute | solution.py:31
  495.4 17.9 %collective-permute-start.33 = (bf16[96,768]{1,0:T(8,128)(2,1)S(1)}, bf16[96,768]{1,0:T(8,128)(2,1)S(1)}, u32[]{:S(2)}, u32[]{:S(2)}) collective-permute-start(bf16[96,768]{1,0:T(8,128)(2,1)S(1)} %fusion.185), channel_id=1, source_target_pairs={{0,16},{1,17},{2,18},{3,19},{4,20},{5,21},{6,22},{7,23},{8,24},{9,... | collective-permute-start | bytes 442376 | tf_op jit(solution)/shard_map/ppermute | solution.py:31
  511.2 13.1 %collective-permute-start.44 = (bf16[1,96,1536]{2,1,0:T(8,128)(2,1)}, bf16[1,96,1536]{2,1,0:T(8,128)(2,1)}, u32[]{:S(2)}, u32[]{:S(2)}) collective-permute-start(bf16[1,96,1536]{2,1,0:T(8,128)(2,1)} %slice.834), channel_id=1, source_target_pairs={{0,16},{1,17},{2,18},{3,19},{4,20},{5,21},{6,22},{7,23},{8,24},{9,... | collective-permute-start | bytes 884744 | tf_op jit(solution)/shard_map/ppermute | solution.py:31
  528.2 134.0 %collective-permute-start.67 = (bf16[16,96,768]{2,1,0:T(8,128)(2,1)}, bf16[16,96,768]{2,1,0:T(8,128)(2,1)}, u32[]{:S(2)}, u32[]{:S(2)}) collective-permute-start(bf16[16,96,768]{2,1,0:T(8,128)(2,1)} %constant_dynamic-update-slice_fusion), channel_id=1, source_target_pairs={{0,4},{1,3},{2,6},{3,1},{4,0},{5,7},{6,2},{7,5},{8,12},{9,11},{10,... | collective-permute-start | bytes 7077896 | tf_op jit(solution)/shard_map/ppermute | solution.py:31
  529.7 28.1 %collective-permute-start.63 = (bf16[96,768]{1,0:T(8,128)(2,1)S(1)}, bf16[96,768]{1,0:T(8,128)(2,1)S(1)}, u32[]{:S(2)}, u32[]{:S(2)}) collective-permute-start(bf16[96,768]{1,0:T(8,128)(2,1)S(1)} %broadcast_select_fusion), channel_id=1, source_target_pairs={{0,1},{1,0},{2,3},{3,2},{4,5},{5,4},{6,7},{7,6},{8,9},{9,8},{10,11... | collective-permute-start | bytes 442376 | tf_op jit(solution)/shard_map/ppermute | solution.py:31
  534.0 23.8 %collective-permute-start.50 = (f32[16,768]{1,0:T(8,128)S(1)}, f32[16,768]{1,0:T(8,128)S(1)}, u32[]{:S(2)}, u32[]{:S(2)}) collective-permute-start(f32[16,768]{1,0:T(8,128)S(1)} %add.885), channel_id=1, source_target_pairs={{0,4},{1,5},{2,6},{3,7},{4,0},{5,1},{6,2},{7,3},{8,12},{9,13},{10,... | collective-permute-start | bytes 147464 | tf_op jit(solution)/shard_map/ppermute | solution.py:31
  557.9 32.6 %collective-permute-start.64 = (bf16[2,96,768]{2,1,0:T(8,128)(2,1)S(1)}, bf16[2,96,768]{2,1,0:T(8,128)(2,1)S(1)}, u32[]{:S(2)}, u32[]{:S(2)}) collective-permute-start(bf16[2,96,768]{2,1,0:T(8,128)(2,1)S(1)} %pad_maximum_fusion.20), channel_id=1, source_target_pairs={{0,16},{1,17},{2,18},{3,19},{4,20},{5,21},{6,22},{7,23},{8,24},{9,... | collective-permute-start | bytes 884744 | tf_op jit(solution)/shard_map/ppermute | solution.py:31
  561.9 13.5 %collective-permute-start.52 = (f32[16,768]{1,0:T(8,128)S(1)}, f32[16,768]{1,0:T(8,128)S(1)}, u32[]{:S(2)}, u32[]{:S(2)}) collective-permute-start(f32[16,768]{1,0:T(8,128)S(1)} %add.887), channel_id=1, source_target_pairs={{0,16},{1,17},{2,18},{3,19},{4,20},{5,21},{6,22},{7,23},{8,24},{9,... | collective-permute-start | bytes 147464 | tf_op jit(solution)/shard_map/ppermute | solution.py:31
  590.6 16.0 %collective-permute-start.65 = (bf16[4,96,768]{2,1,0:T(8,128)(2,1)S(1)}, bf16[4,96,768]{2,1,0:T(8,128)(2,1)S(1)}, u32[]{:S(2)}, u32[]{:S(2)}) collective-permute-start(bf16[4,96,768]{2,1,0:T(8,128)(2,1)S(1)} %pad_maximum_fusion.15), channel_id=1, source_target_pairs={{0,8},{1,9},{2,10},{3,11},{4,12},{5,13},{6,14},{7,15},{8,0},{9,1},... | collective-permute-start | bytes 1769480 | tf_op jit(solution)/shard_map/ppermute | solution.py:31
  596.3 12.6 %collective-permute-start.58 = (bf16[4,96,768]{2,1,0:T(8,128)(2,1)S(1)}, bf16[4,96,768]{2,1,0:T(8,128)(2,1)S(1)}, u32[]{:S(2)}, u32[]{:S(2)}) collective-permute-start(bf16[4,96,768]{2,1,0:T(8,128)(2,1)S(1)} %pad_maximum_fusion.13), channel_id=1, source_target_pairs={{0,1},{1,0},{2,3},{3,2},{4,5},{5,4},{6,7},{7,6},{8,9},{9,8},{10,11... | collective-permute-start | bytes 1769480 | tf_op jit(solution)/shard_map/ppermute | solution.py:31
  606.8 30.1 %collective-permute-start.66 = (bf16[8,96,768]{2,1,0:T(8,128)(2,1)S(1)}, bf16[8,96,768]{2,1,0:T(8,128)(2,1)S(1)}, u32[]{:S(2)}, u32[]{:S(2)}) collective-permute-start(bf16[8,96,768]{2,1,0:T(8,128)(2,1)S(1)} %pad_maximum_fusion.10), channel_id=1, source_target_pairs={{0,2},{1,5},{2,0},{3,7},{4,6},{5,1},{6,4},{7,3},{8,10},{9,13},{10,... | collective-permute-start | bytes 3538952 | tf_op jit(solution)/shard_map/ppermute | solution.py:31
  638.0 29.2 %collective-permute-start.68 = (bf16[16,96,768]{2,1,0:T(8,128)(2,1)}, bf16[16,96,768]{2,1,0:T(8,128)(2,1)}, u32[]{:S(2)}, u32[]{:S(2)}) collective-permute-start(bf16[16,96,768]{2,1,0:T(8,128)(2,1)} %constant_dynamic-update-slice_fusion.5), channel_id=1, source_target_pairs={{0,4},{1,3},{2,6},{3,1},{4,0},{5,7},{6,2},{7,5},{8,12},{9,11},{10,... | collective-permute-start | bytes 7077896 | tf_op jit(solution)/shard_map/ppermute | solution.py:31
  (200 other events, 1412.7 us)

commit v2 on v1

v2 whole, which is shorter than its diff:
```python
import functools
import math

import jax
import jax.numpy as jnp
from jax import lax
from jax.experimental import pallas as pl
from jax.experimental.pallas import tpu as pltpu
from jax.sharding import PartitionSpec as P

H = 12
CLASSES = 21843
STEP = 10


highest = lax.Precision.HIGHEST
newton_one = 3.4445
newton_two = -4.775
newton_three = 2.0315
clip_limit = 0.05
muon_rate = 0.3
decay_rate = 0.05
adam_rate = 0.01
vector_rate = 0.05
momentum_keep = 0.5
adam_first = 0.5
adam_second = 0.999


AXES = ("dp", "cls")


def swap(value, count, masks):
    return lax.ppermute(value, AXES, [(i, i ^ masks[i & 1]) for i in range(count)])


def pick(value, index, axis):
    return lax.dynamic_index_in_dim(value, index, axis, keepdims=False)


def codes(masks):
    found = [0]
    for mask in masks:
        found = found + [code ^ mask for code in found]
    return found


def ordered_pair(bit, mine, other, axis):
    return jnp.where(
        bit == 0, jnp.stack([mine, other], axis=axis), jnp.stack([other, mine], axis=axis)
    )


def product(left_side, right_side):
    return jnp.dot(left_side, right_side, precision=highest)


def low_dot(left_side, right_side):
    return jnp.dot(left_side, right_side, preferred_element_type=jnp.float32)


def contract_rows(left_side, right_side):
    return lax.dot_general(
        left_side, right_side, (((0,), (0,)), ((), ())), preferred_element_type=jnp.float32
    )


def contract_cols(left_side, right_side):
    return lax.dot_general(
        left_side, right_side, (((1,), (1,)), ((), ())), preferred_element_type=jnp.float32
    )


def layer_norm(inputs, gain_row, shift_row):
    mean_row = jnp.mean(inputs, axis=-1, keepdims=True)
    centred = inputs - mean_row
    variance = jnp.mean(centred * centred, axis=-1, keepdims=True)
    return centred * lax.rsqrt(variance + 1e-06) * gain_row + shift_row


def tie(*values):
    return lax.optimization_barrier(values)


class Lane:
    def __init__(self, steps, exchange, what):
        self.steps, self.exchange, self.what = steps, exchange, what
        self.moving, self.result = False, None
        self.value, self.masks = next(steps)

    def advance(self, value):
        masks = self.masks
        if self.moving:
            try:
                value, masks = self.steps.send(value)
            except StopIteration as end:
                self.value, self.result, self.moving = None, end.value, False
                return
        self.moving = True
        self.value, self.masks = self.exchange(value, masks, self.what), masks


def sync(values, *lanes):
    lanes = [lane for lane in lanes if lane.result is None]
    tied = tie(*values, *[lane.value for lane in lanes])
    for lane, value in zip(lanes, tied[len(values) :]):
        lane.advance(value)
    return tied[: len(values)]


def finish(*lanes):
    while any(lane.result is None for lane in lanes):
        sync((), *lanes)
    return [lane.result for lane in lanes]


def collecting(value, stages):
    for stage in stages[:-1]:
        value = jnp.concatenate([value, (yield value, stage)], axis=0)
    return [value, (yield value, stages[-1])]


def gelu_with_slope(value):
    size = jnp.abs(value)
    bell = jnp.exp(-0.5 * value * value)
    t = 1.0 / (1.0 + (0.3275911 * 0.7071067811865476) * size)
    poly = 1.061405429
    for term in (-1.453152027, 1.421413741, -0.284496736, 0.254829592):
        poly = poly * t + term
    tail = 0.5 * poly * t * bell
    share = jnp.where(value < 0, tail, 1.0 - tail)
    return value * share, share + value * (0.3989422804014327 * bell)


def projections(attn_b, vec_w, embedded):
    model_width = attn_b.shape[1]
    normed = layer_norm(embedded, vec_w[4], vec_w[5]).astype(jnp.bfloat16)
    queries = (low_dot(normed, attn_b[:model_width]) + vec_w[0]).astype(jnp.bfloat16)
    key_rows = low_dot(normed, attn_b[model_width : 2 * model_width]).astype(jnp.bfloat16)
    values = (low_dot(normed, attn_b[2 * model_width : 3 * model_width]) + vec_w[1]).astype(
        jnp.bfloat16
    )
    return (normed, queries, key_rows, values)


def half_of(value, half, width):
    lane = lax.broadcasted_iota(jnp.int32, value.shape, 1)
    keep = (lane >= half * width) & (lane < (half + 1) * width)
    return jnp.where(keep, value, jnp.zeros_like(value))


def mixing_kernel(width, rows, ids_down_ref, ids_ref, q_ref, k_ref, v_ref, out_ref, summary_ref, seen_ref):
    step = pl.program_id(0)
    pack = q_ref.shape[1] // width
    keys = [half_of(k_ref[...], half, width) for half in range(pack)]
    values = [half_of(v_ref[...], half, width) for half in range(pack)]
    scale = width ** (-0.5)
    lane = lax.broadcasted_iota(jnp.int32, (rows, seen_ref.shape[1]), 1)
    for start in range(0, q_ref.shape[0], rows):
        here = pl.ds(start, rows)
        same = ids_down_ref[here] == ids_ref[...]
        queries = q_ref[here]
        seen = seen_ref[here]
        total = None
        for half in range(pack):
            scores = jnp.where(same, contract_cols(queries, keys[half]) * scale, -1e30)
            top = jnp.max(scores, axis=1, keepdims=True)
            exponents = jnp.exp(scores - top)
            sums = jnp.sum(exponents, axis=1, keepdims=True)
            probs = (exponents * (1.0 / sums)).astype(jnp.bfloat16)
            mixed = low_dot(probs, values[half])
            total = mixed if total is None else total + mixed
            seen = jnp.where(lane == step * pack + half, top + jnp.log(sums), seen)
        out_ref[here] = total.astype(out_ref.dtype)
        seen_ref[here] = seen

    @pl.when(step == pl.num_programs(0) - 1)
    def _():
        summary_ref[...] = seen_ref[...].T[: summary_ref.shape[0]]


def mixing(queries, key_rows, values, image_index, heads, rows=256):
    token_count, model_width = queries.shape
    width = model_width // heads
    pack = 128 // width
    tile = pl.BlockSpec((token_count, 128), lambda step: (0, step))

    def whole(shape):
        return pl.BlockSpec(shape, lambda step: (0, 0))

    kept = -(-heads // 8) * 8
    return pl.pallas_call(
        functools.partial(mixing_kernel, width, rows),
        grid=(heads // pack,),
        out_shape=(
            jax.ShapeDtypeStruct((token_count, model_width), jnp.bfloat16),
            jax.ShapeDtypeStruct((kept, token_count), jnp.float32),
        ),
        in_specs=[whole((token_count, 1)), whole((1, token_count)), tile, tile, tile],
        out_specs=(tile, whole((kept, token_count))),
        scratch_shapes=[pltpu.VMEM((token_count, 128), jnp.float32)],
        compiler_params=pltpu.CompilerParams(vmem_limit_bytes=32 * 1024 * 1024),
        cost_estimate=pl.CostEstimate(
            flops=4 * token_count * token_count * model_width,
            bytes_accessed=8 * token_count * model_width,
            transcendentals=heads * token_count * token_count,
        ),
        name="mixing",
    )(image_index[:, None], image_index[None, :], queries, key_rows, values)


def mixing_grads_kernel(width, rows, ids_down_ref, ids_ref, summary_ref, q_ref, k_ref, v_ref, d_ref, dq_ref, dk_ref, dv_ref):
    step = pl.program_id(0)
    pack = q_ref.shape[1] // width
    scale = width ** (-0.5)
    keys = [half_of(k_ref[...], half, width) for half in range(pack)]
    values = [half_of(v_ref[...], half, width) for half in range(pack)]
    key_sums, value_sums = 0.0, 0.0
    for start in range(0, q_ref.shape[0], rows):
        here = pl.ds(start, rows)
        same = ids_down_ref[...] == ids_ref[:, here]
        query_sum = 0.0
        for half in range(pack):
            queries, d_mixed = half_of(q_ref[here], half, width), half_of(d_ref[here], half, width)
            scores = contract_cols(keys[half], queries) * scale
            summary = summary_ref[pl.ds(step * pack + half, 1), here]
            probs = jnp.where(same, jnp.exp(jnp.where(same, scores - summary, -1e30)), 0.0)
            d_probs = contract_cols(values[half], d_mixed)
            product = probs * d_probs
            d_scores = product - probs * jnp.sum(product, axis=0, keepdims=True)
            d_scores = d_scores.astype(jnp.bfloat16)
            value_sums = value_sums + low_dot(probs.astype(jnp.bfloat16), d_mixed)
            key_sums = key_sums + low_dot(d_scores, queries)
            query_sum = query_sum + contract_rows(d_scores, keys[half])
        dq_ref[here] = (query_sum * scale).astype(dq_ref.dtype)
    dk_ref[...] = (key_sums * scale).astype(dk_ref.dtype)
    dv_ref[...] = value_sums.astype(dv_ref.dtype)


def mixing_grads(queries, key_rows, values, d_mixed, summary, image_index, heads, rows=256):
    token_count, model_width = queries.shape
    width = model_width // heads
    pack = 128 // width
    tile = pl.BlockSpec((token_count, 128), lambda step: (0, step))

    def whole(shape):
        return pl.BlockSpec(shape, lambda step: (0, 0))

    return pl.pallas_call(
        functools.partial(mixing_grads_kernel, width, rows),
        grid=(heads // pack,),
        out_shape=(jax.ShapeDtypeStruct((token_count, model_width), jnp.bfloat16),) * 3,
        in_specs=[whole((token_count, 1)), whole((1, token_count)), whole(summary.shape)] + [tile] * 4,
        out_specs=(tile,) * 3,
        compiler_params=pltpu.CompilerParams(vmem_limit_bytes=32 * 1024 * 1024),
        cost_estimate=pl.CostEstimate(
            flops=10 * token_count * token_count * model_width,
            bytes_accessed=14 * token_count * model_width,
            transcendentals=heads * token_count * token_count,
        ),
        name="mixing_grads",
    )(image_index[:, None], image_index[None, :], summary, queries, key_rows, values, d_mixed)


IN_VMEM = pl.BlockSpec(memory_space=pltpu.VMEM)
IN_SMEM = pl.BlockSpec(memory_space=pltpu.SMEM)


def hidden_forward_kernel(rows, normed_ref, middle_ref, bias_ref, out_bias_ref, *refs):
    part_refs = refs[:4]
    final_ref, active_ref, slope_ref = refs[4:]
    width = normed_ref.shape[1]

    def block(step, carry):
        here = pl.ds(pl.multiple_of(step * rows, rows), rows)
        normed = normed_ref[here]
        total = middle_ref[here] + out_bias_ref[...]
        for index, part_ref in enumerate(part_refs):
            hidden = contract_cols(normed, part_ref[:, :width]) + bias_ref[pl.ds(index, 1)]
            active, slope = gelu_with_slope(hidden)
            active = active.astype(jnp.bfloat16)
            active_ref[index, here] = active
            slope_ref[index, here] = slope
            total = total + low_dot(active, part_ref[:, width:])
        final_ref[here] = total
        return carry

    lax.fori_loop(0, normed_ref.shape[0] // rows, block, 0)


def hidden_forward(normed, middle, bias, out_bias, parts, rows=256):
    token_count, width = normed.shape
    return pl.pallas_call(
        functools.partial(hidden_forward_kernel, rows),
        out_shape=(
            jax.ShapeDtypeStruct((token_count, width), jnp.float32),
            jax.ShapeDtypeStruct((4, token_count, width), jnp.bfloat16),
            jax.ShapeDtypeStruct((4, token_count, width), jnp.float32),
        ),
        in_specs=[IN_VMEM] * 8,
        out_specs=(IN_VMEM,) * 3,
        compiler_params=pltpu.CompilerParams(vmem_limit_bytes=48 * 1024 * 1024),
        cost_estimate=pl.CostEstimate(
            flops=16 * token_count * width * width,
            bytes_accessed=16 * width * width + 32 * token_count * width,
            transcendentals=8 * token_count * width,
        ),
        name="hidden_forward",
    )(normed, middle, bias, out_bias, *parts)


def hidden_back_kernel(core_ref, d_out_ref, normed_ref, active_ref, slope_ref, *refs):
    part_refs = refs[:4]
    d_hidden_ref, bias_ref, away_ref = refs[4:]
    width = d_out_ref.shape[1]
    first = core_ref[0, 0] == 0
    right = jnp.where(first, d_out_ref[...], normed_ref[...])
    for index, part_ref in enumerate(part_refs):
        d_active = contract_cols(d_out_ref[...], part_ref[:, width:])
        d_hidden = (slope_ref[index] * d_active).astype(jnp.bfloat16)
        d_hidden_ref[index] = d_hidden
        bias_ref[pl.ds(index, 1)] = jnp.sum(d_hidden.astype(jnp.float32), axis=0, keepdims=True)
        left = jnp.where(first, active_ref[index], d_hidden)
        away_ref[index] = contract_rows(left, right).astype(jnp.bfloat16)


def hidden_back(core, d_out, normed, active, slope, parts):
    token_count, width = d_out.shape
    return pl.pallas_call(
        hidden_back_kernel,
        out_shape=(
            jax.ShapeDtypeStruct((4, token_count, width), jnp.bfloat16),
            jax.ShapeDtypeStruct((4, width), jnp.float32),
            jax.ShapeDtypeStruct((4, width, width), jnp.bfloat16),
        ),
        in_specs=[IN_SMEM] + [IN_VMEM] * 8,
        out_specs=(IN_VMEM,) * 3,
        compiler_params=pltpu.CompilerParams(vmem_limit_bytes=48 * 1024 * 1024),
        cost_estimate=pl.CostEstimate(
            flops=16 * token_count * width * width,
            bytes_accessed=16 * width * width + 32 * token_count * width,
            transcendentals=0,
        ),
        name="hidden_back",
    )(core.reshape(1, 1), d_out, normed, active, slope, *parts)


def kept_grads_kernel(core_ref, d_out_ref, normed_ref, active_ref, d_hidden_ref, *refs):
    part_refs = refs[:4]
    d_normed_ref, kept_ref = refs[4:]
    width = d_out_ref.shape[1]
    first = core_ref[0, 0] == 0
    right = jnp.where(first, normed_ref[...], d_out_ref[...])
    total = None
    for index, part_ref in enumerate(part_refs):
        d_hidden = d_hidden_ref[index]
        term = low_dot(d_hidden, part_ref[:, :width])
        total = term if total is None else total + term
        left = jnp.where(first, d_hidden, active_ref[index])
        kept_ref[index] = contract_rows(left, right)
    d_normed_ref[...] = total


def kept_grads(core, d_out, normed, active, d_hidden, parts):
    token_count, width = d_out.shape
    return pl.pallas_call(
        kept_grads_kernel,
        out_shape=(
            jax.ShapeDtypeStruct((token_count, width), jnp.float32),
            jax.ShapeDtypeStruct((4, width, width), jnp.float32),
        ),
        in_specs=[IN_SMEM] + [IN_VMEM] * 8,
        out_specs=(IN_VMEM,) * 2,
        compiler_params=pltpu.CompilerParams(vmem_limit_bytes=48 * 1024 * 1024),
        cost_estimate=pl.CostEstimate(
            flops=16 * token_count * width * width,
            bytes_accessed=32 * width * width + 20 * token_count * width,
            transcendentals=0,
        ),
        name="kept_grads",
    )(core.reshape(1, 1), d_out, normed, active, d_hidden, *parts)


def orthogonal_kernel(part_count, chunk, full_steps, row_count, factor_ref, *refs):
    moment_refs, grad_refs = refs[:part_count], refs[part_count : 2 * part_count]
    out_ref, rows_ref, gram_ref, low_ref, change_ref = refs[2 * part_count :]
    part_rows, width = moment_refs[0].shape
    factor = factor_ref[0, 0]
    chunks = part_rows // chunk
    bf = jnp.bfloat16

    gram_ref[...] = jnp.zeros_like(gram_ref)
    for index in range(part_count):

        def start(step, carry, index=index):
            here = pl.ds(pl.multiple_of(step * chunk, chunk), chunk)
            rows = (
                momentum_keep * moment_refs[index][here].astype(jnp.float32)
                + factor * grad_refs[index][here].astype(jnp.float32)
            ).astype(bf)
            rows_ref[pl.ds(pl.multiple_of(index * part_rows + step * chunk, chunk), chunk)] = rows
            gram_ref[...] += contract_rows(rows, rows)
            return carry

        lax.fori_loop(0, chunks, start, 0)
    gram = gram_ref[...]
    diagonal = lax.broadcasted_iota(jnp.int32, gram.shape, 0) == lax.broadcasted_iota(
        jnp.int32, gram.shape, 1
    )
    trace = jnp.sum(jnp.where(diagonal, gram, 0.0))
    inverse = 1.0 / (jnp.sqrt(jnp.full((1, 1), trace)) + 1e-07)
    gram_ref[...] = gram * (inverse * inverse)
    for step in range(5):
        low_ref[...] = gram_ref[...].astype(bf)
        change_ref[...] = (
            newton_two * gram_ref[...] + newton_three * low_dot(low_ref[...], low_ref[...])
        ).astype(bf)
        if step < full_steps:
            scale = inverse if step == 0 else jnp.ones((1, 1), jnp.float32)
            last = step == full_steps - 1
            if step < 4:
                gram_ref[...] = jnp.zeros_like(gram_ref)

            def advance(index, carry, step=step, scale=scale, last=last):
                here = pl.ds(pl.multiple_of(index * chunk, chunk), chunk)
                old = rows_ref[here]
                new = scale * (newton_one * old.astype(jnp.float32) + low_dot(old, change_ref[...]))
                if last:
                    @pl.when(index == 0)
                    def _():
                        out_ref[...] = new[:row_count]
                new = new.astype(bf)
                if not last:
                    rows_ref[here] = new
                gram_ref[...] += contract_rows(new, new)
                return carry

            lax.fori_loop(0, part_count * chunks, advance, 0)
        else:
            rows = out_ref[...]
            out_ref[...] = newton_one * rows + low_dot(rows.astype(bf), change_ref[...])
            if step < 4:
                gram_ref[...] = newton_one * gram_ref[...] + low_dot(low_ref[...], change_ref[...])
                low_ref[...] = gram_ref[...].astype(bf)
                gram_ref[...] = newton_one * gram_ref[...] + low_dot(low_ref[...], change_ref[...])

def orthogonal_rows(moments, grads, factor, row_count, chunk, full_steps):
    count, (part_rows, width) = len(moments), moments[0].shape
    body = functools.partial(orthogonal_kernel, count, chunk, full_steps, row_count)
    flops = 2 * width * width * (count * part_rows * (2 * full_steps + 1) + 9 * width)
    return pl.pallas_call(
        body,
        out_shape=jax.ShapeDtypeStruct((row_count, width), jnp.float32),
        in_specs=[pl.BlockSpec(memory_space=pltpu.SMEM)]
        + [pl.BlockSpec(memory_space=pltpu.VMEM)] * (2 * count),
        out_specs=pl.BlockSpec(memory_space=pltpu.VMEM),
        scratch_shapes=[
            pltpu.VMEM((count * part_rows, width), jnp.bfloat16),
            pltpu.VMEM((width, width), jnp.float32),
            pltpu.VMEM((width, width), jnp.bfloat16),
            pltpu.VMEM((width, width), jnp.bfloat16),
        ],
        compiler_params=pltpu.CompilerParams(vmem_limit_bytes=48 * 1024 * 1024),
        cost_estimate=pl.CostEstimate(flops=flops, bytes_accessed=4 * count * part_rows * width, transcendentals=0),
        name="orthogonal_rows",
    )(factor.reshape(1, 1), *moments, *grads)


def adam_step(weight, first_moment, second_moment, gradient, step_rate):
    first_moment = adam_first * first_moment + (1.0 - adam_first) * gradient
    second_moment = adam_second * second_moment + (1.0 - adam_second) * gradient * gradient
    first_hat = first_moment / (1.0 - adam_first**STEP)
    second_hat = second_moment / (1.0 - adam_second**STEP)
    weight = weight * (1.0 - step_rate * decay_rate) - step_rate * first_hat / (
        jnp.sqrt(second_hat) + 1e-08
    )
    return (weight, first_moment, second_moment)


def on_device(
    patches,
    image_ids,
    patch_place,
    labels,
    attn_w,
    mlp_w,
    embed_w,
    vec_w,
    head_w,
    attn_mom,
    mlp_mom,
    embed_m,
    embed_v,
    vec_m,
    vec_v,
    head_m,
    head_v,
):
    groups = lax.axis_size("cls")
    owners = lax.axis_size("dp")
    count = groups * owners
    top = count.bit_length() - 1
    low_bits = groups.bit_length() - 1
    member_index = lax.axis_index("cls")
    owner_index = lax.axis_index("dp")
    me = owner_index * groups + member_index
    core = me & 1
    model_width = vec_w.shape[1]
    slot_count = labels.shape[1]
    high_bits = list(range(top - 1, 2, -1))
    third, fourth, pair = (2, 4), (4, 2), (1, 1)
    third_mine = jnp.where(core == 0, third[0], third[1])
    fourth_mine = jnp.where(core == 0, fourth[0], fourth[1])

    def exchange(value, masks, what="small"):
        with jax.named_scope(what):
            return swap(value, count, masks)

    def plain(bit):
        return (1 << bit,) * 2

    def bit_of(bit):
        return (me >> bit) & 1

    def lane(steps, what):
        return Lane(steps, exchange, what)

    def of_core(value):
        left, right = value[:, :model_width], value[:, model_width:]
        return jnp.where(core == 0, left, right), jnp.where(core == 0, right, left)

    attn_rows, embed_rows, mlp_rows = attn_w.shape[0], embed_w.shape[0], mlp_w.shape[0]
    up_stages = [plain(bit) for bit in high_bits]
    down_stages = up_stages[::-1]

    def ordered_weights(block):
        for axis, bit in enumerate(high_bits):
            block = ordered_pair(bit_of(bit), block, (yield block, plain(bit)), axis)
        block = block.reshape(-1, attn_rows + embed_rows, model_width)
        block = jnp.stack([block, (yield block, third)])
        block = jnp.concatenate([block, (yield block, fourth)], axis=0)
        return block, (yield block, pair)

    sibling = me ^ 1
    places = [
        me,
        me ^ third_mine,
        me ^ fourth_mine,
        me ^ 6,
        sibling,
        sibling ^ fourth_mine,
        sibling ^ third_mine,
        sibling ^ 6,
    ]
    attn_lane = lane(
        ordered_weights(jnp.concatenate([attn_w, embed_w], axis=0).astype(jnp.bfloat16)),
        "attn_weights",
    )
    mlp_lane = lane(
        collecting(mlp_w.astype(jnp.bfloat16)[None], up_stages + [third]), "mlp_weights"
    )
    for _ in high_bits:
        sync((), attn_lane)
    sync((), attn_lane, mlp_lane)
    sync((), attn_lane, mlp_lane)

    shard_rows, shard_width = head_w.shape
    chunk = -(-shard_width // (owners * 128)) * 128
    padding = owners * chunk - shard_width
    owner_bits = list(range(low_bits, top))

    def transposed(value, order):
        value = value.reshape((2,) * len(owner_bits) + value.shape[1:])
        for bit in order:
            axis = top - 1 - bit
            mine = bit_of(bit)
            stay, leave = pick(value, mine, axis), pick(value, 1 - mine, axis)
            value = ordered_pair(mine, stay, (yield leave, plain(bit)), axis)
        return value.reshape((owners,) + value.shape[len(owner_bits) :])

    head_low = jnp.pad(head_w.astype(jnp.bfloat16), ((0, 0), (0, padding)))
    head_low = head_low.reshape(shard_rows, owners, chunk).transpose(1, 0, 2)
    head_lane = lane(transposed(head_low, owner_bits[1:] + owner_bits[:1]), "head")

    def of_chip():
        value = mlp_mom.astype(jnp.bfloat16)
        mine, leave = of_core(value)
        rows = jnp.stack([mine, (yield leave, pair)])
        return (yield from collecting(rows, up_stages + [third, fourth]))

    mom_lane = lane(of_chip(), "mlp_moments")
    attn_mom_lane = lane(
        collecting(attn_mom.astype(jnp.bfloat16)[None], up_stages[2:] + [third, fourth, pair]),
        "attn_moments",
    )
    sync((), attn_lane, mlp_lane, head_lane)
    pieces, others = finish(attn_lane)[0]
    attn_b = jnp.zeros((count // 8, 8, attn_rows, model_width), jnp.bfloat16)
    embed_b = jnp.zeros((count // 8, 8, embed_rows, model_width), jnp.bfloat16)
    for index, place in enumerate(places):
        piece = (pieces if index < 4 else others)[index % 4]
        attn_b = lax.dynamic_update_slice_in_dim(attn_b, piece[:, None, :attn_rows], place & 7, 1)
        embed_b = lax.dynamic_update_slice_in_dim(embed_b, piece[:, None, attn_rows:], place & 7, 1)
    attn_b = attn_b.reshape(count * attn_rows, model_width)
    embed_b = embed_b.reshape(count * embed_rows, model_width)

    attn_b, embed_b = sync((attn_b, embed_b), mlp_lane, head_lane)
    part_a = jnp.concatenate(finish(mlp_lane)[0], axis=0)

    def once(value, stage):
        return (yield value, stage)

    b_lane = lane(once(part_a, fourth), "mlp_weights")
    c_lane = lane(once(part_a, pair), "mlp_weights")
    sync((), b_lane)
    sync((), c_lane)
    image_index = lax.dynamic_index_in_dim(image_ids, member_index, 0, keepdims=False)
    my_labels = lax.dynamic_index_in_dim(labels, member_index, 0, keepdims=False)
    position = patch_place[0]
    patch_dim = patches.shape[1]
    grid_size = (embed_b.shape[0] - patch_dim) // 2
    grid_index = jnp.arange(grid_size)
    places_hot = [(position[axis][:, None] == grid_index[None]).astype(jnp.bfloat16) for axis in (0, 1)]
    patch_wide = jnp.concatenate([patches] + places_hot, axis=1)
    embedded = low_dot(patch_wide, embed_b) + vec_w[10]
    normed, queries, key_rows, values = projections(attn_b, vec_w, embedded)
    queries, key_rows, values = sync((queries, key_rows, values), mom_lane)
    mixed_out, summary = mixing(queries, key_rows, values, image_index, H)
    (mixed_out,) = sync((mixed_out,), b_lane, c_lane, mom_lane, head_lane)
    part_b, part_c = b_lane.result, c_lane.result
    d_lane = lane(once(part_b, pair), "mlp_weights")
    sync((), d_lane)

    masks = [1 << bit for bit in high_bits]
    own_codes = [jnp.array(codes(masks + [third[c], fourth[c]]), jnp.int32) for c in (0, 1)]
    arrival = me ^ jnp.where(
        core == 0,
        jnp.concatenate([own_codes[0], own_codes[1] ^ 1]),
        jnp.concatenate([own_codes[1], own_codes[0] ^ 1]),
    )
    first_bias = jnp.take(vec_w[11:].reshape(count, mlp_rows), arrival, axis=0)
    first_bias = first_bias.reshape(4, -1)

    middle = embedded + low_dot(mixed_out, attn_b[3 * model_width :]) + vec_w[2]
    normed_two = layer_norm(middle, vec_w[6], vec_w[7]).astype(jnp.bfloat16)
    (normed_two,) = sync((normed_two,), d_lane)
    mlp_parts = [
        part.reshape(-1, 2 * model_width) for part in (part_a, part_b, part_c, d_lane.result)
    ]
    final_rows, active, slope = hidden_forward(
        normed_two, middle, first_bias, vec_w[3:4], mlp_parts
    )
    (final_rows,) = sync((final_rows,), head_lane, mom_lane, attn_mom_lane)
    closing, close_pull = jax.vjp(layer_norm, final_rows, vec_w[8], vec_w[9])
    member = (image_index[None, :] == jnp.arange(slot_count)[:, None]).astype(jnp.float32)
    slot_sizes = jnp.sum(member, axis=1)
    divisor = jnp.maximum(slot_sizes, 1.0)[:, None]
    pooled = product(member, closing) / divisor
    facts = jnp.stack(
        [(slot_sizes > 0.5).astype(jnp.int32), my_labels // 256, my_labels % 256], axis=1
    )
    facts = jnp.pad(facts, ((0, 0), (0, 125))).astype(jnp.bfloat16)
    block = jnp.concatenate([pooled.astype(jnp.bfloat16), facts], axis=1)
    head_b = finish(head_lane)[0].reshape(owners * shard_rows, chunk)
    for axis, bit in enumerate(range(top - 1, -1, -1)):
        block = ordered_pair(bit_of(bit), block, exchange(block, plain(bit), "pooled"), axis)
    block = block.reshape(count * slot_count, -1)
    all_pooled = block[:, :model_width]
    facts = block[:, model_width : model_width + 3].astype(jnp.int32)
    valid = facts[:, 0] > 0
    all_labels = facts[:, 1] * 256 + facts[:, 2]
    image_total = jnp.sum(valid.astype(jnp.float32))

    (all_pooled,) = sync((all_pooled,), mom_lane, attn_mom_lane)
    logits = low_dot(all_pooled, head_b)
    within = owner_index * chunk + jnp.arange(chunk)
    columns = member_index * shard_width + within
    usable = (within < shard_width) & (columns < CLASSES)
    logits = jnp.where(usable[None], logits, -1e30)
    onehot = (usable[None] & (columns[None, :] == all_labels[:, None])).astype(jnp.float32)
    row_max = jnp.max(logits, axis=1)
    exp_sums = jnp.sum(jnp.exp(logits - row_max[:, None]), axis=1)
    stats = jnp.stack([row_max, exp_sums, jnp.sum(onehot * logits, axis=1)])
    for bit in range(top):
        other = exchange(stats, plain(bit), "stats")
        lower = jnp.where(bit_of(bit) == 0, stats, other)
        upper = jnp.where(bit_of(bit) == 0, other, stats)
        row_max = jnp.maximum(lower[0], upper[0])
        exp_sums = lower[1] * jnp.exp(lower[0] - row_max) + upper[1] * jnp.exp(upper[0] - row_max)
        stats = jnp.stack([row_max, exp_sums, lower[2] + upper[2]])
    (stats,) = sync((stats,), mom_lane, attn_mom_lane)
    normaliser = stats[0] + jnp.log(stats[1])
    loss_sum = jnp.sum(jnp.where(valid, normaliser - stats[2], 0.0))
    probs_class = jnp.exp(logits - normaliser[:, None])
    d_logits = (jnp.where(valid[:, None], probs_class - onehot, 0.0) / image_total).astype(
        jnp.bfloat16
    )
    d_pooled = contract_cols(d_logits, head_b)
    d_pooled = d_pooled.reshape((2,) * top + (slot_count, model_width))
    for bit in range(top):
        axis = top - 1 - bit
        mine = bit_of(bit)
        leave = pick(d_pooled, 1 - mine, axis).astype(jnp.bfloat16)
        d_pooled = pick(d_pooled, mine, axis) + exchange(leave, plain(bit), "d_pooled").astype(
            jnp.float32
        )
    d_closing = product(member.T, d_pooled / divisor)
    d_final, g_gain_final, g_shift_final = close_pull(d_closing)
    d_out = d_final.astype(jnp.bfloat16)
    g_second_bias = jnp.sum(d_out.astype(jnp.float32), axis=0)
    d_out, all_pooled = tie(d_out, all_pooled)
    head_grad = contract_rows(all_pooled, d_logits).astype(jnp.bfloat16)
    head_lane = lane(
        transposed(
            head_grad.reshape(owners, shard_rows, chunk),
            owner_bits[1:-1] + owner_bits[:1] + owner_bits[-1:],
        ),
        "head_grads",
    )
    (d_out,) = sync((d_out,), head_lane, mom_lane, attn_mom_lane)
    mlp_moms, attn_moms = finish(mom_lane, attn_mom_lane)
    mlp_moms = [part.reshape(-1, model_width) for part in mlp_moms]
    attn_moms = jnp.concatenate(attn_moms, axis=0).reshape(-1, model_width)

    d_hidden, bias_grads, away = hidden_back(core, d_out, normed_two, active, slope, mlp_parts)
    (away, d_hidden) = sync((away, d_hidden), head_lane)
    arrived = exchange(away, pair, "mlp_grads")
    d_normed_two, kept = kept_grads(core, d_out, normed_two, active, d_hidden, mlp_parts)
    d_normed_two, kept, arrived = sync((d_normed_two, kept, arrived), head_lane)
    kept = [
        (kept[index] + arrived[(index + 2) % 4].astype(jnp.float32)).reshape(
            -1, mlp_rows, model_width
        )
        for index in range(4)
    ]

    def summing(kept):
        half = kept[0].shape[0] // 2
        leave = [kept[1], kept[2][half:], kept[3][half:]]
        leave = jnp.concatenate([grad.astype(jnp.bfloat16) for grad in leave])
        arrived = (yield leave, fourth).astype(jnp.float32)
        leave = [kept[0][half:] + arrived[half : 2 * half], kept[3][:half] + arrived[3 * half :]]
        kept = [kept[0][:half] + arrived[:half], kept[2][:half] + arrived[2 * half : 3 * half]]
        arrived = yield jnp.stack(leave).astype(jnp.bfloat16), third
        kept = jnp.stack(kept) + arrived.astype(jnp.float32)
        for stage in down_stages:
            half = kept.shape[1] // 2
            arrived = yield kept[:, half:].astype(jnp.bfloat16), stage
            kept = kept[:, :half] + arrived.astype(jnp.float32)
        return kept[:, 0]

    mlp_lane = lane(summing(kept), "mlp_grads")
    (d_normed_two,) = sync((d_normed_two,), mlp_lane)

    d_mid_norm, g_gain_two, g_shift_two = jax.vjp(layer_norm, middle, vec_w[6], vec_w[7])[1](
        d_normed_two
    )
    d_middle = d_final + d_mid_norm
    d_proj = d_middle.astype(jnp.bfloat16)
    g_out_bias = jnp.sum(d_proj.astype(jnp.float32), axis=0)
    d_mixed = contract_cols(d_proj, attn_b[3 * model_width :]).astype(jnp.bfloat16)
    d_queries, d_keys, d_values = mixing_grads(
        queries, key_rows, values, d_mixed, summary, image_index, H
    )
    d_queries, d_keys, d_values = sync((d_queries, d_keys, d_values), mlp_lane, head_lane)
    attn_grad = jnp.concatenate(
        [
            contract_rows(normed, d_queries),
            contract_rows(normed, d_keys),
            contract_rows(normed, d_values),
            contract_rows(mixed_out, d_proj),
        ],
        axis=0,
    )

    quarter = (me >> 1) & 3
    to_third, to_fourth = third_mine >> 1, fourth_mine >> 1

    def quartered(grad, rows):
        grad = grad.reshape(count // 8, 4, 2, rows, model_width)
        leave = pick(grad, 1 - core, 2).astype(jnp.bfloat16)
        grad = pick(grad, core, 2) + (yield leave, pair).astype(jnp.float32)
        leave = [pick(grad, quarter ^ to_fourth, 1), pick(grad, quarter ^ 3, 1)]
        leave = (yield jnp.stack(leave).astype(jnp.bfloat16), fourth).astype(jnp.float32)
        leaving = pick(grad, quarter ^ to_third, 1) + leave[1]
        return pick(grad, quarter, 1) + leave[0], leaving

    def last_sums(grads):
        grad = jnp.concatenate([one[0] for one in grads], axis=1)
        leave = jnp.concatenate([one[1].astype(jnp.bfloat16) for one in grads], axis=1)
        grad = grad + (yield leave, third).astype(jnp.float32)
        grad = grad.reshape((2,) * len(high_bits) + grad.shape[1:])
        for bit in reversed(high_bits):
            axis = top - 1 - bit
            mine = bit_of(bit)
            leave = pick(grad, 1 - mine, axis).astype(jnp.bfloat16)
            grad = pick(grad, mine, axis) + (yield leave, plain(bit)).astype(jnp.float32)
        return grad

    attn_lane = lane(quartered(attn_grad, attn_rows), "attn_grads")
    d_normed = (
        contract_cols(d_queries, attn_b[:model_width])
        + contract_cols(d_keys, attn_b[model_width : 2 * model_width])
        + contract_cols(d_values, attn_b[2 * model_width : 3 * model_width])
    )
    (d_normed,) = sync((d_normed,), mlp_lane, attn_lane)
    d_emb_norm, g_gain_one, g_shift_one = jax.vjp(layer_norm, embedded, vec_w[4], vec_w[5])[1](
        d_normed
    )
    d_embed_low = (d_middle + d_emb_norm).astype(jnp.bfloat16)
    (d_embed_low,) = sync((d_embed_low,), attn_lane)
    embed_grad = contract_rows(patch_wide, d_embed_low)
    embed_lane = lane(quartered(embed_grad, embed_rows), "embed_grads")
    sync((), embed_lane)
    sync((), mlp_lane)
    mlp_grad = finish(mlp_lane)[0]
    all_lane = lane(
        collecting(mlp_grad.astype(jnp.bfloat16), up_stages + [third, fourth]), "mlp_grads_all"
    )
    sync((), all_lane)
    sync((), embed_lane)
    finish(attn_lane, embed_lane)
    sum_lane = lane(last_sums([attn_lane.result, embed_lane.result]), "last_grads")
    sync((), sum_lane)
    while sum_lane.result is None:
        sync((), sum_lane, all_lane)
    attn_sum, embed_sum = sum_lane.result[:attn_rows], sum_lane.result[attn_rows:]
    g_query_bias = jnp.sum(d_queries.astype(jnp.float32), axis=0)
    g_value_bias = jnp.sum(d_values.astype(jnp.float32), axis=0)
    g_patch_bias = jnp.sum(d_embed_low.astype(jnp.float32), axis=0)
    g_first_bias = jnp.take(bias_grads.reshape(count, mlp_rows), jnp.argsort(arrival), axis=0)
    head_grad = finish(head_lane)[0].transpose(1, 0, 2)
    head_grad = head_grad.reshape(shard_rows, owners * chunk)[:, :shard_width].astype(jnp.float32)
    vec_grad = jnp.concatenate(
        [
            jnp.stack(
                [
                    g_query_bias,
                    g_value_bias,
                    g_out_bias,
                    g_second_bias,
                    g_gain_one,
                    g_shift_one,
                    g_gain_two,
                    g_shift_two,
                    g_gain_final,
                    g_shift_final,
                    g_patch_bias,
                ]
            ),
            g_first_bias.reshape(-1, model_width),
        ],
        axis=0,
    )
    local_squares = sum(
        jnp.sum(grad * grad, axis=0) for grad in (attn_sum, embed_sum, mlp_grad[0], mlp_grad[1])
    )
    head_squares = jnp.sum(head_grad * head_grad) / model_width
    small_sums = jnp.concatenate([vec_grad, (local_squares + head_squares)[None]], axis=0)

    def total(value):
        for bit in range(top):
            value = value + (yield value, plain(bit))
        return value

    small_lane = lane(total(small_sums), "small_sums")
    block_lane = lane(
        collecting(attn_sum.astype(jnp.bfloat16)[None], up_stages[2:] + [third, fourth, pair]),
        "attn_grads_all",
    )
    small_sums, attn_grads, mlp_grads = finish(small_lane, block_lane, all_lane)
    attn_grads = jnp.concatenate(attn_grads, axis=0).reshape(-1, model_width)
    mlp_grads = [part.reshape(-1, model_width) for part in mlp_grads]
    vec_sum = small_sums[:-1]
    grad_norm = jnp.sqrt(jnp.sum(small_sums[-1]) + jnp.sum(vec_sum * vec_sum))
    factor = jnp.minimum(1.0, clip_limit / (grad_norm + 1e-06))
    attn_mom_out = momentum_keep * attn_mom + factor * attn_sum
    mine, away = mlp_grad[0], exchange(mlp_grad[1], pair)
    mlp_sum = jnp.concatenate(
        [jnp.where(core == 0, mine, away), jnp.where(core == 0, away, mine)], axis=1
    )
    mlp_mom_out = momentum_keep * mlp_mom + factor * mlp_sum

    mlp_result = orthogonal_rows(mlp_moms, mlp_grads, factor, 2 * mlp_rows, 768, 2)
    mlp_other = exchange(mlp_result[mlp_rows:], pair)
    mlp_result = mlp_result[:mlp_rows]
    mlp_dir = jnp.concatenate(
        [
            jnp.where(core == 0, mlp_result, mlp_other),
            jnp.where(core == 0, mlp_other, mlp_result),
        ],
        axis=1,
    )
    attn_dir = orthogonal_rows([attn_moms], [attn_grads], factor, attn_rows, 768, 4)
    mlp_scale = math.sqrt(mlp_rows * count / model_width)
    attn_out = attn_w * (1.0 - muon_rate * decay_rate) - muon_rate * attn_dir
    mlp_out = mlp_w * (1.0 - muon_rate * decay_rate) - muon_rate * mlp_scale * mlp_dir
    embed_out, embed_m_out, embed_v_out = adam_step(
        embed_w, embed_m, embed_v, factor * embed_sum, adam_rate
    )
    vec_out, vec_m_out, vec_v_out = adam_step(vec_w, vec_m, vec_v, factor * vec_sum, vector_rate)
    head_out, head_m_out, head_v_out = adam_step(
        head_w, head_m, head_v, factor * head_grad, adam_rate
    )
    return (
        loss_sum,
        image_total,
        grad_norm,
        attn_out,
        attn_mom_out,
        attn_out.astype(jnp.bfloat16),
        mlp_out,
        mlp_mom_out,
        mlp_out.astype(jnp.bfloat16),
        embed_out,
        embed_m_out,
        embed_v_out,
        embed_out.astype(jnp.bfloat16),
        vec_out,
        vec_m_out,
        vec_v_out,
        vec_out.astype(jnp.bfloat16),
        head_out,
        head_m_out,
        head_v_out,
        head_out.astype(jnp.bfloat16),
    )


def solution(mesh):
    return jax.shard_map(
        on_device,
        mesh=mesh,
        in_specs=(
            P(("dp", "cls"), None),
            P("dp", None),
            P(("dp", "cls"), None, None),
            P("dp", None),
            P(("dp", "cls"), None),
            P(("dp", "cls"), None),
            P(("dp", "cls"), None),
            P(),
            P("dp", "cls"),
            P(("dp", "cls"), None),
            P(("dp", "cls"), None),
            P(("dp", "cls"), None),
            P(("dp", "cls"), None),
            P(),
            P(),
            P("dp", "cls"),
            P("dp", "cls"),
        ),
        out_specs=(
            P(),
            P(),
            P(),
            P(("dp", "cls"), None),
            P(("dp", "cls"), None),
            P(("dp", "cls"), None),
            P(("dp", "cls"), None),
            P(("dp", "cls"), None),
            P(("dp", "cls"), None),
            P(("dp", "cls"), None),
            P(("dp", "cls"), None),
            P(("dp", "cls"), None),
            P(("dp", "cls"), None),
            P(),
            P(),
            P(),
            P(),
            P("dp", "cls"),
            P("dp", "cls"),
            P("dp", "cls"),
            P("dp", "cls"),
        ),
        check_vma=False,
    )
```

time: 748 us -> 611 us (0.82)
  matrix products: 225 us -> 19 us
  Pallas kernels: 0 us -> 125 us
  local copies, waits for them, and re-layouts: 82.7 us -> 42.9 us
  other arithmetic: 109 us -> 81.4 us
  waiting for transfers between devices: 240 us -> 262 us
    pallas_call x0 -> x7, Pallas kernels: none -> 125 us  [the longest x2 56 us: orthogonal_rows(): pl.pallas_call(body, out_shape=jax.ShapeDtypeStruct((row_count, width), j...]
    dot_general x33 -> x6, matrix products: 91.7 us -> 6.46 us  [low_dot(): return jnp.dot(left_side, right_side, preferred_element_type=jnp.float32)]
    dot_general x27 -> x6, matrix products: 57.6 us -> 5.08 us  [contract_rows(): lax.dot_general(left_side, right_side, (((0,), (0,)), ((), ())), preferre...]
    dot_general x13 -> x5, matrix products: 42 us -> 5.21 us  [contract_cols(): lax.dot_general(left_side, right_side, (((1,), (1,)), ((), ())), preferre...]
    dot_general x6 -> x0, matrix products: 30.1 us -> none  [the longest x1 14.1 us: attention_backward(): jnp.einsum('qhd,khd->hqk', d_mixed, values.reshape(head_shape), preferred...]
    ppermute x70 -> x66, waiting for transfers between devices: 240 us -> 262 us  [swap(): lax.ppermute(value, AXES, [(i, i ^ masks[i & 1]) for i in range(count)])]
    convert_element_type x13 -> x12, other arithmetic: 25.4 us -> 7.62 us  [the longest x2 2.53 us: quartered(): (yield (jnp.stack(leave).astype(jnp.bfloat16), fourth)).astype(jnp.float32)]
    slice x11 -> x9, local copies, waits for them, and re-layouts: 10.2 us -> 1.49 us  [the longest x2 1 us: summing(): arrived = (yield (kept[:, half:].astype(jnp.bfloat16), stage))]
  transfers between devices with their start and end apart: 70 -> 66, of which waited for: 33 -> 45; matrix products, arithmetic and copies ran while one was open for 44% -> 14% of each run, Pallas kernels for 0% -> 14%
where the time goes in v2:
time: 611 us; the launch traced here: 603 us
  waiting for transfers between devices  262 us (43%)
  Pallas kernels  125 us (20%)
  other arithmetic  81.4 us (13%)
  starting transfers between devices  65.8 us (11%)
  local copies, waits for them, and re-layouts  42.9 us (7%)
  matrix products  19 us (3%)
  between operations  7.01 us (1%)
    ppermute x66, waiting for transfers between devices, swap(): lax.ppermute(value, AXES, [(i, i ^ masks[i & 1]) for i in range(count)])  262 us
    ppermute x66, starting transfers between devices, swap(): lax.ppermute(value, AXES, [(i, i ^ masks[i & 1]) for i in range(count)])  65.8 us
    pallas_call x2, Pallas kernels, orthogonal_rows(): pl.pallas_call(body, out_shape=jax.ShapeDtypeStruct((row_count, width), j...  56 us
    unnamed x285, local copies, waits for them, and re-layouts  27.5 us
    pallas_call x1, Pallas kernels, hidden_forward(): pl.pallas_call(functools.partial(hidden_forward_kernel, rows), out_shape=...  16.4 us
    pallas_call x1, Pallas kernels, mixing_grads(): pl.pallas_call(functools.partial(mixing_grads_kernel, width, rows), grid=...  14.8 us
    pallas_call x1, Pallas kernels, hidden_back(): pl.pallas_call(hidden_back_kernel, out_shape=(jax.ShapeDtypeStruct((4, to...  14 us
    pallas_call x1, Pallas kernels, kept_grads(): pl.pallas_call(kept_grads_kernel, out_shape=(jax.ShapeDtypeStruct((token_...  13.8 us
  transfers between devices with their start and end apart: 66, of which 45 were waited for; matrix products, arithmetic and copies ran while one was open for 14% of the time, Pallas kernels for 14%

profile of v2, /device:TPU:0, one launch (start us, length us, event | category | flops | bytes accessed | tf_op | source)
XLA Modules:
  0.0 603.2 jit_solution(9548716705011587091)
XLA Ops:
  2.6 4.1 collective-permute-start
  8.6 7.2 %collective-permute-done = bf16[128,768]{1,0:T(8,128)(2,1)S(1)} collective-permute-done((bf16[128,768]{1,0:T(8,128)(2,1)S(1)}, bf16[128,768]{1,0:T(8,128)(2,1)S(1)}, u32[]{:S(2)}, u32[]{:S(2)}) %collective-permute-start) | collective-permute-done | bytes 196640 | tf_op jit(solution)/shard_map/attn_weights/ppermute | solution.py:34
  16.9 9.4 %collective-permute-done.1 = bf16[2,128,768]{2,1,0:T(8,128)(2,1)S(1)} collective-permute-done((bf16[2,128,768]{2,1,0:T(8,128)(2,1)S(1)}, bf16[2,128,768]{2,1,0:T(8,128)(2,1)S(1)}, u32[]{:S(2)}, u32[]{:S(2)}) %collective-permute-start.1) | collective-permute-done | bytes 393248 | tf_op jit(solution)/shard_map/attn_weights/ppermute | solution.py:34
  29.4 3.4 collective-permute-start.3
  33.3 12.2 %collective-permute-done.3 = bf16[1,96,1536]{2,1,0:T(8,128)(2,1)S(1)} collective-permute-done((bf16[1,96,1536]{2,1,0:T(8,128)(2,1)S(1)}, bf16[1,96,1536]{2,1,0:T(8,128)(2,1)S(1)}, u32[]{:S(2)}, u32[]{:S(2)}) %collective-permute-start.3) | collective-permute-done | bytes 294944 | tf_op jit(solution)/shard_map/mlp_weights/ppermute | solution.py:34
  46.4 2.6 pad_maximum_fusion.5
  55.3 11.1 %collective-permute-done.5 = bf16[2,96,1536]{2,1,0:T(8,128)(2,1)} collective-permute-done((bf16[2,96,1536]{2,1,0:T(8,128)(2,1)}, bf16[2,96,1536]{2,1,0:T(8,128)(2,1)}, u32[]{:S(2)}, u32[]{:S(2)}) %collective-permute-start.5) | collective-permute-done | bytes 589856 | tf_op jit(solution)/shard_map/mlp_weights/ppermute | solution.py:34
  66.5 3.3 collective-permute-done.4
  79.2 11.5 %collective-permute-done.8 = bf16[2,2,96,768]{3,2,1,0:T(8,128)(2,1)S(1)} collective-permute-done((bf16[2,2,96,768]{3,2,1,0:T(8,128)(2,1)S(1)}, bf16[2,2,96,768]{3,2,1,0:T(8,128)(2,1)S(1)}, u32[]{:S(2)}, u32[]{:S(2)}) %collective-permute-start.8) | collective-permute-done | bytes 589856 | tf_op jit(solution)/shard_map/head/ppermute | solution.py:34
  94.8 2.3 collective-permute-start.12
  102.0 10.4 %mixing.1 = (bf16[512,768]{1,0:T(8,128)(2,1)S(1)}, f32[16,512]{1,0:T(8,128)S(1)}) custom-call(s32[512,1]{1,0:T(8,128)S(1)} %copy.160.ids_down_ref, s32[1,512]{1,0:T(1,128)S(1)} %constant_dynamic-slice_fusion.13.ids_ref, bf16[512,768]{1,0:T(8,128)(2,1)S(1)} %add_convert_fusion.4.q_ref, bf16[512,768]{1,0:T(8,128)(2,1)S(1)} %convolution_convert_fusion.2.k_ref, ...), custom_call_target="tpu_custom_call" | custom-call | flops 805306368 | bytes 3145728 | tf_op jit(solution)/shard_map/mixing/pallas_call | solution.py:192
  112.4 11.5 %collective-permute-done.12 = bf16[2,2,96,768]{3,2,1,0:T(8,128)(2,1)S(1)} collective-permute-done((bf16[2,2,96,768]{3,2,1,0:T(8,128)(2,1)S(1)}, bf16[2,2,96,768]{3,2,1,0:T(8,128)(2,1)S(1)}, u32[]{:S(2)}, u32[]{:S(2)}) %collective-permute-start.12) | collective-permute-done | bytes 589856 | tf_op jit(solution)/shard_map/head/ppermute | solution.py:34
  134.8 16.4 %hidden_forward.1 = (f32[512,768]{1,0:T(8,128)S(1)}, bf16[4,512,768]{2,1,0:T(8,128)(2,1)}, f32[4,512,768]{2,1,0:T(8,128)}) custom-call(bf16[512,768]{1,0:T(8,128)(2,1)S(1)} %add_convert_fusion.2.normed_ref, f32[512,768]{1,0:T(8,128)S(1)} %get-tuple-element.335.middle_ref, f32[4,768]{1,0:T(4,128)S(1)} %reshape.1039.bias_ref, ...), custom_call_target="tpu_custom_call" | custom-call | flops 4831838208 | bytes 22020096 | tf_op jit(solution)/shard_map/hidden_forward/pallas_call | solution.py:293
  155.4 2.9 collective-permute-start.16
  160.4 3.4 collective-permute-start.17
  167.5 3.3 collective-permute-done.18
  172.4 4.5 collective-permute-done.19
  181.4 3.1 collective-permute-done.22
  184.4 8.8 %collective-permute-done.21 = bf16[4,96,768]{2,1,0:T(8,128)(2,1)S(1)} collective-permute-done((bf16[4,96,768]{2,1,0:T(8,128)(2,1)S(1)}, bf16[4,96,768]{2,1,0:T(8,128)(2,1)S(1)}, u32[]{:S(2)}, u32[]{:S(2)}) %collective-permute-start.21) | collective-permute-done | bytes 589856 | tf_op jit(solution)/shard_map/mlp_moments/ppermute | solution.py:34
  199.1 2.2 collective-permute-done.24
  213.7 6.9 %collective-permute-done.29 = bf16[2,96,768]{2,1,0:T(8,128)(2,1)} collective-permute-done((bf16[2,96,768]{2,1,0:T(8,128)(2,1)S(1)}, bf16[2,96,768]{2,1,0:T(8,128)(2,1)}, u32[]{:S(2)}, u32[]{:S(2)}) %collective-permute-start.29) | collective-permute-done | bytes 294944 | tf_op jit(solution)/shard_map/attn_moments/ppermute | solution.py:34
  220.5 4.9 collective-permute-done.28
  235.0 5.8 collective-permute-done.31
  246.4 3.3 collective-permute-done.33
  259.5 13.0 %collective-permute-done.35 = bf16[16,96,768]{2,1,0:T(8,128)(2,1)S(1)} collective-permute-done((bf16[16,96,768]{2,1,0:T(8,128)(2,1)S(1)}, bf16[16,96,768]{2,1,0:T(8,128)(2,1)S(1)}, u32[]{:S(2)}, u32[]{:S(2)}) %collective-permute-start.35) | collective-permute-done | bytes 2359328 | tf_op jit(solution)/shard_map/mlp_moments/ppermute | solution.py:34
  273.4 14.0 %hidden_back.1 = (bf16[4,512,768]{2,1,0:T(8,128)(2,1)}, f32[4,768]{1,0:T(4,128)S(1)}, bf16[4,768,768]{2,1,0:T(8,128)(2,1)}) custom-call(s32[1,1]{1,0:T(1,128)} %bitcast.105.core_ref, bf16[512,768]{1,0:T(8,128)(2,1)S(1)} %get-tuple-element.147.d_out_ref, bf16[512,768]{1,0:T(8,128)(2,1)S(1)} %copy-done.6, bf16[4,512,768]{2,1,0:T(8,128)(2,1)} %get-tuple-element.148.active_ref, ...), custom_call_target="tpu_custom_call" | custom-call | flops 4831838208 | bytes 22020096 | tf_op jit(solution)/shard_map/hidden_back/pallas_call | solution.py:329
  291.0 13.8 %kept_grads.1 = (f32[512,768]{1,0:T(8,128)S(1)}, f32[4,768,768]{2,1,0:T(8,128)}) custom-call(s32[1,1]{1,0:T(1,128)} %bitcast.105.core_ref, bf16[512,768]{1,0:T(8,128)(2,1)S(1)} %get-tuple-element.147.d_out_ref, bf16[512,768]{1,0:T(8,128)(2,1)S(1)} %copy-done.6, bf16[4,512,768]{2,1,0:T(8,128)(2,1)} %get-tuple-element.148.active_ref, ...), custom_call_target="tpu_custom_call" | custom-call | flops 4831838208 | bytes 26738688 | tf_op jit(solution)/shard_map/kept_grads/pallas_call | solution.py:366
  309.3 5.6 convert_add_fusion
  322.7 14.8 %mixing_grads.1 = (bf16[512,768]{1,0:T(8,128)(2,1)S(1)}, bf16[512,768]{1,0:T(8,128)(2,1)S(1)}, bf16[512,768]{1,0:T(8,128)(2,1)S(1)}) custom-call(s32[512,1]{1,0:T(8,128)S(1)} %copy.160.ids_down_ref, s32[1,512]{1,0:T(1,128)S(1)} %constant_dynamic-slice_fusion.13.ids_ref, f32[16,512]{1,0:T(8,128)S(1)} %get-tuple-element.142.summary_ref, ...), custom_call_target="tpu_custom_call" | custom-call | flops 2013265920 | bytes 5505024 | tf_op jit(solution)/shard_map/mixing_grads/pallas_call | solution.py:249
  338.3 6.0 collective-permute-done.40
  357.3 8.2 %collective-permute-done.42 = bf16[2,4,96,768]{3,2,1,0:T(8,128)(2,1)S(1)} collective-permute-done((bf16[2,4,96,768]{3,2,1,0:T(8,128)(2,1)S(1)}, bf16[2,4,96,768]{3,2,1,0:T(8,128)(2,1)S(1)}, u32[]{:S(2)}, u32[]{:S(2)}) %collective-permute-start.42) | collective-permute-done | bytes 1179680 | tf_op jit(solution)/shard_map/mlp_grads/ppermute | solution.py:34
  374.3 2.3 bitcast_add_fusion
  384.9 12.6 %collective-permute-done.48 = bf16[2,2,96,768]{3,2,1,0:T(8,128)(2,1)} collective-permute-done((bf16[2,2,96,768]{3,2,1,0:T(8,128)(2,1)}, bf16[2,2,96,768]{3,2,1,0:T(8,128)(2,1)}, u32[]{:S(2)}, u32[]{:S(2)}) %collective-permute-start.48) | collective-permute-done | bytes 589856 | tf_op jit(solution)/shard_map/mlp_grads/ppermute | solution.py:34
  406.0 8.4 %collective-permute-done.49 = bf16[2,1,96,768]{3,2,1,0:T(8,128)(2,1)S(1)} collective-permute-done((bf16[2,1,96,768]{3,2,1,0:T(8,128)(2,1)S(1)}, bf16[2,1,96,768]{3,2,1,0:T(8,128)(2,1)S(1)}, u32[]{:S(2)}, u32[]{:S(2)}) %collective-permute-start.49) | collective-permute-done | bytes 294944 | tf_op jit(solution)/shard_map/mlp_grads/ppermute | solution.py:34
  414.5 14.9 %collective-permute-done.50 = bf16[2,96,768]{2,1,0:T(8,128)(2,1)S(1)} collective-permute-done((bf16[2,96,768]{2,1,0:T(8,128)(2,1)S(1)}, bf16[2,96,768]{2,1,0:T(8,128)(2,1)S(1)}, u32[]{:S(2)}, u32[]{:S(2)}) %collective-permute-start.50) | collective-permute-done | bytes 294944 | tf_op jit(solution)/shard_map/mlp_grads_all/ppermute | solution.py:34
  432.0 21.3 %collective-permute-done.51 = bf16[2,128,768]{2,1,0:T(8,128)(2,1)S(1)} collective-permute-done((bf16[2,128,768]{2,1,0:T(8,128)(2,1)S(1)}, bf16[2,128,768]{2,1,0:T(8,128)(2,1)S(1)}, u32[]{:S(2)}, u32[]{:S(2)}) %collective-permute-start.51) | collective-permute-done | bytes 393248 | tf_op jit(solution)/shard_map/last_grads/ppermute | solution.py:34
  458.2 9.1 %collective-permute-done.53 = bf16[128,768]{1,0:T(8,128)(2,1)S(1)} collective-permute-done((bf16[128,768]{1,0:T(8,128)(2,1)S(1)}, bf16[128,768]{1,0:T(8,128)(2,1)S(1)}, u32[]{:S(2)}, u32[]{:S(2)}) %collective-permute-start.53) | collective-permute-done | bytes 196640 | tf_op jit(solution)/shard_map/last_grads/ppermute | solution.py:34
  467.2 3.8 collective-permute-done.54
  471.0 3.0 pad_maximum_fusion.4
  481.3 21.9 %collective-permute-done.55 = bf16[16,96,768]{2,1,0:T(8,128)(2,1)} collective-permute-done((bf16[16,96,768]{2,1,0:T(8,128)(2,1)}, bf16[16,96,768]{2,1,0:T(8,128)(2,1)}, u32[]{:S(2)}, u32[]{:S(2)}) %collective-permute-start.55) | collective-permute-done | bytes 2359328 | tf_op jit(solution)/shard_map/mlp_grads_all/ppermute | solution.py:34
  504.9 4.0 collective-permute-done.57
  510.2 3.3 collective-permute-done.58
  516.4 3.7 collective-permute-done.60
  521.7 2.5 collective-permute-done.62
  525.0 4.6 collective-permute-done.63
  536.3 41.0 %orthogonal_rows.3 = f32[192,768]{1,0:T(8,128)S(1)} custom-call(f32[1,1]{1,0:T(1,128)} %bitcast.153.factor_ref, bf16[1536,768]{1,0:T(8,128)(2,1)S(1)} %bitcast.355, bf16[1536,768]{1,0:T(8,128)(2,1)S(1)} %bitcast.356, bf16[1536,768]{1,0:T(8,128)(2,1)} %bitcast.158.refs_2_, bf16[1536,768]{1,0:T(8,128)(2,1)} %bitcast.159.refs_3_), custom_call_target="tpu_custom_call" | custom-call | flops 26273120256 | bytes 9437184 | tf_op jit(solution)/shard_map/orthogonal_rows/pallas_call | solution.py:451
  577.5 4.8 fusion.120
  584.0 15.0 %orthogonal_rows.2 = f32[96,768]{1,0:T(8,128)S(1)} custom-call(f32[1,1]{1,0:T(1,128)} %bitcast.153.factor_ref, bf16[768,768]{1,0:T(8,128)(2,1)S(1)} %bitcast.350, bf16[768,768]{1,0:T(8,128)(2,1)S(1)} %bitcast.351), custom_call_target="tpu_custom_call" | custom-call | flops 16307453952 | bytes 2359296 | tf_op jit(solution)/shard_map/orthogonal_rows/pallas_call | solution.py:451
  (641 shorter events, 189.9 us)
Async XLA Ops:
  2.6 13.2 %collective-permute-start = (bf16[128,768]{1,0:T(8,128)(2,1)S(1)}, bf16[128,768]{1,0:T(8,128)(2,1)S(1)}, u32[]{:S(2)}, u32[]{:S(2)}) collective-permute-start(bf16[128,768]{1,0:T(8,128)(2,1)S(1)} %pad_maximum_fusion.26), channel_id=1, source_target_pairs={{0,16},{1,17},{2,18},{3,19},{4,20},{5,21},{6,22},{7,23},{8,24},{9,... | collective-permute-start | bytes 589832 | tf_op jit(solution)/shard_map/attn_weights/ppermute | solution.py:34
  15.9 10.4 %collective-permute-start.1 = (bf16[2,128,768]{2,1,0:T(8,128)(2,1)S(1)}, bf16[2,128,768]{2,1,0:T(8,128)(2,1)S(1)}, u32[]{:S(2)}, u32[]{:S(2)}) collective-permute-start(bf16[2,128,768]{2,1,0:T(8,128)(2,1)S(1)} %maximum_select_fusion.11), channel_id=1, source_target_pairs={{0,8},{1,9},{2,10},{3,11},{4,12},{5,13},{6,14},{7,15},{8,0},{9,1},... | collective-permute-start | bytes 1179656 | tf_op jit(solution)/shard_map/attn_weights/ppermute | solution.py:34
  26.4 19.1 %collective-permute-start.2 = (bf16[4,128,768]{2,1,0:T(8,128)(2,1)S(1)}, bf16[4,128,768]{2,1,0:T(8,128)(2,1)S(1)}, u32[]{:S(2)}, u32[]{:S(2)}) collective-permute-start(bf16[4,128,768]{2,1,0:T(8,128)(2,1)S(1)} %bitcast.361), channel_id=1, source_target_pairs={{0,2},{1,5},{2,0},{3,7},{4,6},{5,1},{6,4},{7,3},{8,10},{9,13},{10,... | collective-permute-start | bytes 2359304 | tf_op jit(solution)/shard_map/attn_weights/ppermute | solution.py:34
  29.4 16.1 %collective-permute-start.3 = (bf16[1,96,1536]{2,1,0:T(8,128)(2,1)S(1)}, bf16[1,96,1536]{2,1,0:T(8,128)(2,1)S(1)}, u32[]{:S(2)}, u32[]{:S(2)}) collective-permute-start(bf16[1,96,1536]{2,1,0:T(8,128)(2,1)S(1)} %convert_bitcast_fusion.1), channel_id=1, source_target_pairs={{0,16},{1,17},{2,18},{3,19},{4,20},{5,21},{6,22},{7,23},{8,24},{9,... | collective-permute-start | bytes 884744 | tf_op jit(solution)/shard_map/mlp_weights/ppermute | solution.py:34
  49.0 20.7 %collective-permute-start.4 = (bf16[2,4,128,768]{3,2,1,0:T(8,128)(2,1)}, bf16[2,4,128,768]{3,2,1,0:T(8,128)(2,1)}, u32[]{:S(2)}, u32[]{:S(2)}) collective-permute-start(bf16[2,4,128,768]{3,2,1,0:T(8,128)(2,1)} %pad_maximum_fusion.5), channel_id=1, source_target_pairs={{0,4},{1,3},{2,6},{3,1},{4,0},{5,7},{6,2},{7,5},{8,12},{9,11},{10,... | collective-permute-start | bytes 4718600 | tf_op jit(solution)/shard_map/attn_weights/ppermute | solution.py:34
  50.5 15.9 %collective-permute-start.5 = (bf16[2,96,1536]{2,1,0:T(8,128)(2,1)}, bf16[2,96,1536]{2,1,0:T(8,128)(2,1)}, u32[]{:S(2)}, u32[]{:S(2)}) collective-permute-start(bf16[2,96,1536]{2,1,0:T(8,128)(2,1)} %pad_maximum_fusion.15), channel_id=1, source_target_pairs={{0,8},{1,9},{2,10},{3,11},{4,12},{5,13},{6,14},{7,15},{8,0},{9,1},... | collective-permute-start | bytes 1769480 | tf_op jit(solution)/shard_map/mlp_weights/ppermute | solution.py:34
  71.5 7.1 %collective-permute-start.6 = (bf16[4,4,128,768]{3,2,1,0:T(8,128)(2,1)S(1)}, bf16[4,4,128,768]{3,2,1,0:T(8,128)(2,1)S(1)}, u32[]{:S(2)}, u32[]{:S(2)}) collective-permute-start(bf16[4,4,128,768]{3,2,1,0:T(8,128)(2,1)S(1)} %pad_maximum_fusion.1), channel_id=1, source_target_pairs={{0,1},{1,0},{2,3},{3,2},{4,5},{5,4},{6,7},{7,6},{8,9},{9,8},{10,11... | collective-permute-start | bytes 9437192 | tf_op jit(solution)/shard_map/attn_weights/ppermute | solution.py:34
  74.7 16.3 %collective-permute-start.7 = (bf16[4,96,1536]{2,1,0:T(8,128)(2,1)S(1)}, bf16[4,96,1536]{2,1,0:T(8,128)(2,1)S(1)}, u32[]{:S(2)}, u32[]{:S(2)}) collective-permute-start(bf16[4,96,1536]{2,1,0:T(8,128)(2,1)S(1)} %pad_maximum_fusion.6), channel_id=1, source_target_pairs={{0,2},{1,5},{2,0},{3,7},{4,6},{5,1},{6,4},{7,3},{8,10},{9,13},{10,... | collective-permute-start | bytes 3538952 | tf_op jit(solution)/shard_map/mlp_weights/ppermute | solution.py:34
  76.3 14.5 %collective-permute-start.8 = (bf16[2,2,96,768]{3,2,1,0:T(8,128)(2,1)S(1)}, bf16[2,2,96,768]{3,2,1,0:T(8,128)(2,1)S(1)}, u32[]{:S(2)}, u32[]{:S(2)}) collective-permute-start(bf16[2,2,96,768]{3,2,1,0:T(8,128)(2,1)S(1)} %get-tuple-element.116), channel_id=1, source_target_pairs={{0,8},{1,9},{2,10},{3,11},{4,12},{5,13},{6,14},{7,15},{8,0},{9,1},... | collective-permute-start | bytes 1769480 | tf_op jit(solution)/shard_map/head/ppermute | solution.py:34
  92.3 31.7 %collective-permute-start.10 = (bf16[8,96,1536]{2,1,0:T(8,128)(2,1)S(1)}, bf16[8,96,1536]{2,1,0:T(8,128)(2,1)S(1)}, u32[]{:S(2)}, u32[]{:S(2)}) collective-permute-start(bf16[8,96,1536]{2,1,0:T(8,128)(2,1)S(1)} %pad_maximum_fusion.2), channel_id=1, source_target_pairs={{0,1},{1,0},{2,3},{3,2},{4,5},{5,4},{6,7},{7,6},{8,9},{9,8},{10,11... | collective-permute-start | bytes 7077896 | tf_op jit(solution)/shard_map/mlp_weights/ppermute | solution.py:34
  92.4 31.6 %collective-permute-start.9 = (bf16[8,96,1536]{2,1,0:T(8,128)(2,1)S(1)}, bf16[8,96,1536]{2,1,0:T(8,128)(2,1)}, u32[]{:S(2)}, u32[]{:S(2)}) collective-permute-start(bf16[8,96,1536]{2,1,0:T(8,128)(2,1)S(1)} %pad_maximum_fusion.2), channel_id=1, source_target_pairs={{0,4},{1,3},{2,6},{3,1},{4,0},{5,7},{6,2},{7,5},{8,12},{9,11},{10,... | collective-permute-start | bytes 7077896 | tf_op jit(solution)/shard_map/mlp_weights/ppermute | solution.py:34
  94.8 29.1 %collective-permute-start.12 = (bf16[2,2,96,768]{3,2,1,0:T(8,128)(2,1)S(1)}, bf16[2,2,96,768]{3,2,1,0:T(8,128)(2,1)S(1)}, u32[]{:S(2)}, u32[]{:S(2)}) collective-permute-start(bf16[2,2,96,768]{3,2,1,0:T(8,128)(2,1)S(1)} %get-tuple-element.298), channel_id=1, source_target_pairs={{0,16},{1,17},{2,18},{3,19},{4,20},{5,21},{6,22},{7,23},{8,24},{9,... | collective-permute-start | bytes 1769480 | tf_op jit(solution)/shard_map/head/ppermute | solution.py:34
  101.8 10.6 %collective-permute-start.11 = (bf16[96,768]{1,0:T(8,128)(2,1)S(1)}, bf16[96,768]{1,0:T(8,128)(2,1)S(1)}, u32[]{:S(2)}, u32[]{:S(2)}) collective-permute-start(bf16[96,768]{1,0:T(8,128)(2,1)S(1)} %broadcast_select_fusion), channel_id=1, source_target_pairs={{0,1},{1,0},{2,3},{3,2},{4,5},{5,4},{6,7},{7,6},{8,9},{9,8},{10,11... | collective-permute-start | bytes 442376 | tf_op jit(solution)/shard_map/mlp_moments/ppermute | solution.py:34
  125.6 9.2 %collective-permute-start.13 = (bf16[8,96,1536]{2,1,0:T(8,128)(2,1)}, bf16[8,96,1536]{2,1,0:T(8,128)(2,1)}, u32[]{:S(2)}, u32[]{:S(2)}) collective-permute-start(bf16[8,96,1536]{2,1,0:T(8,128)(2,1)} %collective-permute-done.9), channel_id=1, source_target_pairs={{0,1},{1,0},{2,3},{3,2},{4,5},{5,4},{6,7},{7,6},{8,9},{9,8},{10,11... | collective-permute-start | bytes 7077896 | tf_op jit(solution)/shard_map/mlp_weights/ppermute | solution.py:34
  131.0 20.9 %collective-permute-start.14 = (bf16[2,2,96,768]{3,2,1,0:T(8,128)(2,1)S(1)}, bf16[2,2,96,768]{3,2,1,0:T(8,128)(2,1)S(1)}, u32[]{:S(2)}, u32[]{:S(2)}) collective-permute-start(bf16[2,2,96,768]{3,2,1,0:T(8,128)(2,1)S(1)} %get-tuple-element.296), channel_id=1, source_target_pairs={{0,4},{1,5},{2,6},{3,7},{4,0},{5,1},{6,2},{7,3},{8,12},{9,13},{10,... | collective-permute-start | bytes 1769480 | tf_op jit(solution)/shard_map/head/ppermute | solution.py:34
  131.8 19.3 %collective-permute-start.15 = (bf16[2,96,768]{2,1,0:T(8,128)(2,1)S(1)}, bf16[2,96,768]{2,1,0:T(8,128)(2,1)S(1)}, u32[]{:S(2)}, u32[]{:S(2)}) collective-permute-start(bf16[2,96,768]{2,1,0:T(8,128)(2,1)S(1)} %pad_maximum_fusion.23), channel_id=1, source_target_pairs={{0,16},{1,17},{2,18},{3,19},{4,20},{5,21},{6,22},{7,23},{8,24},{9,... | collective-permute-start | bytes 884744 | tf_op jit(solution)/shard_map/mlp_moments/ppermute | solution.py:34
  155.4 5.0 collective-permute-start.16
  160.4 5.5 collective-permute-start.17
  170.8 6.1 %collective-permute-start.19 = (bf16[2,2,2,16,896]{4,3,0,1,2:T(8,128)(2,1)S(1)}, bf16[2,2,2,16,896]{4,3,0,1,2:T(8,128)(2,1)S(1)}, u32[]{:S(2)}, u32[]{:S(2)}) collective-permute-start(bf16[2,2,2,16,896]{4,3,0,1,2:T(8,128)(2,1)S(1)} %maximum_select_fusion.13), channel_id=1, source_target_pairs={{0,2},{1,3},{2,0},{3,1},{4,6},{5,7},{6,4},{7,5},{8,10},{9,11},{10,... | collective-permute-start | bytes 688136 | tf_op jit(solution)/shard_map/pooled/ppermute | solution.py:34
  177.2 16.0 %collective-permute-start.21 = (bf16[4,96,768]{2,1,0:T(8,128)(2,1)S(1)}, bf16[4,96,768]{2,1,0:T(8,128)(2,1)S(1)}, u32[]{:S(2)}, u32[]{:S(2)}) collective-permute-start(bf16[4,96,768]{2,1,0:T(8,128)(2,1)S(1)} %pad_maximum_fusion.16), channel_id=1, source_target_pairs={{0,8},{1,9},{2,10},{3,11},{4,12},{5,13},{6,14},{7,15},{8,0},{9,1},... | collective-permute-start | bytes 1769480 | tf_op jit(solution)/shard_map/mlp_moments/ppermute | solution.py:34
  179.3 5.1 collective-permute-start.22
  207.2 18.2 %collective-permute-start.28 = (bf16[8,96,768]{2,1,0:T(8,128)(2,1)S(1)}, bf16[8,96,768]{2,1,0:T(8,128)(2,1)}, u32[]{:S(2)}, u32[]{:S(2)}) collective-permute-start(bf16[8,96,768]{2,1,0:T(8,128)(2,1)S(1)} %pad_maximum_fusion.7), channel_id=1, source_target_pairs={{0,2},{1,5},{2,0},{3,7},{4,6},{5,1},{6,4},{7,3},{8,10},{9,13},{10,... | collective-permute-start | bytes 3538952 | tf_op jit(solution)/shard_map/mlp_moments/ppermute | solution.py:34
  210.4 10.1 %collective-permute-start.29 = (bf16[2,96,768]{2,1,0:T(8,128)(2,1)S(1)}, bf16[2,96,768]{2,1,0:T(8,128)(2,1)}, u32[]{:S(2)}, u32[]{:S(2)}) collective-permute-start(bf16[2,96,768]{2,1,0:T(8,128)(2,1)S(1)} %pad_maximum_fusion.24), channel_id=1, source_target_pairs={{0,4},{1,3},{2,6},{3,1},{4,0},{5,7},{6,2},{7,5},{8,12},{9,11},{10,... | collective-permute-start | bytes 884744 | tf_op jit(solution)/shard_map/attn_moments/ppermute | solution.py:34
  233.8 6.9 %collective-permute-start.31 = (bf16[2,2,2,16,768]{4,3,0,1,2:T(8,128)(2,1)S(1)}, bf16[2,2,2,16,768]{4,3,0,1,2:T(8,128)(2,1)S(1)}, u32[]{:S(2)}, u32[]{:S(2)}) collective-permute-start(bf16[2,2,2,16,768]{4,3,0,1,2:T(8,128)(2,1)S(1)} %fusion.66), channel_id=1, source_target_pairs={{0,2},{1,3},{2,0},{3,1},{4,6},{5,7},{6,4},{7,5},{8,10},{9,11},{10,... | collective-permute-start | bytes 589832 | tf_op jit(solution)/shard_map/d_pooled/ppermute | solution.py:34
  243.5 28.9 %collective-permute-start.35 = (bf16[16,96,768]{2,1,0:T(8,128)(2,1)S(1)}, bf16[16,96,768]{2,1,0:T(8,128)(2,1)S(1)}, u32[]{:S(2)}, u32[]{:S(2)}) collective-permute-start(bf16[16,96,768]{2,1,0:T(8,128)(2,1)S(1)} %constant_dynamic-update-slice_fusion), channel_id=1, source_target_pairs={{0,4},{1,3},{2,6},{3,1},{4,0},{5,7},{6,2},{7,5},{8,12},{9,11},{10,... | collective-permute-start | bytes 7077896 | tf_op jit(solution)/shard_map/mlp_moments/ppermute | solution.py:34
  252.8 6.7 %collective-permute-start.36 = (bf16[4,96,768]{2,1,0:T(8,128)(2,1)S(1)}, bf16[4,96,768]{2,1,0:T(8,128)(2,1)S(1)}, u32[]{:S(2)}, u32[]{:S(2)}) collective-permute-start(bf16[4,96,768]{2,1,0:T(8,128)(2,1)S(1)} %pad_maximum_fusion.17), channel_id=1, source_target_pairs={{0,1},{1,0},{2,3},{3,2},{4,5},{5,4},{6,7},{7,6},{8,9},{9,8},{10,11... | collective-permute-start | bytes 1769480 | tf_op jit(solution)/shard_map/attn_moments/ppermute | solution.py:34
  272.4 14.9 %collective-permute-start.37 = (bf16[2,2,96,768]{3,2,1,0:T(8,128)(2,1)S(1)}, bf16[2,2,96,768]{3,2,1,0:T(8,128)(2,1)S(1)}, u32[]{:S(2)}, u32[]{:S(2)}) collective-permute-start(bf16[2,2,96,768]{3,2,1,0:T(8,128)(2,1)S(1)} %get-tuple-element.152), channel_id=1, source_target_pairs={{0,8},{1,9},{2,10},{3,11},{4,12},{5,13},{6,14},{7,15},{8,0},{9,1},... | collective-permute-start | bytes 1769480 | tf_op jit(solution)/shard_map/head_grads/ppermute | solution.py:34
  287.4 17.4 %collective-permute-start.38 = (bf16[4,768,768]{2,1,0:T(8,128)(2,1)}, bf16[4,768,768]{2,1,0:T(8,128)(2,1)}, u32[]{:S(2)}, u32[]{:S(2)}) collective-permute-start(bf16[4,768,768]{2,1,0:T(8,128)(2,1)} %get-tuple-element.156), channel_id=1, source_target_pairs={{0,1},{1,0},{2,3},{3,2},{4,5},{5,4},{6,7},{7,6},{8,9},{9,8},{10,11... | collective-permute-start | bytes 14155784 | tf_op jit(solution)/shard_map/mlp_grads/ppermute | solution.py:34
  288.8 16.0 %collective-permute-start.39 = (bf16[2,2,96,768]{3,2,1,0:T(8,128)(2,1)}, bf16[2,2,96,768]{3,2,1,0:T(8,128)(2,1)}, u32[]{:S(2)}, u32[]{:S(2)}) collective-permute-start(bf16[2,2,96,768]{3,2,1,0:T(8,128)(2,1)} %get-tuple-element.292), channel_id=1, source_target_pairs={{0,4},{1,5},{2,6},{3,7},{4,0},{5,1},{6,2},{7,3},{8,12},{9,13},{10,... | collective-permute-start | bytes 1769480 | tf_op jit(solution)/shard_map/head_grads/ppermute | solution.py:34
  307.2 31.2 %collective-permute-start.41 = (bf16[2,2,96,768]{3,2,1,0:T(8,128)(2,1)S(1)}, bf16[2,2,96,768]{3,2,1,0:T(8,128)(2,1)S(1)}, u32[]{:S(2)}, u32[]{:S(2)}) collective-permute-start(bf16[2,2,96,768]{3,2,1,0:T(8,128)(2,1)S(1)} %get-tuple-element.290), channel_id=1, source_target_pairs={{0,16},{1,17},{2,18},{3,19},{4,20},{5,21},{6,22},{7,23},{8,24},{9,... | collective-permute-start | bytes 1769480 | tf_op jit(solution)/shard_map/head_grads/ppermute | solution.py:34
  315.4 28.9 %collective-permute-start.40 = (bf16[16,96,768]{2,1,0:T(8,128)(2,1)S(1)}, bf16[16,96,768]{2,1,0:T(8,128)(2,1)S(1)}, u32[]{:S(2)}, u32[]{:S(2)}) collective-permute-start(bf16[16,96,768]{2,1,0:T(8,128)(2,1)S(1)} %pad_maximum_fusion.3), channel_id=1, source_target_pairs={{0,4},{1,3},{2,6},{3,1},{4,0},{5,7},{6,2},{7,5},{8,12},{9,11},{10,... | collective-permute-start | bytes 7077896 | tf_op jit(solution)/shard_map/mlp_grads/ppermute | solution.py:34
  349.2 16.3 %collective-permute-start.42 = (bf16[2,4,96,768]{3,2,1,0:T(8,128)(2,1)S(1)}, bf16[2,4,96,768]{3,2,1,0:T(8,128)(2,1)S(1)}, u32[]{:S(2)}, u32[]{:S(2)}) collective-permute-start(bf16[2,4,96,768]{3,2,1,0:T(8,128)(2,1)S(1)} %pad_maximum_fusion.8), channel_id=1, source_target_pairs={{0,2},{1,5},{2,0},{3,7},{4,6},{5,1},{6,4},{7,3},{8,10},{9,13},{10,... | collective-permute-start | bytes 3538952 | tf_op jit(solution)/shard_map/mlp_grads/ppermute | solution.py:34
  373.7 9.1 %collective-permute-start.45 = (bf16[4,4,32,768]{3,2,0,1:T(8,128)(2,1)S(1)}, bf16[4,4,32,768]{3,2,0,1:T(8,128)(2,1)S(1)}, u32[]{:S(2)}, u32[]{:S(2)}) collective-permute-start(bf16[4,4,32,768]{3,2,0,1:T(8,128)(2,1)S(1)} %fusion.36), channel_id=1, source_target_pairs={{0,1},{1,0},{2,3},{3,2},{4,5},{5,4},{6,7},{7,6},{8,9},{9,8},{10,11... | collective-permute-start | bytes 2359304 | tf_op jit(solution)/shard_map/embed_grads/ppermute | solution.py:34
  379.6 20.7 %collective-permute-start.44 = (bf16[2,4,96,768]{3,2,1,0:T(8,128)(2,1)}, bf16[2,4,96,768]{3,2,1,0:T(8,128)(2,1)}, u32[]{:S(2)}, u32[]{:S(2)}) collective-permute-start(bf16[2,4,96,768]{3,2,1,0:T(8,128)(2,1)} %pad_maximum_fusion.9), channel_id=1, source_target_pairs={{0,4},{1,3},{2,6},{3,1},{4,0},{5,7},{6,2},{7,5},{8,12},{9,11},{10,... | collective-permute-start | bytes 3538952 | tf_op jit(solution)/shard_map/attn_grads/ppermute | solution.py:34
  382.0 15.5 %collective-permute-start.48 = (bf16[2,2,96,768]{3,2,1,0:T(8,128)(2,1)}, bf16[2,2,96,768]{3,2,1,0:T(8,128)(2,1)}, u32[]{:S(2)}, u32[]{:S(2)}) collective-permute-start(bf16[2,2,96,768]{3,2,1,0:T(8,128)(2,1)} %slice.838), channel_id=1, source_target_pairs={{0,8},{1,9},{2,10},{3,11},{4,12},{5,13},{6,14},{7,15},{8,0},{9,1},... | collective-permute-start | bytes 1769480 | tf_op jit(solution)/shard_map/mlp_grads/ppermute | solution.py:34
  383.8 16.5 %collective-permute-start.46 = (bf16[2,4,32,768]{3,2,1,0:T(8,128)(2,1)}, bf16[2,4,32,768]{3,2,1,0:T(8,128)(2,1)}, u32[]{:S(2)}, u32[]{:S(2)}) collective-permute-start(bf16[2,4,32,768]{3,2,1,0:T(8,128)(2,1)} %pad_maximum_fusion.22), channel_id=1, source_target_pairs={{0,4},{1,3},{2,6},{3,1},{4,0},{5,7},{6,2},{7,5},{8,12},{9,11},{10,... | collective-permute-start | bytes 1179656 | tf_op jit(solution)/shard_map/embed_grads/ppermute | solution.py:34
  399.1 15.3 %collective-permute-start.49 = (bf16[2,1,96,768]{3,2,1,0:T(8,128)(2,1)S(1)}, bf16[2,1,96,768]{3,2,1,0:T(8,128)(2,1)S(1)}, u32[]{:S(2)}, u32[]{:S(2)}) collective-permute-start(bf16[2,1,96,768]{3,2,1,0:T(8,128)(2,1)S(1)} %slice.841), channel_id=1, source_target_pairs={{0,16},{1,17},{2,18},{3,19},{4,20},{5,21},{6,22},{7,23},{8,24},{9,... | collective-permute-start | bytes 884744 | tf_op jit(solution)/shard_map/mlp_grads/ppermute | solution.py:34
  404.9 24.6 %collective-permute-start.47 = (bf16[4,128,768]{2,1,0:T(8,128)(2,1)S(1)}, bf16[4,128,768]{2,1,0:T(8,128)(2,1)S(1)}, u32[]{:S(2)}, u32[]{:S(2)}) collective-permute-start(bf16[4,128,768]{2,1,0:T(8,128)(2,1)S(1)} %pad_maximum_fusion.14), channel_id=1, source_target_pairs={{0,2},{1,5},{2,0},{3,7},{4,6},{5,1},{6,4},{7,3},{8,10},{9,13},{10,... | collective-permute-start | bytes 2359304 | tf_op jit(solution)/shard_map/last_grads/ppermute | solution.py:34
  414.4 15.0 %collective-permute-start.50 = (bf16[2,96,768]{2,1,0:T(8,128)(2,1)S(1)}, bf16[2,96,768]{2,1,0:T(8,128)(2,1)S(1)}, u32[]{:S(2)}, u32[]{:S(2)}) collective-permute-start(bf16[2,96,768]{2,1,0:T(8,128)(2,1)S(1)} %get-tuple-element.236), channel_id=1, source_target_pairs={{0,16},{1,17},{2,18},{3,19},{4,20},{5,21},{6,22},{7,23},{8,24},{9,... | collective-permute-start | bytes 884744 | tf_op jit(solution)/shard_map/mlp_grads_all/ppermute | solution.py:34
  429.5 23.7 %collective-permute-start.52 = (bf16[4,96,768]{2,1,0:T(8,128)(2,1)S(1)}, bf16[4,96,768]{2,1,0:T(8,128)(2,1)S(1)}, u32[]{:S(2)}, u32[]{:S(2)}) collective-permute-start(bf16[4,96,768]{2,1,0:T(8,128)(2,1)S(1)} %pad_maximum_fusion.18), channel_id=1, source_target_pairs={{0,8},{1,9},{2,10},{3,11},{4,12},{5,13},{6,14},{7,15},{8,0},{9,1},... | collective-permute-start | bytes 1769480 | tf_op jit(solution)/shard_map/mlp_grads_all/ppermute | solution.py:34
  429.9 23.4 %collective-permute-start.51 = (bf16[2,128,768]{2,1,0:T(8,128)(2,1)S(1)}, bf16[2,128,768]{2,1,0:T(8,128)(2,1)S(1)}, u32[]{:S(2)}, u32[]{:S(2)}) collective-permute-start(bf16[2,128,768]{2,1,0:T(8,128)(2,1)S(1)} %fusion.55), channel_id=1, source_target_pairs={{0,8},{1,9},{2,10},{3,11},{4,12},{5,13},{6,14},{7,15},{8,0},{9,1},... | collective-permute-start | bytes 1179656 | tf_op jit(solution)/shard_map/last_grads/ppermute | solution.py:34
  454.5 16.5 %collective-permute-start.54 = (bf16[8,96,768]{2,1,0:T(8,128)(2,1)}, bf16[8,96,768]{2,1,0:T(8,128)(2,1)}, u32[]{:S(2)}, u32[]{:S(2)}) collective-permute-start(bf16[8,96,768]{2,1,0:T(8,128)(2,1)} %pad_maximum_fusion.10), channel_id=1, source_target_pairs={{0,2},{1,5},{2,0},{3,7},{4,6},{5,1},{6,4},{7,3},{8,10},{9,13},{10,... | collective-permute-start | bytes 3538952 | tf_op jit(solution)/shard_map/mlp_grads_all/ppermute | solution.py:34
  455.9 11.3 %collective-permute-start.53 = (bf16[128,768]{1,0:T(8,128)(2,1)S(1)}, bf16[128,768]{1,0:T(8,128)(2,1)S(1)}, u32[]{:S(2)}, u32[]{:S(2)}) collective-permute-start(bf16[128,768]{1,0:T(8,128)(2,1)S(1)} %fusion.69), channel_id=1, source_target_pairs={{0,16},{1,17},{2,18},{3,19},{4,20},{5,21},{6,22},{7,23},{8,24},{9,... | collective-permute-start | bytes 589832 | tf_op jit(solution)/shard_map/last_grads/ppermute | solution.py:34
  474.0 29.2 %collective-permute-start.55 = (bf16[16,96,768]{2,1,0:T(8,128)(2,1)}, bf16[16,96,768]{2,1,0:T(8,128)(2,1)}, u32[]{:S(2)}, u32[]{:S(2)}) collective-permute-start(bf16[16,96,768]{2,1,0:T(8,128)(2,1)} %pad_maximum_fusion.4), channel_id=1, source_target_pairs={{0,4},{1,3},{2,6},{3,1},{4,0},{5,7},{6,2},{7,5},{8,12},{9,11},{10,... | collective-permute-start | bytes 7077896 | tf_op jit(solution)/shard_map/mlp_grads_all/ppermute | solution.py:34
  503.2 5.7 collective-permute-start.57
  509.0 6.8 %collective-permute-start.59 = (bf16[2,96,768]{2,1,0:T(8,128)(2,1)S(1)}, bf16[2,96,768]{2,1,0:T(8,128)(2,1)S(1)}, u32[]{:S(2)}, u32[]{:S(2)}) collective-permute-start(bf16[2,96,768]{2,1,0:T(8,128)(2,1)S(1)} %pad_maximum_fusion.25), channel_id=1, source_target_pairs={{0,4},{1,3},{2,6},{3,1},{4,0},{5,7},{6,2},{7,5},{8,12},{9,11},{10,... | collective-permute-start | bytes 884744 | tf_op jit(solution)/shard_map/attn_grads_all/ppermute | solution.py:34
  524.3 5.3 collective-permute-start.63
  577.4 23.2 %collective-permute-start.64 = (f32[96,768]{1,0:T(8,128)S(1)}, f32[96,768]{1,0:T(8,128)S(1)}, u32[]{:S(2)}, u32[]{:S(2)}) collective-permute-start(f32[96,768]{1,0:T(8,128)S(1)} %slice.595), channel_id=1, source_target_pairs={{0,1},{1,0},{2,3},{3,2},{4,5},{5,4},{6,7},{7,6},{8,9},{9,8},{10,11... | collective-permute-start | bytes 884744 | tf_op jit(solution)/shard_map/small/ppermute | solution.py:34
  (158 other events, 1462.4 us)

commit v3 on v2

--- a/solution.py
+++ b/solution.py
@@ -88,7 +88,7 @@
         self.moving, self.result = False, None
         self.value, self.masks = next(steps)
 
-    def advance(self, value):
+    def advance(self, value, start):
         masks = self.masks
         if self.moving:
             try:
@@ -96,15 +96,18 @@
             except StopIteration as end:
                 self.value, self.result, self.moving = None, end.value, False
                 return
+            if not start:
+                self.value, self.masks, self.moving = value, masks, False
+                return
         self.moving = True
         self.value, self.masks = self.exchange(value, masks, self.what), masks
 
 
-def sync(values, *lanes):
+def sync(values, *lanes, hold=()):
     lanes = [lane for lane in lanes if lane.result is None]
     tied = tie(*values, *[lane.value for lane in lanes])
     for lane, value in zip(lanes, tied[len(values) :]):
-        lane.advance(value)
+        lane.advance(value, lane not in hold)
     return tied[: len(values)]
 
 
@@ -266,15 +269,15 @@
 IN_SMEM = pl.BlockSpec(memory_space=pltpu.SMEM)
 
 
-def hidden_forward_kernel(rows, normed_ref, middle_ref, bias_ref, out_bias_ref, *refs):
-    part_refs = refs[:4]
-    final_ref, active_ref, slope_ref = refs[4:]
+def hidden_forward_kernel(rows, normed_ref, middle_ref, bias_ref, *refs):
+    part_refs = refs[:-3]
+    final_ref, active_ref, slope_ref = refs[-3:]
     width = normed_ref.shape[1]
 
     def block(step, carry):
         here = pl.ds(pl.multiple_of(step * rows, rows), rows)
         normed = normed_ref[here]
-        total = middle_ref[here] + out_bias_ref[...]
+        total = middle_ref[here]
         for index, part_ref in enumerate(part_refs):
             hidden = contract_cols(normed, part_ref[:, :width]) + bias_ref[pl.ds(index, 1)]
             active, slope = gelu_with_slope(hidden)
@@ -288,40 +291,46 @@
     lax.fori_loop(0, normed_ref.shape[0] // rows, block, 0)
 
 
-def hidden_forward(normed, middle, bias, out_bias, parts, rows=256):
+def hidden_forward(normed, middle, bias, parts, rows=256):
     token_count, width = normed.shape
+    count = len(parts)
     return pl.pallas_call(
         functools.partial(hidden_forward_kernel, rows),
         out_shape=(
             jax.ShapeDtypeStruct((token_count, width), jnp.float32),
-            jax.ShapeDtypeStruct((4, token_count, width), jnp.bfloat16),
-            jax.ShapeDtypeStruct((4, token_count, width), jnp.float32),
+            jax.ShapeDtypeStruct((count, token_count, width), jnp.bfloat16),
+            jax.ShapeDtypeStruct((count, token_count, width), jnp.float32),
         ),
-        in_specs=[IN_VMEM] * 8,
+        in_specs=[IN_VMEM] * (3 + count),
         out_specs=(IN_VMEM,) * 3,
         compiler_params=pltpu.CompilerParams(vmem_limit_bytes=48 * 1024 * 1024),
         cost_estimate=pl.CostEstimate(
-            flops=16 * token_count * width * width,
-            bytes_accessed=16 * width * width + 32 * token_count * width,
-            transcendentals=8 * token_count * width,
+            flops=4 * count * token_count * width * width,
+            bytes_accessed=4 * count * width * width + 8 * count * token_count * width,
+            transcendentals=2 * count * token_count * width,
         ),
         name="hidden_forward",
-    )(normed, middle, bias, out_bias, *parts)
-
-
-def hidden_back_kernel(core_ref, d_out_ref, normed_ref, active_ref, slope_ref, *refs):
-    part_refs = refs[:4]
-    d_hidden_ref, bias_ref, away_ref = refs[4:]
+    )(normed, middle, bias, *parts)
+
+
+def hidden_back_kernel(core_ref, d_out_ref, normed_ref, *refs):
+    active_refs, slope_refs, part_refs = refs[:2], refs[2:4], refs[4:8]
+    d_hidden_ref, bias_ref, away_ref = refs[8:]
     width = d_out_ref.shape[1]
+    half = width // 2
     first = core_ref[0, 0] == 0
     right = jnp.where(first, d_out_ref[...], normed_ref[...])
+    slots = ((7, 3), (5, 1), (6, 4), (2, 0))
     for index, part_ref in enumerate(part_refs):
         d_active = contract_cols(d_out_ref[...], part_ref[:, width:])
-        d_hidden = (slope_ref[index] * d_active).astype(jnp.bfloat16)
+        slope = slope_refs[index % 2][index // 2]
+        d_hidden = (slope * d_active).astype(jnp.bfloat16)
         d_hidden_ref[index] = d_hidden
         bias_ref[pl.ds(index, 1)] = jnp.sum(d_hidden.astype(jnp.float32), axis=0, keepdims=True)
-        left = jnp.where(first, active_ref[index], d_hidden)
-        away_ref[index] = contract_rows(left, right).astype(jnp.bfloat16)
+        left = jnp.where(first, active_refs[index % 2][index // 2], d_hidden)
+        grad = contract_rows(left, right).astype(jnp.bfloat16)
+        for side, slot in enumerate(slots[index]):
+            away_ref[pl.ds(slot * half, half)] = grad[side * half : (side + 1) * half]
 
 
 def hidden_back(core, d_out, normed, active, slope, parts):
@@ -331,9 +340,9 @@
         out_shape=(
             jax.ShapeDtypeStruct((4, token_count, width), jnp.bfloat16),
             jax.ShapeDtypeStruct((4, width), jnp.float32),
-            jax.ShapeDtypeStruct((4, width, width), jnp.bfloat16),
+            jax.ShapeDtypeStruct((4 * width, width), jnp.bfloat16),
         ),
-        in_specs=[IN_SMEM] + [IN_VMEM] * 8,
+        in_specs=[IN_SMEM] + [IN_VMEM] * 10,
         out_specs=(IN_VMEM,) * 3,
         compiler_params=pltpu.CompilerParams(vmem_limit_bytes=48 * 1024 * 1024),
         cost_estimate=pl.CostEstimate(
@@ -342,43 +351,54 @@
             transcendentals=0,
         ),
         name="hidden_back",
-    )(core.reshape(1, 1), d_out, normed, active, slope, *parts)
-
-
-def kept_grads_kernel(core_ref, d_out_ref, normed_ref, active_ref, d_hidden_ref, *refs):
-    part_refs = refs[:4]
-    d_normed_ref, kept_ref = refs[4:]
+    )(core.reshape(1, 1), d_out, normed, *active, *slope, *parts)
+
+
+def kept_grads_kernel(plan, core_ref, d_out_ref, normed_ref, even_ref, odd_ref, d_hidden_ref, *refs):
+    kept_ref = refs[-1]
+    active_refs = (even_ref, odd_ref)
     width = d_out_ref.shape[1]
+    half = width // 2
     first = core_ref[0, 0] == 0
     right = jnp.where(first, normed_ref[...], d_out_ref[...])
-    total = None
-    for index, part_ref in enumerate(part_refs):
-        d_hidden = d_hidden_ref[index]
-        term = low_dot(d_hidden, part_ref[:, :width])
-        total = term if total is None else total + term
-        left = jnp.where(first, d_hidden, active_ref[index])
-        kept_ref[index] = contract_rows(left, right)
-    d_normed_ref[...] = total
-
-
-def kept_grads(core, d_out, normed, active, d_hidden, parts):
+    for index, side, slot in plan:
+        columns = slice(None) if side is None else slice(side * half, (side + 1) * half)
+        left = jnp.where(
+            first,
+            d_hidden_ref[index, :, columns],
+            active_refs[index % 2][index // 2, :, columns],
+        )
+        grad = contract_rows(left, right)
+        if side is None:
+            kept_ref[pl.ds(slot[0] * half, half)] = grad[:half]
+            kept_ref[pl.ds(slot[1] * half, half)] = grad[half:]
+        else:
+            kept_ref[pl.ds(slot * half, half)] = grad
+    if len(refs) > 1:
+        part_refs, total_ref = refs[:4], refs[4]
+        total = low_dot(d_hidden_ref[0], part_refs[0][:, :width])
+        for index in range(1, 4):
+            total = total + low_dot(d_hidden_ref[index], part_refs[index][:, :width])
+        total_ref[...] = total
+
+
+def kept_grads(plan, core, d_out, normed, active, d_hidden, parts=()):
     token_count, width = d_out.shape
+    grads = jax.ShapeDtypeStruct((2 * width, width), jnp.float32)
+    back = jax.ShapeDtypeStruct((token_count, width), jnp.float32)
     return pl.pallas_call(
-        kept_grads_kernel,
-        out_shape=(
-            jax.ShapeDtypeStruct((token_count, width), jnp.float32),
-            jax.ShapeDtypeStruct((4, width, width), jnp.float32),
-        ),
-        in_specs=[IN_SMEM] + [IN_VMEM] * 8,
-        out_specs=(IN_VMEM,) * 2,
+        functools.partial(kept_grads_kernel, plan),
+        out_shape=(back, grads) if parts else grads,
+        in_specs=[IN_SMEM] + [IN_VMEM] * (5 + len(parts)),
+        out_specs=(IN_VMEM,) * 2 if parts else IN_VMEM,
         compiler_params=pltpu.CompilerParams(vmem_limit_bytes=48 * 1024 * 1024),
         cost_estimate=pl.CostEstimate(
-            flops=16 * token_count * width * width,
-            bytes_accessed=32 * width * width + 20 * token_count * width,
+            flops=4 * token_count * width * width,
+            bytes_accessed=8 * width * width + 20 * token_count * width,
             transcendentals=0,
         ),
         name="kept_grads",
-    )(core.reshape(1, 1), d_out, normed, active, d_hidden, *parts)
+    )(core.reshape(1, 1), d_out, normed, *active, d_hidden, *parts)
 
 
 def orthogonal_kernel(part_count, chunk, full_steps, row_count, factor_ref, *refs):
@@ -398,7 +418,16 @@
                 momentum_keep * moment_refs[index][here].astype(jnp.float32)
                 + factor * grad_refs[index][here].astype(jnp.float32)
             ).astype(bf)
-            rows_ref[pl.ds(pl.multiple_of(index * part_rows + step * chunk, chunk), chunk)] = rows
+            if full_steps:
+                rows_ref[
+                    pl.ds(pl.multiple_of(index * part_rows + step * chunk, chunk), chunk)
+                ] = rows
+            elif index == 0:
+
+                @pl.when(step == 0)
+                def _():
+                    out_ref[...] = rows[:row_count].astype(jnp.float32)
+
             gram_ref[...] += contract_rows(rows, rows)
             return carry
 
@@ -410,6 +439,8 @@
     trace = jnp.sum(jnp.where(diagonal, gram, 0.0))
     inverse = 1.0 / (jnp.sqrt(jnp.full((1, 1), trace)) + 1e-07)
     gram_ref[...] = gram * (inverse * inverse)
+    if not full_steps:
+        out_ref[...] = inverse * out_ref[...]
     for step in range(5):
         low_ref[...] = gram_ref[...].astype(bf)
         change_ref[...] = (
@@ -455,7 +486,7 @@
         + [pl.BlockSpec(memory_space=pltpu.VMEM)] * (2 * count),
         out_specs=pl.BlockSpec(memory_space=pltpu.VMEM),
         scratch_shapes=[
-            pltpu.VMEM((count * part_rows, width), jnp.bfloat16),
+            pltpu.VMEM((count * part_rows if full_steps else 16, width), jnp.bfloat16),
             pltpu.VMEM((width, width), jnp.float32),
             pltpu.VMEM((width, width), jnp.bfloat16),
             pltpu.VMEM((width, width), jnp.bfloat16),
@@ -624,12 +655,9 @@
     patch_wide = jnp.concatenate([patches] + places_hot, axis=1)
     embedded = low_dot(patch_wide, embed_b) + vec_w[10]
     normed, queries, key_rows, values = projections(attn_b, vec_w, embedded)
-    queries, key_rows, values = sync((queries, key_rows, values), mom_lane)
     mixed_out, summary = mixing(queries, key_rows, values, image_index, H)
-    (mixed_out,) = sync((mixed_out,), b_lane, c_lane, mom_lane, head_lane)
-    part_b, part_c = b_lane.result, c_lane.result
-    d_lane = lane(once(part_b, pair), "mlp_weights")
-    sync((), d_lane)
+    (mixed_out,) = sync((mixed_out,), c_lane, mom_lane)
+    part_c = c_lane.result
 
     masks = [1 << bit for bit in high_bits]
     own_codes = [jnp.array(codes(masks + [third[c], fourth[c]]), jnp.int32) for c in (0, 1)]
@@ -643,14 +671,24 @@
 
     middle = embedded + low_dot(mixed_out, attn_b[3 * model_width :]) + vec_w[2]
     normed_two = layer_norm(middle, vec_w[6], vec_w[7]).astype(jnp.bfloat16)
-    (normed_two,) = sync((normed_two,), d_lane)
+    final_rows, active_even, slope_even = hidden_forward(
+        normed_two, middle + vec_w[3], first_bias[::2], [part_a.reshape(-1, 2 * model_width), part_c.reshape(-1, 2 * model_width)]
+    )
+    final_rows, slope_even = sync((final_rows, slope_even), b_lane, head_lane)
+    part_b = b_lane.result
+    d_lane = lane(once(part_b, pair), "mlp_weights")
+    sync((), d_lane)
+    (final_rows,) = sync((final_rows,), d_lane, mom_lane, attn_mom_lane)
     mlp_parts = [
         part.reshape(-1, 2 * model_width) for part in (part_a, part_b, part_c, d_lane.result)
     ]
-    final_rows, active, slope = hidden_forward(
-        normed_two, middle, first_bias, vec_w[3:4], mlp_parts
-    )
-    (final_rows,) = sync((final_rows,), head_lane, mom_lane, attn_mom_lane)
+    final_rows, active_odd, slope_odd = hidden_forward(
+        normed_two, final_rows, first_bias[1::2], mlp_parts[1::2]
+    )
+    active, slope = (active_even, active_odd), (slope_even, slope_odd)
+    (final_rows,) = sync(
+        (final_rows,), head_lane, mom_lane, attn_mom_lane, hold=(mom_lane, attn_mom_lane)
+    )
     closing, close_pull = jax.vjp(layer_norm, final_rows, vec_w[8], vec_w[9])
     member = (image_index[None, :] == jnp.arange(slot_count)[:, None]).astype(jnp.float32)
     slot_sizes = jnp.sum(member, axis=1)
@@ -671,7 +709,6 @@
     all_labels = facts[:, 1] * 256 + facts[:, 2]
     image_total = jnp.sum(valid.astype(jnp.float32))
 
-    (all_pooled,) = sync((all_pooled,), mom_lane, attn_mom_lane)
     logits = low_dot(all_pooled, head_b)
     within = owner_index * chunk + jnp.arange(chunk)
     columns = member_index * shard_width + within
@@ -688,7 +725,6 @@
         row_max = jnp.maximum(lower[0], upper[0])
         exp_sums = lower[1] * jnp.exp(lower[0] - row_max) + upper[1] * jnp.exp(upper[0] - row_max)
         stats = jnp.stack([row_max, exp_sums, lower[2] + upper[2]])
-    (stats,) = sync((stats,), mom_lane, attn_mom_lane)
     normaliser = stats[0] + jnp.log(stats[1])
     loss_sum = jnp.sum(jnp.where(valid, normaliser - stats[2], 0.0))
     probs_class = jnp.exp(logits - normaliser[:, None])
@@ -709,48 +745,49 @@
     d_out = d_final.astype(jnp.bfloat16)
     g_second_bias = jnp.sum(d_out.astype(jnp.float32), axis=0)
     d_out, all_pooled = tie(d_out, all_pooled)
-    head_grad = contract_rows(all_pooled, d_logits).astype(jnp.bfloat16)
+    head_grad = contract_rows(all_pooled, d_logits)
+    head_squares = jnp.sum(head_grad * head_grad) / model_width
     head_lane = lane(
         transposed(
-            head_grad.reshape(owners, shard_rows, chunk),
-            owner_bits[1:-1] + owner_bits[:1] + owner_bits[-1:],
+            head_grad.astype(jnp.bfloat16).reshape(owners, shard_rows, chunk),
+            owner_bits[1:] + owner_bits[:1],
         ),
         "head_grads",
     )
-    (d_out,) = sync((d_out,), head_lane, mom_lane, attn_mom_lane)
-    mlp_moms, attn_moms = finish(mom_lane, attn_mom_lane)
-    mlp_moms = [part.reshape(-1, model_width) for part in mlp_moms]
-    attn_moms = jnp.concatenate(attn_moms, axis=0).reshape(-1, model_width)
+    (d_out,) = sync((d_out,), mom_lane, attn_mom_lane)
 
     d_hidden, bias_grads, away = hidden_back(core, d_out, normed_two, active, slope, mlp_parts)
-    (away, d_hidden) = sync((away, d_hidden), head_lane)
+    (away, d_hidden) = sync((away, d_hidden), mom_lane, attn_mom_lane)
     arrived = exchange(away, pair, "mlp_grads")
-    d_normed_two, kept = kept_grads(core, d_out, normed_two, active, d_hidden, mlp_parts)
-    d_normed_two, kept, arrived = sync((d_normed_two, kept, arrived), head_lane)
-    kept = [
-        (kept[index] + arrived[(index + 2) % 4].astype(jnp.float32)).reshape(
-            -1, mlp_rows, model_width
-        )
-        for index in range(4)
-    ]
-
-    def summing(kept):
-        half = kept[0].shape[0] // 2
-        leave = [kept[1], kept[2][half:], kept[3][half:]]
-        leave = jnp.concatenate([grad.astype(jnp.bfloat16) for grad in leave])
-        arrived = (yield leave, fourth).astype(jnp.float32)
-        leave = [kept[0][half:] + arrived[half : 2 * half], kept[3][:half] + arrived[3 * half :]]
-        kept = [kept[0][:half] + arrived[:half], kept[2][:half] + arrived[2 * half : 3 * half]]
-        arrived = yield jnp.stack(leave).astype(jnp.bfloat16), third
-        kept = jnp.stack(kept) + arrived.astype(jnp.float32)
+    operands = (core, d_out, normed_two, active, d_hidden)
+    leave = kept_grads(((1, None, (2, 0)), (3, 1, 1), (2, 1, 3)), *operands)
+    leave, arrived, d_hidden = sync(
+        (leave, arrived, d_hidden), mom_lane, attn_mom_lane, hold=(mom_lane,)
+    )
+    operands = (core, d_out, normed_two, active, d_hidden)
+    half = 2 * model_width
+    leave = (leave + arrived[:half].astype(jnp.float32)).astype(jnp.bfloat16)
+
+    def summing(leave, kept, arrived):
+        far = yield leave, fourth
+        summed = kept() + arrived.astype(jnp.float32) + far.astype(jnp.float32)
+        arrived = yield summed[:model_width].astype(jnp.bfloat16), third
+        kept = summed[model_width:] + arrived.astype(jnp.float32)
+        kept = kept.reshape(2, -1, mlp_rows, model_width)
         for stage in down_stages:
             half = kept.shape[1] // 2
             arrived = yield kept[:, half:].astype(jnp.bfloat16), stage
             kept = kept[:, :half] + arrived.astype(jnp.float32)
         return kept[:, 0]
 
-    mlp_lane = lane(summing(kept), "mlp_grads")
-    (d_normed_two,) = sync((d_normed_two,), mlp_lane)
+    own = []
+    mlp_lane = lane(summing(leave, lambda: own[0], arrived[half:]), "mlp_grads")
+    sync((), mlp_lane)
+    d_normed_two, grads = kept_grads(
+        ((0, None, (2, 0)), (3, 0, 1), (2, 0, 3)), *operands, mlp_parts
+    )
+    own.append(grads)
+    (d_normed_two,) = sync((d_normed_two,), head_lane)
 
     d_mid_norm, g_gain_two, g_shift_two = jax.vjp(layer_norm, middle, vec_w[6], vec_w[7])[1](
         d_normed_two
@@ -762,7 +799,12 @@
     d_queries, d_keys, d_values = mixing_grads(
         queries, key_rows, values, d_mixed, summary, image_index, H
     )
-    d_queries, d_keys, d_values = sync((d_queries, d_keys, d_values), mlp_lane, head_lane)
+    d_queries, d_keys, d_values, own[0] = sync(
+        (d_queries, d_keys, d_values, own[0]),
+        mlp_lane,
+        head_lane,
+        hold=(head_lane,),
+    )
     attn_grad = jnp.concatenate(
         [
             contract_rows(normed, d_queries),
@@ -803,25 +845,26 @@
         + contract_cols(d_keys, attn_b[model_width : 2 * model_width])
         + contract_cols(d_values, attn_b[2 * model_width : 3 * model_width])
     )
+    sync((), attn_lane)
     (d_normed,) = sync((d_normed,), mlp_lane, attn_lane)
     d_emb_norm, g_gain_one, g_shift_one = jax.vjp(layer_norm, embedded, vec_w[4], vec_w[5])[1](
         d_normed
     )
     d_embed_low = (d_middle + d_emb_norm).astype(jnp.bfloat16)
-    (d_embed_low,) = sync((d_embed_low,), attn_lane)
     embed_grad = contract_rows(patch_wide, d_embed_low)
     embed_lane = lane(quartered(embed_grad, embed_rows), "embed_grads")
     sync((), embed_lane)
-    sync((), mlp_lane)
+    sync((), embed_lane, mlp_lane)
+    finish(attn_lane, embed_lane)
+    sum_lane = lane(last_sums([attn_lane.result, embed_lane.result]), "last_grads")
+    sync((), sum_lane)
     mlp_grad = finish(mlp_lane)[0]
     all_lane = lane(
         collecting(mlp_grad.astype(jnp.bfloat16), up_stages + [third, fourth]), "mlp_grads_all"
     )
-    sync((), all_lane)
-    sync((), embed_lane)
-    finish(attn_lane, embed_lane)
-    sum_lane = lane(last_sums([attn_lane.result, embed_lane.result]), "last_grads")
-    sync((), sum_lane)
+    sync((), all_lane, mom_lane)
+    sync((), sum_lane, all_lane)
+    sync((), sum_lane, all_lane, mom_lane)
     while sum_lane.result is None:
         sync((), sum_lane, all_lane)
     attn_sum, embed_sum = sum_lane.result[:attn_rows], sum_lane.result[attn_rows:]
@@ -829,8 +872,6 @@
     g_value_bias = jnp.sum(d_values.astype(jnp.float32), axis=0)
     g_patch_bias = jnp.sum(d_embed_low.astype(jnp.float32), axis=0)
     g_first_bias = jnp.take(bias_grads.reshape(count, mlp_rows), jnp.argsort(arrival), axis=0)
-    head_grad = finish(head_lane)[0].transpose(1, 0, 2)
-    head_grad = head_grad.reshape(shard_rows, owners * chunk)[:, :shard_width].astype(jnp.float32)
     vec_grad = jnp.concatenate(
         [
             jnp.stack(
@@ -855,7 +896,6 @@
     local_squares = sum(
         jnp.sum(grad * grad, axis=0) for grad in (attn_sum, embed_sum, mlp_grad[0], mlp_grad[1])
     )
-    head_squares = jnp.sum(head_grad * head_grad) / model_width
     small_sums = jnp.concatenate([vec_grad, (local_squares + head_squares)[None]], axis=0)
 
     def total(value):
@@ -868,9 +908,10 @@
         collecting(attn_sum.astype(jnp.bfloat16)[None], up_stages[2:] + [third, fourth, pair]),
         "attn_grads_all",
     )
-    small_sums, attn_grads, mlp_grads = finish(small_lane, block_lane, all_lane)
+    sync((), small_lane, block_lane)
+    small_sums, attn_grads = finish(small_lane, block_lane)
+    attn_moms = jnp.concatenate(finish(attn_mom_lane)[0], axis=0).reshape(-1, model_width)
     attn_grads = jnp.concatenate(attn_grads, axis=0).reshape(-1, model_width)
-    mlp_grads = [part.reshape(-1, model_width) for part in mlp_grads]
     vec_sum = small_sums[:-1]
     grad_norm = jnp.sqrt(jnp.sum(small_sums[-1]) + jnp.sum(vec_sum * vec_sum))
     factor = jnp.minimum(1.0, clip_limit / (grad_norm + 1e-06))
@@ -881,7 +922,19 @@
     )
     mlp_mom_out = momentum_keep * mlp_mom + factor * mlp_sum
 
-    mlp_result = orthogonal_rows(mlp_moms, mlp_grads, factor, 2 * mlp_rows, 768, 2)
+    (factor,) = sync((factor,), head_lane)
+    attn_dir = orthogonal_rows([attn_moms], [attn_grads], factor, attn_rows, 768, 4)
+    (attn_dir,) = sync((attn_dir,), all_lane, mom_lane, head_lane)
+    mlp_grads, mlp_moms = finish(all_lane, mom_lane)
+    mlp_result = orthogonal_rows(
+        [part.reshape(-1, model_width) for part in mlp_moms],
+        [part.reshape(-1, model_width) for part in mlp_grads],
+        factor,
+        2 * mlp_rows,
+        768,
+        0,
+    )
+    (mlp_result,) = sync((mlp_result,), head_lane)
     mlp_other = exchange(mlp_result[mlp_rows:], pair)
     mlp_result = mlp_result[:mlp_rows]
     mlp_dir = jnp.concatenate(
@@ -891,7 +944,8 @@
         ],
         axis=1,
     )
-    attn_dir = orthogonal_rows([attn_moms], [attn_grads], factor, attn_rows, 768, 4)
+    head_grad = finish(head_lane)[0].transpose(1, 0, 2)
+    head_grad = head_grad.reshape(shard_rows, owners * chunk)[:, :shard_width].astype(jnp.float32)
     mlp_scale = math.sqrt(mlp_rows * count / model_width)
     attn_out = attn_w * (1.0 - muon_rate * decay_rate) - muon_rate * attn_dir
     mlp_out = mlp_w * (1.0 - muon_rate * decay_rate) - muon_rate * mlp_scale * mlp_dir

time: 611 us -> 533 us (0.87)
  waiting for transfers between devices: 262 us -> 206 us
  Pallas kernels: 125 us -> 112 us
  starting transfers between devices: 65.8 us -> 58.7 us
    ppermute x66, waiting for transfers between devices: 262 us -> 206 us  [swap(): lax.ppermute(value, AXES, [(i, i ^ masks[i & 1]) for i in range(count)])]
    pallas_call x2, Pallas kernels: 56 us -> 41.1 us  [orthogonal_rows(): pl.pallas_call(body, out_shape=jax.ShapeDtypeStruct((row_count, width), j...]
    ppermute x66, starting transfers between devices: 65.8 us -> 58.7 us  [swap(): lax.ppermute(value, AXES, [(i, i ^ masks[i & 1]) for i in range(count)])]
    concatenate x11, other arithmetic: 8.88 us -> 15.6 us  [collecting(): value = jnp.concatenate([value, (yield (value, stage))], axis=0)]
    unnamed x285 -> x233, local copies, waits for them, and re-layouts: 27.5 us -> 25.2 us
    pallas_call x1 -> x2, Pallas kernels: 13.8 us -> 15.2 us  [kept_grads(): pl.pallas_call(functools.partial(kept_grads_kernel, plan), out_shape=(bac...]
    pallas_call x1 -> x2, Pallas kernels: 16.4 us -> 17.4 us  [hidden_forward(): pl.pallas_call(functools.partial(hidden_forward_kernel, rows), out_shape=...]
  transfers between devices with their start and end apart: 66 -> 66, of which waited for: 45 -> 40; matrix products, arithmetic and copies ran while one was open for 14% -> 16% of each run, Pallas kernels for 14% -> 21%
where the time goes in v3:
time: 533 us; the launch traced here: 525 us
  waiting for transfers between devices  206 us (39%)
  Pallas kernels  112 us (21%)
  other arithmetic  78.7 us (15%)
  starting transfers between devices  58.7 us (11%)
  local copies, waits for them, and re-layouts  44.4 us (8%)
  matrix products  18.7 us (4%)
  between operations  6.62 us (1%)
    ppermute x66, waiting for transfers between devices, swap(): lax.ppermute(value, AXES, [(i, i ^ masks[i & 1]) for i in range(count)])  206 us
    ppermute x66, starting transfers between devices, swap(): lax.ppermute(value, AXES, [(i, i ^ masks[i & 1]) for i in range(count)])  58.7 us
    pallas_call x2, Pallas kernels, orthogonal_rows(): pl.pallas_call(body, out_shape=jax.ShapeDtypeStruct((row_count, width), j...  41.1 us
    unnamed x233, local copies, waits for them, and re-layouts  25.2 us
    pallas_call x2, Pallas kernels, hidden_forward(): pl.pallas_call(functools.partial(hidden_forward_kernel, rows), out_shape=...  17.4 us
    concatenate x11, other arithmetic, collecting(): value = jnp.concatenate([value, (yield (value, stage))], axis=0)  15.6 us
    pallas_call x2, Pallas kernels, kept_grads(): pl.pallas_call(functools.partial(kept_grads_kernel, plan), out_shape=(bac...  15.2 us
    pallas_call x1, Pallas kernels, mixing_grads(): pl.pallas_call(functools.partial(mixing_grads_kernel, width, rows), grid=...  14.4 us
  transfers between devices with their start and end apart: 66, of which 40 were waited for; matrix products, arithmetic and copies ran while one was open for 16% of the time, Pallas kernels for 21%

profile of v3, /device:TPU:0, one launch (start us, length us, event | category | flops | bytes accessed | tf_op | source)
XLA Modules:
  0.0 525.3 jit_solution(10990665970061021974)
XLA Ops:
  2.6 4.1 collective-permute-start
  8.7 7.2 %collective-permute-done = bf16[128,768]{1,0:T(8,128)(2,1)S(1)} collective-permute-done((bf16[128,768]{1,0:T(8,128)(2,1)S(1)}, bf16[128,768]{1,0:T(8,128)(2,1)S(1)}, u32[]{:S(2)}, u32[]{:S(2)}) %collective-permute-start) | collective-permute-done | bytes 196640 | tf_op jit(solution)/shard_map/attn_weights/ppermute | solution.py:34
  16.9 9.5 %collective-permute-done.1 = bf16[2,128,768]{2,1,0:T(8,128)(2,1)S(1)} collective-permute-done((bf16[2,128,768]{2,1,0:T(8,128)(2,1)S(1)}, bf16[2,128,768]{2,1,0:T(8,128)(2,1)S(1)}, u32[]{:S(2)}, u32[]{:S(2)}) %collective-permute-start.1) | collective-permute-done | bytes 393248 | tf_op jit(solution)/shard_map/attn_weights/ppermute | solution.py:34
  27.7 3.3 collective-permute-start.3
  31.1 12.7 %collective-permute-done.3 = bf16[1,96,1536]{2,1,0:T(8,128)(2,1)S(1)} collective-permute-done((bf16[1,96,1536]{2,1,0:T(8,128)(2,1)S(1)}, bf16[1,96,1536]{2,1,0:T(8,128)(2,1)S(1)}, u32[]{:S(2)}, u32[]{:S(2)}) %collective-permute-start.3) | collective-permute-done | bytes 294944 | tf_op jit(solution)/shard_map/mlp_weights/ppermute | solution.py:34
  55.3 10.9 %collective-permute-done.5 = bf16[2,96,1536]{2,1,0:T(8,128)(2,1)} collective-permute-done((bf16[2,96,1536]{2,1,0:T(8,128)(2,1)}, bf16[2,96,1536]{2,1,0:T(8,128)(2,1)}, u32[]{:S(2)}, u32[]{:S(2)}) %collective-permute-start.5) | collective-permute-done | bytes 589856 | tf_op jit(solution)/shard_map/mlp_weights/ppermute | solution.py:34
  76.0 11.5 %collective-permute-done.8 = bf16[2,2,96,768]{3,2,1,0:T(8,128)(2,1)S(1)} collective-permute-done((bf16[2,2,96,768]{3,2,1,0:T(8,128)(2,1)S(1)}, bf16[2,2,96,768]{3,2,1,0:T(8,128)(2,1)S(1)}, u32[]{:S(2)}, u32[]{:S(2)}) %collective-permute-start.8) | collective-permute-done | bytes 589856 | tf_op jit(solution)/shard_map/head/ppermute | solution.py:34
  90.8 2.4 collective-permute-start.11
  97.4 10.4 %mixing.1 = (bf16[512,768]{1,0:T(8,128)(2,1)S(1)}, f32[16,512]{1,0:T(8,128)S(1)}) custom-call(s32[512,1]{1,0:T(8,128)S(1)} %copy.160.ids_down_ref, s32[1,512]{1,0:T(1,128)S(1)} %constant_dynamic-slice_fusion.13.ids_ref, bf16[512,768]{1,0:T(8,128)(2,1)S(1)} %add_convert_fusion.4.q_ref, bf16[512,768]{1,0:T(8,128)(2,1)S(1)} %convolution_convert_fusion.1.k_ref, ...), custom_call_target="tpu_custom_call" | custom-call | flops 805306368 | bytes 3145728 | tf_op jit(solution)/shard_map/mixing/pallas_call | solution.py:195
  110.7 8.9 %hidden_forward.2 = (f32[512,768]{1,0:T(8,128)S(1)}, bf16[2,512,768]{2,1,0:T(8,128)(2,1)S(1)}, f32[2,512,768]{2,1,0:T(8,128)}) custom-call(bf16[512,768]{1,0:T(8,128)(2,1)S(1)} %get-tuple-element.296.normed_ref, f32[512,768]{1,0:T(8,128)S(1)} %get-tuple-element.295.middle_ref, f32[2,768]{1,0:T(2,128)S(1)} %slice.365.bias_ref, bf16[768,1536]{1,0:T(8,128)(2,1)} %bitcast.342, ...), custom_call_target="tpu_custom_call" | custom-call | flops 2415919104 | bytes 11010048 | tf_op jit(solution)/shard_map/hidden_forward/pallas_call | solution.py:297
  134.9 8.5 %hidden_forward.3 = (f32[512,768]{1,0:T(8,128)S(1)}, bf16[2,512,768]{2,1,0:T(8,128)(2,1)S(1)}, f32[2,512,768]{2,1,0:T(8,128)}) custom-call(bf16[512,768]{1,0:T(8,128)(2,1)S(1)} %copy-done.7, f32[512,768]{1,0:T(8,128)S(1)} %copy-done.15, f32[2,768]{1,0:T(2,128)S(1)} %slice.366.bias_ref, bf16[768,1536]{1,0:T(8,128)(2,1)} %bitcast.62.refs_0_.refs_5_.refs_1_, ...), custom_call_target="tpu_custom_call" | custom-call | flops 2415919104 | bytes 11010048 | tf_op jit(solution)/shard_map/hidden_forward/pallas_call | solution.py:297
  149.4 4.9 collective-permute-done.17
  154.5 4.1 collective-permute-done.18
  159.8 3.7 collective-permute-done.19
  164.7 4.9 collective-permute-done.20
  177.9 2.6 collective-permute-done.23
  181.7 2.6 collective-permute-done.24
  184.4 3.6 collective-permute-done.25
  189.8 2.9 collective-permute-done.26
  193.3 2.7 divide_convert_fusion
  204.9 6.2 %collective-permute-done.28 = bf16[2,2,2,16,768]{4,3,0,1,2:T(8,128)(2,1)} collective-permute-done((bf16[2,2,2,16,768]{4,3,0,1,2:T(8,128)(2,1)}, bf16[2,2,2,16,768]{4,3,0,1,2:T(8,128)(2,1)}, u32[]{:S(2)}, u32[]{:S(2)}) %collective-permute-start.28) | collective-permute-done | bytes 196640 | tf_op jit(solution)/shard_map/d_pooled/ppermute | solution.py:34
  213.4 3.5 collective-permute-done.29
  218.1 3.0 collective-permute-done.30
  230.5 13.9 %hidden_back.1 = (bf16[4,512,768]{2,1,0:T(8,128)(2,1)}, f32[4,768]{1,0:T(4,128)S(1)}, bf16[3072,768]{1,0:T(8,128)(2,1)}) custom-call(s32[1,1]{1,0:T(1,128)} %bitcast.108.core_ref, bf16[512,768]{1,0:T(8,128)(2,1)S(1)} %get-tuple-element.148.d_out_ref, bf16[512,768]{1,0:T(8,128)(2,1)S(1)} %copy-done.8, ...), custom_call_target="tpu_custom_call" | custom-call | flops 4831838208 | bytes 22020096 | tf_op jit(solution)/shard_map/hidden_back/pallas_call | solution.py:338
  249.7 3.0 multiply_reduce_fusion
  254.5 5.5 %kept_grads.2 = f32[1536,768]{1,0:T(8,128)} custom-call(s32[1,1]{1,0:T(1,128)} %bitcast.108.core_ref, bf16[512,768]{1,0:T(8,128)(2,1)S(1)} %copy-done.5, bf16[512,768]{1,0:T(8,128)(2,1)S(1)} %copy-done.9, bf16[2,512,768]{2,1,0:T(8,128)(2,1)S(1)} %get-tuple-element.149.refs_0_.even_ref, bf16[2,512,768]{2,1,0:T(8,128)(2,1)S(1)} %copy-done.3, ...), custom_call_target="tpu_custom_call" | custom-call | flops 1207959552 | bytes 12582912 | tf_op jit(solution)/shard_map/kept_grads/pallas_call | solution.py:389
  260.0 3.3 collective-permute-done.35
  263.3 5.2 add_convert_fusion
  269.6 9.7 %kept_grads.3 = (f32[512,768]{1,0:T(8,128)S(1)}, f32[1536,768]{1,0:T(8,128)}) custom-call(s32[1,1]{1,0:T(1,128)} %bitcast.108.core_ref, bf16[512,768]{1,0:T(8,128)(2,1)S(1)} %copy-done.5, bf16[512,768]{1,0:T(8,128)(2,1)S(1)} %copy-done.9, bf16[2,512,768]{2,1,0:T(8,128)(2,1)S(1)} %get-tuple-element.149.refs_0_.even_ref, bf16[2,512,768]{2,1,0:T(8,128)(2,1)} %copy-done.2, ...), custom_call_target="tpu_custom_call" | custom-call | flops 1207959552 | bytes 12582912 | tf_op jit(solution)/shard_map/kept_grads/pallas_call | solution.py:389
  284.2 14.4 %mixing_grads.1 = (bf16[512,768]{1,0:T(8,128)(2,1)S(1)}, bf16[512,768]{1,0:T(8,128)(2,1)S(1)}, bf16[512,768]{1,0:T(8,128)(2,1)S(1)}) custom-call(s32[512,1]{1,0:T(8,128)S(1)} %copy.160.ids_down_ref, s32[1,512]{1,0:T(1,128)S(1)} %constant_dynamic-slice_fusion.13.ids_ref, f32[16,512]{1,0:T(8,128)S(1)} %get-tuple-element.144.summary_ref, ...), custom_call_target="tpu_custom_call" | custom-call | flops 2013265920 | bytes 5505024 | tf_op jit(solution)/shard_map/mixing_grads/pallas_call | solution.py:252
  305.6 4.4 convert_add_fusion
  316.3 10.1 %collective-permute-done.39 = bf16[768,768]{1,0:T(8,128)(2,1)S(1)} collective-permute-done((bf16[768,768]{1,0:T(8,128)(2,1)S(1)}, bf16[768,768]{1,0:T(8,128)(2,1)S(1)}, u32[]{:S(2)}, u32[]{:S(2)}) %collective-permute-start.39) | collective-permute-done | bytes 1179680 | tf_op jit(solution)/shard_map/mlp_grads/ppermute | solution.py:34
  335.3 11.1 %collective-permute-done.43 = bf16[2,2,96,768]{3,2,1,0:T(8,128)(2,1)S(1)} collective-permute-done((bf16[2,2,96,768]{3,2,1,0:T(8,128)(2,1)S(1)}, bf16[2,2,96,768]{3,2,1,0:T(8,128)(2,1)S(1)}, u32[]{:S(2)}, u32[]{:S(2)}) %collective-permute-start.43) | collective-permute-done | bytes 589856 | tf_op jit(solution)/shard_map/mlp_grads/ppermute | solution.py:34
  349.7 2.5 constant_dynamic-update-slice_fusion
  352.2 10.3 %collective-permute-done.46 = bf16[2,1,96,768]{3,2,1,0:T(8,128)(2,1)S(1)} collective-permute-done((bf16[2,1,96,768]{3,2,1,0:T(8,128)(2,1)S(1)}, bf16[2,1,96,768]{3,2,1,0:T(8,128)(2,1)S(1)}, u32[]{:S(2)}, u32[]{:S(2)}) %collective-permute-start.46) | collective-permute-done | bytes 294944 | tf_op jit(solution)/shard_map/mlp_grads/ppermute | solution.py:34
  366.4 14.2 %collective-permute-done.47 = bf16[2,96,768]{2,1,0:T(8,128)(2,1)S(1)} collective-permute-done((bf16[2,96,768]{2,1,0:T(8,128)(2,1)S(1)}, bf16[2,96,768]{2,1,0:T(8,128)(2,1)S(1)}, u32[]{:S(2)}, u32[]{:S(2)}) %collective-permute-start.47) | collective-permute-done | bytes 294944 | tf_op jit(solution)/shard_map/mlp_grads_all/ppermute | solution.py:34
  380.6 5.2 collective-permute-done.45
  390.3 18.2 %collective-permute-done.48 = bf16[2,128,768]{2,1,0:T(8,128)(2,1)} collective-permute-done((bf16[2,128,768]{2,1,0:T(8,128)(2,1)}, bf16[2,128,768]{2,1,0:T(8,128)(2,1)}, u32[]{:S(2)}, u32[]{:S(2)}) %collective-permute-start.48) | collective-permute-done | bytes 393248 | tf_op jit(solution)/shard_map/last_grads/ppermute | solution.py:34
  408.6 2.4 pad_maximum_fusion.8
  417.3 10.1 %collective-permute-done.51 = bf16[128,768]{1,0:T(8,128)(2,1)S(1)} collective-permute-done((bf16[128,768]{1,0:T(8,128)(2,1)S(1)}, bf16[128,768]{1,0:T(8,128)(2,1)S(1)}, u32[]{:S(2)}, u32[]{:S(2)}) %collective-permute-start.51) | collective-permute-done | bytes 196640 | tf_op jit(solution)/shard_map/last_grads/ppermute | solution.py:34
  430.0 2.9 collective-permute-done.54
  435.6 3.4 collective-permute-done.55
  446.2 3.1 pad_maximum_fusion.3
  452.8 3.3 collective-permute-done.60
  462.0 15.0 %orthogonal_rows.2 = f32[96,768]{1,0:T(8,128)S(1)} custom-call(f32[1,1]{1,0:T(1,128)} %bitcast.141.factor_ref, bf16[768,768]{1,0:T(8,128)(2,1)S(1)} %bitcast.335, bf16[768,768]{1,0:T(8,128)(2,1)S(1)} %bitcast.336), custom_call_target="tpu_custom_call" | custom-call | flops 16307453952 | bytes 2359296 | tf_op jit(solution)/shard_map/orthogonal_rows/pallas_call | solution.py:482
  478.6 7.2 %collective-permute-done.62 = bf16[2,2,96,768]{3,2,1,0:T(8,128)(2,1)S(1)} collective-permute-done((bf16[2,2,96,768]{3,2,1,0:T(8,128)(2,1)}, bf16[2,2,96,768]{3,2,1,0:T(8,128)(2,1)S(1)}, u32[]{:S(2)}, u32[]{:S(2)}) %collective-permute-start.62) | collective-permute-done | bytes 589856 | tf_op jit(solution)/shard_map/head_grads/ppermute | solution.py:34
  487.6 26.2 %orthogonal_rows.3 = f32[192,768]{1,0:T(8,128)S(1)} custom-call(f32[1,1]{1,0:T(1,128)} %bitcast.141.factor_ref, bf16[1536,768]{1,0:T(8,128)(2,1)} %bitcast.144.refs_0_, bf16[1536,768]{1,0:T(8,128)(2,1)} %bitcast.145.refs_1_, bf16[1536,768]{1,0:T(8,128)(2,1)} %bitcast.146.refs_2_, bf16[1536,768]{1,0:T(8,128)(2,1)} %bitcast.147.refs_3_), custom_call_target="tpu_custom_call" | custom-call | flops 11777605632 | bytes 9437184 | tf_op jit(solution)/shard_map/orthogonal_rows/pallas_call | solution.py:482
  516.8 4.8 fusion.115
  (581 shorter events, 175.5 us)
Async XLA Ops:
  2.6 13.2 %collective-permute-start = (bf16[128,768]{1,0:T(8,128)(2,1)S(1)}, bf16[128,768]{1,0:T(8,128)(2,1)S(1)}, u32[]{:S(2)}, u32[]{:S(2)}) collective-permute-start(bf16[128,768]{1,0:T(8,128)(2,1)S(1)} %pad_maximum_fusion.24), channel_id=1, source_target_pairs={{0,16},{1,17},{2,18},{3,19},{4,20},{5,21},{6,22},{7,23},{8,24},{9,... | collective-permute-start | bytes 589832 | tf_op jit(solution)/shard_map/attn_weights/ppermute | solution.py:34
  15.9 10.4 %collective-permute-start.1 = (bf16[2,128,768]{2,1,0:T(8,128)(2,1)S(1)}, bf16[2,128,768]{2,1,0:T(8,128)(2,1)S(1)}, u32[]{:S(2)}, u32[]{:S(2)}) collective-permute-start(bf16[2,128,768]{2,1,0:T(8,128)(2,1)S(1)} %maximum_select_fusion.11), channel_id=1, source_target_pairs={{0,8},{1,9},{2,10},{3,11},{4,12},{5,13},{6,14},{7,15},{8,0},{9,1},... | collective-permute-start | bytes 1179656 | tf_op jit(solution)/shard_map/attn_weights/ppermute | solution.py:34
  26.4 17.4 %collective-permute-start.2 = (bf16[4,128,768]{2,1,0:T(8,128)(2,1)S(1)}, bf16[4,128,768]{2,1,0:T(8,128)(2,1)S(1)}, u32[]{:S(2)}, u32[]{:S(2)}) collective-permute-start(bf16[4,128,768]{2,1,0:T(8,128)(2,1)S(1)} %bitcast.345), channel_id=1, source_target_pairs={{0,2},{1,5},{2,0},{3,7},{4,6},{5,1},{6,4},{7,3},{8,10},{9,13},{10,... | collective-permute-start | bytes 2359304 | tf_op jit(solution)/shard_map/attn_weights/ppermute | solution.py:34
  27.7 16.1 %collective-permute-start.3 = (bf16[1,96,1536]{2,1,0:T(8,128)(2,1)S(1)}, bf16[1,96,1536]{2,1,0:T(8,128)(2,1)S(1)}, u32[]{:S(2)}, u32[]{:S(2)}) collective-permute-start(bf16[1,96,1536]{2,1,0:T(8,128)(2,1)S(1)} %convert_bitcast_fusion.1), channel_id=1, source_target_pairs={{0,16},{1,17},{2,18},{3,19},{4,20},{5,21},{6,22},{7,23},{8,24},{9,... | collective-permute-start | bytes 884744 | tf_op jit(solution)/shard_map/mlp_weights/ppermute | solution.py:34
  45.8 20.7 %collective-permute-start.4 = (bf16[2,4,128,768]{3,2,1,0:T(8,128)(2,1)}, bf16[2,4,128,768]{3,2,1,0:T(8,128)(2,1)}, u32[]{:S(2)}, u32[]{:S(2)}) collective-permute-start(bf16[2,4,128,768]{3,2,1,0:T(8,128)(2,1)} %pad_maximum_fusion.4), channel_id=1, source_target_pairs={{0,4},{1,3},{2,6},{3,1},{4,0},{5,7},{6,2},{7,5},{8,12},{9,11},{10,... | collective-permute-start | bytes 4718600 | tf_op jit(solution)/shard_map/attn_weights/ppermute | solution.py:34
  50.3 15.9 %collective-permute-start.5 = (bf16[2,96,1536]{2,1,0:T(8,128)(2,1)}, bf16[2,96,1536]{2,1,0:T(8,128)(2,1)}, u32[]{:S(2)}, u32[]{:S(2)}) collective-permute-start(bf16[2,96,1536]{2,1,0:T(8,128)(2,1)} %pad_maximum_fusion.13), channel_id=1, source_target_pairs={{0,8},{1,9},{2,10},{3,11},{4,12},{5,13},{6,14},{7,15},{8,0},{9,1},... | collective-permute-start | bytes 1769480 | tf_op jit(solution)/shard_map/mlp_weights/ppermute | solution.py:34
  68.3 7.1 %collective-permute-start.6 = (bf16[4,4,128,768]{3,2,1,0:T(8,128)(2,1)S(1)}, bf16[4,4,128,768]{3,2,1,0:T(8,128)(2,1)S(1)}, u32[]{:S(2)}, u32[]{:S(2)}) collective-permute-start(bf16[4,4,128,768]{3,2,1,0:T(8,128)(2,1)S(1)} %pad_maximum_fusion.1), channel_id=1, source_target_pairs={{0,1},{1,0},{2,3},{3,2},{4,5},{5,4},{6,7},{7,6},{8,9},{9,8},{10,11... | collective-permute-start | bytes 9437192 | tf_op jit(solution)/shard_map/attn_weights/ppermute | solution.py:34
  71.5 16.3 %collective-permute-start.7 = (bf16[4,96,1536]{2,1,0:T(8,128)(2,1)S(1)}, bf16[4,96,1536]{2,1,0:T(8,128)(2,1)S(1)}, u32[]{:S(2)}, u32[]{:S(2)}) collective-permute-start(bf16[4,96,1536]{2,1,0:T(8,128)(2,1)S(1)} %pad_maximum_fusion.5), channel_id=1, source_target_pairs={{0,2},{1,5},{2,0},{3,7},{4,6},{5,1},{6,4},{7,3},{8,10},{9,13},{10,... | collective-permute-start | bytes 3538952 | tf_op jit(solution)/shard_map/mlp_weights/ppermute | solution.py:34
  73.1 14.5 %collective-permute-start.8 = (bf16[2,2,96,768]{3,2,1,0:T(8,128)(2,1)S(1)}, bf16[2,2,96,768]{3,2,1,0:T(8,128)(2,1)S(1)}, u32[]{:S(2)}, u32[]{:S(2)}) collective-permute-start(bf16[2,2,96,768]{3,2,1,0:T(8,128)(2,1)S(1)} %get-tuple-element.123), channel_id=1, source_target_pairs={{0,8},{1,9},{2,10},{3,11},{4,12},{5,13},{6,14},{7,15},{8,0},{9,1},... | collective-permute-start | bytes 1769480 | tf_op jit(solution)/shard_map/head/ppermute | solution.py:34
  89.1 18.8 %collective-permute-start.9 = (bf16[8,96,1536]{2,1,0:T(8,128)(2,1)S(1)}, bf16[8,96,1536]{2,1,0:T(8,128)(2,1)S(1)}, u32[]{:S(2)}, u32[]{:S(2)}) collective-permute-start(bf16[8,96,1536]{2,1,0:T(8,128)(2,1)S(1)} %pad_maximum_fusion.2), channel_id=1, source_target_pairs={{0,1},{1,0},{2,3},{3,2},{4,5},{5,4},{6,7},{7,6},{8,9},{9,8},{10,11... | collective-permute-start | bytes 7077896 | tf_op jit(solution)/shard_map/mlp_weights/ppermute | solution.py:34
  89.2 31.6 %collective-permute-start.10 = (bf16[8,96,1536]{2,1,0:T(8,128)(2,1)S(1)}, bf16[8,96,1536]{2,1,0:T(8,128)(2,1)}, u32[]{:S(2)}, u32[]{:S(2)}) collective-permute-start(bf16[8,96,1536]{2,1,0:T(8,128)(2,1)S(1)} %pad_maximum_fusion.2), channel_id=1, source_target_pairs={{0,4},{1,3},{2,6},{3,1},{4,0},{5,7},{6,2},{7,5},{8,12},{9,11},{10,... | collective-permute-start | bytes 7077896 | tf_op jit(solution)/shard_map/mlp_weights/ppermute | solution.py:34
  90.8 29.9 %collective-permute-start.11 = (bf16[2,2,96,768]{3,2,1,0:T(8,128)(2,1)S(1)}, bf16[2,2,96,768]{3,2,1,0:T(8,128)(2,1)S(1)}, u32[]{:S(2)}, u32[]{:S(2)}) collective-permute-start(bf16[2,2,96,768]{3,2,1,0:T(8,128)(2,1)S(1)} %get-tuple-element.308), channel_id=1, source_target_pairs={{0,16},{1,17},{2,18},{3,19},{4,20},{5,21},{6,22},{7,23},{8,24},{9,... | collective-permute-start | bytes 1769480 | tf_op jit(solution)/shard_map/head/ppermute | solution.py:34
  121.5 7.2 %collective-permute-start.12 = (bf16[8,96,1536]{2,1,0:T(8,128)(2,1)}, bf16[8,96,1536]{2,1,0:T(8,128)(2,1)}, u32[]{:S(2)}, u32[]{:S(2)}) collective-permute-start(bf16[8,96,1536]{2,1,0:T(8,128)(2,1)} %collective-permute-done.10), channel_id=1, source_target_pairs={{0,1},{1,0},{2,3},{3,2},{4,5},{5,4},{6,7},{7,6},{8,9},{9,8},{10,11... | collective-permute-start | bytes 7077896 | tf_op jit(solution)/shard_map/mlp_weights/ppermute | solution.py:34
  126.4 18.2 %collective-permute-start.14 = (bf16[2,2,96,768]{3,2,1,0:T(8,128)(2,1)}, bf16[2,2,96,768]{3,2,1,0:T(8,128)(2,1)}, u32[]{:S(2)}, u32[]{:S(2)}) collective-permute-start(bf16[2,2,96,768]{3,2,1,0:T(8,128)(2,1)} %get-tuple-element.306), channel_id=1, source_target_pairs={{0,4},{1,5},{2,6},{3,7},{4,0},{5,1},{6,2},{7,3},{8,12},{9,13},{10,... | collective-permute-start | bytes 1769480 | tf_op jit(solution)/shard_map/head/ppermute | solution.py:34
  130.1 16.7 %collective-permute-start.15 = (bf16[2,96,768]{2,1,0:T(8,128)(2,1)}, bf16[2,96,768]{2,1,0:T(8,128)(2,1)}, u32[]{:S(2)}, u32[]{:S(2)}) collective-permute-start(bf16[2,96,768]{2,1,0:T(8,128)(2,1)} %pad_maximum_fusion.21), channel_id=1, source_target_pairs={{0,16},{1,17},{2,18},{3,19},{4,20},{5,21},{6,22},{7,23},{8,24},{9,... | collective-permute-start | bytes 884744 | tf_op jit(solution)/shard_map/mlp_moments/ppermute | solution.py:34
  131.4 13.2 %collective-permute-start.16 = (bf16[1,96,768]{2,1,0:T(8,128)(2,1)}, bf16[1,96,768]{2,1,0:T(8,128)(2,1)}, u32[]{:S(2)}, u32[]{:S(2)}) collective-permute-start(bf16[1,96,768]{2,1,0:T(8,128)(2,1)} %convert_bitcast_fusion.2), channel_id=1, source_target_pairs={{0,2},{1,5},{2,0},{3,7},{4,6},{5,1},{6,4},{7,3},{8,10},{9,13},{10,... | collective-permute-start | bytes 442376 | tf_op jit(solution)/shard_map/attn_moments/ppermute | solution.py:34
  163.5 6.1 %collective-permute-start.20 = (bf16[2,2,2,16,896]{4,3,0,1,2:T(8,128)(2,1)S(1)}, bf16[2,2,2,16,896]{4,3,0,1,2:T(8,128)(2,1)S(1)}, u32[]{:S(2)}, u32[]{:S(2)}) collective-permute-start(bf16[2,2,2,16,896]{4,3,0,1,2:T(8,128)(2,1)S(1)} %maximum_select_fusion.13), channel_id=1, source_target_pairs={{0,2},{1,3},{2,0},{3,1},{4,6},{5,7},{6,4},{7,5},{8,10},{9,11},{10,... | collective-permute-start | bytes 688136 | tf_op jit(solution)/shard_map/pooled/ppermute | solution.py:34
  203.8 7.3 %collective-permute-start.28 = (bf16[2,2,2,16,768]{4,3,0,1,2:T(8,128)(2,1)}, bf16[2,2,2,16,768]{4,3,0,1,2:T(8,128)(2,1)}, u32[]{:S(2)}, u32[]{:S(2)}) collective-permute-start(bf16[2,2,2,16,768]{4,3,0,1,2:T(8,128)(2,1)} %fusion.59), channel_id=1, source_target_pairs={{0,2},{1,3},{2,0},{3,1},{4,6},{5,7},{6,4},{7,5},{8,10},{9,11},{10,... | collective-permute-start | bytes 589832 | tf_op jit(solution)/shard_map/d_pooled/ppermute | solution.py:34
  228.3 16.1 %collective-permute-start.32 = (bf16[4,96,768]{2,1,0:T(8,128)(2,1)S(1)}, bf16[4,96,768]{2,1,0:T(8,128)(2,1)S(1)}, u32[]{:S(2)}, u32[]{:S(2)}) collective-permute-start(bf16[4,96,768]{2,1,0:T(8,128)(2,1)S(1)} %pad_maximum_fusion.14), channel_id=1, source_target_pairs={{0,8},{1,9},{2,10},{3,11},{4,12},{5,13},{6,14},{7,15},{8,0},{9,1},... | collective-permute-start | bytes 1769480 | tf_op jit(solution)/shard_map/mlp_moments/ppermute | solution.py:34
  228.3 16.0 %collective-permute-start.33 = (bf16[2,96,768]{2,1,0:T(8,128)(2,1)S(1)}, bf16[2,96,768]{2,1,0:T(8,128)(2,1)S(1)}, u32[]{:S(2)}, u32[]{:S(2)}) collective-permute-start(bf16[2,96,768]{2,1,0:T(8,128)(2,1)S(1)} %pad_maximum_fusion.22), channel_id=1, source_target_pairs={{0,4},{1,3},{2,6},{3,1},{4,0},{5,7},{6,2},{7,5},{8,12},{9,11},{10,... | collective-permute-start | bytes 884744 | tf_op jit(solution)/shard_map/attn_moments/ppermute | solution.py:34
  244.4 18.9 %collective-permute-start.34 = (bf16[3072,768]{1,0:T(8,128)(2,1)}, bf16[3072,768]{1,0:T(8,128)(2,1)}, u32[]{:S(2)}, u32[]{:S(2)}) collective-permute-start(bf16[3072,768]{1,0:T(8,128)(2,1)} %get-tuple-element.158), channel_id=1, source_target_pairs={{0,1},{1,0},{2,3},{3,2},{4,5},{5,4},{6,7},{7,6},{8,9},{9,8},{10,11... | collective-permute-start | bytes 14155784 | tf_op jit(solution)/shard_map/mlp_grads/ppermute | solution.py:34
  246.8 16.5 %collective-permute-start.35 = (bf16[8,96,768]{2,1,0:T(8,128)(2,1)}, bf16[8,96,768]{2,1,0:T(8,128)(2,1)}, u32[]{:S(2)}, u32[]{:S(2)}) collective-permute-start(bf16[8,96,768]{2,1,0:T(8,128)(2,1)} %pad_maximum_fusion.6), channel_id=1, source_target_pairs={{0,2},{1,5},{2,0},{3,7},{4,6},{5,1},{6,4},{7,3},{8,10},{9,13},{10,... | collective-permute-start | bytes 3538952 | tf_op jit(solution)/shard_map/mlp_moments/ppermute | solution.py:34
  249.7 10.3 %collective-permute-start.36 = (bf16[4,96,768]{2,1,0:T(8,128)(2,1)}, bf16[4,96,768]{2,1,0:T(8,128)(2,1)}, u32[]{:S(2)}, u32[]{:S(2)}) collective-permute-start(bf16[4,96,768]{2,1,0:T(8,128)(2,1)} %pad_maximum_fusion.15), channel_id=1, source_target_pairs={{0,1},{1,0},{2,3},{3,2},{4,5},{5,4},{6,7},{7,6},{8,9},{9,8},{10,11... | collective-permute-start | bytes 1769480 | tf_op jit(solution)/shard_map/attn_moments/ppermute | solution.py:34
  268.5 30.9 %collective-permute-start.37 = (bf16[1536,768]{1,0:T(8,128)(2,1)}, bf16[1536,768]{1,0:T(8,128)(2,1)}, u32[]{:S(2)}, u32[]{:S(2)}) collective-permute-start(bf16[1536,768]{1,0:T(8,128)(2,1)} %add_convert_fusion), channel_id=1, source_target_pairs={{0,4},{1,3},{2,6},{3,1},{4,0},{5,7},{6,2},{7,5},{8,12},{9,11},{10,... | collective-permute-start | bytes 7077896 | tf_op jit(solution)/shard_map/mlp_grads/ppermute | solution.py:34
  279.3 20.1 %collective-permute-start.38 = (bf16[2,2,96,768]{3,2,1,0:T(8,128)(2,1)}, bf16[2,2,96,768]{3,2,1,0:T(8,128)(2,1)S(1)}, u32[]{:S(2)}, u32[]{:S(2)}) collective-permute-start(bf16[2,2,96,768]{3,2,1,0:T(8,128)(2,1)} %get-tuple-element.171), channel_id=1, source_target_pairs={{0,8},{1,9},{2,10},{3,11},{4,12},{5,13},{6,14},{7,15},{8,0},{9,1},... | collective-permute-start | bytes 1769480 | tf_op jit(solution)/shard_map/head_grads/ppermute | solution.py:34
  304.9 21.5 %collective-permute-start.40 = (bf16[4,4,96,768]{3,2,0,1:T(8,128)(2,1)}, bf16[4,4,96,768]{3,2,0,1:T(8,128)(2,1)}, u32[]{:S(2)}, u32[]{:S(2)}) collective-permute-start(bf16[4,4,96,768]{3,2,0,1:T(8,128)(2,1)} %fusion), channel_id=1, source_target_pairs={{0,1},{1,0},{2,3},{3,2},{4,5},{5,4},{6,7},{7,6},{8,9},{9,8},{10,11... | collective-permute-start | bytes 7077896 | tf_op jit(solution)/shard_map/attn_grads/ppermute | solution.py:34
  310.1 16.3 %collective-permute-start.39 = (bf16[768,768]{1,0:T(8,128)(2,1)S(1)}, bf16[768,768]{1,0:T(8,128)(2,1)S(1)}, u32[]{:S(2)}, u32[]{:S(2)}) collective-permute-start(bf16[768,768]{1,0:T(8,128)(2,1)S(1)} %slice.711), channel_id=1, source_target_pairs={{0,2},{1,5},{2,0},{3,7},{4,6},{5,1},{6,4},{7,3},{8,10},{9,13},{10,... | collective-permute-start | bytes 3538952 | tf_op jit(solution)/shard_map/mlp_grads/ppermute | solution.py:34
  330.1 16.3 %collective-permute-start.42 = (bf16[4,4,32,768]{3,2,0,1:T(8,128)(2,1)S(1)}, bf16[4,4,32,768]{3,2,0,1:T(8,128)(2,1)S(1)}, u32[]{:S(2)}, u32[]{:S(2)}) collective-permute-start(bf16[4,4,32,768]{3,2,0,1:T(8,128)(2,1)S(1)} %fusion.31), channel_id=1, source_target_pairs={{0,1},{1,0},{2,3},{3,2},{4,5},{5,4},{6,7},{7,6},{8,9},{9,8},{10,11... | collective-permute-start | bytes 2359304 | tf_op jit(solution)/shard_map/embed_grads/ppermute | solution.py:34
  330.6 15.8 %collective-permute-start.43 = (bf16[2,2,96,768]{3,2,1,0:T(8,128)(2,1)S(1)}, bf16[2,2,96,768]{3,2,1,0:T(8,128)(2,1)S(1)}, u32[]{:S(2)}, u32[]{:S(2)}) collective-permute-start(bf16[2,2,96,768]{3,2,1,0:T(8,128)(2,1)S(1)} %slice.712), channel_id=1, source_target_pairs={{0,8},{1,9},{2,10},{3,11},{4,12},{5,13},{6,14},{7,15},{8,0},{9,1},... | collective-permute-start | bytes 1769480 | tf_op jit(solution)/shard_map/mlp_grads/ppermute | solution.py:34
  334.3 30.2 %collective-permute-start.41 = (bf16[2,4,96,768]{3,2,1,0:T(8,128)(2,1)S(1)}, bf16[2,4,96,768]{3,2,1,0:T(8,128)(2,1)S(1)}, u32[]{:S(2)}, u32[]{:S(2)}) collective-permute-start(bf16[2,4,96,768]{3,2,1,0:T(8,128)(2,1)S(1)} %pad_maximum_fusion.7), channel_id=1, source_target_pairs={{0,4},{1,3},{2,6},{3,1},{4,0},{5,7},{6,2},{7,5},{8,12},{9,11},{10,... | collective-permute-start | bytes 3538952 | tf_op jit(solution)/shard_map/attn_grads/ppermute | solution.py:34
  346.6 15.9 %collective-permute-start.46 = (bf16[2,1,96,768]{3,2,1,0:T(8,128)(2,1)S(1)}, bf16[2,1,96,768]{3,2,1,0:T(8,128)(2,1)S(1)}, u32[]{:S(2)}, u32[]{:S(2)}) collective-permute-start(bf16[2,1,96,768]{3,2,1,0:T(8,128)(2,1)S(1)} %slice.713), channel_id=1, source_target_pairs={{0,16},{1,17},{2,18},{3,19},{4,20},{5,21},{6,22},{7,23},{8,24},{9,... | collective-permute-start | bytes 884744 | tf_op jit(solution)/shard_map/mlp_grads/ppermute | solution.py:34
  348.6 15.9 %collective-permute-start.44 = (bf16[2,4,32,768]{3,2,1,0:T(8,128)(2,1)S(1)}, bf16[2,4,32,768]{3,2,1,0:T(8,128)(2,1)S(1)}, u32[]{:S(2)}, u32[]{:S(2)}) collective-permute-start(bf16[2,4,32,768]{3,2,1,0:T(8,128)(2,1)S(1)} %pad_maximum_fusion.20), channel_id=1, source_target_pairs={{0,4},{1,3},{2,6},{3,1},{4,0},{5,7},{6,2},{7,5},{8,12},{9,11},{10,... | collective-permute-start | bytes 1179656 | tf_op jit(solution)/shard_map/embed_grads/ppermute | solution.py:34
  363.4 45.2 %collective-permute-start.50 = (bf16[16,96,768]{2,1,0:T(8,128)(2,1)}, bf16[16,96,768]{2,1,0:T(8,128)(2,1)}, u32[]{:S(2)}, u32[]{:S(2)}) collective-permute-start(bf16[16,96,768]{2,1,0:T(8,128)(2,1)} %constant_dynamic-update-slice_fusion), channel_id=1, source_target_pairs={{0,4},{1,3},{2,6},{3,1},{4,0},{5,7},{6,2},{7,5},{8,12},{9,11},{10,... | collective-permute-start | bytes 7077896 | tf_op jit(solution)/shard_map/mlp_moments/ppermute | solution.py:34
  365.3 20.5 %collective-permute-start.45 = (bf16[4,128,768]{2,1,0:T(8,128)(2,1)S(1)}, bf16[4,128,768]{2,1,0:T(8,128)(2,1)S(1)}, u32[]{:S(2)}, u32[]{:S(2)}) collective-permute-start(bf16[4,128,768]{2,1,0:T(8,128)(2,1)S(1)} %pad_maximum_fusion.12), channel_id=1, source_target_pairs={{0,2},{1,5},{2,0},{3,7},{4,6},{5,1},{6,4},{7,3},{8,10},{9,13},{10,... | collective-permute-start | bytes 2359304 | tf_op jit(solution)/shard_map/last_grads/ppermute | solution.py:34
  366.4 14.2 %collective-permute-start.47 = (bf16[2,96,768]{2,1,0:T(8,128)(2,1)S(1)}, bf16[2,96,768]{2,1,0:T(8,128)(2,1)S(1)}, u32[]{:S(2)}, u32[]{:S(2)}) collective-permute-start(bf16[2,96,768]{2,1,0:T(8,128)(2,1)S(1)} %get-tuple-element.186), channel_id=1, source_target_pairs={{0,16},{1,17},{2,18},{3,19},{4,20},{5,21},{6,22},{7,23},{8,24},{9,... | collective-permute-start | bytes 884744 | tf_op jit(solution)/shard_map/mlp_grads_all/ppermute | solution.py:34
  386.7 21.9 %collective-permute-start.49 = (bf16[4,96,768]{2,1,0:T(8,128)(2,1)}, bf16[4,96,768]{2,1,0:T(8,128)(2,1)}, u32[]{:S(2)}, u32[]{:S(2)}) collective-permute-start(bf16[4,96,768]{2,1,0:T(8,128)(2,1)} %pad_maximum_fusion.16), channel_id=1, source_target_pairs={{0,8},{1,9},{2,10},{3,11},{4,12},{5,13},{6,14},{7,15},{8,0},{9,1},... | collective-permute-start | bytes 1769480 | tf_op jit(solution)/shard_map/mlp_grads_all/ppermute | solution.py:34
  387.6 20.9 %collective-permute-start.48 = (bf16[2,128,768]{2,1,0:T(8,128)(2,1)}, bf16[2,128,768]{2,1,0:T(8,128)(2,1)}, u32[]{:S(2)}, u32[]{:S(2)}) collective-permute-start(bf16[2,128,768]{2,1,0:T(8,128)(2,1)} %fusion.48), channel_id=1, source_target_pairs={{0,8},{1,9},{2,10},{3,11},{4,12},{5,13},{6,14},{7,15},{8,0},{9,1},... | collective-permute-start | bytes 1179656 | tf_op jit(solution)/shard_map/last_grads/ppermute | solution.py:34
  410.9 16.5 %collective-permute-start.52 = (bf16[8,96,768]{2,1,0:T(8,128)(2,1)}, bf16[8,96,768]{2,1,0:T(8,128)(2,1)}, u32[]{:S(2)}, u32[]{:S(2)}) collective-permute-start(bf16[8,96,768]{2,1,0:T(8,128)(2,1)} %pad_maximum_fusion.8), channel_id=1, source_target_pairs={{0,2},{1,5},{2,0},{3,7},{4,6},{5,1},{6,4},{7,3},{8,10},{9,13},{10,... | collective-permute-start | bytes 3538952 | tf_op jit(solution)/shard_map/mlp_grads_all/ppermute | solution.py:34
  415.0 12.3 %collective-permute-start.51 = (bf16[128,768]{1,0:T(8,128)(2,1)S(1)}, bf16[128,768]{1,0:T(8,128)(2,1)S(1)}, u32[]{:S(2)}, u32[]{:S(2)}) collective-permute-start(bf16[128,768]{1,0:T(8,128)(2,1)S(1)} %fusion.62), channel_id=1, source_target_pairs={{0,16},{1,17},{2,18},{3,19},{4,20},{5,21},{6,22},{7,23},{8,24},{9,... | collective-permute-start | bytes 589832 | tf_op jit(solution)/shard_map/last_grads/ppermute | solution.py:34
  427.7 5.2 collective-permute-start.54
  432.9 6.8 %collective-permute-start.56 = (bf16[2,96,768]{2,1,0:T(8,128)(2,1)S(1)}, bf16[2,96,768]{2,1,0:T(8,128)(2,1)S(1)}, u32[]{:S(2)}, u32[]{:S(2)}) collective-permute-start(bf16[2,96,768]{2,1,0:T(8,128)(2,1)S(1)} %pad_maximum_fusion.23), channel_id=1, source_target_pairs={{0,4},{1,3},{2,6},{3,1},{4,0},{5,7},{6,2},{7,5},{8,12},{9,11},{10,... | collective-permute-start | bytes 884744 | tf_op jit(solution)/shard_map/attn_grads_all/ppermute | solution.py:34
  439.8 5.8 %collective-permute-start.58 = (bf16[4,96,768]{2,1,0:T(8,128)(2,1)S(1)}, bf16[4,96,768]{2,1,0:T(8,128)(2,1)S(1)}, u32[]{:S(2)}, u32[]{:S(2)}) collective-permute-start(bf16[4,96,768]{2,1,0:T(8,128)(2,1)S(1)} %pad_maximum_fusion.17), channel_id=1, source_target_pairs={{0,1},{1,0},{2,3},{3,2},{4,5},{5,4},{6,7},{7,6},{8,9},{9,8},{10,11... | collective-permute-start | bytes 1769480 | tf_op jit(solution)/shard_map/attn_grads_all/ppermute | solution.py:34
  445.6 5.4 %collective-permute-start.59 = (f32[16,768]{1,0:T(8,128)S(1)}, f32[16,768]{1,0:T(8,128)S(1)}, u32[]{:S(2)}, u32[]{:S(2)}) collective-permute-start(f32[16,768]{1,0:T(8,128)S(1)} %add.650), channel_id=1, source_target_pairs={{0,8},{1,9},{2,10},{3,11},{4,12},{5,13},{6,14},{7,15},{8,0},{9,1},... | collective-permute-start | bytes 147464 | tf_op jit(solution)/shard_map/small_sums/ppermute | solution.py:34
  449.2 36.5 %collective-permute-start.61 = (bf16[16,96,768]{2,1,0:T(8,128)(2,1)}, bf16[16,96,768]{2,1,0:T(8,128)(2,1)}, u32[]{:S(2)}, u32[]{:S(2)}) collective-permute-start(bf16[16,96,768]{2,1,0:T(8,128)(2,1)} %pad_maximum_fusion.3), channel_id=1, source_target_pairs={{0,4},{1,3},{2,6},{3,1},{4,0},{5,7},{6,2},{7,5},{8,12},{9,11},{10,... | collective-permute-start | bytes 7077896 | tf_op jit(solution)/shard_map/mlp_grads_all/ppermute | solution.py:34
  451.0 5.1 collective-permute-start.60
  459.6 26.2 %collective-permute-start.62 = (bf16[2,2,96,768]{3,2,1,0:T(8,128)(2,1)}, bf16[2,2,96,768]{3,2,1,0:T(8,128)(2,1)S(1)}, u32[]{:S(2)}, u32[]{:S(2)}) collective-permute-start(bf16[2,2,96,768]{3,2,1,0:T(8,128)(2,1)} %get-tuple-element.205), channel_id=1, source_target_pairs={{0,16},{1,17},{2,18},{3,19},{4,20},{5,21},{6,22},{7,23},{8,24},{9,... | collective-permute-start | bytes 1769480 | tf_op jit(solution)/shard_map/head_grads/ppermute | solution.py:34
  486.1 28.5 %collective-permute-start.63 = (bf16[2,2,96,768]{3,2,1,0:T(8,128)(2,1)S(1)}, bf16[2,2,96,768]{3,2,1,0:T(8,128)(2,1)S(1)}, u32[]{:S(2)}, u32[]{:S(2)}) collective-permute-start(bf16[2,2,96,768]{3,2,1,0:T(8,128)(2,1)S(1)} %get-tuple-element.300), channel_id=1, source_target_pairs={{0,4},{1,5},{2,6},{3,7},{4,0},{5,1},{6,2},{7,3},{8,12},{9,13},{10,... | collective-permute-start | bytes 1769480 | tf_op jit(solution)/shard_map/head_grads/ppermute | solution.py:34
  514.8 6.8 %collective-permute-start.64 = (f32[96,768]{1,0:T(8,128)S(1)}, f32[96,768]{1,0:T(8,128)S(1)}, u32[]{:S(2)}, u32[]{:S(2)}) collective-permute-start(f32[96,768]{1,0:T(8,128)S(1)} %slice.423), channel_id=1, source_target_pairs={{0,1},{1,0},{2,3},{3,2},{4,5},{5,4},{6,7},{7,6},{8,9},{9,8},{10,11... | collective-permute-start | bytes 884744 | tf_op jit(solution)/shard_map/small/ppermute | solution.py:34
  (132 other events, 995.6 us)

commit v4 on v3

--- a/solution.py
+++ b/solution.py
@@ -267,6 +267,7 @@
 
 IN_VMEM = pl.BlockSpec(memory_space=pltpu.VMEM)
 IN_SMEM = pl.BlockSpec(memory_space=pltpu.SMEM)
+ANYWHERE = pl.BlockSpec(memory_space=pl.ANY)
 
 
 def hidden_forward_kernel(rows, normed_ref, middle_ref, bias_ref, *refs):
@@ -315,35 +316,77 @@
 
 def hidden_back_kernel(core_ref, d_out_ref, normed_ref, *refs):
     active_refs, slope_refs, part_refs = refs[:2], refs[2:4], refs[4:8]
-    d_hidden_ref, bias_ref, away_ref = refs[8:]
+    d_hidden_ref, bias_ref, away_ref = refs[8:11]
+    weights, actives, slopes, d_hiddens, aways, in_sems, out_sems = refs[11:]
     width = d_out_ref.shape[1]
     half = width // 2
+    arriving = []
+    for index, part_ref in enumerate(part_refs):
+        sources = (
+            part_ref.at[:, pl.ds(width, width)],
+            slope_refs[index % 2].at[index // 2],
+            active_refs[index % 2].at[index // 2],
+        )
+        copies = [
+            pltpu.make_async_copy(source, target.at[index], in_sems.at[which, index])
+            for which, (source, target) in enumerate(zip(sources, (weights, slopes, actives)))
+        ]
+        for copy in copies:
+            copy.start()
+        arriving.append(copies)
     first = core_ref[0, 0] == 0
     right = jnp.where(first, d_out_ref[...], normed_ref[...])
     slots = ((7, 3), (5, 1), (6, 4), (2, 0))
-    for index, part_ref in enumerate(part_refs):
-        d_active = contract_cols(d_out_ref[...], part_ref[:, width:])
-        slope = slope_refs[index % 2][index // 2]
-        d_hidden = (slope * d_active).astype(jnp.bfloat16)
-        d_hidden_ref[index] = d_hidden
+    leaving = []
+    for index in range(4):
+        for copy in arriving[index]:
+            copy.wait()
+        d_active = contract_cols(d_out_ref[...], weights[index])
+        d_hidden = (slopes[index] * d_active).astype(jnp.bfloat16)
+        d_hiddens[index] = d_hidden
         bias_ref[pl.ds(index, 1)] = jnp.sum(d_hidden.astype(jnp.float32), axis=0, keepdims=True)
-        left = jnp.where(first, active_refs[index % 2][index // 2], d_hidden)
+        left = jnp.where(first, actives[index], d_hidden)
         grad = contract_rows(left, right).astype(jnp.bfloat16)
+        aways[index] = grad
+        copies = [
+            pltpu.make_async_copy(d_hiddens.at[index], d_hidden_ref.at[index], out_sems.at[2, index])
+        ]
         for side, slot in enumerate(slots[index]):
-            away_ref[pl.ds(slot * half, half)] = grad[side * half : (side + 1) * half]
+            copies.append(
+                pltpu.make_async_copy(
+                    aways.at[index, pl.ds(side * half, half)],
+                    away_ref.at[pl.ds(slot * half, half)],
+                    out_sems.at[side, index],
+                )
+            )
+        for copy in copies:
+            copy.start()
+        leaving += copies
+    for copy in leaving:
+        copy.wait()
 
 
 def hidden_back(core, d_out, normed, active, slope, parts):
     token_count, width = d_out.shape
+    kept = (4, token_count, width)
     return pl.pallas_call(
         hidden_back_kernel,
         out_shape=(
-            jax.ShapeDtypeStruct((4, token_count, width), jnp.bfloat16),
+            jax.ShapeDtypeStruct(kept, jnp.bfloat16),
             jax.ShapeDtypeStruct((4, width), jnp.float32),
             jax.ShapeDtypeStruct((4 * width, width), jnp.bfloat16),
         ),
-        in_specs=[IN_SMEM] + [IN_VMEM] * 10,
-        out_specs=(IN_VMEM,) * 3,
+        in_specs=[IN_SMEM, IN_VMEM, IN_VMEM] + [ANYWHERE] * 8,
+        out_specs=(ANYWHERE, IN_VMEM, ANYWHERE),
+        scratch_shapes=[
+            pltpu.VMEM((4, width, width), jnp.bfloat16),
+            pltpu.VMEM(kept, jnp.bfloat16),
+            pltpu.VMEM(kept, jnp.float32),
+            pltpu.VMEM(kept, jnp.bfloat16),
+            pltpu.VMEM((4, width, width), jnp.bfloat16),
+            pltpu.SemaphoreType.DMA((3, 4)),
+            pltpu.SemaphoreType.DMA((3, 4)),
+        ],
         compiler_params=pltpu.CompilerParams(vmem_limit_bytes=48 * 1024 * 1024),
         cost_estimate=pl.CostEstimate(
             flops=16 * token_count * width * width,
@@ -403,35 +446,43 @@
 
 def orthogonal_kernel(part_count, chunk, full_steps, row_count, factor_ref, *refs):
     moment_refs, grad_refs = refs[:part_count], refs[part_count : 2 * part_count]
-    out_ref, rows_ref, gram_ref, low_ref, change_ref = refs[2 * part_count :]
+    out_ref, rows_ref, gram_ref, low_ref, change_ref, moments, grads, in_sems = refs[
+        2 * part_count :
+    ]
     part_rows, width = moment_refs[0].shape
     factor = factor_ref[0, 0]
     chunks = part_rows // chunk
     bf = jnp.bfloat16
 
-    gram_ref[...] = jnp.zeros_like(gram_ref)
+    arriving = []
     for index in range(part_count):
-
-        def start(step, carry, index=index):
-            here = pl.ds(pl.multiple_of(step * chunk, chunk), chunk)
-            rows = (
-                momentum_keep * moment_refs[index][here].astype(jnp.float32)
-                + factor * grad_refs[index][here].astype(jnp.float32)
-            ).astype(bf)
-            if full_steps:
-                rows_ref[
-                    pl.ds(pl.multiple_of(index * part_rows + step * chunk, chunk), chunk)
-                ] = rows
-            elif index == 0:
-
-                @pl.when(step == 0)
-                def _():
-                    out_ref[...] = rows[:row_count].astype(jnp.float32)
-
+        for step in range(chunks):
+            here = pl.ds(step * chunk, chunk)
+            spot = index * chunks + step
+            copies = [
+                pltpu.make_async_copy(source.at[here], target.at[spot], in_sems.at[which, spot])
+                for which, (source, target) in enumerate(
+                    ((moment_refs[index], moments), (grad_refs[index], grads))
+                )
+            ]
+            for copy in copies:
+                copy.start()
+            arriving.append(copies)
+    for spot, copies in enumerate(arriving):
+        for copy in copies:
+            copy.wait()
+        rows = (
+            momentum_keep * moments[spot].astype(jnp.float32)
+            + factor * grads[spot].astype(jnp.float32)
+        ).astype(bf)
+        if full_steps:
+            rows_ref[pl.ds(spot * chunk, chunk)] = rows
+        elif spot == 0:
+            out_ref[...] = rows[:row_count].astype(jnp.float32)
+        if spot == 0:
+            gram_ref[...] = contract_rows(rows, rows)
+        else:
             gram_ref[...] += contract_rows(rows, rows)
-            return carry
-
-        lax.fori_loop(0, chunks, start, 0)
     gram = gram_ref[...]
     diagonal = lax.broadcasted_iota(jnp.int32, gram.shape, 0) == lax.broadcasted_iota(
         jnp.int32, gram.shape, 1
@@ -483,13 +534,16 @@
         body,
         out_shape=jax.ShapeDtypeStruct((row_count, width), jnp.float32),
         in_specs=[pl.BlockSpec(memory_space=pltpu.SMEM)]
-        + [pl.BlockSpec(memory_space=pltpu.VMEM)] * (2 * count),
+        + [pl.BlockSpec(memory_space=pl.ANY)] * (2 * count),
         out_specs=pl.BlockSpec(memory_space=pltpu.VMEM),
         scratch_shapes=[
             pltpu.VMEM((count * part_rows if full_steps else 16, width), jnp.bfloat16),
             pltpu.VMEM((width, width), jnp.float32),
             pltpu.VMEM((width, width), jnp.bfloat16),
             pltpu.VMEM((width, width), jnp.bfloat16),
+            pltpu.VMEM((count * part_rows // chunk, chunk, width), jnp.bfloat16),
+            pltpu.VMEM((count * part_rows // chunk, chunk, width), jnp.bfloat16),
+            pltpu.SemaphoreType.DMA((2, count * part_rows // chunk)),
         ],
         compiler_params=pltpu.CompilerParams(vmem_limit_bytes=48 * 1024 * 1024),
         cost_estimate=pl.CostEstimate(flops=flops, bytes_accessed=4 * count * part_rows * width, transcendentals=0),
@@ -750,7 +804,7 @@
     head_lane = lane(
         transposed(
             head_grad.astype(jnp.bfloat16).reshape(owners, shard_rows, chunk),
-            owner_bits[1:] + owner_bits[:1],
+            owner_bits[1:-1] + owner_bits[:1] + owner_bits[-1:],
         ),
         "head_grads",
     )
@@ -760,9 +814,11 @@
     (away, d_hidden) = sync((away, d_hidden), mom_lane, attn_mom_lane)
     arrived = exchange(away, pair, "mlp_grads")
     operands = (core, d_out, normed_two, active, d_hidden)
-    leave = kept_grads(((1, None, (2, 0)), (3, 1, 1), (2, 1, 3)), *operands)
+    first_plan = ((1, None, (2, 0)), (3, 1, 1), (2, 1, 3))
+    second_plan = ((0, None, (2, 0)), (3, 0, 1), (2, 0, 3))
+    leave = kept_grads(first_plan, *operands)
     leave, arrived, d_hidden = sync(
-        (leave, arrived, d_hidden), mom_lane, attn_mom_lane, hold=(mom_lane,)
+        (leave, arrived, d_hidden), attn_mom_lane
     )
     operands = (core, d_out, normed_two, active, d_hidden)
     half = 2 * model_width
@@ -783,9 +839,7 @@
     own = []
     mlp_lane = lane(summing(leave, lambda: own[0], arrived[half:]), "mlp_grads")
     sync((), mlp_lane)
-    d_normed_two, grads = kept_grads(
-        ((0, None, (2, 0)), (3, 0, 1), (2, 0, 3)), *operands, mlp_parts
-    )
+    d_normed_two, grads = kept_grads(second_plan, *operands, mlp_parts)
     own.append(grads)
     (d_normed_two,) = sync((d_normed_two,), head_lane)
 
@@ -802,8 +856,9 @@
     d_queries, d_keys, d_values, own[0] = sync(
         (d_queries, d_keys, d_values, own[0]),
         mlp_lane,
+        mom_lane,
         head_lane,
-        hold=(head_lane,),
+        hold=(mom_lane, head_lane),
     )
     attn_grad = jnp.concatenate(
         [
@@ -846,7 +901,7 @@
         + contract_cols(d_values, attn_b[2 * model_width : 3 * model_width])
     )
     sync((), attn_lane)
-    (d_normed,) = sync((d_normed,), mlp_lane, attn_lane)
+    (d_normed,) = sync((d_normed,), mlp_lane, attn_lane, head_lane)
     d_emb_norm, g_gain_one, g_shift_one = jax.vjp(layer_norm, embedded, vec_w[4], vec_w[5])[1](
         d_normed
     )
@@ -854,7 +909,7 @@
     embed_grad = contract_rows(patch_wide, d_embed_low)
     embed_lane = lane(quartered(embed_grad, embed_rows), "embed_grads")
     sync((), embed_lane)
-    sync((), embed_lane, mlp_lane)
+    sync((), embed_lane, mlp_lane, head_lane, hold=(head_lane,))
     finish(attn_lane, embed_lane)
     sum_lane = lane(last_sums([attn_lane.result, embed_lane.result]), "last_grads")
     sync((), sum_lane)
@@ -866,7 +921,7 @@
     sync((), sum_lane, all_lane)
     sync((), sum_lane, all_lane, mom_lane)
     while sum_lane.result is None:
-        sync((), sum_lane, all_lane)
+        sync((), sum_lane, all_lane, hold=(all_lane,))
     attn_sum, embed_sum = sum_lane.result[:attn_rows], sum_lane.result[attn_rows:]
     g_query_bias = jnp.sum(d_queries.astype(jnp.float32), axis=0)
     g_value_bias = jnp.sum(d_values.astype(jnp.float32), axis=0)
@@ -899,7 +954,7 @@
     small_sums = jnp.concatenate([vec_grad, (local_squares + head_squares)[None]], axis=0)
 
     def total(value):
-        for bit in range(top):
+        for bit in [1, 2, 0] + list(range(3, top)):
             value = value + (yield value, plain(bit))
         return value
 
@@ -909,6 +964,8 @@
         "attn_grads_all",
     )
     sync((), small_lane, block_lane)
+    sync((), small_lane, block_lane)
+    sync((), small_lane, block_lane, all_lane)
     small_sums, attn_grads = finish(small_lane, block_lane)
     attn_moms = jnp.concatenate(finish(attn_mom_lane)[0], axis=0).reshape(-1, model_width)
     attn_grads = jnp.concatenate(attn_grads, axis=0).reshape(-1, model_width)
@@ -924,7 +981,7 @@
 
     (factor,) = sync((factor,), head_lane)
     attn_dir = orthogonal_rows([attn_moms], [attn_grads], factor, attn_rows, 768, 4)
-    (attn_dir,) = sync((attn_dir,), all_lane, mom_lane, head_lane)
+    (attn_dir,) = sync((attn_dir,), all_lane, mom_lane)
     mlp_grads, mlp_moms = finish(all_lane, mom_lane)
     mlp_result = orthogonal_rows(
         [part.reshape(-1, model_width) for part in mlp_moms],

time: 533 us -> 521 us (0.977)
  waiting for transfers between devices: 206 us -> 199 us
    ppermute x66, waiting for transfers between devices: 206 us -> 199 us  [swap(): lax.ppermute(value, AXES, [(i, i ^ masks[i & 1]) for i in range(count)])]
    unnamed x233 -> x231, local copies, waits for them, and re-layouts: 25.2 us -> 28 us
  transfers between devices with their start and end apart: 66 -> 66, of which waited for: 40 -> 37; matrix products, arithmetic and copies ran while one was open for 16% -> 18% of each run, Pallas kernels for 21% -> 21%
where the time goes in v4:
time: 521 us; the launch traced here: 513 us
  waiting for transfers between devices  199 us (38%)
  Pallas kernels  107 us (21%)
  other arithmetic  81.1 us (16%)
  starting transfers between devices  54.7 us (10%)
  local copies, waits for them, and re-layouts  46.7 us (9%)
  matrix products  18.7 us (4%)
  between operations  6.57 us (1%)
    ppermute x66, waiting for transfers between devices, swap(): lax.ppermute(value, AXES, [(i, i ^ masks[i & 1]) for i in range(count)])  199 us
    ppermute x66, starting transfers between devices, swap(): lax.ppermute(value, AXES, [(i, i ^ masks[i & 1]) for i in range(count)])  54.7 us
    pallas_call x2, Pallas kernels, orthogonal_rows(): pl.pallas_call(body, out_shape=jax.ShapeDtypeStruct((row_count, width), j...  39.2 us
    unnamed x231, local copies, waits for them, and re-layouts  28 us
    pallas_call x2, Pallas kernels, hidden_forward(): pl.pallas_call(functools.partial(hidden_forward_kernel, rows), out_shape=...  17.4 us
    pallas_call x2, Pallas kernels, kept_grads(): pl.pallas_call(functools.partial(kept_grads_kernel, plan), out_shape=(bac...  15.2 us
    concatenate x11, other arithmetic, collecting(): value = jnp.concatenate([value, (yield (value, stage))], axis=0)  15 us
    pallas_call x1, Pallas kernels, mixing_grads(): pl.pallas_call(functools.partial(mixing_grads_kernel, width, rows), grid=...  14.4 us
  transfers between devices with their start and end apart: 66, of which 37 were waited for; matrix products, arithmetic and copies ran while one was open for 18% of the time, Pallas kernels for 21%

profile of v4, /device:TPU:0, one launch (start us, length us, event | category | flops | bytes accessed | tf_op | source)
XLA Modules:
  0.0 513.2 jit_solution(7256902408575406360)
XLA Ops:
  2.6 4.1 collective-permute-start
  8.7 7.2 %collective-permute-done = bf16[128,768]{1,0:T(8,128)(2,1)S(1)} collective-permute-done((bf16[128,768]{1,0:T(8,128)(2,1)S(1)}, bf16[128,768]{1,0:T(8,128)(2,1)S(1)}, u32[]{:S(2)}, u32[]{:S(2)}) %collective-permute-start) | collective-permute-done | bytes 196640 | tf_op jit(solution)/shard_map/attn_weights/ppermute | solution.py:34
  16.9 9.5 %collective-permute-done.1 = bf16[2,128,768]{2,1,0:T(8,128)(2,1)S(1)} collective-permute-done((bf16[2,128,768]{2,1,0:T(8,128)(2,1)S(1)}, bf16[2,128,768]{2,1,0:T(8,128)(2,1)S(1)}, u32[]{:S(2)}, u32[]{:S(2)}) %collective-permute-start.1) | collective-permute-done | bytes 393248 | tf_op jit(solution)/shard_map/attn_weights/ppermute | solution.py:34
  27.7 3.3 collective-permute-start.3
  31.1 12.7 %collective-permute-done.3 = bf16[1,96,1536]{2,1,0:T(8,128)(2,1)S(1)} collective-permute-done((bf16[1,96,1536]{2,1,0:T(8,128)(2,1)S(1)}, bf16[1,96,1536]{2,1,0:T(8,128)(2,1)S(1)}, u32[]{:S(2)}, u32[]{:S(2)}) %collective-permute-start.3) | collective-permute-done | bytes 294944 | tf_op jit(solution)/shard_map/mlp_weights/ppermute | solution.py:34
  55.4 10.9 %collective-permute-done.5 = bf16[2,96,1536]{2,1,0:T(8,128)(2,1)} collective-permute-done((bf16[2,96,1536]{2,1,0:T(8,128)(2,1)}, bf16[2,96,1536]{2,1,0:T(8,128)(2,1)}, u32[]{:S(2)}, u32[]{:S(2)}) %collective-permute-start.5) | collective-permute-done | bytes 589856 | tf_op jit(solution)/shard_map/mlp_weights/ppermute | solution.py:34
  76.0 11.5 %collective-permute-done.8 = bf16[2,2,96,768]{3,2,1,0:T(8,128)(2,1)S(1)} collective-permute-done((bf16[2,2,96,768]{3,2,1,0:T(8,128)(2,1)S(1)}, bf16[2,2,96,768]{3,2,1,0:T(8,128)(2,1)S(1)}, u32[]{:S(2)}, u32[]{:S(2)}) %collective-permute-start.8) | collective-permute-done | bytes 589856 | tf_op jit(solution)/shard_map/head/ppermute | solution.py:34
  90.8 2.5 collective-permute-start.11
  97.5 10.4 %mixing.1 = (bf16[512,768]{1,0:T(8,128)(2,1)S(1)}, f32[16,512]{1,0:T(8,128)S(1)}) custom-call(s32[512,1]{1,0:T(8,128)S(1)} %copy.160.ids_down_ref, s32[1,512]{1,0:T(1,128)S(1)} %constant_dynamic-slice_fusion.13.ids_ref, bf16[512,768]{1,0:T(8,128)(2,1)S(1)} %add_convert_fusion.4.q_ref, bf16[512,768]{1,0:T(8,128)(2,1)S(1)} %convolution_convert_fusion.1.k_ref, ...), custom_call_target="tpu_custom_call" | custom-call | flops 805306368 | bytes 3145728 | tf_op jit(solution)/shard_map/mixing/pallas_call | solution.py:195
  110.8 8.9 %hidden_forward.2 = (f32[512,768]{1,0:T(8,128)S(1)}, bf16[2,512,768]{2,1,0:T(8,128)(2,1)S(1)}, f32[2,512,768]{2,1,0:T(8,128)}) custom-call(bf16[512,768]{1,0:T(8,128)(2,1)S(1)} %get-tuple-element.300.normed_ref, f32[512,768]{1,0:T(8,128)S(1)} %get-tuple-element.299.middle_ref, f32[2,768]{1,0:T(2,128)S(1)} %slice.365.bias_ref, bf16[768,1536]{1,0:T(8,128)(2,1)} %bitcast.342, ...), custom_call_target="tpu_custom_call" | custom-call | flops 2415919104 | bytes 11010048 | tf_op jit(solution)/shard_map/hidden_forward/pallas_call | solution.py:298
  135.1 8.5 %hidden_forward.3 = (f32[512,768]{1,0:T(8,128)S(1)}, bf16[2,512,768]{2,1,0:T(8,128)(2,1)S(1)}, f32[2,512,768]{2,1,0:T(8,128)}) custom-call(bf16[512,768]{1,0:T(8,128)(2,1)S(1)} %copy-done.7, f32[512,768]{1,0:T(8,128)S(1)} %copy-done.15, f32[2,768]{1,0:T(2,128)S(1)} %slice.366.bias_ref, bf16[768,1536]{1,0:T(8,128)(2,1)} %bitcast.62.refs_0_.refs_5_.refs_1_, ...), custom_call_target="tpu_custom_call" | custom-call | flops 2415919104 | bytes 11010048 | tf_op jit(solution)/shard_map/hidden_forward/pallas_call | solution.py:298
  144.8 2.2 collective-permute-done.15
  149.6 4.9 collective-permute-done.17
  154.7 4.1 collective-permute-done.18
  159.9 3.7 collective-permute-done.19
  164.9 4.9 collective-permute-done.20
  178.1 2.6 collective-permute-done.23
  181.8 2.6 collective-permute-done.24
  184.6 3.6 collective-permute-done.25
  190.0 2.8 collective-permute-done.26
  193.5 2.7 divide_convert_fusion
  205.1 6.2 %collective-permute-done.28 = bf16[2,2,2,16,768]{4,3,0,1,2:T(8,128)(2,1)} collective-permute-done((bf16[2,2,2,16,768]{4,3,0,1,2:T(8,128)(2,1)}, bf16[2,2,2,16,768]{4,3,0,1,2:T(8,128)(2,1)}, u32[]{:S(2)}, u32[]{:S(2)}) %collective-permute-start.28) | collective-permute-done | bytes 196640 | tf_op jit(solution)/shard_map/d_pooled/ppermute | solution.py:34
  213.5 3.6 collective-permute-done.29
  218.3 3.0 collective-permute-done.30
  224.0 2.1 collective-permute-done.31
  230.6 10.3 %hidden_back.1 = (bf16[4,512,768]{2,1,0:T(8,128)(2,1)}, f32[4,768]{1,0:T(4,128)S(1)}, bf16[3072,768]{1,0:T(8,128)(2,1)}) custom-call(s32[1,1]{1,0:T(1,128)} %bitcast.108.core_ref, bf16[512,768]{1,0:T(8,128)(2,1)S(1)} %get-tuple-element.150.d_out_ref, bf16[512,768]{1,0:T(8,128)(2,1)S(1)} %copy-done.8, ...), custom_call_target="tpu_custom_call" | custom-call | flops 4831838208 | bytes 22020096 | tf_op jit(solution)/shard_map/hidden_back/pallas_call | solution.py:372
  244.9 3.0 multiply_reduce_fusion
  249.0 2.4 pad_maximum_fusion.6
  252.5 5.5 %kept_grads.2 = f32[1536,768]{1,0:T(8,128)} custom-call(s32[1,1]{1,0:T(1,128)} %bitcast.108.core_ref, bf16[512,768]{1,0:T(8,128)(2,1)S(1)} %copy-done.5, bf16[512,768]{1,0:T(8,128)(2,1)S(1)} %copy-done.9, bf16[2,512,768]{2,1,0:T(8,128)(2,1)S(1)} %get-tuple-element.151.refs_0_.even_ref, bf16[2,512,768]{2,1,0:T(8,128)(2,1)S(1)} %copy-done.3, ...), custom_call_target="tpu_custom_call" | custom-call | flops 1207959552 | bytes 12582912 | tf_op jit(solution)/shard_map/kept_grads/pallas_call | solution.py:432
  258.0 5.3 %add_convert_fusion = bf16[1536,768]{1,0:T(8,128)(2,1)} fusion(f32[1536,768]{1,0:T(8,128)} %kept_grads.2, bf16[3072,768]{1,0:T(8,128)(2,1)} %collective-permute-done.34), kind=kLoop, calls=%fused_computation.6 | loop fusion | flops 3538944 | bytes 9437184 | tf_op jit(solution)/shard_map/convert_element_type | solution.py:825
  264.5 9.7 %kept_grads.3 = (f32[512,768]{1,0:T(8,128)S(1)}, f32[1536,768]{1,0:T(8,128)}) custom-call(s32[1,1]{1,0:T(1,128)} %bitcast.108.core_ref, bf16[512,768]{1,0:T(8,128)(2,1)S(1)} %copy-done.5, bf16[512,768]{1,0:T(8,128)(2,1)S(1)} %copy-done.9, bf16[2,512,768]{2,1,0:T(8,128)(2,1)S(1)} %get-tuple-element.151.refs_0_.even_ref, bf16[2,512,768]{2,1,0:T(8,128)(2,1)} %copy-done.2, ...), custom_call_target="tpu_custom_call" | custom-call | flops 1207959552 | bytes 12582912 | tf_op jit(solution)/shard_map/kept_grads/pallas_call | solution.py:432
  279.3 14.4 %mixing_grads.1 = (bf16[512,768]{1,0:T(8,128)(2,1)S(1)}, bf16[512,768]{1,0:T(8,128)(2,1)S(1)}, bf16[512,768]{1,0:T(8,128)(2,1)S(1)}) custom-call(s32[512,1]{1,0:T(8,128)S(1)} %copy.160.ids_down_ref, s32[1,512]{1,0:T(1,128)S(1)} %constant_dynamic-slice_fusion.13.ids_ref, f32[16,512]{1,0:T(8,128)S(1)} %get-tuple-element.146.summary_ref, ...), custom_call_target="tpu_custom_call" | custom-call | flops 2013265920 | bytes 5505024 | tf_op jit(solution)/shard_map/mixing_grads/pallas_call | solution.py:252
  304.4 4.4 convert_add_fusion
  313.5 11.7 %collective-permute-done.39 = bf16[768,768]{1,0:T(8,128)(2,1)S(1)} collective-permute-done((bf16[768,768]{1,0:T(8,128)(2,1)S(1)}, bf16[768,768]{1,0:T(8,128)(2,1)S(1)}, u32[]{:S(2)}, u32[]{:S(2)}) %collective-permute-start.39) | collective-permute-done | bytes 1179680 | tf_op jit(solution)/shard_map/mlp_grads/ppermute | solution.py:34
  331.6 2.1 bitcast_add_fusion
  335.2 10.0 %collective-permute-done.43 = bf16[2,2,96,768]{3,2,1,0:T(8,128)(2,1)S(1)} collective-permute-done((bf16[2,2,96,768]{3,2,1,0:T(8,128)(2,1)S(1)}, bf16[2,2,96,768]{3,2,1,0:T(8,128)(2,1)S(1)}, u32[]{:S(2)}, u32[]{:S(2)}) %collective-permute-start.43) | collective-permute-done | bytes 589856 | tf_op jit(solution)/shard_map/mlp_grads/ppermute | solution.py:34
  350.8 11.7 %collective-permute-done.47 = bf16[2,1,96,768]{3,2,1,0:T(8,128)(2,1)S(1)} collective-permute-done((bf16[2,1,96,768]{3,2,1,0:T(8,128)(2,1)S(1)}, bf16[2,1,96,768]{3,2,1,0:T(8,128)(2,1)S(1)}, u32[]{:S(2)}, u32[]{:S(2)}) %collective-permute-start.47) | collective-permute-done | bytes 294944 | tf_op jit(solution)/shard_map/mlp_grads/ppermute | solution.py:34
  366.2 14.8 %collective-permute-done.48 = bf16[2,96,768]{2,1,0:T(8,128)(2,1)S(1)} collective-permute-done((bf16[2,96,768]{2,1,0:T(8,128)(2,1)S(1)}, bf16[2,96,768]{2,1,0:T(8,128)(2,1)S(1)}, u32[]{:S(2)}, u32[]{:S(2)}) %collective-permute-start.48) | collective-permute-done | bytes 294944 | tf_op jit(solution)/shard_map/mlp_grads_all/ppermute | solution.py:34
  381.0 4.7 collective-permute-done.46
  390.2 18.7 %collective-permute-done.49 = bf16[2,128,768]{2,1,0:T(8,128)(2,1)} collective-permute-done((bf16[2,128,768]{2,1,0:T(8,128)(2,1)}, bf16[2,128,768]{2,1,0:T(8,128)(2,1)}, u32[]{:S(2)}, u32[]{:S(2)}) %collective-permute-start.49) | collective-permute-done | bytes 393248 | tf_op jit(solution)/shard_map/last_grads/ppermute | solution.py:34
  408.8 2.4 pad_maximum_fusion.8
  417.3 10.6 %collective-permute-done.52 = bf16[128,768]{1,0:T(8,128)(2,1)S(1)} collective-permute-done((bf16[128,768]{1,0:T(8,128)(2,1)S(1)}, bf16[128,768]{1,0:T(8,128)(2,1)S(1)}, u32[]{:S(2)}, u32[]{:S(2)}) %collective-permute-start.52) | collective-permute-done | bytes 196640 | tf_op jit(solution)/shard_map/last_grads/ppermute | solution.py:34
  430.3 3.7 collective-permute-done.54
  436.1 3.1 pad_maximum_fusion.3
  449.3 4.4 collective-permute-done.61
  462.9 15.5 %orthogonal_rows.2 = f32[96,768]{1,0:T(8,128)S(1)} custom-call(f32[1,1]{1,0:T(1,128)} %bitcast.143.factor_ref, bf16[768,768]{1,0:T(8,128)(2,1)S(1)} %bitcast.335, bf16[768,768]{1,0:T(8,128)(2,1)S(1)} %bitcast.336), custom_call_target="tpu_custom_call" | custom-call | flops 16307453952 | bytes 2359296 | tf_op jit(solution)/shard_map/orthogonal_rows/pallas_call | solution.py:533
  478.5 23.8 %orthogonal_rows.3 = f32[192,768]{1,0:T(8,128)S(1)} custom-call(f32[1,1]{1,0:T(1,128)} %bitcast.143.factor_ref, bf16[1536,768]{1,0:T(8,128)(2,1)} %bitcast.146.refs_0_, bf16[1536,768]{1,0:T(8,128)(2,1)} %bitcast.147.refs_1_, bf16[1536,768]{1,0:T(8,128)(2,1)} %bitcast.148.refs_2_, bf16[1536,768]{1,0:T(8,128)(2,1)} %bitcast.149.refs_3_), custom_call_target="tpu_custom_call" | custom-call | flops 11777605632 | bytes 9437184 | tf_op jit(solution)/shard_map/orthogonal_rows/pallas_call | solution.py:533
  504.5 4.8 fusion.115
  (579 shorter events, 171.3 us)
Async XLA Ops:
  2.6 13.2 %collective-permute-start = (bf16[128,768]{1,0:T(8,128)(2,1)S(1)}, bf16[128,768]{1,0:T(8,128)(2,1)S(1)}, u32[]{:S(2)}, u32[]{:S(2)}) collective-permute-start(bf16[128,768]{1,0:T(8,128)(2,1)S(1)} %pad_maximum_fusion.24), channel_id=1, source_target_pairs={{0,16},{1,17},{2,18},{3,19},{4,20},{5,21},{6,22},{7,23},{8,24},{9,... | collective-permute-start | bytes 589832 | tf_op jit(solution)/shard_map/attn_weights/ppermute | solution.py:34
  15.9 10.4 %collective-permute-start.1 = (bf16[2,128,768]{2,1,0:T(8,128)(2,1)S(1)}, bf16[2,128,768]{2,1,0:T(8,128)(2,1)S(1)}, u32[]{:S(2)}, u32[]{:S(2)}) collective-permute-start(bf16[2,128,768]{2,1,0:T(8,128)(2,1)S(1)} %maximum_select_fusion.11), channel_id=1, source_target_pairs={{0,8},{1,9},{2,10},{3,11},{4,12},{5,13},{6,14},{7,15},{8,0},{9,1},... | collective-permute-start | bytes 1179656 | tf_op jit(solution)/shard_map/attn_weights/ppermute | solution.py:34
  26.4 17.4 %collective-permute-start.2 = (bf16[4,128,768]{2,1,0:T(8,128)(2,1)S(1)}, bf16[4,128,768]{2,1,0:T(8,128)(2,1)S(1)}, u32[]{:S(2)}, u32[]{:S(2)}) collective-permute-start(bf16[4,128,768]{2,1,0:T(8,128)(2,1)S(1)} %bitcast.345), channel_id=1, source_target_pairs={{0,2},{1,5},{2,0},{3,7},{4,6},{5,1},{6,4},{7,3},{8,10},{9,13},{10,... | collective-permute-start | bytes 2359304 | tf_op jit(solution)/shard_map/attn_weights/ppermute | solution.py:34
  27.7 16.1 %collective-permute-start.3 = (bf16[1,96,1536]{2,1,0:T(8,128)(2,1)S(1)}, bf16[1,96,1536]{2,1,0:T(8,128)(2,1)S(1)}, u32[]{:S(2)}, u32[]{:S(2)}) collective-permute-start(bf16[1,96,1536]{2,1,0:T(8,128)(2,1)S(1)} %convert_bitcast_fusion.1), channel_id=1, source_target_pairs={{0,16},{1,17},{2,18},{3,19},{4,20},{5,21},{6,22},{7,23},{8,24},{9,... | collective-permute-start | bytes 884744 | tf_op jit(solution)/shard_map/mlp_weights/ppermute | solution.py:34
  45.8 20.7 %collective-permute-start.4 = (bf16[2,4,128,768]{3,2,1,0:T(8,128)(2,1)}, bf16[2,4,128,768]{3,2,1,0:T(8,128)(2,1)}, u32[]{:S(2)}, u32[]{:S(2)}) collective-permute-start(bf16[2,4,128,768]{3,2,1,0:T(8,128)(2,1)} %pad_maximum_fusion.4), channel_id=1, source_target_pairs={{0,4},{1,3},{2,6},{3,1},{4,0},{5,7},{6,2},{7,5},{8,12},{9,11},{10,... | collective-permute-start | bytes 4718600 | tf_op jit(solution)/shard_map/attn_weights/ppermute | solution.py:34
  50.4 15.9 %collective-permute-start.5 = (bf16[2,96,1536]{2,1,0:T(8,128)(2,1)}, bf16[2,96,1536]{2,1,0:T(8,128)(2,1)}, u32[]{:S(2)}, u32[]{:S(2)}) collective-permute-start(bf16[2,96,1536]{2,1,0:T(8,128)(2,1)} %pad_maximum_fusion.13), channel_id=1, source_target_pairs={{0,8},{1,9},{2,10},{3,11},{4,12},{5,13},{6,14},{7,15},{8,0},{9,1},... | collective-permute-start | bytes 1769480 | tf_op jit(solution)/shard_map/mlp_weights/ppermute | solution.py:34
  68.3 7.1 %collective-permute-start.6 = (bf16[4,4,128,768]{3,2,1,0:T(8,128)(2,1)S(1)}, bf16[4,4,128,768]{3,2,1,0:T(8,128)(2,1)S(1)}, u32[]{:S(2)}, u32[]{:S(2)}) collective-permute-start(bf16[4,4,128,768]{3,2,1,0:T(8,128)(2,1)S(1)} %pad_maximum_fusion.1), channel_id=1, source_target_pairs={{0,1},{1,0},{2,3},{3,2},{4,5},{5,4},{6,7},{7,6},{8,9},{9,8},{10,11... | collective-permute-start | bytes 9437192 | tf_op jit(solution)/shard_map/attn_weights/ppermute | solution.py:34
  71.5 16.3 %collective-permute-start.7 = (bf16[4,96,1536]{2,1,0:T(8,128)(2,1)S(1)}, bf16[4,96,1536]{2,1,0:T(8,128)(2,1)S(1)}, u32[]{:S(2)}, u32[]{:S(2)}) collective-permute-start(bf16[4,96,1536]{2,1,0:T(8,128)(2,1)S(1)} %pad_maximum_fusion.5), channel_id=1, source_target_pairs={{0,2},{1,5},{2,0},{3,7},{4,6},{5,1},{6,4},{7,3},{8,10},{9,13},{10,... | collective-permute-start | bytes 3538952 | tf_op jit(solution)/shard_map/mlp_weights/ppermute | solution.py:34
  73.1 14.5 %collective-permute-start.8 = (bf16[2,2,96,768]{3,2,1,0:T(8,128)(2,1)S(1)}, bf16[2,2,96,768]{3,2,1,0:T(8,128)(2,1)S(1)}, u32[]{:S(2)}, u32[]{:S(2)}) collective-permute-start(bf16[2,2,96,768]{3,2,1,0:T(8,128)(2,1)S(1)} %get-tuple-element.125), channel_id=1, source_target_pairs={{0,8},{1,9},{2,10},{3,11},{4,12},{5,13},{6,14},{7,15},{8,0},{9,1},... | collective-permute-start | bytes 1769480 | tf_op jit(solution)/shard_map/head/ppermute | solution.py:34
  89.1 18.8 %collective-permute-start.9 = (bf16[8,96,1536]{2,1,0:T(8,128)(2,1)S(1)}, bf16[8,96,1536]{2,1,0:T(8,128)(2,1)S(1)}, u32[]{:S(2)}, u32[]{:S(2)}) collective-permute-start(bf16[8,96,1536]{2,1,0:T(8,128)(2,1)S(1)} %pad_maximum_fusion.2), channel_id=1, source_target_pairs={{0,1},{1,0},{2,3},{3,2},{4,5},{5,4},{6,7},{7,6},{8,9},{9,8},{10,11... | collective-permute-start | bytes 7077896 | tf_op jit(solution)/shard_map/mlp_weights/ppermute | solution.py:34
  89.2 31.7 %collective-permute-start.10 = (bf16[8,96,1536]{2,1,0:T(8,128)(2,1)S(1)}, bf16[8,96,1536]{2,1,0:T(8,128)(2,1)}, u32[]{:S(2)}, u32[]{:S(2)}) collective-permute-start(bf16[8,96,1536]{2,1,0:T(8,128)(2,1)S(1)} %pad_maximum_fusion.2), channel_id=1, source_target_pairs={{0,4},{1,3},{2,6},{3,1},{4,0},{5,7},{6,2},{7,5},{8,12},{9,11},{10,... | collective-permute-start | bytes 7077896 | tf_op jit(solution)/shard_map/mlp_weights/ppermute | solution.py:34
  90.8 30.1 %collective-permute-start.11 = (bf16[2,2,96,768]{3,2,1,0:T(8,128)(2,1)S(1)}, bf16[2,2,96,768]{3,2,1,0:T(8,128)(2,1)S(1)}, u32[]{:S(2)}, u32[]{:S(2)}) collective-permute-start(bf16[2,2,96,768]{3,2,1,0:T(8,128)(2,1)S(1)} %get-tuple-element.312), channel_id=1, source_target_pairs={{0,16},{1,17},{2,18},{3,19},{4,20},{5,21},{6,22},{7,23},{8,24},{9,... | collective-permute-start | bytes 1769480 | tf_op jit(solution)/shard_map/head/ppermute | solution.py:34
  121.7 7.2 %collective-permute-start.12 = (bf16[8,96,1536]{2,1,0:T(8,128)(2,1)}, bf16[8,96,1536]{2,1,0:T(8,128)(2,1)}, u32[]{:S(2)}, u32[]{:S(2)}) collective-permute-start(bf16[8,96,1536]{2,1,0:T(8,128)(2,1)} %collective-permute-done.10), channel_id=1, source_target_pairs={{0,1},{1,0},{2,3},{3,2},{4,5},{5,4},{6,7},{7,6},{8,9},{9,8},{10,11... | collective-permute-start | bytes 7077896 | tf_op jit(solution)/shard_map/mlp_weights/ppermute | solution.py:34
  126.5 18.2 %collective-permute-start.14 = (bf16[2,2,96,768]{3,2,1,0:T(8,128)(2,1)}, bf16[2,2,96,768]{3,2,1,0:T(8,128)(2,1)}, u32[]{:S(2)}, u32[]{:S(2)}) collective-permute-start(bf16[2,2,96,768]{3,2,1,0:T(8,128)(2,1)} %get-tuple-element.310), channel_id=1, source_target_pairs={{0,4},{1,5},{2,6},{3,7},{4,0},{5,1},{6,2},{7,3},{8,12},{9,13},{10,... | collective-permute-start | bytes 1769480 | tf_op jit(solution)/shard_map/head/ppermute | solution.py:34
  130.3 16.7 %collective-permute-start.15 = (bf16[2,96,768]{2,1,0:T(8,128)(2,1)}, bf16[2,96,768]{2,1,0:T(8,128)(2,1)}, u32[]{:S(2)}, u32[]{:S(2)}) collective-permute-start(bf16[2,96,768]{2,1,0:T(8,128)(2,1)} %pad_maximum_fusion.21), channel_id=1, source_target_pairs={{0,16},{1,17},{2,18},{3,19},{4,20},{5,21},{6,22},{7,23},{8,24},{9,... | collective-permute-start | bytes 884744 | tf_op jit(solution)/shard_map/mlp_moments/ppermute | solution.py:34
  131.6 13.1 %collective-permute-start.16 = (bf16[1,96,768]{2,1,0:T(8,128)(2,1)}, bf16[1,96,768]{2,1,0:T(8,128)(2,1)}, u32[]{:S(2)}, u32[]{:S(2)}) collective-permute-start(bf16[1,96,768]{2,1,0:T(8,128)(2,1)} %convert_bitcast_fusion.2), channel_id=1, source_target_pairs={{0,2},{1,5},{2,0},{3,7},{4,6},{5,1},{6,4},{7,3},{8,10},{9,13},{10,... | collective-permute-start | bytes 442376 | tf_op jit(solution)/shard_map/attn_moments/ppermute | solution.py:34
  149.6 5.0 collective-permute-start.17
  163.7 6.1 %collective-permute-start.20 = (bf16[2,2,2,16,896]{4,3,0,1,2:T(8,128)(2,1)S(1)}, bf16[2,2,2,16,896]{4,3,0,1,2:T(8,128)(2,1)S(1)}, u32[]{:S(2)}, u32[]{:S(2)}) collective-permute-start(bf16[2,2,2,16,896]{4,3,0,1,2:T(8,128)(2,1)S(1)} %maximum_select_fusion.13), channel_id=1, source_target_pairs={{0,2},{1,3},{2,0},{3,1},{4,6},{5,7},{6,4},{7,5},{8,10},{9,11},{10,... | collective-permute-start | bytes 688136 | tf_op jit(solution)/shard_map/pooled/ppermute | solution.py:34
  204.0 7.3 %collective-permute-start.28 = (bf16[2,2,2,16,768]{4,3,0,1,2:T(8,128)(2,1)}, bf16[2,2,2,16,768]{4,3,0,1,2:T(8,128)(2,1)}, u32[]{:S(2)}, u32[]{:S(2)}) collective-permute-start(bf16[2,2,2,16,768]{4,3,0,1,2:T(8,128)(2,1)} %fusion.59), channel_id=1, source_target_pairs={{0,2},{1,3},{2,0},{3,1},{4,6},{5,7},{6,4},{7,5},{8,10},{9,11},{10,... | collective-permute-start | bytes 589832 | tf_op jit(solution)/shard_map/d_pooled/ppermute | solution.py:34
  228.4 13.2 %collective-permute-start.32 = (bf16[4,96,768]{2,1,0:T(8,128)(2,1)S(1)}, bf16[4,96,768]{2,1,0:T(8,128)(2,1)}, u32[]{:S(2)}, u32[]{:S(2)}) collective-permute-start(bf16[4,96,768]{2,1,0:T(8,128)(2,1)S(1)} %pad_maximum_fusion.14), channel_id=1, source_target_pairs={{0,8},{1,9},{2,10},{3,11},{4,12},{5,13},{6,14},{7,15},{8,0},{9,1},... | collective-permute-start | bytes 1769480 | tf_op jit(solution)/shard_map/mlp_moments/ppermute | solution.py:34
  228.5 12.4 %collective-permute-start.33 = (bf16[2,96,768]{2,1,0:T(8,128)(2,1)S(1)}, bf16[2,96,768]{2,1,0:T(8,128)(2,1)S(1)}, u32[]{:S(2)}, u32[]{:S(2)}) collective-permute-start(bf16[2,96,768]{2,1,0:T(8,128)(2,1)S(1)} %pad_maximum_fusion.22), channel_id=1, source_target_pairs={{0,4},{1,3},{2,6},{3,1},{4,0},{5,7},{6,2},{7,5},{8,12},{9,11},{10,... | collective-permute-start | bytes 884744 | tf_op jit(solution)/shard_map/attn_moments/ppermute | solution.py:34
  241.7 16.3 %collective-permute-start.34 = (bf16[3072,768]{1,0:T(8,128)(2,1)}, bf16[3072,768]{1,0:T(8,128)(2,1)}, u32[]{:S(2)}, u32[]{:S(2)}) collective-permute-start(bf16[3072,768]{1,0:T(8,128)(2,1)} %get-tuple-element.160), channel_id=1, source_target_pairs={{0,1},{1,0},{2,3},{3,2},{4,5},{5,4},{6,7},{7,6},{8,9},{9,8},{10,11... | collective-permute-start | bytes 14155784 | tf_op jit(solution)/shard_map/mlp_grads/ppermute | solution.py:34
  244.4 13.6 %collective-permute-start.35 = (bf16[4,96,768]{2,1,0:T(8,128)(2,1)S(1)}, bf16[4,96,768]{2,1,0:T(8,128)(2,1)S(1)}, u32[]{:S(2)}, u32[]{:S(2)}) collective-permute-start(bf16[4,96,768]{2,1,0:T(8,128)(2,1)S(1)} %pad_maximum_fusion.15), channel_id=1, source_target_pairs={{0,1},{1,0},{2,3},{3,2},{4,5},{5,4},{6,7},{7,6},{8,9},{9,8},{10,11... | collective-permute-start | bytes 1769480 | tf_op jit(solution)/shard_map/attn_moments/ppermute | solution.py:34
  251.4 43.0 %collective-permute-start.37 = (bf16[8,96,768]{2,1,0:T(8,128)(2,1)}, bf16[8,96,768]{2,1,0:T(8,128)(2,1)S(1)}, u32[]{:S(2)}, u32[]{:S(2)}) collective-permute-start(bf16[8,96,768]{2,1,0:T(8,128)(2,1)} %pad_maximum_fusion.6), channel_id=1, source_target_pairs={{0,2},{1,5},{2,0},{3,7},{4,6},{5,1},{6,4},{7,3},{8,10},{9,13},{10,... | collective-permute-start | bytes 3538952 | tf_op jit(solution)/shard_map/mlp_moments/ppermute | solution.py:34
  263.3 31.2 %collective-permute-start.36 = (bf16[1536,768]{1,0:T(8,128)(2,1)}, bf16[1536,768]{1,0:T(8,128)(2,1)}, u32[]{:S(2)}, u32[]{:S(2)}) collective-permute-start(bf16[1536,768]{1,0:T(8,128)(2,1)} %add_convert_fusion), channel_id=1, source_target_pairs={{0,4},{1,3},{2,6},{3,1},{4,0},{5,7},{6,2},{7,5},{8,12},{9,11},{10,... | collective-permute-start | bytes 7077896 | tf_op jit(solution)/shard_map/mlp_grads/ppermute | solution.py:34
  274.2 20.3 %collective-permute-start.38 = (bf16[2,2,96,768]{3,2,1,0:T(8,128)(2,1)}, bf16[2,2,96,768]{3,2,1,0:T(8,128)(2,1)S(1)}, u32[]{:S(2)}, u32[]{:S(2)}) collective-permute-start(bf16[2,2,96,768]{3,2,1,0:T(8,128)(2,1)} %get-tuple-element.173), channel_id=1, source_target_pairs={{0,8},{1,9},{2,10},{3,11},{4,12},{5,13},{6,14},{7,15},{8,0},{9,1},... | collective-permute-start | bytes 1769480 | tf_op jit(solution)/shard_map/head_grads/ppermute | solution.py:34
  300.7 24.4 %collective-permute-start.40 = (bf16[4,4,96,768]{3,2,0,1:T(8,128)(2,1)}, bf16[4,4,96,768]{3,2,0,1:T(8,128)(2,1)}, u32[]{:S(2)}, u32[]{:S(2)}) collective-permute-start(bf16[4,4,96,768]{3,2,0,1:T(8,128)(2,1)} %fusion), channel_id=1, source_target_pairs={{0,1},{1,0},{2,3},{3,2},{4,5},{5,4},{6,7},{7,6},{8,9},{9,8},{10,11... | collective-permute-start | bytes 7077896 | tf_op jit(solution)/shard_map/attn_grads/ppermute | solution.py:34
  308.9 16.3 %collective-permute-start.39 = (bf16[768,768]{1,0:T(8,128)(2,1)S(1)}, bf16[768,768]{1,0:T(8,128)(2,1)S(1)}, u32[]{:S(2)}, u32[]{:S(2)}) collective-permute-start(bf16[768,768]{1,0:T(8,128)(2,1)S(1)} %slice.711), channel_id=1, source_target_pairs={{0,2},{1,5},{2,0},{3,7},{4,6},{5,1},{6,4},{7,3},{8,10},{9,13},{10,... | collective-permute-start | bytes 3538952 | tf_op jit(solution)/shard_map/mlp_grads/ppermute | solution.py:34
  328.9 17.2 %collective-permute-start.42 = (bf16[4,4,32,768]{3,2,0,1:T(8,128)(2,1)S(1)}, bf16[4,4,32,768]{3,2,0,1:T(8,128)(2,1)S(1)}, u32[]{:S(2)}, u32[]{:S(2)}) collective-permute-start(bf16[4,4,32,768]{3,2,0,1:T(8,128)(2,1)S(1)} %fusion.31), channel_id=1, source_target_pairs={{0,1},{1,0},{2,3},{3,2},{4,5},{5,4},{6,7},{7,6},{8,9},{9,8},{10,11... | collective-permute-start | bytes 2359304 | tf_op jit(solution)/shard_map/embed_grads/ppermute | solution.py:34
  329.4 15.8 %collective-permute-start.43 = (bf16[2,2,96,768]{3,2,1,0:T(8,128)(2,1)S(1)}, bf16[2,2,96,768]{3,2,1,0:T(8,128)(2,1)S(1)}, u32[]{:S(2)}, u32[]{:S(2)}) collective-permute-start(bf16[2,2,96,768]{3,2,1,0:T(8,128)(2,1)S(1)} %slice.712), channel_id=1, source_target_pairs={{0,8},{1,9},{2,10},{3,11},{4,12},{5,13},{6,14},{7,15},{8,0},{9,1},... | collective-permute-start | bytes 1769480 | tf_op jit(solution)/shard_map/mlp_grads/ppermute | solution.py:34
  330.7 15.4 %collective-permute-start.44 = (bf16[2,2,96,768]{3,2,1,0:T(8,128)(2,1)S(1)}, bf16[2,2,96,768]{3,2,1,0:T(8,128)(2,1)S(1)}, u32[]{:S(2)}, u32[]{:S(2)}) collective-permute-start(bf16[2,2,96,768]{3,2,1,0:T(8,128)(2,1)S(1)} %get-tuple-element.184), channel_id=1, source_target_pairs={{0,4},{1,5},{2,6},{3,7},{4,0},{5,1},{6,2},{7,3},{8,12},{9,13},{10,... | collective-permute-start | bytes 1769480 | tf_op jit(solution)/shard_map/head_grads/ppermute | solution.py:34
  334.0 30.3 %collective-permute-start.41 = (bf16[2,4,96,768]{3,2,1,0:T(8,128)(2,1)S(1)}, bf16[2,4,96,768]{3,2,1,0:T(8,128)(2,1)S(1)}, u32[]{:S(2)}, u32[]{:S(2)}) collective-permute-start(bf16[2,4,96,768]{3,2,1,0:T(8,128)(2,1)S(1)} %pad_maximum_fusion.7), channel_id=1, source_target_pairs={{0,4},{1,3},{2,6},{3,1},{4,0},{5,7},{6,2},{7,5},{8,12},{9,11},{10,... | collective-permute-start | bytes 3538952 | tf_op jit(solution)/shard_map/attn_grads/ppermute | solution.py:34
  346.9 15.5 %collective-permute-start.47 = (bf16[2,1,96,768]{3,2,1,0:T(8,128)(2,1)S(1)}, bf16[2,1,96,768]{3,2,1,0:T(8,128)(2,1)S(1)}, u32[]{:S(2)}, u32[]{:S(2)}) collective-permute-start(bf16[2,1,96,768]{3,2,1,0:T(8,128)(2,1)S(1)} %slice.713), channel_id=1, source_target_pairs={{0,16},{1,17},{2,18},{3,19},{4,20},{5,21},{6,22},{7,23},{8,24},{9,... | collective-permute-start | bytes 884744 | tf_op jit(solution)/shard_map/mlp_grads/ppermute | solution.py:34
  348.5 15.8 %collective-permute-start.45 = (bf16[2,4,32,768]{3,2,1,0:T(8,128)(2,1)S(1)}, bf16[2,4,32,768]{3,2,1,0:T(8,128)(2,1)S(1)}, u32[]{:S(2)}, u32[]{:S(2)}) collective-permute-start(bf16[2,4,32,768]{3,2,1,0:T(8,128)(2,1)S(1)} %pad_maximum_fusion.20), channel_id=1, source_target_pairs={{0,4},{1,3},{2,6},{3,1},{4,0},{5,7},{6,2},{7,5},{8,12},{9,11},{10,... | collective-permute-start | bytes 1179656 | tf_op jit(solution)/shard_map/embed_grads/ppermute | solution.py:34
  363.4 45.5 %collective-permute-start.51 = (bf16[16,96,768]{2,1,0:T(8,128)(2,1)}, bf16[16,96,768]{2,1,0:T(8,128)(2,1)}, u32[]{:S(2)}, u32[]{:S(2)}) collective-permute-start(bf16[16,96,768]{2,1,0:T(8,128)(2,1)} %constant_dynamic-update-slice_fusion), channel_id=1, source_target_pairs={{0,4},{1,3},{2,6},{3,1},{4,0},{5,7},{6,2},{7,5},{8,12},{9,11},{10,... | collective-permute-start | bytes 7077896 | tf_op jit(solution)/shard_map/mlp_moments/ppermute | solution.py:34
  365.1 20.5 %collective-permute-start.46 = (bf16[4,128,768]{2,1,0:T(8,128)(2,1)S(1)}, bf16[4,128,768]{2,1,0:T(8,128)(2,1)S(1)}, u32[]{:S(2)}, u32[]{:S(2)}) collective-permute-start(bf16[4,128,768]{2,1,0:T(8,128)(2,1)S(1)} %pad_maximum_fusion.12), channel_id=1, source_target_pairs={{0,2},{1,5},{2,0},{3,7},{4,6},{5,1},{6,4},{7,3},{8,10},{9,13},{10,... | collective-permute-start | bytes 2359304 | tf_op jit(solution)/shard_map/last_grads/ppermute | solution.py:34
  366.1 14.9 %collective-permute-start.48 = (bf16[2,96,768]{2,1,0:T(8,128)(2,1)S(1)}, bf16[2,96,768]{2,1,0:T(8,128)(2,1)S(1)}, u32[]{:S(2)}, u32[]{:S(2)}) collective-permute-start(bf16[2,96,768]{2,1,0:T(8,128)(2,1)S(1)} %get-tuple-element.190), channel_id=1, source_target_pairs={{0,16},{1,17},{2,18},{3,19},{4,20},{5,21},{6,22},{7,23},{8,24},{9,... | collective-permute-start | bytes 884744 | tf_op jit(solution)/shard_map/mlp_grads_all/ppermute | solution.py:34
  386.5 22.3 %collective-permute-start.50 = (bf16[4,96,768]{2,1,0:T(8,128)(2,1)}, bf16[4,96,768]{2,1,0:T(8,128)(2,1)}, u32[]{:S(2)}, u32[]{:S(2)}) collective-permute-start(bf16[4,96,768]{2,1,0:T(8,128)(2,1)} %pad_maximum_fusion.16), channel_id=1, source_target_pairs={{0,8},{1,9},{2,10},{3,11},{4,12},{5,13},{6,14},{7,15},{8,0},{9,1},... | collective-permute-start | bytes 1769480 | tf_op jit(solution)/shard_map/mlp_grads_all/ppermute | solution.py:34
  387.5 21.4 %collective-permute-start.49 = (bf16[2,128,768]{2,1,0:T(8,128)(2,1)}, bf16[2,128,768]{2,1,0:T(8,128)(2,1)}, u32[]{:S(2)}, u32[]{:S(2)}) collective-permute-start(bf16[2,128,768]{2,1,0:T(8,128)(2,1)} %fusion.48), channel_id=1, source_target_pairs={{0,8},{1,9},{2,10},{3,11},{4,12},{5,13},{6,14},{7,15},{8,0},{9,1},... | collective-permute-start | bytes 1179656 | tf_op jit(solution)/shard_map/last_grads/ppermute | solution.py:34
  411.2 16.7 %collective-permute-start.53 = (bf16[8,96,768]{2,1,0:T(8,128)(2,1)}, bf16[8,96,768]{2,1,0:T(8,128)(2,1)}, u32[]{:S(2)}, u32[]{:S(2)}) collective-permute-start(bf16[8,96,768]{2,1,0:T(8,128)(2,1)} %pad_maximum_fusion.8), channel_id=1, source_target_pairs={{0,2},{1,5},{2,0},{3,7},{4,6},{5,1},{6,4},{7,3},{8,10},{9,13},{10,... | collective-permute-start | bytes 3538952 | tf_op jit(solution)/shard_map/mlp_grads_all/ppermute | solution.py:34
  415.7 12.2 %collective-permute-start.52 = (bf16[128,768]{1,0:T(8,128)(2,1)S(1)}, bf16[128,768]{1,0:T(8,128)(2,1)S(1)}, u32[]{:S(2)}, u32[]{:S(2)}) collective-permute-start(bf16[128,768]{1,0:T(8,128)(2,1)S(1)} %fusion.62), channel_id=1, source_target_pairs={{0,16},{1,17},{2,18},{3,19},{4,20},{5,21},{6,22},{7,23},{8,24},{9,... | collective-permute-start | bytes 589832 | tf_op jit(solution)/shard_map/last_grads/ppermute | solution.py:34
  428.2 5.8 %collective-permute-start.55 = (bf16[1,96,768]{2,1,0:T(8,128)(2,1)S(1)}, bf16[1,96,768]{2,1,0:T(8,128)(2,1)S(1)}, u32[]{:S(2)}, u32[]{:S(2)}) collective-permute-start(bf16[1,96,768]{2,1,0:T(8,128)(2,1)S(1)} %fusion.70), channel_id=1, source_target_pairs={{0,2},{1,5},{2,0},{3,7},{4,6},{5,1},{6,4},{7,3},{8,10},{9,13},{10,... | collective-permute-start | bytes 442376 | tf_op jit(solution)/shard_map/attn_grads_all/ppermute | solution.py:34
  434.0 7.3 %collective-permute-start.57 = (bf16[2,96,768]{2,1,0:T(8,128)(2,1)S(1)}, bf16[2,96,768]{2,1,0:T(8,128)(2,1)S(1)}, u32[]{:S(2)}, u32[]{:S(2)}) collective-permute-start(bf16[2,96,768]{2,1,0:T(8,128)(2,1)S(1)} %pad_maximum_fusion.23), channel_id=1, source_target_pairs={{0,4},{1,3},{2,6},{3,1},{4,0},{5,7},{6,2},{7,5},{8,12},{9,11},{10,... | collective-permute-start | bytes 884744 | tf_op jit(solution)/shard_map/attn_grads_all/ppermute | solution.py:34
  435.3 5.9 %collective-permute-start.56 = (f32[16,768]{1,0:T(8,128)S(1)}, f32[16,768]{1,0:T(8,128)S(1)}, u32[]{:S(2)}, u32[]{:S(2)}) collective-permute-start(f32[16,768]{1,0:T(8,128)S(1)} %add.648), channel_id=1, source_target_pairs={{0,4},{1,5},{2,6},{3,7},{4,0},{5,1},{6,2},{7,3},{8,12},{9,13},{10,... | collective-permute-start | bytes 147464 | tf_op jit(solution)/shard_map/small_sums/ppermute | solution.py:34
  445.2 33.2 %collective-permute-start.62 = (bf16[16,96,768]{2,1,0:T(8,128)(2,1)}, bf16[16,96,768]{2,1,0:T(8,128)(2,1)}, u32[]{:S(2)}, u32[]{:S(2)}) collective-permute-start(bf16[16,96,768]{2,1,0:T(8,128)(2,1)} %pad_maximum_fusion.3), channel_id=1, source_target_pairs={{0,4},{1,3},{2,6},{3,1},{4,0},{5,7},{6,2},{7,5},{8,12},{9,11},{10,... | collective-permute-start | bytes 7077896 | tf_op jit(solution)/shard_map/mlp_grads_all/ppermute | solution.py:34
  448.2 5.5 %collective-permute-start.61 = (f32[16,768]{1,0:T(8,128)S(1)}, f32[16,768]{1,0:T(8,128)S(1)}, u32[]{:S(2)}, u32[]{:S(2)}) collective-permute-start(f32[16,768]{1,0:T(8,128)S(1)} %add.651), channel_id=1, source_target_pairs={{0,16},{1,17},{2,18},{3,19},{4,20},{5,21},{6,22},{7,23},{8,24},{9,... | collective-permute-start | bytes 147464 | tf_op jit(solution)/shard_map/small_sums/ppermute | solution.py:34
  456.3 45.9 %collective-permute-start.63 = (bf16[2,2,96,768]{3,2,1,0:T(8,128)(2,1)}, bf16[2,2,96,768]{3,2,1,0:T(8,128)(2,1)S(1)}, u32[]{:S(2)}, u32[]{:S(2)}) collective-permute-start(bf16[2,2,96,768]{3,2,1,0:T(8,128)(2,1)} %get-tuple-element.213), channel_id=1, source_target_pairs={{0,16},{1,17},{2,18},{3,19},{4,20},{5,21},{6,22},{7,23},{8,24},{9,... | collective-permute-start | bytes 1769480 | tf_op jit(solution)/shard_map/head_grads/ppermute | solution.py:34
  502.6 7.6 %collective-permute-start.64 = (f32[96,768]{1,0:T(8,128)S(1)}, f32[96,768]{1,0:T(8,128)S(1)}, u32[]{:S(2)}, u32[]{:S(2)}) collective-permute-start(f32[96,768]{1,0:T(8,128)S(1)} %slice.423), channel_id=1, source_target_pairs={{0,1},{1,0},{2,3},{3,2},{4,5},{5,4},{6,7},{7,6},{8,9},{9,8},{10,11... | collective-permute-start | bytes 884744 | tf_op jit(solution)/shard_map/small/ppermute | solution.py:34
  (131 other events, 911.6 us)

commit v5 on v4

--- a/solution.py
+++ b/solution.py
@@ -397,14 +397,17 @@
     )(core.reshape(1, 1), d_out, normed, *active, *slope, *parts)
 
 
-def kept_grads_kernel(plan, core_ref, d_out_ref, normed_ref, even_ref, odd_ref, d_hidden_ref, *refs):
-    kept_ref = refs[-1]
+def kept_grads_kernel(
+    plan, core_ref, d_out_ref, normed_ref, even_ref, odd_ref, d_hidden_ref, *refs
+):
     active_refs = (even_ref, odd_ref)
     width = d_out_ref.shape[1]
     half = width // 2
     first = core_ref[0, 0] == 0
     right = jnp.where(first, normed_ref[...], d_out_ref[...])
-    for index, side, slot in plan:
+    kept_ref = refs[-1]
+    arrived_ref = refs[0]
+    for index, side, slots in plan:
         columns = slice(None) if side is None else slice(side * half, (side + 1) * half)
         left = jnp.where(
             first,
@@ -412,27 +415,30 @@
             active_refs[index % 2][index // 2, :, columns],
         )
         grad = contract_rows(left, right)
-        if side is None:
-            kept_ref[pl.ds(slot[0] * half, half)] = grad[:half]
-            kept_ref[pl.ds(slot[1] * half, half)] = grad[half:]
-        else:
-            kept_ref[pl.ds(slot * half, half)] = grad
-    if len(refs) > 1:
-        part_refs, total_ref = refs[:4], refs[4]
+        for position, slot in enumerate(slots):
+            here = pl.ds(slot * half, half)
+            rows = grad[position * half : (position + 1) * half]
+            rows = rows + arrived_ref[here].astype(jnp.float32)
+            kept_ref[here] = rows.astype(kept_ref.dtype)
+    if len(refs) > 2:
+        part_refs, total_ref = refs[1:5], refs[5]
         total = low_dot(d_hidden_ref[0], part_refs[0][:, :width])
         for index in range(1, 4):
             total = total + low_dot(d_hidden_ref[index], part_refs[index][:, :width])
         total_ref[...] = total
 
 
-def kept_grads(plan, core, d_out, normed, active, d_hidden, parts=()):
+def kept_grads(plan, core, d_out, normed, active, d_hidden, arrived, parts=()):
     token_count, width = d_out.shape
-    grads = jax.ShapeDtypeStruct((2 * width, width), jnp.float32)
+    grads = jax.ShapeDtypeStruct((2 * width, width), jnp.float32 if parts else jnp.bfloat16)
     back = jax.ShapeDtypeStruct((token_count, width), jnp.float32)
+    side = 1 if parts else 0
+    arrived_spec = pl.BlockSpec((2 * width, width), lambda step: (side, 0))
     return pl.pallas_call(
         functools.partial(kept_grads_kernel, plan),
+        grid=(1,),
         out_shape=(back, grads) if parts else grads,
-        in_specs=[IN_SMEM] + [IN_VMEM] * (5 + len(parts)),
+        in_specs=[IN_SMEM] + [IN_VMEM] * 5 + [arrived_spec] + [IN_VMEM] * len(parts),
         out_specs=(IN_VMEM,) * 2 if parts else IN_VMEM,
         compiler_params=pltpu.CompilerParams(vmem_limit_bytes=48 * 1024 * 1024),
         cost_estimate=pl.CostEstimate(
@@ -441,7 +447,7 @@
             transcendentals=0,
         ),
         name="kept_grads",
-    )(core.reshape(1, 1), d_out, normed, *active, d_hidden, *parts)
+    )(core.reshape(1, 1), d_out, normed, *active, d_hidden, arrived, *parts)
 
 
 def orthogonal_kernel(part_count, chunk, full_steps, row_count, factor_ref, *refs):
@@ -814,19 +820,17 @@
     (away, d_hidden) = sync((away, d_hidden), mom_lane, attn_mom_lane)
     arrived = exchange(away, pair, "mlp_grads")
     operands = (core, d_out, normed_two, active, d_hidden)
-    first_plan = ((1, None, (2, 0)), (3, 1, 1), (2, 1, 3))
-    second_plan = ((0, None, (2, 0)), (3, 0, 1), (2, 0, 3))
-    leave = kept_grads(first_plan, *operands)
+    first_plan = ((1, None, (2, 0)), (3, 1, (1,)), (2, 1, (3,)))
+    second_plan = ((0, None, (2, 0)), (3, 0, (1,)), (2, 0, (3,)))
+    leave = kept_grads(first_plan, *operands, arrived)
     leave, arrived, d_hidden = sync(
         (leave, arrived, d_hidden), attn_mom_lane
     )
     operands = (core, d_out, normed_two, active, d_hidden)
-    half = 2 * model_width
-    leave = (leave + arrived[:half].astype(jnp.float32)).astype(jnp.bfloat16)
-
-    def summing(leave, kept, arrived):
+
+    def summing(leave, kept):
         far = yield leave, fourth
-        summed = kept() + arrived.astype(jnp.float32) + far.astype(jnp.float32)
+        summed = kept() + far.astype(jnp.float32)
         arrived = yield summed[:model_width].astype(jnp.bfloat16), third
         kept = summed[model_width:] + arrived.astype(jnp.float32)
         kept = kept.reshape(2, -1, mlp_rows, model_width)
@@ -837,9 +841,9 @@
         return kept[:, 0]
 
     own = []
-    mlp_lane = lane(summing(leave, lambda: own[0], arrived[half:]), "mlp_grads")
+    mlp_lane = lane(summing(leave, lambda: own[0]), "mlp_grads")
     sync((), mlp_lane)
-    d_normed_two, grads = kept_grads(second_plan, *operands, mlp_parts)
+    d_normed_two, grads = kept_grads(second_plan, *operands, arrived, mlp_parts)
     own.append(grads)
     (d_normed_two,) = sync((d_normed_two,), head_lane)
 
@@ -917,11 +921,11 @@
     all_lane = lane(
         collecting(mlp_grad.astype(jnp.bfloat16), up_stages + [third, fourth]), "mlp_grads_all"
     )
-    sync((), all_lane, mom_lane)
+    sync((), all_lane)
+    sync((), sum_lane, all_lane, mom_lane)
     sync((), sum_lane, all_lane)
-    sync((), sum_lane, all_lane, mom_lane)
     while sum_lane.result is None:
-        sync((), sum_lane, all_lane, hold=(all_lane,))
+        sync((), sum_lane, all_lane, mom_lane, hold=(all_lane,))
     attn_sum, embed_sum = sum_lane.result[:attn_rows], sum_lane.result[attn_rows:]
     g_query_bias = jnp.sum(d_queries.astype(jnp.float32), axis=0)
     g_value_bias = jnp.sum(d_values.astype(jnp.float32), axis=0)

time: 521 us -> 516 us (level)
  waiting for transfers between devices: 199 us -> 183 us
  matrix products: 18.7 us -> 25.4 us
    ppermute x66, waiting for transfers between devices: 199 us -> 183 us  [swap(): lax.ppermute(value, AXES, [(i, i ^ masks[i & 1]) for i in range(count)])]
    dot_general x5, matrix products: 4.09 us -> 9.77 us  [contract_cols(): lax.dot_general(left_side, right_side, (((1,), (1,)), ((), ())), preferre...]
    convert_element_type x1 -> x0, other arithmetic: 5.27 us -> none  [on_device(): leave = (leave + arrived[:half].astype(jnp.float32)).astype(jnp.bfloat16)]
    unnamed x231 -> x259, local copies, waits for them, and re-layouts: 28 us -> 31.6 us
  transfers between devices with their start and end apart: 66 -> 66, of which waited for: 37 -> 37; matrix products, arithmetic and copies ran while one was open for 18% -> 20% of each run, Pallas kernels for 21% -> 21%
where the time goes in v5:
time: 516 us; the launch traced here: 507 us
  waiting for transfers between devices  183 us (35%)
  Pallas kernels  107 us (21%)
  other arithmetic  83.6 us (16%)
  starting transfers between devices  51.5 us (10%)
  local copies, waits for them, and re-layouts  49.5 us (10%)
  matrix products  25.4 us (5%)
  between operations  6.64 us (1%)
    ppermute x66, waiting for transfers between devices, swap(): lax.ppermute(value, AXES, [(i, i ^ masks[i & 1]) for i in range(count)])  183 us
    ppermute x66, starting transfers between devices, swap(): lax.ppermute(value, AXES, [(i, i ^ masks[i & 1]) for i in range(count)])  51.5 us
    pallas_call x2, Pallas kernels, orthogonal_rows(): pl.pallas_call(body, out_shape=jax.ShapeDtypeStruct((row_count, width), j...  39.3 us
    unnamed x259, local copies, waits for them, and re-layouts  31.6 us
    pallas_call x2, Pallas kernels, hidden_forward(): pl.pallas_call(functools.partial(hidden_forward_kernel, rows), out_shape=...  17.3 us
    pallas_call x2, Pallas kernels, kept_grads(): pl.pallas_call(functools.partial(kept_grads_kernel, plan), grid=(1,), out...  15.7 us
    pallas_call x1, Pallas kernels, mixing_grads(): pl.pallas_call(functools.partial(mixing_grads_kernel, width, rows), grid=...  14.4 us
    concatenate x11, other arithmetic, collecting(): value = jnp.concatenate([value, (yield (value, stage))], axis=0)  14.1 us
  transfers between devices with their start and end apart: 66, of which 37 were waited for; matrix products, arithmetic and copies ran while one was open for 20% of the time, Pallas kernels for 21%

profile of v5, /device:TPU:0, one launch (start us, length us, event | category | flops | bytes accessed | tf_op | source)
XLA Modules:
  0.0 507.5 jit_solution(12603552910520289622)
XLA Ops:
  2.7 4.1 collective-permute-start
  8.7 7.2 %collective-permute-done = bf16[128,768]{1,0:T(8,128)(2,1)S(1)} collective-permute-done((bf16[128,768]{1,0:T(8,128)(2,1)S(1)}, bf16[128,768]{1,0:T(8,128)(2,1)S(1)}, u32[]{:S(2)}, u32[]{:S(2)}) %collective-permute-start) | collective-permute-done | bytes 196640 | tf_op jit(solution)/shard_map/attn_weights/ppermute | solution.py:34
  16.9 9.4 %collective-permute-done.1 = bf16[2,128,768]{2,1,0:T(8,128)(2,1)S(1)} collective-permute-done((bf16[2,128,768]{2,1,0:T(8,128)(2,1)S(1)}, bf16[2,128,768]{2,1,0:T(8,128)(2,1)S(1)}, u32[]{:S(2)}, u32[]{:S(2)}) %collective-permute-start.1) | collective-permute-done | bytes 393248 | tf_op jit(solution)/shard_map/attn_weights/ppermute | solution.py:34
  27.7 3.3 collective-permute-start.3
  31.1 12.7 %collective-permute-done.3 = bf16[1,96,1536]{2,1,0:T(8,128)(2,1)S(1)} collective-permute-done((bf16[1,96,1536]{2,1,0:T(8,128)(2,1)S(1)}, bf16[1,96,1536]{2,1,0:T(8,128)(2,1)S(1)}, u32[]{:S(2)}, u32[]{:S(2)}) %collective-permute-start.3) | collective-permute-done | bytes 294944 | tf_op jit(solution)/shard_map/mlp_weights/ppermute | solution.py:34
  54.8 11.5 %collective-permute-done.5 = bf16[2,96,1536]{2,1,0:T(8,128)(2,1)} collective-permute-done((bf16[2,96,1536]{2,1,0:T(8,128)(2,1)}, bf16[2,96,1536]{2,1,0:T(8,128)(2,1)}, u32[]{:S(2)}, u32[]{:S(2)}) %collective-permute-start.5) | collective-permute-done | bytes 589856 | tf_op jit(solution)/shard_map/mlp_weights/ppermute | solution.py:34
  75.7 10.1 %collective-permute-done.8 = bf16[2,2,96,768]{3,2,1,0:T(8,128)(2,1)S(1)} collective-permute-done((bf16[2,2,96,768]{3,2,1,0:T(8,128)(2,1)S(1)}, bf16[2,2,96,768]{3,2,1,0:T(8,128)(2,1)S(1)}, u32[]{:S(2)}, u32[]{:S(2)}) %collective-permute-start.8) | collective-permute-done | bytes 589856 | tf_op jit(solution)/shard_map/head/ppermute | solution.py:34
  85.8 2.7 collective-permute-done.7
  91.5 3.4 collective-permute-start.11
  99.1 10.4 %mixing.1 = (bf16[512,768]{1,0:T(8,128)(2,1)S(1)}, f32[16,512]{1,0:T(8,128)S(1)}) custom-call(s32[512,1]{1,0:T(8,128)S(1)} %copy.160.ids_down_ref, s32[1,512]{1,0:T(1,128)S(1)} %constant_dynamic-slice_fusion.13.ids_ref, bf16[512,768]{1,0:T(8,128)(2,1)S(1)} %add_convert_fusion.3.q_ref, bf16[512,768]{1,0:T(8,128)(2,1)S(1)} %convolution_convert_fusion.1.k_ref, ...), custom_call_target="tpu_custom_call" | custom-call | flops 805306368 | bytes 3145728 | tf_op jit(solution)/shard_map/mixing/pallas_call | solution.py:195
  112.4 8.8 %hidden_forward.2 = (f32[512,768]{1,0:T(8,128)S(1)}, bf16[2,512,768]{2,1,0:T(8,128)(2,1)S(1)}, f32[2,512,768]{2,1,0:T(8,128)}) custom-call(bf16[512,768]{1,0:T(8,128)(2,1)S(1)} %get-tuple-element.298.normed_ref, f32[512,768]{1,0:T(8,128)S(1)} %get-tuple-element.297.middle_ref, f32[2,768]{1,0:T(2,128)S(1)} %slice.359.bias_ref, bf16[768,1536]{1,0:T(8,128)(2,1)} %bitcast.344, ...), custom_call_target="tpu_custom_call" | custom-call | flops 2415919104 | bytes 11010048 | tf_op jit(solution)/shard_map/hidden_forward/pallas_call | solution.py:298
  135.5 8.5 %hidden_forward.3 = (f32[512,768]{1,0:T(8,128)S(1)}, bf16[2,512,768]{2,1,0:T(8,128)(2,1)S(1)}, f32[2,512,768]{2,1,0:T(8,128)}) custom-call(bf16[512,768]{1,0:T(8,128)(2,1)S(1)} %copy-done.7, f32[512,768]{1,0:T(8,128)S(1)} %copy-done.15, f32[2,768]{1,0:T(2,128)S(1)} %slice.360.bias_ref, bf16[768,1536]{1,0:T(8,128)(2,1)} %bitcast.62.refs_0_.refs_5_.refs_2_, ...), custom_call_target="tpu_custom_call" | custom-call | flops 2415919104 | bytes 11010048 | tf_op jit(solution)/shard_map/hidden_forward/pallas_call | solution.py:298
  145.2 2.7 collective-permute-done.15
  150.5 4.9 collective-permute-done.17
  155.6 4.1 collective-permute-done.18
  160.3 4.3 collective-permute-done.19
  165.7 5.0 collective-permute-done.20
  180.5 2.7 collective-permute-done.23
  183.8 3.2 collective-permute-done.24
  187.1 3.6 collective-permute-done.25
  192.1 3.3 collective-permute-done.26
  196.1 2.7 divide_convert_fusion
  207.6 6.3 %collective-permute-done.28 = bf16[2,2,2,16,768]{4,3,0,1,2:T(8,128)(2,1)} collective-permute-done((bf16[2,2,2,16,768]{4,3,0,1,2:T(8,128)(2,1)}, bf16[2,2,2,16,768]{4,3,0,1,2:T(8,128)(2,1)}, u32[]{:S(2)}, u32[]{:S(2)}) %collective-permute-start.28) | collective-permute-done | bytes 196640 | tf_op jit(solution)/shard_map/d_pooled/ppermute | solution.py:34
  215.6 4.1 collective-permute-done.29
  220.9 3.0 collective-permute-done.30
  226.2 2.6 collective-permute-done.31
  233.1 10.3 %hidden_back.1 = (bf16[4,512,768]{2,1,0:T(8,128)(2,1)}, f32[4,768]{1,0:T(4,128)S(1)}, bf16[3072,768]{1,0:T(8,128)(2,1)}) custom-call(s32[1,1]{1,0:T(1,128)} %bitcast.108.core_ref, bf16[512,768]{1,0:T(8,128)(2,1)S(1)} %get-tuple-element.149.d_out_ref, bf16[512,768]{1,0:T(8,128)(2,1)S(1)} %copy-done.8, ...), custom_call_target="tpu_custom_call" | custom-call | flops 4831838208 | bytes 22020096 | tf_op jit(solution)/shard_map/hidden_back/pallas_call | solution.py:372
  245.8 3.0 multiply_reduce_fusion
  250.0 2.4 pad_maximum_fusion.6
  253.4 5.4 %kept_grads.2 = bf16[1536,768]{1,0:T(8,128)(2,1)} custom-call(s32[1,1]{1,0:T(1,128)} %bitcast.108.core_ref, bf16[512,768]{1,0:T(8,128)(2,1)S(1)} %copy-done.5, bf16[512,768]{1,0:T(8,128)(2,1)S(1)} %copy-done.9, bf16[2,512,768]{2,1,0:T(8,128)(2,1)S(1)} %get-tuple-element.150.refs_0_.even_ref, bf16[2,512,768]{2,1,0:T(8,128)(2,1)S(1)} %copy-done.3, ...), custom_call_target="tpu_custom_call" | custom-call | flops 1207959552 | bytes 12582912 | tf_op jit(solution)/shard_map/kept_grads/pallas_call | solution.py:437
  259.4 10.3 %kept_grads.3 = (f32[512,768]{1,0:T(8,128)S(1)}, f32[1536,768]{1,0:T(8,128)}) custom-call(s32[1,1]{1,0:T(1,128)} %bitcast.108.core_ref, bf16[512,768]{1,0:T(8,128)(2,1)S(1)} %copy-done.5, bf16[512,768]{1,0:T(8,128)(2,1)S(1)} %copy-done.9, bf16[2,512,768]{2,1,0:T(8,128)(2,1)S(1)} %get-tuple-element.150.refs_0_.even_ref, bf16[2,512,768]{2,1,0:T(8,128)(2,1)} %copy-done.2, ...), custom_call_target="tpu_custom_call" | custom-call | flops 1207959552 | bytes 12582912 | tf_op jit(solution)/shard_map/kept_grads/pallas_call | solution.py:437
  273.5 2.7 convolution_convert_fusion.d_ref
  276.2 14.4 %mixing_grads.1 = (bf16[512,768]{1,0:T(8,128)(2,1)S(1)}, bf16[512,768]{1,0:T(8,128)(2,1)S(1)}, bf16[512,768]{1,0:T(8,128)(2,1)S(1)}) custom-call(s32[512,1]{1,0:T(8,128)S(1)} %copy.160.ids_down_ref, s32[1,512]{1,0:T(1,128)S(1)} %constant_dynamic-slice_fusion.13.ids_ref, f32[16,512]{1,0:T(8,128)S(1)} %get-tuple-element.145.summary_ref, ...), custom_call_target="tpu_custom_call" | custom-call | flops 2013265920 | bytes 5505024 | tf_op jit(solution)/shard_map/mixing_grads/pallas_call | solution.py:252
  296.8 3.5 copy-done.20
  302.8 3.6 convert_add_fusion
  315.0 7.8 %collective-permute-done.39 = bf16[768,768]{1,0:T(8,128)(2,1)S(1)} collective-permute-done((bf16[768,768]{1,0:T(8,128)(2,1)S(1)}, bf16[768,768]{1,0:T(8,128)(2,1)S(1)}, u32[]{:S(2)}, u32[]{:S(2)}) %collective-permute-start.39) | collective-permute-done | bytes 1179680 | tf_op jit(solution)/shard_map/mlp_grads/ppermute | solution.py:34
  335.9 4.1 collective-permute-done.43
  346.0 7.0 %collective-permute-done.41 = bf16[2,4,96,768]{3,2,1,0:T(8,128)(2,1)} collective-permute-done((bf16[2,4,96,768]{3,2,1,0:T(8,128)(2,1)}, bf16[2,4,96,768]{3,2,1,0:T(8,128)(2,1)}, u32[]{:S(2)}, u32[]{:S(2)}) %collective-permute-start.41) | collective-permute-done | bytes 1179680 | tf_op jit(solution)/shard_map/attn_grads/ppermute | solution.py:34
  352.9 4.2 collective-permute-done.45
  370.3 8.1 %collective-permute-done.48 = bf16[2,96,768]{2,1,0:T(8,128)(2,1)S(1)} collective-permute-done((bf16[2,96,768]{2,1,0:T(8,128)(2,1)S(1)}, bf16[2,96,768]{2,1,0:T(8,128)(2,1)S(1)}, u32[]{:S(2)}, u32[]{:S(2)}) %collective-permute-start.48) | collective-permute-done | bytes 294944 | tf_op jit(solution)/shard_map/mlp_grads_all/ppermute | solution.py:34
  384.0 19.6 %collective-permute-done.49 = bf16[2,128,768]{2,1,0:T(8,128)(2,1)} collective-permute-done((bf16[2,128,768]{2,1,0:T(8,128)(2,1)}, bf16[2,128,768]{2,1,0:T(8,128)(2,1)}, u32[]{:S(2)}, u32[]{:S(2)}) %collective-permute-start.49) | collective-permute-done | bytes 393248 | tf_op jit(solution)/shard_map/last_grads/ppermute | solution.py:34
  411.5 10.8 %collective-permute-done.51 = bf16[128,768]{1,0:T(8,128)(2,1)S(1)} collective-permute-done((bf16[128,768]{1,0:T(8,128)(2,1)S(1)}, bf16[128,768]{1,0:T(8,128)(2,1)S(1)}, u32[]{:S(2)}, u32[]{:S(2)}) %collective-permute-start.51) | collective-permute-done | bytes 196640 | tf_op jit(solution)/shard_map/last_grads/ppermute | solution.py:34
  424.8 3.7 collective-permute-done.54
  430.8 3.2 pad_maximum_fusion.3
  443.5 5.1 collective-permute-done.61
  457.2 15.5 %orthogonal_rows.2 = f32[96,768]{1,0:T(8,128)S(1)} custom-call(f32[1,1]{1,0:T(1,128)} %bitcast.143.factor_ref, bf16[768,768]{1,0:T(8,128)(2,1)S(1)} %bitcast.335, bf16[768,768]{1,0:T(8,128)(2,1)S(1)} %bitcast.336), custom_call_target="tpu_custom_call" | custom-call | flops 16307453952 | bytes 2359296 | tf_op jit(solution)/shard_map/orthogonal_rows/pallas_call | solution.py:539
  472.7 23.8 %orthogonal_rows.3 = f32[192,768]{1,0:T(8,128)S(1)} custom-call(f32[1,1]{1,0:T(1,128)} %bitcast.143.factor_ref, bf16[1536,768]{1,0:T(8,128)(2,1)} %bitcast.146.refs_0_, bf16[1536,768]{1,0:T(8,128)(2,1)} %bitcast.147.refs_1_, bf16[1536,768]{1,0:T(8,128)(2,1)} %bitcast.148.refs_2_, bf16[1536,768]{1,0:T(8,128)(2,1)} %bitcast.149.refs_3_), custom_call_target="tpu_custom_call" | custom-call | flops 11777605632 | bytes 9437184 | tf_op jit(solution)/shard_map/orthogonal_rows/pallas_call | solution.py:539
  498.8 4.9 fusion.115
  (606 shorter events, 182.9 us)
Async XLA Ops:
  2.7 13.2 %collective-permute-start = (bf16[128,768]{1,0:T(8,128)(2,1)S(1)}, bf16[128,768]{1,0:T(8,128)(2,1)S(1)}, u32[]{:S(2)}, u32[]{:S(2)}) collective-permute-start(bf16[128,768]{1,0:T(8,128)(2,1)S(1)} %pad_maximum_fusion.24), channel_id=1, source_target_pairs={{0,16},{1,17},{2,18},{3,19},{4,20},{5,21},{6,22},{7,23},{8,24},{9,... | collective-permute-start | bytes 589832 | tf_op jit(solution)/shard_map/attn_weights/ppermute | solution.py:34
  15.9 10.4 %collective-permute-start.1 = (bf16[2,128,768]{2,1,0:T(8,128)(2,1)S(1)}, bf16[2,128,768]{2,1,0:T(8,128)(2,1)S(1)}, u32[]{:S(2)}, u32[]{:S(2)}) collective-permute-start(bf16[2,128,768]{2,1,0:T(8,128)(2,1)S(1)} %maximum_select_fusion.11), channel_id=1, source_target_pairs={{0,8},{1,9},{2,10},{3,11},{4,12},{5,13},{6,14},{7,15},{8,0},{9,1},... | collective-permute-start | bytes 1179656 | tf_op jit(solution)/shard_map/attn_weights/ppermute | solution.py:34
  26.4 17.4 %collective-permute-start.2 = (bf16[4,128,768]{2,1,0:T(8,128)(2,1)S(1)}, bf16[4,128,768]{2,1,0:T(8,128)(2,1)S(1)}, u32[]{:S(2)}, u32[]{:S(2)}) collective-permute-start(bf16[4,128,768]{2,1,0:T(8,128)(2,1)S(1)} %bitcast.347), channel_id=1, source_target_pairs={{0,2},{1,5},{2,0},{3,7},{4,6},{5,1},{6,4},{7,3},{8,10},{9,13},{10,... | collective-permute-start | bytes 2359304 | tf_op jit(solution)/shard_map/attn_weights/ppermute | solution.py:34
  27.7 16.1 %collective-permute-start.3 = (bf16[1,96,1536]{2,1,0:T(8,128)(2,1)S(1)}, bf16[1,96,1536]{2,1,0:T(8,128)(2,1)S(1)}, u32[]{:S(2)}, u32[]{:S(2)}) collective-permute-start(bf16[1,96,1536]{2,1,0:T(8,128)(2,1)S(1)} %convert_bitcast_fusion.1), channel_id=1, source_target_pairs={{0,16},{1,17},{2,18},{3,19},{4,20},{5,21},{6,22},{7,23},{8,24},{9,... | collective-permute-start | bytes 884744 | tf_op jit(solution)/shard_map/mlp_weights/ppermute | solution.py:34
  45.3 21.0 %collective-permute-start.4 = (bf16[2,4,128,768]{3,2,1,0:T(8,128)(2,1)}, bf16[2,4,128,768]{3,2,1,0:T(8,128)(2,1)}, u32[]{:S(2)}, u32[]{:S(2)}) collective-permute-start(bf16[2,4,128,768]{3,2,1,0:T(8,128)(2,1)} %pad_maximum_fusion.4), channel_id=1, source_target_pairs={{0,4},{1,3},{2,6},{3,1},{4,0},{5,7},{6,2},{7,5},{8,12},{9,11},{10,... | collective-permute-start | bytes 4718600 | tf_op jit(solution)/shard_map/attn_weights/ppermute | solution.py:34
  50.4 15.8 %collective-permute-start.5 = (bf16[2,96,1536]{2,1,0:T(8,128)(2,1)}, bf16[2,96,1536]{2,1,0:T(8,128)(2,1)}, u32[]{:S(2)}, u32[]{:S(2)}) collective-permute-start(bf16[2,96,1536]{2,1,0:T(8,128)(2,1)} %pad_maximum_fusion.13), channel_id=1, source_target_pairs={{0,8},{1,9},{2,10},{3,11},{4,12},{5,13},{6,14},{7,15},{8,0},{9,1},... | collective-permute-start | bytes 1769480 | tf_op jit(solution)/shard_map/mlp_weights/ppermute | solution.py:34
  68.0 7.0 %collective-permute-start.6 = (bf16[4,4,128,768]{3,2,1,0:T(8,128)(2,1)S(1)}, bf16[4,4,128,768]{3,2,1,0:T(8,128)(2,1)S(1)}, u32[]{:S(2)}, u32[]{:S(2)}) collective-permute-start(bf16[4,4,128,768]{3,2,1,0:T(8,128)(2,1)S(1)} %pad_maximum_fusion.1), channel_id=1, source_target_pairs={{0,1},{1,0},{2,3},{3,2},{4,5},{5,4},{6,7},{7,6},{8,9},{9,8},{10,11... | collective-permute-start | bytes 9437192 | tf_op jit(solution)/shard_map/attn_weights/ppermute | solution.py:34
  70.0 15.8 %collective-permute-start.8 = (bf16[2,2,96,768]{3,2,1,0:T(8,128)(2,1)S(1)}, bf16[2,2,96,768]{3,2,1,0:T(8,128)(2,1)S(1)}, u32[]{:S(2)}, u32[]{:S(2)}) collective-permute-start(bf16[2,2,96,768]{3,2,1,0:T(8,128)(2,1)S(1)} %get-tuple-element.124), channel_id=1, source_target_pairs={{0,8},{1,9},{2,10},{3,11},{4,12},{5,13},{6,14},{7,15},{8,0},{9,1},... | collective-permute-start | bytes 1769480 | tf_op jit(solution)/shard_map/head/ppermute | solution.py:34
  72.2 16.3 %collective-permute-start.7 = (bf16[4,96,1536]{2,1,0:T(8,128)(2,1)S(1)}, bf16[4,96,1536]{2,1,0:T(8,128)(2,1)S(1)}, u32[]{:S(2)}, u32[]{:S(2)}) collective-permute-start(bf16[4,96,1536]{2,1,0:T(8,128)(2,1)S(1)} %pad_maximum_fusion.5), channel_id=1, source_target_pairs={{0,2},{1,5},{2,0},{3,7},{4,6},{5,1},{6,4},{7,3},{8,10},{9,13},{10,... | collective-permute-start | bytes 3538952 | tf_op jit(solution)/shard_map/mlp_weights/ppermute | solution.py:34
  89.8 32.6 %collective-permute-start.10 = (bf16[8,96,1536]{2,1,0:T(8,128)(2,1)S(1)}, bf16[8,96,1536]{2,1,0:T(8,128)(2,1)}, u32[]{:S(2)}, u32[]{:S(2)}) collective-permute-start(bf16[8,96,1536]{2,1,0:T(8,128)(2,1)S(1)} %pad_maximum_fusion.2), channel_id=1, source_target_pairs={{0,4},{1,3},{2,6},{3,1},{4,0},{5,7},{6,2},{7,5},{8,12},{9,11},{10,... | collective-permute-start | bytes 7077896 | tf_op jit(solution)/shard_map/mlp_weights/ppermute | solution.py:34
  90.4 19.2 %collective-permute-start.9 = (bf16[8,96,1536]{2,1,0:T(8,128)(2,1)S(1)}, bf16[8,96,1536]{2,1,0:T(8,128)(2,1)S(1)}, u32[]{:S(2)}, u32[]{:S(2)}) collective-permute-start(bf16[8,96,1536]{2,1,0:T(8,128)(2,1)S(1)} %pad_maximum_fusion.2), channel_id=1, source_target_pairs={{0,1},{1,0},{2,3},{3,2},{4,5},{5,4},{6,7},{7,6},{8,9},{9,8},{10,11... | collective-permute-start | bytes 7077896 | tf_op jit(solution)/shard_map/mlp_weights/ppermute | solution.py:34
  91.5 30.9 %collective-permute-start.11 = (bf16[2,2,96,768]{3,2,1,0:T(8,128)(2,1)S(1)}, bf16[2,2,96,768]{3,2,1,0:T(8,128)(2,1)S(1)}, u32[]{:S(2)}, u32[]{:S(2)}) collective-permute-start(bf16[2,2,96,768]{3,2,1,0:T(8,128)(2,1)S(1)} %get-tuple-element.310), channel_id=1, source_target_pairs={{0,16},{1,17},{2,18},{3,19},{4,20},{5,21},{6,22},{7,23},{8,24},{9,... | collective-permute-start | bytes 1769480 | tf_op jit(solution)/shard_map/head/ppermute | solution.py:34
  123.2 6.9 %collective-permute-start.12 = (bf16[8,96,1536]{2,1,0:T(8,128)(2,1)}, bf16[8,96,1536]{2,1,0:T(8,128)(2,1)}, u32[]{:S(2)}, u32[]{:S(2)}) collective-permute-start(bf16[8,96,1536]{2,1,0:T(8,128)(2,1)} %collective-permute-done.10), channel_id=1, source_target_pairs={{0,1},{1,0},{2,3},{3,2},{4,5},{5,4},{6,7},{7,6},{8,9},{9,8},{10,11... | collective-permute-start | bytes 7077896 | tf_op jit(solution)/shard_map/mlp_weights/ppermute | solution.py:34
  128.6 16.6 %collective-permute-start.14 = (bf16[2,2,96,768]{3,2,1,0:T(8,128)(2,1)}, bf16[2,2,96,768]{3,2,1,0:T(8,128)(2,1)}, u32[]{:S(2)}, u32[]{:S(2)}) collective-permute-start(bf16[2,2,96,768]{3,2,1,0:T(8,128)(2,1)} %get-tuple-element.308), channel_id=1, source_target_pairs={{0,4},{1,5},{2,6},{3,7},{4,0},{5,1},{6,2},{7,3},{8,12},{9,13},{10,... | collective-permute-start | bytes 1769480 | tf_op jit(solution)/shard_map/head/ppermute | solution.py:34
  131.5 16.4 %collective-permute-start.15 = (bf16[2,96,768]{2,1,0:T(8,128)(2,1)}, bf16[2,96,768]{2,1,0:T(8,128)(2,1)}, u32[]{:S(2)}, u32[]{:S(2)}) collective-permute-start(bf16[2,96,768]{2,1,0:T(8,128)(2,1)} %pad_maximum_fusion.21), channel_id=1, source_target_pairs={{0,16},{1,17},{2,18},{3,19},{4,20},{5,21},{6,22},{7,23},{8,24},{9,... | collective-permute-start | bytes 884744 | tf_op jit(solution)/shard_map/mlp_moments/ppermute | solution.py:34
  132.0 13.2 %collective-permute-start.16 = (bf16[1,96,768]{2,1,0:T(8,128)(2,1)}, bf16[1,96,768]{2,1,0:T(8,128)(2,1)}, u32[]{:S(2)}, u32[]{:S(2)}) collective-permute-start(bf16[1,96,768]{2,1,0:T(8,128)(2,1)} %convert_bitcast_fusion.2), channel_id=1, source_target_pairs={{0,2},{1,5},{2,0},{3,7},{4,6},{5,1},{6,4},{7,3},{8,10},{9,13},{10,... | collective-permute-start | bytes 442376 | tf_op jit(solution)/shard_map/attn_moments/ppermute | solution.py:34
  150.5 5.0 collective-permute-start.17
  164.6 6.1 %collective-permute-start.20 = (bf16[2,2,2,16,896]{4,3,0,1,2:T(8,128)(2,1)S(1)}, bf16[2,2,2,16,896]{4,3,0,1,2:T(8,128)(2,1)S(1)}, u32[]{:S(2)}, u32[]{:S(2)}) collective-permute-start(bf16[2,2,2,16,896]{4,3,0,1,2:T(8,128)(2,1)S(1)} %maximum_select_fusion.13), channel_id=1, source_target_pairs={{0,2},{1,3},{2,0},{3,1},{4,6},{5,7},{6,4},{7,5},{8,10},{9,11},{10,... | collective-permute-start | bytes 688136 | tf_op jit(solution)/shard_map/pooled/ppermute | solution.py:34
  206.6 7.3 %collective-permute-start.28 = (bf16[2,2,2,16,768]{4,3,0,1,2:T(8,128)(2,1)}, bf16[2,2,2,16,768]{4,3,0,1,2:T(8,128)(2,1)}, u32[]{:S(2)}, u32[]{:S(2)}) collective-permute-start(bf16[2,2,2,16,768]{4,3,0,1,2:T(8,128)(2,1)} %fusion.59), channel_id=1, source_target_pairs={{0,2},{1,3},{2,0},{3,1},{4,6},{5,7},{6,4},{7,5},{8,10},{9,11},{10,... | collective-permute-start | bytes 589832 | tf_op jit(solution)/shard_map/d_pooled/ppermute | solution.py:34
  230.9 13.2 %collective-permute-start.32 = (bf16[4,96,768]{2,1,0:T(8,128)(2,1)S(1)}, bf16[4,96,768]{2,1,0:T(8,128)(2,1)}, u32[]{:S(2)}, u32[]{:S(2)}) collective-permute-start(bf16[4,96,768]{2,1,0:T(8,128)(2,1)S(1)} %pad_maximum_fusion.14), channel_id=1, source_target_pairs={{0,8},{1,9},{2,10},{3,11},{4,12},{5,13},{6,14},{7,15},{8,0},{9,1},... | collective-permute-start | bytes 1769480 | tf_op jit(solution)/shard_map/mlp_moments/ppermute | solution.py:34
  231.0 12.4 %collective-permute-start.33 = (bf16[2,96,768]{2,1,0:T(8,128)(2,1)S(1)}, bf16[2,96,768]{2,1,0:T(8,128)(2,1)S(1)}, u32[]{:S(2)}, u32[]{:S(2)}) collective-permute-start(bf16[2,96,768]{2,1,0:T(8,128)(2,1)S(1)} %pad_maximum_fusion.22), channel_id=1, source_target_pairs={{0,4},{1,3},{2,6},{3,1},{4,0},{5,7},{6,2},{7,5},{8,12},{9,11},{10,... | collective-permute-start | bytes 884744 | tf_op jit(solution)/shard_map/attn_moments/ppermute | solution.py:34
  244.1 9.2 %collective-permute-start.34 = (bf16[3072,768]{1,0:T(8,128)(2,1)}, bf16[3072,768]{1,0:T(8,128)(2,1)}, u32[]{:S(2)}, u32[]{:S(2)}) collective-permute-start(bf16[3072,768]{1,0:T(8,128)(2,1)} %get-tuple-element.159), channel_id=1, source_target_pairs={{0,1},{1,0},{2,3},{3,2},{4,5},{5,4},{6,7},{7,6},{8,9},{9,8},{10,11... | collective-permute-start | bytes 14155784 | tf_op jit(solution)/shard_map/mlp_grads/ppermute | solution.py:34
  245.3 13.5 %collective-permute-start.35 = (bf16[4,96,768]{2,1,0:T(8,128)(2,1)S(1)}, bf16[4,96,768]{2,1,0:T(8,128)(2,1)S(1)}, u32[]{:S(2)}, u32[]{:S(2)}) collective-permute-start(bf16[4,96,768]{2,1,0:T(8,128)(2,1)S(1)} %pad_maximum_fusion.15), channel_id=1, source_target_pairs={{0,1},{1,0},{2,3},{3,2},{4,5},{5,4},{6,7},{7,6},{8,9},{9,8},{10,11... | collective-permute-start | bytes 1769480 | tf_op jit(solution)/shard_map/attn_moments/ppermute | solution.py:34
  252.4 39.0 %collective-permute-start.37 = (bf16[8,96,768]{2,1,0:T(8,128)(2,1)}, bf16[8,96,768]{2,1,0:T(8,128)(2,1)S(1)}, u32[]{:S(2)}, u32[]{:S(2)}) collective-permute-start(bf16[8,96,768]{2,1,0:T(8,128)(2,1)} %pad_maximum_fusion.6), channel_id=1, source_target_pairs={{0,2},{1,5},{2,0},{3,7},{4,6},{5,1},{6,4},{7,3},{8,10},{9,13},{10,... | collective-permute-start | bytes 3538952 | tf_op jit(solution)/shard_map/mlp_moments/ppermute | solution.py:34
  258.8 34.3 %collective-permute-start.36 = (bf16[1536,768]{1,0:T(8,128)(2,1)}, bf16[1536,768]{1,0:T(8,128)(2,1)S(1)}, u32[]{:S(2)}, u32[]{:S(2)}) collective-permute-start(bf16[1536,768]{1,0:T(8,128)(2,1)} %kept_grads.2), channel_id=1, source_target_pairs={{0,4},{1,3},{2,6},{3,1},{4,0},{5,7},{6,2},{7,5},{8,12},{9,11},{10,... | collective-permute-start | bytes 7077896 | tf_op jit(solution)/shard_map/mlp_grads/ppermute | solution.py:34
  269.7 21.7 %collective-permute-start.38 = (bf16[2,2,96,768]{3,2,1,0:T(8,128)(2,1)}, bf16[2,2,96,768]{3,2,1,0:T(8,128)(2,1)S(1)}, u32[]{:S(2)}, u32[]{:S(2)}) collective-permute-start(bf16[2,2,96,768]{3,2,1,0:T(8,128)(2,1)} %get-tuple-element.172), channel_id=1, source_target_pairs={{0,8},{1,9},{2,10},{3,11},{4,12},{5,13},{6,14},{7,15},{8,0},{9,1},... | collective-permute-start | bytes 1769480 | tf_op jit(solution)/shard_map/head_grads/ppermute | solution.py:34
  302.0 20.8 %collective-permute-start.40 = (bf16[4,4,96,768]{3,2,0,1:T(8,128)(2,1)}, bf16[4,4,96,768]{3,2,0,1:T(8,128)(2,1)}, u32[]{:S(2)}, u32[]{:S(2)}) collective-permute-start(bf16[4,4,96,768]{3,2,0,1:T(8,128)(2,1)} %fusion), channel_id=1, source_target_pairs={{0,1},{1,0},{2,3},{3,2},{4,5},{5,4},{6,7},{7,6},{8,9},{9,8},{10,11... | collective-permute-start | bytes 7077896 | tf_op jit(solution)/shard_map/attn_grads/ppermute | solution.py:34
  306.5 16.3 %collective-permute-start.39 = (bf16[768,768]{1,0:T(8,128)(2,1)S(1)}, bf16[768,768]{1,0:T(8,128)(2,1)S(1)}, u32[]{:S(2)}, u32[]{:S(2)}) collective-permute-start(bf16[768,768]{1,0:T(8,128)(2,1)S(1)} %slice.701), channel_id=1, source_target_pairs={{0,2},{1,5},{2,0},{3,7},{4,6},{5,1},{6,4},{7,3},{8,10},{9,13},{10,... | collective-permute-start | bytes 3538952 | tf_op jit(solution)/shard_map/mlp_grads/ppermute | solution.py:34
  325.6 14.4 %collective-permute-start.43 = (bf16[2,2,96,768]{3,2,1,0:T(8,128)(2,1)S(1)}, bf16[2,2,96,768]{3,2,1,0:T(8,128)(2,1)S(1)}, u32[]{:S(2)}, u32[]{:S(2)}) collective-permute-start(bf16[2,2,96,768]{3,2,1,0:T(8,128)(2,1)S(1)} %slice.702), channel_id=1, source_target_pairs={{0,8},{1,9},{2,10},{3,11},{4,12},{5,13},{6,14},{7,15},{8,0},{9,1},... | collective-permute-start | bytes 1769480 | tf_op jit(solution)/shard_map/mlp_grads/ppermute | solution.py:34
  326.1 14.1 %collective-permute-start.44 = (bf16[2,2,96,768]{3,2,1,0:T(8,128)(2,1)S(1)}, bf16[2,2,96,768]{3,2,1,0:T(8,128)(2,1)S(1)}, u32[]{:S(2)}, u32[]{:S(2)}) collective-permute-start(bf16[2,2,96,768]{3,2,1,0:T(8,128)(2,1)S(1)} %get-tuple-element.183), channel_id=1, source_target_pairs={{0,4},{1,5},{2,6},{3,7},{4,0},{5,1},{6,2},{7,3},{8,12},{9,13},{10,... | collective-permute-start | bytes 1769480 | tf_op jit(solution)/shard_map/head_grads/ppermute | solution.py:34
  330.4 10.7 %collective-permute-start.42 = (bf16[4,4,32,768]{3,2,0,1:T(8,128)(2,1)S(1)}, bf16[4,4,32,768]{3,2,0,1:T(8,128)(2,1)S(1)}, u32[]{:S(2)}, u32[]{:S(2)}) collective-permute-start(bf16[4,4,32,768]{3,2,0,1:T(8,128)(2,1)S(1)} %fusion.31), channel_id=1, source_target_pairs={{0,1},{1,0},{2,3},{3,2},{4,5},{5,4},{6,7},{7,6},{8,9},{9,8},{10,11... | collective-permute-start | bytes 2359304 | tf_op jit(solution)/shard_map/embed_grads/ppermute | solution.py:34
  335.4 17.5 %collective-permute-start.41 = (bf16[2,4,96,768]{3,2,1,0:T(8,128)(2,1)}, bf16[2,4,96,768]{3,2,1,0:T(8,128)(2,1)}, u32[]{:S(2)}, u32[]{:S(2)}) collective-permute-start(bf16[2,4,96,768]{3,2,1,0:T(8,128)(2,1)} %pad_maximum_fusion.7), channel_id=1, source_target_pairs={{0,4},{1,3},{2,6},{3,1},{4,0},{5,7},{6,2},{7,5},{8,12},{9,11},{10,... | collective-permute-start | bytes 3538952 | tf_op jit(solution)/shard_map/attn_grads/ppermute | solution.py:34
  342.1 15.0 %collective-permute-start.45 = (bf16[2,4,32,768]{3,2,1,0:T(8,128)(2,1)}, bf16[2,4,32,768]{3,2,1,0:T(8,128)(2,1)}, u32[]{:S(2)}, u32[]{:S(2)}) collective-permute-start(bf16[2,4,32,768]{3,2,1,0:T(8,128)(2,1)} %pad_maximum_fusion.20), channel_id=1, source_target_pairs={{0,4},{1,3},{2,6},{3,1},{4,0},{5,7},{6,2},{7,5},{8,12},{9,11},{10,... | collective-permute-start | bytes 1179656 | tf_op jit(solution)/shard_map/embed_grads/ppermute | solution.py:34
  345.1 17.8 %collective-permute-start.47 = (bf16[2,1,96,768]{3,2,1,0:T(8,128)(2,1)S(1)}, bf16[2,1,96,768]{3,2,1,0:T(8,128)(2,1)S(1)}, u32[]{:S(2)}, u32[]{:S(2)}) collective-permute-start(bf16[2,1,96,768]{3,2,1,0:T(8,128)(2,1)S(1)} %slice.703), channel_id=1, source_target_pairs={{0,16},{1,17},{2,18},{3,19},{4,20},{5,21},{6,22},{7,23},{8,24},{9,... | collective-permute-start | bytes 884744 | tf_op jit(solution)/shard_map/mlp_grads/ppermute | solution.py:34
  361.2 17.2 %collective-permute-start.46 = (bf16[4,128,768]{2,1,0:T(8,128)(2,1)S(1)}, bf16[4,128,768]{2,1,0:T(8,128)(2,1)S(1)}, u32[]{:S(2)}, u32[]{:S(2)}) collective-permute-start(bf16[4,128,768]{2,1,0:T(8,128)(2,1)S(1)} %pad_maximum_fusion.12), channel_id=1, source_target_pairs={{0,2},{1,5},{2,0},{3,7},{4,6},{5,1},{6,4},{7,3},{8,10},{9,13},{10,... | collective-permute-start | bytes 2359304 | tf_op jit(solution)/shard_map/last_grads/ppermute | solution.py:34
  363.8 14.6 %collective-permute-start.48 = (bf16[2,96,768]{2,1,0:T(8,128)(2,1)S(1)}, bf16[2,96,768]{2,1,0:T(8,128)(2,1)S(1)}, u32[]{:S(2)}, u32[]{:S(2)}) collective-permute-start(bf16[2,96,768]{2,1,0:T(8,128)(2,1)S(1)} %get-tuple-element.255), channel_id=1, source_target_pairs={{0,16},{1,17},{2,18},{3,19},{4,20},{5,21},{6,22},{7,23},{8,24},{9,... | collective-permute-start | bytes 884744 | tf_op jit(solution)/shard_map/mlp_grads_all/ppermute | solution.py:34
  378.4 44.1 %collective-permute-start.53 = (bf16[16,96,768]{2,1,0:T(8,128)(2,1)}, bf16[16,96,768]{2,1,0:T(8,128)(2,1)}, u32[]{:S(2)}, u32[]{:S(2)}) collective-permute-start(bf16[16,96,768]{2,1,0:T(8,128)(2,1)} %constant_dynamic-update-slice_fusion), channel_id=1, source_target_pairs={{0,4},{1,3},{2,6},{3,1},{4,0},{5,7},{6,2},{7,5},{8,12},{9,11},{10,... | collective-permute-start | bytes 7077896 | tf_op jit(solution)/shard_map/mlp_moments/ppermute | solution.py:34
  380.2 23.3 %collective-permute-start.50 = (bf16[4,96,768]{2,1,0:T(8,128)(2,1)}, bf16[4,96,768]{2,1,0:T(8,128)(2,1)}, u32[]{:S(2)}, u32[]{:S(2)}) collective-permute-start(bf16[4,96,768]{2,1,0:T(8,128)(2,1)} %pad_maximum_fusion.16), channel_id=1, source_target_pairs={{0,8},{1,9},{2,10},{3,11},{4,12},{5,13},{6,14},{7,15},{8,0},{9,1},... | collective-permute-start | bytes 1769480 | tf_op jit(solution)/shard_map/mlp_grads_all/ppermute | solution.py:34
  381.3 22.3 %collective-permute-start.49 = (bf16[2,128,768]{2,1,0:T(8,128)(2,1)}, bf16[2,128,768]{2,1,0:T(8,128)(2,1)}, u32[]{:S(2)}, u32[]{:S(2)}) collective-permute-start(bf16[2,128,768]{2,1,0:T(8,128)(2,1)} %fusion.48), channel_id=1, source_target_pairs={{0,8},{1,9},{2,10},{3,11},{4,12},{5,13},{6,14},{7,15},{8,0},{9,1},... | collective-permute-start | bytes 1179656 | tf_op jit(solution)/shard_map/last_grads/ppermute | solution.py:34
  405.9 16.5 %collective-permute-start.52 = (bf16[8,96,768]{2,1,0:T(8,128)(2,1)}, bf16[8,96,768]{2,1,0:T(8,128)(2,1)}, u32[]{:S(2)}, u32[]{:S(2)}) collective-permute-start(bf16[8,96,768]{2,1,0:T(8,128)(2,1)} %pad_maximum_fusion.8), channel_id=1, source_target_pairs={{0,2},{1,5},{2,0},{3,7},{4,6},{5,1},{6,4},{7,3},{8,10},{9,13},{10,... | collective-permute-start | bytes 3538952 | tf_op jit(solution)/shard_map/mlp_grads_all/ppermute | solution.py:34
  410.1 12.2 %collective-permute-start.51 = (bf16[128,768]{1,0:T(8,128)(2,1)S(1)}, bf16[128,768]{1,0:T(8,128)(2,1)S(1)}, u32[]{:S(2)}, u32[]{:S(2)}) collective-permute-start(bf16[128,768]{1,0:T(8,128)(2,1)S(1)} %fusion.62), channel_id=1, source_target_pairs={{0,16},{1,17},{2,18},{3,19},{4,20},{5,21},{6,22},{7,23},{8,24},{9,... | collective-permute-start | bytes 589832 | tf_op jit(solution)/shard_map/last_grads/ppermute | solution.py:34
  422.7 5.8 %collective-permute-start.55 = (bf16[1,96,768]{2,1,0:T(8,128)(2,1)S(1)}, bf16[1,96,768]{2,1,0:T(8,128)(2,1)S(1)}, u32[]{:S(2)}, u32[]{:S(2)}) collective-permute-start(bf16[1,96,768]{2,1,0:T(8,128)(2,1)S(1)} %fusion.70), channel_id=1, source_target_pairs={{0,2},{1,5},{2,0},{3,7},{4,6},{5,1},{6,4},{7,3},{8,10},{9,13},{10,... | collective-permute-start | bytes 442376 | tf_op jit(solution)/shard_map/attn_grads_all/ppermute | solution.py:34
  428.6 7.3 %collective-permute-start.57 = (bf16[2,96,768]{2,1,0:T(8,128)(2,1)S(1)}, bf16[2,96,768]{2,1,0:T(8,128)(2,1)S(1)}, u32[]{:S(2)}, u32[]{:S(2)}) collective-permute-start(bf16[2,96,768]{2,1,0:T(8,128)(2,1)S(1)} %pad_maximum_fusion.23), channel_id=1, source_target_pairs={{0,4},{1,3},{2,6},{3,1},{4,0},{5,7},{6,2},{7,5},{8,12},{9,11},{10,... | collective-permute-start | bytes 884744 | tf_op jit(solution)/shard_map/attn_grads_all/ppermute | solution.py:34
  429.8 6.1 %collective-permute-start.56 = (f32[16,768]{1,0:T(8,128)S(1)}, f32[16,768]{1,0:T(8,128)S(1)}, u32[]{:S(2)}, u32[]{:S(2)}) collective-permute-start(f32[16,768]{1,0:T(8,128)S(1)} %add.640), channel_id=1, source_target_pairs={{0,4},{1,5},{2,6},{3,7},{4,0},{5,1},{6,2},{7,3},{8,12},{9,13},{10,... | collective-permute-start | bytes 147464 | tf_op jit(solution)/shard_map/small_sums/ppermute | solution.py:34
  440.3 32.4 %collective-permute-start.62 = (bf16[16,96,768]{2,1,0:T(8,128)(2,1)}, bf16[16,96,768]{2,1,0:T(8,128)(2,1)}, u32[]{:S(2)}, u32[]{:S(2)}) collective-permute-start(bf16[16,96,768]{2,1,0:T(8,128)(2,1)} %pad_maximum_fusion.3), channel_id=1, source_target_pairs={{0,4},{1,3},{2,6},{3,1},{4,0},{5,7},{6,2},{7,5},{8,12},{9,11},{10,... | collective-permute-start | bytes 7077896 | tf_op jit(solution)/shard_map/mlp_grads_all/ppermute | solution.py:34
  442.8 5.8 %collective-permute-start.61 = (f32[16,768]{1,0:T(8,128)S(1)}, f32[16,768]{1,0:T(8,128)S(1)}, u32[]{:S(2)}, u32[]{:S(2)}) collective-permute-start(f32[16,768]{1,0:T(8,128)S(1)} %add.643), channel_id=1, source_target_pairs={{0,16},{1,17},{2,18},{3,19},{4,20},{5,21},{6,22},{7,23},{8,24},{9,... | collective-permute-start | bytes 147464 | tf_op jit(solution)/shard_map/small_sums/ppermute | solution.py:34
  451.2 45.3 %collective-permute-start.63 = (bf16[2,2,96,768]{3,2,1,0:T(8,128)(2,1)}, bf16[2,2,96,768]{3,2,1,0:T(8,128)(2,1)S(1)}, u32[]{:S(2)}, u32[]{:S(2)}) collective-permute-start(bf16[2,2,96,768]{3,2,1,0:T(8,128)(2,1)} %get-tuple-element.211), channel_id=1, source_target_pairs={{0,16},{1,17},{2,18},{3,19},{4,20},{5,21},{6,22},{7,23},{8,24},{9,... | collective-permute-start | bytes 1769480 | tf_op jit(solution)/shard_map/head_grads/ppermute | solution.py:34
  496.9 7.6 %collective-permute-start.64 = (f32[96,768]{1,0:T(8,128)S(1)}, f32[96,768]{1,0:T(8,128)S(1)}, u32[]{:S(2)}, u32[]{:S(2)}) collective-permute-start(f32[96,768]{1,0:T(8,128)S(1)} %slice.415), channel_id=1, source_target_pairs={{0,1},{1,0},{2,3},{3,2},{4,5},{5,4},{6,7},{7,6},{8,9},{9,8},{10,11... | collective-permute-start | bytes 884744 | tf_op jit(solution)/shard_map/small/ppermute | solution.py:34
  (145 other events, 862.0 us)

commit v6 on v5

--- a/solution.py
+++ b/solution.py
@@ -760,8 +760,14 @@
     facts = jnp.pad(facts, ((0, 0), (0, 125))).astype(jnp.bfloat16)
     block = jnp.concatenate([pooled.astype(jnp.bfloat16), facts], axis=1)
     head_b = finish(head_lane)[0].reshape(owners * shard_rows, chunk)
-    for axis, bit in enumerate(range(top - 1, -1, -1)):
+    for axis, bit in enumerate(high_bits):
         block = ordered_pair(bit_of(bit), block, exchange(block, plain(bit), "pooled"), axis)
+    axis = len(high_bits)
+    for step, stage in enumerate((third, fourth)):
+        bit = jnp.where(core == step, bit_of(1), bit_of(2))
+        block = ordered_pair(bit, block, exchange(block, stage, "pooled"), axis + step)
+    block = jnp.where(core == 0, jnp.swapaxes(block, axis, axis + 1), block)
+    block = ordered_pair(core, block, exchange(block, pair, "pooled"), axis + 2)
     block = block.reshape(count * slot_count, -1)
     all_pooled = block[:, :model_width]
     facts = block[:, model_width : model_width + 3].astype(jnp.int32)
@@ -792,14 +798,33 @@
         jnp.bfloat16
     )
     d_pooled = contract_cols(d_logits, head_b)
-    d_pooled = d_pooled.reshape((2,) * top + (slot_count, model_width))
-    for bit in range(top):
-        axis = top - 1 - bit
-        mine = bit_of(bit)
-        leave = pick(d_pooled, 1 - mine, axis).astype(jnp.bfloat16)
-        d_pooled = pick(d_pooled, mine, axis) + exchange(leave, plain(bit), "d_pooled").astype(
-            jnp.float32
-        )
+    quarter = (me >> 1) & 3
+    to_third, to_fourth = third_mine >> 1, fourth_mine >> 1
+
+    def quartered(grad, rows):
+        grad = grad.reshape(count // 8, 4, 2, rows, model_width)
+        leave = pick(grad, 1 - core, 2).astype(jnp.bfloat16)
+        grad = pick(grad, core, 2) + (yield leave, pair).astype(jnp.float32)
+        leave = [pick(grad, quarter ^ to_fourth, 1), pick(grad, quarter ^ 3, 1)]
+        leave = (yield jnp.stack(leave).astype(jnp.bfloat16), fourth).astype(jnp.float32)
+        leaving = pick(grad, quarter ^ to_third, 1) + leave[1]
+        return pick(grad, quarter, 1) + leave[0], leaving
+
+    def last_sums(grads):
+        grad = jnp.concatenate([one[0] for one in grads], axis=1)
+        leave = jnp.concatenate([one[1].astype(jnp.bfloat16) for one in grads], axis=1)
+        grad = grad + (yield leave, third).astype(jnp.float32)
+        grad = grad.reshape((2,) * len(high_bits) + grad.shape[1:])
+        for bit in reversed(high_bits):
+            axis = top - 1 - bit
+            mine = bit_of(bit)
+            leave = pick(grad, 1 - mine, axis).astype(jnp.bfloat16)
+            grad = pick(grad, mine, axis) + (yield leave, plain(bit)).astype(jnp.float32)
+        return grad
+
+    (parts,) = finish(lane(quartered(d_pooled, slot_count), "d_pooled"))
+    (d_pooled,) = finish(lane(last_sums([parts]), "d_pooled"))
+
     d_closing = product(member.T, d_pooled / divisor)
     d_final, g_gain_final, g_shift_final = close_pull(d_closing)
     d_out = d_final.astype(jnp.bfloat16)
@@ -873,30 +898,6 @@
         ],
         axis=0,
     )
-
-    quarter = (me >> 1) & 3
-    to_third, to_fourth = third_mine >> 1, fourth_mine >> 1
-
-    def quartered(grad, rows):
-        grad = grad.reshape(count // 8, 4, 2, rows, model_width)
-        leave = pick(grad, 1 - core, 2).astype(jnp.bfloat16)
-        grad = pick(grad, core, 2) + (yield leave, pair).astype(jnp.float32)
-        leave = [pick(grad, quarter ^ to_fourth, 1), pick(grad, quarter ^ 3, 1)]
-        leave = (yield jnp.stack(leave).astype(jnp.bfloat16), fourth).astype(jnp.float32)
-        leaving = pick(grad, quarter ^ to_third, 1) + leave[1]
-        return pick(grad, quarter, 1) + leave[0], leaving
-
-    def last_sums(grads):
-        grad = jnp.concatenate([one[0] for one in grads], axis=1)
-        leave = jnp.concatenate([one[1].astype(jnp.bfloat16) for one in grads], axis=1)
-        grad = grad + (yield leave, third).astype(jnp.float32)
-        grad = grad.reshape((2,) * len(high_bits) + grad.shape[1:])
-        for bit in reversed(high_bits):
-            axis = top - 1 - bit
-            mine = bit_of(bit)
-            leave = pick(grad, 1 - mine, axis).astype(jnp.bfloat16)
-            grad = pick(grad, mine, axis) + (yield leave, plain(bit)).astype(jnp.float32)
-        return grad
 
     attn_lane = lane(quartered(attn_grad, attn_rows), "attn_grads")
     d_normed = (

time: 516 us -> 515 us (level)
  waiting for transfers between devices: 183 us -> 190 us
  starting transfers between devices: 51.5 us -> 58.3 us
  local copies, waits for them, and re-layouts: 49.5 us -> 43.2 us
  matrix products: 25.4 us -> 19.7 us
    ppermute x66, waiting for transfers between devices: 183 us -> 190 us  [swap(): lax.ppermute(value, AXES, [(i, i ^ masks[i & 1]) for i in range(count)])]
    ppermute x66, starting transfers between devices: 51.5 us -> 58.3 us  [swap(): lax.ppermute(value, AXES, [(i, i ^ masks[i & 1]) for i in range(count)])]
    unnamed x259 -> x247, local copies, waits for them, and re-layouts: 31.6 us -> 26.8 us
  transfers between devices with their start and end apart: 66 -> 66, of which waited for: 37 -> 39; matrix products, arithmetic and copies ran while one was open for 20% -> 17% of each run, Pallas kernels for 21% -> 21%
where the time goes in v6:
time: 515 us; the launch traced here: 507 us
  waiting for transfers between devices  190 us (37%)
  Pallas kernels  108 us (21%)
  other arithmetic  80.9 us (16%)
  starting transfers between devices  58.3 us (11%)
  local copies, waits for them, and re-layouts  43.2 us (8%)
  matrix products  19.7 us (4%)
  between operations  6.57 us (1%)
    ppermute x66, waiting for transfers between devices, swap(): lax.ppermute(value, AXES, [(i, i ^ masks[i & 1]) for i in range(count)])  190 us
    ppermute x66, starting transfers between devices, swap(): lax.ppermute(value, AXES, [(i, i ^ masks[i & 1]) for i in range(count)])  58.3 us
    pallas_call x2, Pallas kernels, orthogonal_rows(): pl.pallas_call(body, out_shape=jax.ShapeDtypeStruct((row_count, width), j...  39.2 us
    unnamed x247, local copies, waits for them, and re-layouts  26.8 us
    pallas_call x2, Pallas kernels, hidden_forward(): pl.pallas_call(functools.partial(hidden_forward_kernel, rows), out_shape=...  17.4 us
    pallas_call x2, Pallas kernels, kept_grads(): pl.pallas_call(functools.partial(kept_grads_kernel, plan), grid=(1,), out...  15.9 us
    pallas_call x1, Pallas kernels, mixing_grads(): pl.pallas_call(functools.partial(mixing_grads_kernel, width, rows), grid=...  14.4 us
    concatenate x11, other arithmetic, collecting(): value = jnp.concatenate([value, (yield (value, stage))], axis=0)  14 us
  transfers between devices with their start and end apart: 66, of which 39 were waited for; matrix products, arithmetic and copies ran while one was open for 17% of the time, Pallas kernels for 21%

profile of v6, /device:TPU:0, one launch (start us, length us, event | category | flops | bytes accessed | tf_op | source)
XLA Modules:
  0.0 506.6 jit_solution(14959811902779832201)
XLA Ops:
  2.7 4.1 collective-permute-start
  8.7 7.2 %collective-permute-done = bf16[128,768]{1,0:T(8,128)(2,1)S(1)} collective-permute-done((bf16[128,768]{1,0:T(8,128)(2,1)S(1)}, bf16[128,768]{1,0:T(8,128)(2,1)S(1)}, u32[]{:S(2)}, u32[]{:S(2)}) %collective-permute-start) | collective-permute-done | bytes 196640 | tf_op jit(solution)/shard_map/attn_weights/ppermute | solution.py:34
  16.9 9.4 %collective-permute-done.1 = bf16[2,128,768]{2,1,0:T(8,128)(2,1)S(1)} collective-permute-done((bf16[2,128,768]{2,1,0:T(8,128)(2,1)S(1)}, bf16[2,128,768]{2,1,0:T(8,128)(2,1)S(1)}, u32[]{:S(2)}, u32[]{:S(2)}) %collective-permute-start.1) | collective-permute-done | bytes 393248 | tf_op jit(solution)/shard_map/attn_weights/ppermute | solution.py:34
  27.7 3.3 collective-permute-start.3
  31.1 12.7 %collective-permute-done.3 = bf16[1,96,1536]{2,1,0:T(8,128)(2,1)S(1)} collective-permute-done((bf16[1,96,1536]{2,1,0:T(8,128)(2,1)S(1)}, bf16[1,96,1536]{2,1,0:T(8,128)(2,1)S(1)}, u32[]{:S(2)}, u32[]{:S(2)}) %collective-permute-start.3) | collective-permute-done | bytes 294944 | tf_op jit(solution)/shard_map/mlp_weights/ppermute | solution.py:34
  54.7 11.5 %collective-permute-done.5 = bf16[2,96,1536]{2,1,0:T(8,128)(2,1)} collective-permute-done((bf16[2,96,1536]{2,1,0:T(8,128)(2,1)}, bf16[2,96,1536]{2,1,0:T(8,128)(2,1)}, u32[]{:S(2)}, u32[]{:S(2)}) %collective-permute-start.5) | collective-permute-done | bytes 589856 | tf_op jit(solution)/shard_map/mlp_weights/ppermute | solution.py:34
  75.6 10.1 %collective-permute-done.8 = bf16[2,2,96,768]{3,2,1,0:T(8,128)(2,1)S(1)} collective-permute-done((bf16[2,2,96,768]{3,2,1,0:T(8,128)(2,1)S(1)}, bf16[2,2,96,768]{3,2,1,0:T(8,128)(2,1)S(1)}, u32[]{:S(2)}, u32[]{:S(2)}) %collective-permute-start.8) | collective-permute-done | bytes 589856 | tf_op jit(solution)/shard_map/head/ppermute | solution.py:34
  85.8 2.7 collective-permute-done.7
  91.5 3.4 collective-permute-start.11
  99.5 10.4 %mixing.1 = (bf16[512,768]{1,0:T(8,128)(2,1)S(1)}, f32[16,512]{1,0:T(8,128)S(1)}) custom-call(s32[512,1]{1,0:T(8,128)S(1)} %copy.163.ids_down_ref, s32[1,512]{1,0:T(1,128)S(1)} %constant_dynamic-slice_fusion.11.ids_ref, bf16[512,768]{1,0:T(8,128)(2,1)S(1)} %add_convert_fusion.3.q_ref, bf16[512,768]{1,0:T(8,128)(2,1)S(1)} %convolution_convert_fusion.1.k_ref, ...), custom_call_target="tpu_custom_call" | custom-call | flops 805306368 | bytes 3145728 | tf_op jit(solution)/shard_map/mixing/pallas_call | solution.py:195
  112.8 8.9 %hidden_forward.2 = (f32[512,768]{1,0:T(8,128)S(1)}, bf16[2,512,768]{2,1,0:T(8,128)(2,1)S(1)}, f32[2,512,768]{2,1,0:T(8,128)}) custom-call(bf16[512,768]{1,0:T(8,128)(2,1)S(1)} %get-tuple-element.298.normed_ref, f32[512,768]{1,0:T(8,128)S(1)} %get-tuple-element.297.middle_ref, f32[2,768]{1,0:T(2,128)S(1)} %slice.365.bias_ref, bf16[768,1536]{1,0:T(8,128)(2,1)} %bitcast.366, ...), custom_call_target="tpu_custom_call" | custom-call | flops 2415919104 | bytes 11010048 | tf_op jit(solution)/shard_map/hidden_forward/pallas_call | solution.py:298
  136.0 8.5 %hidden_forward.3 = (f32[512,768]{1,0:T(8,128)S(1)}, bf16[2,512,768]{2,1,0:T(8,128)(2,1)S(1)}, f32[2,512,768]{2,1,0:T(8,128)}) custom-call(bf16[512,768]{1,0:T(8,128)(2,1)S(1)} %copy-done.5, f32[512,768]{1,0:T(8,128)S(1)} %copy-done.12, f32[2,768]{1,0:T(2,128)S(1)} %slice.366.bias_ref, bf16[768,1536]{1,0:T(8,128)(2,1)} %bitcast.62.refs_0_.refs_5_.refs_2_, ...), custom_call_target="tpu_custom_call" | custom-call | flops 2415919104 | bytes 11010048 | tf_op jit(solution)/shard_map/hidden_forward/pallas_call | solution.py:298
  145.7 2.7 collective-permute-done.15
  150.5 4.9 collective-permute-done.17
  155.5 4.1 collective-permute-done.18
  160.7 4.8 collective-permute-done.19
  166.2 5.5 %collective-permute-done.20 = bf16[2,2,2,16,896]{4,3,0,1,2:T(8,128)(2,1)S(1)} collective-permute-done((bf16[2,2,2,16,896]{4,3,0,1,2:T(8,128)(2,1)S(1)}, bf16[2,2,2,16,896]{4,3,0,1,2:T(8,128)(2,1)S(1)}, u32[]{:S(2)}, u32[]{:S(2)}) %collective-permute-start.20) | collective-permute-done | bytes 229408 | tf_op jit(solution)/shard_map/pooled/ppermute | solution.py:34
  182.4 2.8 collective-permute-done.23
  185.8 3.2 collective-permute-done.24
  189.1 3.6 collective-permute-done.25
  193.9 3.4 collective-permute-done.26
  198.0 2.7 divide_convert_fusion
  209.1 5.5 %collective-permute-done.28 = bf16[2,4,16,768]{3,2,1,0:T(8,128)(2,1)} collective-permute-done((bf16[2,4,16,768]{3,2,1,0:T(8,128)(2,1)}, bf16[2,4,16,768]{3,2,1,0:T(8,128)(2,1)}, u32[]{:S(2)}, u32[]{:S(2)}) %collective-permute-start.28) | collective-permute-done | bytes 196640 | tf_op jit(solution)/shard_map/d_pooled/ppermute | solution.py:34
  218.7 4.0 collective-permute-done.29
  225.0 2.9 collective-permute-done.30
  229.2 3.6 collective-permute-done.31
  236.3 10.3 %hidden_back.1 = (bf16[4,512,768]{2,1,0:T(8,128)(2,1)}, f32[4,768]{1,0:T(4,128)S(1)}, bf16[3072,768]{1,0:T(8,128)(2,1)}) custom-call(s32[1,1]{1,0:T(1,128)} %bitcast.111.core_ref, bf16[512,768]{1,0:T(8,128)(2,1)S(1)} %get-tuple-element.149.d_out_ref, bf16[512,768]{1,0:T(8,128)(2,1)S(1)} %copy-done.6, ...), custom_call_target="tpu_custom_call" | custom-call | flops 4831838208 | bytes 22020096 | tf_op jit(solution)/shard_map/hidden_back/pallas_call | solution.py:372
  257.0 5.5 %kept_grads.2 = bf16[1536,768]{1,0:T(8,128)(2,1)} custom-call(s32[1,1]{1,0:T(1,128)} %bitcast.111.core_ref, bf16[512,768]{1,0:T(8,128)(2,1)S(1)} %get-tuple-element.149.d_out_ref, bf16[512,768]{1,0:T(8,128)(2,1)S(1)} %copy-done.6, bf16[2,512,768]{2,1,0:T(8,128)(2,1)S(1)} %get-tuple-element.150.refs_0_.even_ref, bf16[2,512,768]{2,1,0:T(8,128)(2,1)S(1)} %copy-done.3, ...), custom_call_target="tpu_custom_call" | custom-call | flops 1207959552 | bytes 12582912 | tf_op jit(solution)/shard_map/kept_grads/pallas_call | solution.py:437
  263.5 10.4 %kept_grads.3 = (f32[512,768]{1,0:T(8,128)S(1)}, f32[1536,768]{1,0:T(8,128)}) custom-call(s32[1,1]{1,0:T(1,128)} %bitcast.111.core_ref, bf16[512,768]{1,0:T(8,128)(2,1)S(1)} %get-tuple-element.149.d_out_ref, bf16[512,768]{1,0:T(8,128)(2,1)S(1)} %copy-done.6, bf16[2,512,768]{2,1,0:T(8,128)(2,1)S(1)} %get-tuple-element.150.refs_0_.even_ref, ...), custom_call_target="tpu_custom_call" | custom-call | flops 1207959552 | bytes 12582912 | tf_op jit(solution)/shard_map/kept_grads/pallas_call | solution.py:437
  279.9 14.4 %mixing_grads.1 = (bf16[512,768]{1,0:T(8,128)(2,1)S(1)}, bf16[512,768]{1,0:T(8,128)(2,1)S(1)}, bf16[512,768]{1,0:T(8,128)(2,1)S(1)}) custom-call(s32[512,1]{1,0:T(8,128)S(1)} %copy.163.ids_down_ref, s32[1,512]{1,0:T(1,128)S(1)} %constant_dynamic-slice_fusion.11.ids_ref, f32[16,512]{1,0:T(8,128)S(1)} %get-tuple-element.145.summary_ref, ...), custom_call_target="tpu_custom_call" | custom-call | flops 2013265920 | bytes 5505024 | tf_op jit(solution)/shard_map/mixing_grads/pallas_call | solution.py:252
  298.9 3.6 convert_add_fusion
  308.8 10.1 %collective-permute-done.39 = bf16[768,768]{1,0:T(8,128)(2,1)S(1)} collective-permute-done((bf16[768,768]{1,0:T(8,128)(2,1)S(1)}, bf16[768,768]{1,0:T(8,128)(2,1)S(1)}, u32[]{:S(2)}, u32[]{:S(2)}) %collective-permute-start.39) | collective-permute-done | bytes 1179680 | tf_op jit(solution)/shard_map/mlp_grads/ppermute | solution.py:34
  329.1 8.4 %collective-permute-done.43 = bf16[2,2,96,768]{3,2,1,0:T(8,128)(2,1)S(1)} collective-permute-done((bf16[2,2,96,768]{3,2,1,0:T(8,128)(2,1)S(1)}, bf16[2,2,96,768]{3,2,1,0:T(8,128)(2,1)S(1)}, u32[]{:S(2)}, u32[]{:S(2)}) %collective-permute-start.43) | collective-permute-done | bytes 589856 | tf_op jit(solution)/shard_map/mlp_grads/ppermute | solution.py:34
  341.3 9.2 %collective-permute-done.41 = bf16[2,4,96,768]{3,2,1,0:T(8,128)(2,1)S(1)} collective-permute-done((bf16[2,4,96,768]{3,2,1,0:T(8,128)(2,1)S(1)}, bf16[2,4,96,768]{3,2,1,0:T(8,128)(2,1)S(1)}, u32[]{:S(2)}, u32[]{:S(2)}) %collective-permute-start.41) | collective-permute-done | bytes 1179680 | tf_op jit(solution)/shard_map/attn_grads/ppermute | solution.py:34
  350.4 7.1 %collective-permute-done.45 = bf16[2,4,32,768]{3,2,1,0:T(8,128)(2,1)S(1)} collective-permute-done((bf16[2,4,32,768]{3,2,1,0:T(8,128)(2,1)S(1)}, bf16[2,4,32,768]{3,2,1,0:T(8,128)(2,1)S(1)}, u32[]{:S(2)}, u32[]{:S(2)}) %collective-permute-start.45) | collective-permute-done | bytes 393248 | tf_op jit(solution)/shard_map/embed_grads/ppermute | solution.py:34
  360.8 2.9 collective-permute-start.48
  369.9 4.8 collective-permute-done.46
  374.7 3.3 collective-permute-start.53
  382.5 10.7 %collective-permute-done.49 = bf16[2,128,768]{2,1,0:T(8,128)(2,1)} collective-permute-done((bf16[2,128,768]{2,1,0:T(8,128)(2,1)}, bf16[2,128,768]{2,1,0:T(8,128)(2,1)}, u32[]{:S(2)}, u32[]{:S(2)}) %collective-permute-start.49) | collective-permute-done | bytes 393248 | tf_op jit(solution)/shard_map/last_grads/ppermute | solution.py:34
  401.7 10.3 %collective-permute-done.51 = bf16[128,768]{1,0:T(8,128)(2,1)S(1)} collective-permute-done((bf16[128,768]{1,0:T(8,128)(2,1)S(1)}, bf16[128,768]{1,0:T(8,128)(2,1)S(1)}, u32[]{:S(2)}, u32[]{:S(2)}) %collective-permute-start.51) | collective-permute-done | bytes 196640 | tf_op jit(solution)/shard_map/last_grads/ppermute | solution.py:34
  412.1 7.2 %collective-permute-done.53 = bf16[16,96,768]{2,1,0:T(8,128)(2,1)} collective-permute-done((bf16[16,96,768]{2,1,0:T(8,128)(2,1)}, bf16[16,96,768]{2,1,0:T(8,128)(2,1)}, u32[]{:S(2)}, u32[]{:S(2)}) %collective-permute-start.53) | collective-permute-done | bytes 2359328 | tf_op jit(solution)/shard_map/mlp_moments/ppermute | solution.py:34
  421.7 4.4 collective-permute-done.54
  428.3 3.2 pad_maximum_fusion.3
  436.1 3.1 collective-permute-start.60
  443.1 3.5 collective-permute-done.61
  456.3 15.5 %orthogonal_rows.2 = f32[96,768]{1,0:T(8,128)S(1)} custom-call(f32[1,1]{1,0:T(1,128)} %bitcast.146.factor_ref, bf16[768,768]{1,0:T(8,128)(2,1)S(1)} %bitcast.359, bf16[768,768]{1,0:T(8,128)(2,1)S(1)} %bitcast.360), custom_call_target="tpu_custom_call" | custom-call | flops 16307453952 | bytes 2359296 | tf_op jit(solution)/shard_map/orthogonal_rows/pallas_call | solution.py:539
  471.8 23.8 %orthogonal_rows.3 = f32[192,768]{1,0:T(8,128)S(1)} custom-call(f32[1,1]{1,0:T(1,128)} %bitcast.146.factor_ref, bf16[1536,768]{1,0:T(8,128)(2,1)} %bitcast.149.refs_0_, bf16[1536,768]{1,0:T(8,128)(2,1)} %bitcast.150.refs_1_, bf16[1536,768]{1,0:T(8,128)(2,1)} %bitcast.151.refs_2_, bf16[1536,768]{1,0:T(8,128)(2,1)} %bitcast.152.refs_3_), custom_call_target="tpu_custom_call" | custom-call | flops 11777605632 | bytes 9437184 | tf_op jit(solution)/shard_map/orthogonal_rows/pallas_call | solution.py:539
  497.9 4.9 fusion.119
  (595 shorter events, 177.6 us)
Async XLA Ops:
  2.7 13.2 %collective-permute-start = (bf16[128,768]{1,0:T(8,128)(2,1)S(1)}, bf16[128,768]{1,0:T(8,128)(2,1)S(1)}, u32[]{:S(2)}, u32[]{:S(2)}) collective-permute-start(bf16[128,768]{1,0:T(8,128)(2,1)S(1)} %pad_maximum_fusion.24), channel_id=1, source_target_pairs={{0,16},{1,17},{2,18},{3,19},{4,20},{5,21},{6,22},{7,23},{8,24},{9,... | collective-permute-start | bytes 589832 | tf_op jit(solution)/shard_map/attn_weights/ppermute | solution.py:34
  15.9 10.4 %collective-permute-start.1 = (bf16[2,128,768]{2,1,0:T(8,128)(2,1)S(1)}, bf16[2,128,768]{2,1,0:T(8,128)(2,1)S(1)}, u32[]{:S(2)}, u32[]{:S(2)}) collective-permute-start(bf16[2,128,768]{2,1,0:T(8,128)(2,1)S(1)} %maximum_select_fusion.10), channel_id=1, source_target_pairs={{0,8},{1,9},{2,10},{3,11},{4,12},{5,13},{6,14},{7,15},{8,0},{9,1},... | collective-permute-start | bytes 1179656 | tf_op jit(solution)/shard_map/attn_weights/ppermute | solution.py:34
  26.4 17.4 %collective-permute-start.2 = (bf16[4,128,768]{2,1,0:T(8,128)(2,1)S(1)}, bf16[4,128,768]{2,1,0:T(8,128)(2,1)S(1)}, u32[]{:S(2)}, u32[]{:S(2)}) collective-permute-start(bf16[4,128,768]{2,1,0:T(8,128)(2,1)S(1)} %bitcast.369), channel_id=1, source_target_pairs={{0,2},{1,5},{2,0},{3,7},{4,6},{5,1},{6,4},{7,3},{8,10},{9,13},{10,... | collective-permute-start | bytes 2359304 | tf_op jit(solution)/shard_map/attn_weights/ppermute | solution.py:34
  27.7 16.1 %collective-permute-start.3 = (bf16[1,96,1536]{2,1,0:T(8,128)(2,1)S(1)}, bf16[1,96,1536]{2,1,0:T(8,128)(2,1)S(1)}, u32[]{:S(2)}, u32[]{:S(2)}) collective-permute-start(bf16[1,96,1536]{2,1,0:T(8,128)(2,1)S(1)} %convert_bitcast_fusion.1), channel_id=1, source_target_pairs={{0,16},{1,17},{2,18},{3,19},{4,20},{5,21},{6,22},{7,23},{8,24},{9,... | collective-permute-start | bytes 884744 | tf_op jit(solution)/shard_map/mlp_weights/ppermute | solution.py:34
  45.3 21.0 %collective-permute-start.4 = (bf16[2,4,128,768]{3,2,1,0:T(8,128)(2,1)}, bf16[2,4,128,768]{3,2,1,0:T(8,128)(2,1)}, u32[]{:S(2)}, u32[]{:S(2)}) collective-permute-start(bf16[2,4,128,768]{3,2,1,0:T(8,128)(2,1)} %pad_maximum_fusion.4), channel_id=1, source_target_pairs={{0,4},{1,3},{2,6},{3,1},{4,0},{5,7},{6,2},{7,5},{8,12},{9,11},{10,... | collective-permute-start | bytes 4718600 | tf_op jit(solution)/shard_map/attn_weights/ppermute | solution.py:34
  50.4 15.8 %collective-permute-start.5 = (bf16[2,96,1536]{2,1,0:T(8,128)(2,1)}, bf16[2,96,1536]{2,1,0:T(8,128)(2,1)}, u32[]{:S(2)}, u32[]{:S(2)}) collective-permute-start(bf16[2,96,1536]{2,1,0:T(8,128)(2,1)} %pad_maximum_fusion.13), channel_id=1, source_target_pairs={{0,8},{1,9},{2,10},{3,11},{4,12},{5,13},{6,14},{7,15},{8,0},{9,1},... | collective-permute-start | bytes 1769480 | tf_op jit(solution)/shard_map/mlp_weights/ppermute | solution.py:34
  68.0 7.0 %collective-permute-start.6 = (bf16[4,4,128,768]{3,2,1,0:T(8,128)(2,1)S(1)}, bf16[4,4,128,768]{3,2,1,0:T(8,128)(2,1)S(1)}, u32[]{:S(2)}, u32[]{:S(2)}) collective-permute-start(bf16[4,4,128,768]{3,2,1,0:T(8,128)(2,1)S(1)} %pad_maximum_fusion.1), channel_id=1, source_target_pairs={{0,1},{1,0},{2,3},{3,2},{4,5},{5,4},{6,7},{7,6},{8,9},{9,8},{10,11... | collective-permute-start | bytes 9437192 | tf_op jit(solution)/shard_map/attn_weights/ppermute | solution.py:34
  70.0 15.8 %collective-permute-start.8 = (bf16[2,2,96,768]{3,2,1,0:T(8,128)(2,1)S(1)}, bf16[2,2,96,768]{3,2,1,0:T(8,128)(2,1)S(1)}, u32[]{:S(2)}, u32[]{:S(2)}) collective-permute-start(bf16[2,2,96,768]{3,2,1,0:T(8,128)(2,1)S(1)} %get-tuple-element.124), channel_id=1, source_target_pairs={{0,8},{1,9},{2,10},{3,11},{4,12},{5,13},{6,14},{7,15},{8,0},{9,1},... | collective-permute-start | bytes 1769480 | tf_op jit(solution)/shard_map/head/ppermute | solution.py:34
  72.2 16.3 %collective-permute-start.7 = (bf16[4,96,1536]{2,1,0:T(8,128)(2,1)S(1)}, bf16[4,96,1536]{2,1,0:T(8,128)(2,1)S(1)}, u32[]{:S(2)}, u32[]{:S(2)}) collective-permute-start(bf16[4,96,1536]{2,1,0:T(8,128)(2,1)S(1)} %pad_maximum_fusion.5), channel_id=1, source_target_pairs={{0,2},{1,5},{2,0},{3,7},{4,6},{5,1},{6,4},{7,3},{8,10},{9,13},{10,... | collective-permute-start | bytes 3538952 | tf_op jit(solution)/shard_map/mlp_weights/ppermute | solution.py:34
  89.8 33.0 %collective-permute-start.10 = (bf16[8,96,1536]{2,1,0:T(8,128)(2,1)S(1)}, bf16[8,96,1536]{2,1,0:T(8,128)(2,1)}, u32[]{:S(2)}, u32[]{:S(2)}) collective-permute-start(bf16[8,96,1536]{2,1,0:T(8,128)(2,1)S(1)} %pad_maximum_fusion.2), channel_id=1, source_target_pairs={{0,4},{1,3},{2,6},{3,1},{4,0},{5,7},{6,2},{7,5},{8,12},{9,11},{10,... | collective-permute-start | bytes 7077896 | tf_op jit(solution)/shard_map/mlp_weights/ppermute | solution.py:34
  90.3 19.6 %collective-permute-start.9 = (bf16[8,96,1536]{2,1,0:T(8,128)(2,1)S(1)}, bf16[8,96,1536]{2,1,0:T(8,128)(2,1)S(1)}, u32[]{:S(2)}, u32[]{:S(2)}) collective-permute-start(bf16[8,96,1536]{2,1,0:T(8,128)(2,1)S(1)} %pad_maximum_fusion.2), channel_id=1, source_target_pairs={{0,1},{1,0},{2,3},{3,2},{4,5},{5,4},{6,7},{7,6},{8,9},{9,8},{10,11... | collective-permute-start | bytes 7077896 | tf_op jit(solution)/shard_map/mlp_weights/ppermute | solution.py:34
  91.5 31.4 %collective-permute-start.11 = (bf16[2,2,96,768]{3,2,1,0:T(8,128)(2,1)S(1)}, bf16[2,2,96,768]{3,2,1,0:T(8,128)(2,1)S(1)}, u32[]{:S(2)}, u32[]{:S(2)}) collective-permute-start(bf16[2,2,96,768]{3,2,1,0:T(8,128)(2,1)S(1)} %get-tuple-element.310), channel_id=1, source_target_pairs={{0,16},{1,17},{2,18},{3,19},{4,20},{5,21},{6,22},{7,23},{8,24},{9,... | collective-permute-start | bytes 1769480 | tf_op jit(solution)/shard_map/head/ppermute | solution.py:34
  123.6 6.9 %collective-permute-start.12 = (bf16[8,96,1536]{2,1,0:T(8,128)(2,1)}, bf16[8,96,1536]{2,1,0:T(8,128)(2,1)}, u32[]{:S(2)}, u32[]{:S(2)}) collective-permute-start(bf16[8,96,1536]{2,1,0:T(8,128)(2,1)} %collective-permute-done.10), channel_id=1, source_target_pairs={{0,1},{1,0},{2,3},{3,2},{4,5},{5,4},{6,7},{7,6},{8,9},{9,8},{10,11... | collective-permute-start | bytes 7077896 | tf_op jit(solution)/shard_map/mlp_weights/ppermute | solution.py:34
  129.0 16.6 %collective-permute-start.14 = (bf16[2,2,96,768]{3,2,1,0:T(8,128)(2,1)}, bf16[2,2,96,768]{3,2,1,0:T(8,128)(2,1)}, u32[]{:S(2)}, u32[]{:S(2)}) collective-permute-start(bf16[2,2,96,768]{3,2,1,0:T(8,128)(2,1)} %get-tuple-element.308), channel_id=1, source_target_pairs={{0,4},{1,5},{2,6},{3,7},{4,0},{5,1},{6,2},{7,3},{8,12},{9,13},{10,... | collective-permute-start | bytes 1769480 | tf_op jit(solution)/shard_map/head/ppermute | solution.py:34
  132.0 16.4 %collective-permute-start.15 = (bf16[2,96,768]{2,1,0:T(8,128)(2,1)}, bf16[2,96,768]{2,1,0:T(8,128)(2,1)}, u32[]{:S(2)}, u32[]{:S(2)}) collective-permute-start(bf16[2,96,768]{2,1,0:T(8,128)(2,1)} %pad_maximum_fusion.21), channel_id=1, source_target_pairs={{0,16},{1,17},{2,18},{3,19},{4,20},{5,21},{6,22},{7,23},{8,24},{9,... | collective-permute-start | bytes 884744 | tf_op jit(solution)/shard_map/mlp_moments/ppermute | solution.py:34
  132.5 13.2 %collective-permute-start.16 = (bf16[1,96,768]{2,1,0:T(8,128)(2,1)}, bf16[1,96,768]{2,1,0:T(8,128)(2,1)}, u32[]{:S(2)}, u32[]{:S(2)}) collective-permute-start(bf16[1,96,768]{2,1,0:T(8,128)(2,1)} %convert_bitcast_fusion.2), channel_id=1, source_target_pairs={{0,2},{1,5},{2,0},{3,7},{4,6},{5,1},{6,4},{7,3},{8,10},{9,13},{10,... | collective-permute-start | bytes 442376 | tf_op jit(solution)/shard_map/attn_moments/ppermute | solution.py:34
  159.7 5.9 %collective-permute-start.19 = (bf16[2,2,16,896]{3,2,0,1:T(8,128)(2,1)S(1)}, bf16[2,2,16,896]{3,2,0,1:T(8,128)(2,1)S(1)}, u32[]{:S(2)}, u32[]{:S(2)}) collective-permute-start(bf16[2,2,16,896]{3,2,0,1:T(8,128)(2,1)S(1)} %maximum_select_fusion.14), channel_id=1, source_target_pairs={{0,2},{1,5},{2,0},{3,7},{4,6},{5,1},{6,4},{7,3},{8,10},{9,13},{10,... | collective-permute-start | bytes 344072 | tf_op jit(solution)/shard_map/pooled/ppermute | solution.py:34
  165.6 6.1 %collective-permute-start.20 = (bf16[2,2,2,16,896]{4,3,0,1,2:T(8,128)(2,1)S(1)}, bf16[2,2,2,16,896]{4,3,0,1,2:T(8,128)(2,1)S(1)}, u32[]{:S(2)}, u32[]{:S(2)}) collective-permute-start(bf16[2,2,2,16,896]{4,3,0,1,2:T(8,128)(2,1)S(1)} %maximum_select_fusion.12), channel_id=1, source_target_pairs={{0,4},{1,3},{2,6},{3,1},{4,0},{5,7},{6,2},{7,5},{8,12},{9,11},{10,... | collective-permute-start | bytes 688136 | tf_op jit(solution)/shard_map/pooled/ppermute | solution.py:34
  208.6 6.0 %collective-permute-start.28 = (bf16[2,4,16,768]{3,2,1,0:T(8,128)(2,1)}, bf16[2,4,16,768]{3,2,1,0:T(8,128)(2,1)}, u32[]{:S(2)}, u32[]{:S(2)}) collective-permute-start(bf16[2,4,16,768]{3,2,1,0:T(8,128)(2,1)} %pad_maximum_fusion.25), channel_id=1, source_target_pairs={{0,4},{1,3},{2,6},{3,1},{4,0},{5,7},{6,2},{7,5},{8,12},{9,11},{10,... | collective-permute-start | bytes 589832 | tf_op jit(solution)/shard_map/d_pooled/ppermute | solution.py:34
  235.0 11.7 %collective-permute-start.32 = (bf16[4,96,768]{2,1,0:T(8,128)(2,1)S(1)}, bf16[4,96,768]{2,1,0:T(8,128)(2,1)S(1)}, u32[]{:S(2)}, u32[]{:S(2)}) collective-permute-start(bf16[4,96,768]{2,1,0:T(8,128)(2,1)S(1)} %pad_maximum_fusion.14), channel_id=1, source_target_pairs={{0,8},{1,9},{2,10},{3,11},{4,12},{5,13},{6,14},{7,15},{8,0},{9,1},... | collective-permute-start | bytes 1769480 | tf_op jit(solution)/shard_map/mlp_moments/ppermute | solution.py:34
  235.2 11.5 %collective-permute-start.33 = (bf16[2,96,768]{2,1,0:T(8,128)(2,1)S(1)}, bf16[2,96,768]{2,1,0:T(8,128)(2,1)S(1)}, u32[]{:S(2)}, u32[]{:S(2)}) collective-permute-start(bf16[2,96,768]{2,1,0:T(8,128)(2,1)S(1)} %pad_maximum_fusion.22), channel_id=1, source_target_pairs={{0,4},{1,3},{2,6},{3,1},{4,0},{5,7},{6,2},{7,5},{8,12},{9,11},{10,... | collective-permute-start | bytes 884744 | tf_op jit(solution)/shard_map/attn_moments/ppermute | solution.py:34
  246.7 8.2 %collective-permute-start.34 = (bf16[3072,768]{1,0:T(8,128)(2,1)}, bf16[3072,768]{1,0:T(8,128)(2,1)S(1)}, u32[]{:S(2)}, u32[]{:S(2)}) collective-permute-start(bf16[3072,768]{1,0:T(8,128)(2,1)} %get-tuple-element.159), channel_id=1, source_target_pairs={{0,1},{1,0},{2,3},{3,2},{4,5},{5,4},{6,7},{7,6},{8,9},{9,8},{10,11... | collective-permute-start | bytes 14155784 | tf_op jit(solution)/shard_map/mlp_grads/ppermute | solution.py:34
  248.0 14.5 %collective-permute-start.35 = (bf16[4,96,768]{2,1,0:T(8,128)(2,1)S(1)}, bf16[4,96,768]{2,1,0:T(8,128)(2,1)S(1)}, u32[]{:S(2)}, u32[]{:S(2)}) collective-permute-start(bf16[4,96,768]{2,1,0:T(8,128)(2,1)S(1)} %pad_maximum_fusion.15), channel_id=1, source_target_pairs={{0,1},{1,0},{2,3},{3,2},{4,5},{5,4},{6,7},{7,6},{8,9},{9,8},{10,11... | collective-permute-start | bytes 1769480 | tf_op jit(solution)/shard_map/attn_moments/ppermute | solution.py:34
  253.3 41.8 %collective-permute-start.37 = (bf16[8,96,768]{2,1,0:T(8,128)(2,1)}, bf16[8,96,768]{2,1,0:T(8,128)(2,1)}, u32[]{:S(2)}, u32[]{:S(2)}) collective-permute-start(bf16[8,96,768]{2,1,0:T(8,128)(2,1)} %pad_maximum_fusion.6), channel_id=1, source_target_pairs={{0,2},{1,5},{2,0},{3,7},{4,6},{5,1},{6,4},{7,3},{8,10},{9,13},{10,... | collective-permute-start | bytes 3538952 | tf_op jit(solution)/shard_map/mlp_moments/ppermute | solution.py:34
  262.6 32.5 %collective-permute-start.36 = (bf16[1536,768]{1,0:T(8,128)(2,1)}, bf16[1536,768]{1,0:T(8,128)(2,1)}, u32[]{:S(2)}, u32[]{:S(2)}) collective-permute-start(bf16[1536,768]{1,0:T(8,128)(2,1)} %kept_grads.2), channel_id=1, source_target_pairs={{0,4},{1,3},{2,6},{3,1},{4,0},{5,7},{6,2},{7,5},{8,12},{9,11},{10,... | collective-permute-start | bytes 7077896 | tf_op jit(solution)/shard_map/mlp_grads/ppermute | solution.py:34
  273.9 21.2 %collective-permute-start.38 = (bf16[2,2,96,768]{3,2,1,0:T(8,128)(2,1)}, bf16[2,2,96,768]{3,2,1,0:T(8,128)(2,1)S(1)}, u32[]{:S(2)}, u32[]{:S(2)}) collective-permute-start(bf16[2,2,96,768]{3,2,1,0:T(8,128)(2,1)} %get-tuple-element.172), channel_id=1, source_target_pairs={{0,8},{1,9},{2,10},{3,11},{4,12},{5,13},{6,14},{7,15},{8,0},{9,1},... | collective-permute-start | bytes 1769480 | tf_op jit(solution)/shard_map/head_grads/ppermute | solution.py:34
  298.8 20.1 %collective-permute-start.40 = (bf16[4,4,96,768]{3,2,0,1:T(8,128)(2,1)S(1)}, bf16[4,4,96,768]{3,2,0,1:T(8,128)(2,1)S(1)}, u32[]{:S(2)}, u32[]{:S(2)}) collective-permute-start(bf16[4,4,96,768]{3,2,0,1:T(8,128)(2,1)S(1)} %fusion), channel_id=1, source_target_pairs={{0,1},{1,0},{2,3},{3,2},{4,5},{5,4},{6,7},{7,6},{8,9},{9,8},{10,11... | collective-permute-start | bytes 7077896 | tf_op jit(solution)/shard_map/attn_grads/ppermute | solution.py:34
  302.6 16.3 %collective-permute-start.39 = (bf16[768,768]{1,0:T(8,128)(2,1)S(1)}, bf16[768,768]{1,0:T(8,128)(2,1)S(1)}, u32[]{:S(2)}, u32[]{:S(2)}) collective-permute-start(bf16[768,768]{1,0:T(8,128)(2,1)S(1)} %slice.721), channel_id=1, source_target_pairs={{0,2},{1,5},{2,0},{3,7},{4,6},{5,1},{6,4},{7,3},{8,10},{9,13},{10,... | collective-permute-start | bytes 3538952 | tf_op jit(solution)/shard_map/mlp_grads/ppermute | solution.py:34
  322.5 14.9 %collective-permute-start.43 = (bf16[2,2,96,768]{3,2,1,0:T(8,128)(2,1)S(1)}, bf16[2,2,96,768]{3,2,1,0:T(8,128)(2,1)S(1)}, u32[]{:S(2)}, u32[]{:S(2)}) collective-permute-start(bf16[2,2,96,768]{3,2,1,0:T(8,128)(2,1)S(1)} %slice.722), channel_id=1, source_target_pairs={{0,8},{1,9},{2,10},{3,11},{4,12},{5,13},{6,14},{7,15},{8,0},{9,1},... | collective-permute-start | bytes 1769480 | tf_op jit(solution)/shard_map/mlp_grads/ppermute | solution.py:34
  323.3 14.4 %collective-permute-start.44 = (bf16[2,2,96,768]{3,2,1,0:T(8,128)(2,1)}, bf16[2,2,96,768]{3,2,1,0:T(8,128)(2,1)S(1)}, u32[]{:S(2)}, u32[]{:S(2)}) collective-permute-start(bf16[2,2,96,768]{3,2,1,0:T(8,128)(2,1)} %get-tuple-element.183), channel_id=1, source_target_pairs={{0,4},{1,5},{2,6},{3,7},{4,0},{5,1},{6,2},{7,3},{8,12},{9,13},{10,... | collective-permute-start | bytes 1769480 | tf_op jit(solution)/shard_map/head_grads/ppermute | solution.py:34
  327.3 11.3 %collective-permute-start.42 = (bf16[4,4,32,768]{3,2,0,1:T(8,128)(2,1)S(1)}, bf16[4,4,32,768]{3,2,0,1:T(8,128)(2,1)S(1)}, u32[]{:S(2)}, u32[]{:S(2)}) collective-permute-start(bf16[4,4,32,768]{3,2,0,1:T(8,128)(2,1)S(1)} %fusion.31), channel_id=1, source_target_pairs={{0,1},{1,0},{2,3},{3,2},{4,5},{5,4},{6,7},{7,6},{8,9},{9,8},{10,11... | collective-permute-start | bytes 2359304 | tf_op jit(solution)/shard_map/embed_grads/ppermute | solution.py:34
  328.6 21.9 %collective-permute-start.41 = (bf16[2,4,96,768]{3,2,1,0:T(8,128)(2,1)S(1)}, bf16[2,4,96,768]{3,2,1,0:T(8,128)(2,1)S(1)}, u32[]{:S(2)}, u32[]{:S(2)}) collective-permute-start(bf16[2,4,96,768]{3,2,1,0:T(8,128)(2,1)S(1)} %pad_maximum_fusion.7), channel_id=1, source_target_pairs={{0,4},{1,3},{2,6},{3,1},{4,0},{5,7},{6,2},{7,5},{8,12},{9,11},{10,... | collective-permute-start | bytes 3538952 | tf_op jit(solution)/shard_map/attn_grads/ppermute | solution.py:34
  338.9 18.6 %collective-permute-start.45 = (bf16[2,4,32,768]{3,2,1,0:T(8,128)(2,1)S(1)}, bf16[2,4,32,768]{3,2,1,0:T(8,128)(2,1)S(1)}, u32[]{:S(2)}, u32[]{:S(2)}) collective-permute-start(bf16[2,4,32,768]{3,2,1,0:T(8,128)(2,1)S(1)} %pad_maximum_fusion.20), channel_id=1, source_target_pairs={{0,4},{1,3},{2,6},{3,1},{4,0},{5,7},{6,2},{7,5},{8,12},{9,11},{10,... | collective-permute-start | bytes 1179656 | tf_op jit(solution)/shard_map/embed_grads/ppermute | solution.py:34
  340.5 19.4 %collective-permute-start.47 = (bf16[2,1,96,768]{3,2,1,0:T(8,128)(2,1)S(1)}, bf16[2,1,96,768]{3,2,1,0:T(8,128)(2,1)S(1)}, u32[]{:S(2)}, u32[]{:S(2)}) collective-permute-start(bf16[2,1,96,768]{3,2,1,0:T(8,128)(2,1)S(1)} %slice.723), channel_id=1, source_target_pairs={{0,16},{1,17},{2,18},{3,19},{4,20},{5,21},{6,22},{7,23},{8,24},{9,... | collective-permute-start | bytes 884744 | tf_op jit(solution)/shard_map/mlp_grads/ppermute | solution.py:34
  358.3 16.4 %collective-permute-start.46 = (bf16[4,128,768]{2,1,0:T(8,128)(2,1)S(1)}, bf16[4,128,768]{2,1,0:T(8,128)(2,1)S(1)}, u32[]{:S(2)}, u32[]{:S(2)}) collective-permute-start(bf16[4,128,768]{2,1,0:T(8,128)(2,1)S(1)} %pad_maximum_fusion.12), channel_id=1, source_target_pairs={{0,2},{1,5},{2,0},{3,7},{4,6},{5,1},{6,4},{7,3},{8,10},{9,13},{10,... | collective-permute-start | bytes 2359304 | tf_op jit(solution)/shard_map/last_grads/ppermute | solution.py:34
  360.8 9.1 %collective-permute-start.48 = (bf16[2,96,768]{2,1,0:T(8,128)(2,1)S(1)}, bf16[2,96,768]{2,1,0:T(8,128)(2,1)S(1)}, u32[]{:S(2)}, u32[]{:S(2)}) collective-permute-start(bf16[2,96,768]{2,1,0:T(8,128)(2,1)S(1)} %get-tuple-element.255), channel_id=1, source_target_pairs={{0,16},{1,17},{2,18},{3,19},{4,20},{5,21},{6,22},{7,23},{8,24},{9,... | collective-permute-start | bytes 884744 | tf_op jit(solution)/shard_map/mlp_grads_all/ppermute | solution.py:34
  374.7 44.6 %collective-permute-start.53 = (bf16[16,96,768]{2,1,0:T(8,128)(2,1)}, bf16[16,96,768]{2,1,0:T(8,128)(2,1)}, u32[]{:S(2)}, u32[]{:S(2)}) collective-permute-start(bf16[16,96,768]{2,1,0:T(8,128)(2,1)} %constant_dynamic-update-slice_fusion), channel_id=1, source_target_pairs={{0,4},{1,3},{2,6},{3,1},{4,0},{5,7},{6,2},{7,5},{8,12},{9,11},{10,... | collective-permute-start | bytes 7077896 | tf_op jit(solution)/shard_map/mlp_moments/ppermute | solution.py:34
  378.8 14.4 %collective-permute-start.50 = (bf16[4,96,768]{2,1,0:T(8,128)(2,1)}, bf16[4,96,768]{2,1,0:T(8,128)(2,1)}, u32[]{:S(2)}, u32[]{:S(2)}) collective-permute-start(bf16[4,96,768]{2,1,0:T(8,128)(2,1)} %pad_maximum_fusion.16), channel_id=1, source_target_pairs={{0,8},{1,9},{2,10},{3,11},{4,12},{5,13},{6,14},{7,15},{8,0},{9,1},... | collective-permute-start | bytes 1769480 | tf_op jit(solution)/shard_map/mlp_grads_all/ppermute | solution.py:34
  381.0 12.2 %collective-permute-start.49 = (bf16[2,128,768]{2,1,0:T(8,128)(2,1)}, bf16[2,128,768]{2,1,0:T(8,128)(2,1)}, u32[]{:S(2)}, u32[]{:S(2)}) collective-permute-start(bf16[2,128,768]{2,1,0:T(8,128)(2,1)} %fusion.49), channel_id=1, source_target_pairs={{0,8},{1,9},{2,10},{3,11},{4,12},{5,13},{6,14},{7,15},{8,0},{9,1},... | collective-permute-start | bytes 1179656 | tf_op jit(solution)/shard_map/last_grads/ppermute | solution.py:34
  395.6 16.5 %collective-permute-start.52 = (bf16[8,96,768]{2,1,0:T(8,128)(2,1)}, bf16[8,96,768]{2,1,0:T(8,128)(2,1)}, u32[]{:S(2)}, u32[]{:S(2)}) collective-permute-start(bf16[8,96,768]{2,1,0:T(8,128)(2,1)} %pad_maximum_fusion.8), channel_id=1, source_target_pairs={{0,2},{1,5},{2,0},{3,7},{4,6},{5,1},{6,4},{7,3},{8,10},{9,13},{10,... | collective-permute-start | bytes 3538952 | tf_op jit(solution)/shard_map/mlp_grads_all/ppermute | solution.py:34
  399.6 12.5 %collective-permute-start.51 = (bf16[128,768]{1,0:T(8,128)(2,1)S(1)}, bf16[128,768]{1,0:T(8,128)(2,1)S(1)}, u32[]{:S(2)}, u32[]{:S(2)}) collective-permute-start(bf16[128,768]{1,0:T(8,128)(2,1)S(1)} %fusion.61), channel_id=1, source_target_pairs={{0,16},{1,17},{2,18},{3,19},{4,20},{5,21},{6,22},{7,23},{8,24},{9,... | collective-permute-start | bytes 589832 | tf_op jit(solution)/shard_map/last_grads/ppermute | solution.py:34
  419.6 6.5 %collective-permute-start.55 = (bf16[1,96,768]{2,1,0:T(8,128)(2,1)S(1)}, bf16[1,96,768]{2,1,0:T(8,128)(2,1)S(1)}, u32[]{:S(2)}, u32[]{:S(2)}) collective-permute-start(bf16[1,96,768]{2,1,0:T(8,128)(2,1)S(1)} %fusion.73), channel_id=1, source_target_pairs={{0,2},{1,5},{2,0},{3,7},{4,6},{5,1},{6,4},{7,3},{8,10},{9,13},{10,... | collective-permute-start | bytes 442376 | tf_op jit(solution)/shard_map/attn_grads_all/ppermute | solution.py:34
  420.5 5.6 %collective-permute-start.54 = (f32[16,768]{1,0:T(8,128)S(1)}, f32[16,768]{1,0:T(8,128)S(1)}, u32[]{:S(2)}, u32[]{:S(2)}) collective-permute-start(f32[16,768]{1,0:T(8,128)S(1)} %concatenate.231), channel_id=1, source_target_pairs={{0,2},{1,3},{2,0},{3,1},{4,6},{5,7},{6,4},{7,5},{8,10},{9,11},{10,... | collective-permute-start | bytes 147464 | tf_op jit(solution)/shard_map/small_sums/ppermute | solution.py:34
  426.1 7.3 %collective-permute-start.57 = (bf16[2,96,768]{2,1,0:T(8,128)(2,1)S(1)}, bf16[2,96,768]{2,1,0:T(8,128)(2,1)S(1)}, u32[]{:S(2)}, u32[]{:S(2)}) collective-permute-start(bf16[2,96,768]{2,1,0:T(8,128)(2,1)S(1)} %pad_maximum_fusion.23), channel_id=1, source_target_pairs={{0,4},{1,3},{2,6},{3,1},{4,0},{5,7},{6,2},{7,5},{8,12},{9,11},{10,... | collective-permute-start | bytes 884744 | tf_op jit(solution)/shard_map/attn_grads_all/ppermute | solution.py:34
  427.8 5.6 %collective-permute-start.56 = (f32[16,768]{1,0:T(8,128)S(1)}, f32[16,768]{1,0:T(8,128)S(1)}, u32[]{:S(2)}, u32[]{:S(2)}) collective-permute-start(f32[16,768]{1,0:T(8,128)S(1)} %add.629), channel_id=1, source_target_pairs={{0,4},{1,5},{2,6},{3,7},{4,0},{5,1},{6,2},{7,3},{8,12},{9,13},{10,... | collective-permute-start | bytes 147464 | tf_op jit(solution)/shard_map/small_sums/ppermute | solution.py:34
  440.1 31.7 %collective-permute-start.62 = (bf16[16,96,768]{2,1,0:T(8,128)(2,1)}, bf16[16,96,768]{2,1,0:T(8,128)(2,1)}, u32[]{:S(2)}, u32[]{:S(2)}) collective-permute-start(bf16[16,96,768]{2,1,0:T(8,128)(2,1)} %pad_maximum_fusion.3), channel_id=1, source_target_pairs={{0,4},{1,3},{2,6},{3,1},{4,0},{5,7},{6,2},{7,5},{8,12},{9,11},{10,... | collective-permute-start | bytes 7077896 | tf_op jit(solution)/shard_map/mlp_grads_all/ppermute | solution.py:34
  449.2 46.4 %collective-permute-start.63 = (bf16[2,2,96,768]{3,2,1,0:T(8,128)(2,1)}, bf16[2,2,96,768]{3,2,1,0:T(8,128)(2,1)S(1)}, u32[]{:S(2)}, u32[]{:S(2)}) collective-permute-start(bf16[2,2,96,768]{3,2,1,0:T(8,128)(2,1)} %get-tuple-element.211), channel_id=1, source_target_pairs={{0,16},{1,17},{2,18},{3,19},{4,20},{5,21},{6,22},{7,23},{8,24},{9,... | collective-permute-start | bytes 1769480 | tf_op jit(solution)/shard_map/head_grads/ppermute | solution.py:34
  496.0 7.6 %collective-permute-start.64 = (f32[96,768]{1,0:T(8,128)S(1)}, f32[96,768]{1,0:T(8,128)S(1)}, u32[]{:S(2)}, u32[]{:S(2)}) collective-permute-start(f32[96,768]{1,0:T(8,128)S(1)} %slice.423), channel_id=1, source_target_pairs={{0,1},{1,0},{2,3},{3,2},{4,5},{5,4},{6,7},{7,6},{8,9},{9,8},{10,11... | collective-permute-start | bytes 884744 | tf_op jit(solution)/shard_map/small/ppermute | solution.py:34
  (139 other events, 919.4 us)
